TPU v7x, 32 devices: a whole 2x2x4 slice. The times are simulated.
32 devices in a mesh: dp: 8 (over y, x, core), fsdp: 4 (over z).
Axes of the slice: x: 2, y: 2, z: 4, core: 2. Of those that a mesh axis runs over, the one named last changes fastest.
Arguments:
- tokens: bfloat16 [3, 16384, 512], P(None, ('dp', 'fsdp')), may hold values from -6 to 6
- memory: bfloat16 [3, 16384, 512], P(None, ('dp', 'fsdp')), may hold values from -6 to 6
- cotangent: bfloat16 [3, 16384, 512], P(None, ('dp', 'fsdp')), may hold values from -6 to 6
- lengths: int32 [3, 8, 4], P(None, 'dp'), may hold values from 1 to 1024, 2048 in all within a row
- seq_order: int32 [3, 8, 4], P(None, 'dp'), may hold values from 0 to 3, each once within a row
- memory_pick: int32 [3, 8, 4], P(None, 'dp'), may hold values from 0 to 1
- self_attn: bfloat16 [2048, 512], P(('dp', 'fsdp'))
- cross_attn: bfloat16 [2048, 512], P(('dp', 'fsdp'))
- ffn_in: bfloat16 [512, 2048], P(('dp', 'fsdp')), may hold values from -0.25 to 0.25
- ffn_in_bias: bfloat16 [2048], P(('dp', 'fsdp')), may hold values from -1.75 to 1.75
- ffn_out: bfloat16 [2048, 512], P(('dp', 'fsdp')), may hold values from -0.125 to 0.125
- ffn_out_bias: bfloat16 [512], P(('dp', 'fsdp')), may hold values from -1.75 to 1.75
- norm_gain: bfloat16 [512, 3], P(('dp', 'fsdp')), may hold values from 0.5 to 1.5
- norm_bias: bfloat16 [512, 3], P(('dp', 'fsdp')), may hold values from -1.75 to 1.75
Outputs:
- layer_output: float32 [3, 16384, 512], P(None, ('dp', 'fsdp'))
- input_grad: float32 [3, 16384, 512], P(None, ('dp', 'fsdp'))
- memory_grad: float32 [3, 16384, 512], P(None, ('dp', 'fsdp'))
- self_attn_grad: float32 [2048, 512], P(('dp', 'fsdp'))
- cross_attn_grad: float32 [2048, 512], P(('dp', 'fsdp'))
- ffn_in_grad: float32 [512, 2048], P(('dp', 'fsdp'))
- ffn_in_bias_grad: float32 [2048], P(('dp', 'fsdp'))
- ffn_out_grad: float32 [2048, 512], P(('dp', 'fsdp'))
- ffn_out_bias_grad: float32 [512], P(('dp', 'fsdp'))
- norm_gain_grad: float32 [512, 3], P(('dp', 'fsdp'))
- norm_bias_grad: float32 [512, 3], P(('dp', 'fsdp'))
Inputs may be any that keep to these rules, and one draw needn't show every extreme that they name: Each row holds the 4 sequence lengths of one group; they sum to 2048 and the longest is exactly 1024. `seq_order`: each row is a permutation of the 4 sequences of one group.
All inputs are finite; a program needn't handle non-finite values.
Results may differ from a plain program's by a relative error of at most 0.025.
The roundings to bfloat16 on the way count: a program that leaves them out, or rounds other values in their place, can miss the bound.
Values may be sent and summed in bfloat16 or wider, within the bound.
No kernel may reach another device: no remote copies, remote signals or barrier semaphores. Data moves between devices by JAX's collectives and lax.ppermute only.
A program may use at most 576 MiB of HBM per device.

v0:
```python
import math

import jax
import jax.numpy as jnp
from jax import lax
from jax.sharding import PartitionSpec as P

D = 512
HEAD_DIM = 64
FF = 2048
MEM_LEN = 1024


def project(left, right):
    return jnp.dot(left, right, preferred_element_type=jnp.float32)


def contract_rows(left, right):
    return lax.dot_general(
        left, right, (((0,), (0,)), ((), ())), preferred_element_type=jnp.float32
    )


def times_transposed(left, right):
    return lax.dot_general(
        left, right, (((1,), (1,)), ((), ())), preferred_element_type=jnp.float32
    )


def split_four(stack):
    return [stack[block_index * D : (block_index + 1) * D] for block_index in range(4)]


def head_split(matrix):
    return matrix.reshape(matrix.shape[0], -1, HEAD_DIM)


def gelu_slope(value):
    factor = math.sqrt(2.0 / math.pi)
    inner = factor * (value + 0.044715 * value * value * value)
    tangent = jnp.tanh(inner)
    return 0.5 * (1.0 + tangent) + 0.5 * value * (1.0 - tangent * tangent) * factor * (
        1.0 + 3.0 * 0.044715 * value * value
    )


def layer_norm(resid, gain, shift):
    center = resid - jnp.mean(resid, axis=-1, keepdims=True)
    inv_std = lax.rsqrt(jnp.mean(center * center, axis=-1, keepdims=True) + 1e-06)
    normed = center * inv_std
    return (normed * gain + shift, normed, inv_std)


def norm_back(grad_out, normed, inv_std, gain):
    scaled = grad_out * gain
    return inv_std * (
        scaled
        - jnp.mean(scaled, axis=-1, keepdims=True)
        - normed * jnp.mean(scaled * normed, axis=-1, keepdims=True)
    )


def masked_scores(queries, key_rows, allowed):
    scores = jnp.einsum(
        "qhd,khd->hqk",
        head_split(queries),
        head_split(key_rows),
        preferred_element_type=jnp.float32,
    ) * HEAD_DIM ** (-0.5)
    return jnp.where(allowed[None], scores, -1e30)


def attend_forward(queries, key_rows, value_rows, allowed):
    scores = masked_scores(queries, key_rows, allowed)
    highest = jnp.max(scores, axis=-1, keepdims=True)
    exponent = jnp.exp(scores - highest)
    totals = jnp.sum(exponent, axis=-1, keepdims=True)
    softmax_w = (exponent / totals).astype(jnp.bfloat16)
    mixed = jnp.einsum(
        "hqk,khd->qhd", softmax_w, head_split(value_rows), preferred_element_type=jnp.float32
    )
    return (mixed.reshape(queries.shape[0], -1), (highest + jnp.log(totals))[..., 0])


def attend_backward(queries, key_rows, value_rows, allowed, log_total, grad_mixed):
    softmax_w = jnp.exp(masked_scores(queries, key_rows, allowed) - log_total[..., None])
    grad_heads = head_split(grad_mixed)
    value_grad = jnp.einsum(
        "hqk,qhd->khd",
        softmax_w.astype(jnp.bfloat16),
        grad_heads,
        preferred_element_type=jnp.float32,
    )
    soft_grad = jnp.einsum(
        "qhd,khd->hqk", grad_heads, head_split(value_rows), preferred_element_type=jnp.float32
    )
    score_grad = (
        softmax_w * (soft_grad - jnp.sum(softmax_w * soft_grad, axis=-1, keepdims=True))
    ).astype(jnp.bfloat16)
    query_grad = jnp.einsum(
        "hqk,khd->qhd", score_grad, head_split(key_rows), preferred_element_type=jnp.float32
    ) * HEAD_DIM ** (-0.5)
    key_grad = jnp.einsum(
        "hqk,qhd->khd", score_grad, head_split(queries), preferred_element_type=jnp.float32
    ) * HEAD_DIM ** (-0.5)
    return (
        query_grad.reshape(queries.shape[0], -1),
        key_grad.reshape(key_rows.shape[0], -1),
        value_grad.reshape(key_rows.shape[0], -1),
    )


def processing_rows(seq_lengths, seq_rows, position):
    ends = jnp.cumsum(seq_lengths)
    starts = ends - seq_lengths
    proc_len = seq_lengths[seq_rows]
    proc_end = jnp.cumsum(proc_len)
    proc_start = proc_end - proc_len
    slot = jnp.sum((position[:, None] >= proc_end[None, :]).astype(jnp.int32), axis=1)
    seg_proc = seq_rows[slot]
    order_rows = starts[seg_proc] + position - proc_start[slot]
    return (seg_proc, order_rows)


def local(
    tokens,
    memory,
    cotangent,
    lengths,
    seq_order,
    memory_pick,
    self_attn,
    cross_attn,
    ffn_in,
    ffn_in_bias,
    ffn_out,
    ffn_out_bias,
    norm_gain,
    norm_bias,
):
    group_size = lax.axis_size("fsdp")
    member = lax.axis_index("fsdp")
    tok_rows = tokens.shape[1]
    mem_rows = memory.shape[1]
    group_rows = tok_rows * group_size
    mem_total = mem_rows * group_size
    position = jnp.arange(group_rows, dtype=jnp.int32)
    local_rows = member * tok_rows + jnp.arange(tok_rows, dtype=jnp.int32)
    memory_owner = jnp.arange(mem_total, dtype=jnp.int32) // MEM_LEN
    grad_sums = [
        jnp.zeros((4 * D, D), jnp.float32),
        jnp.zeros((4 * D, D), jnp.float32),
        jnp.zeros((D, FF), jnp.float32),
        jnp.zeros((FF,), jnp.float32),
        jnp.zeros((FF, D), jnp.float32),
        jnp.zeros((D,), jnp.float32),
        jnp.zeros((D, 3), jnp.float32),
        jnp.zeros((D, 3), jnp.float32),
    ]
    output_list = []
    token_grads = []
    memory_grads = []
    for batch_index in range(tokens.shape[0]):
        weights = (
            lax.all_gather(self_attn, ("dp", "fsdp"), axis=0, tiled=True),
            lax.all_gather(cross_attn, ("dp", "fsdp"), axis=0, tiled=True),
            lax.all_gather(ffn_in, ("dp", "fsdp"), axis=0, tiled=True),
            lax.all_gather(ffn_in_bias, ("dp", "fsdp"), axis=0, tiled=True),
            lax.all_gather(ffn_out, ("dp", "fsdp"), axis=0, tiled=True),
            lax.all_gather(ffn_out_bias, ("dp", "fsdp"), axis=0, tiled=True),
            lax.all_gather(norm_gain, ("dp", "fsdp"), axis=0, tiled=True),
            lax.all_gather(norm_bias, ("dp", "fsdp"), axis=0, tiled=True),
        )
        self_w, cross_w, first_w, first_b, second_w, second_b, gains_b, shifts_b = weights
        gains = gains_b.astype(jnp.float32)
        shifts = shifts_b.astype(jnp.float32)
        self_query, self_key, self_value, self_out = split_four(self_w)
        cross_query, cross_key, cross_value, cross_out = split_four(cross_w)
        token_in = tokens[batch_index]
        memory_in = memory[batch_index]
        seg_proc, order_rows = processing_rows(
            lengths[batch_index, 0], seq_order[batch_index, 0], position
        )
        seg_local = seg_proc[local_rows]
        memory_of_all = memory_pick[batch_index, 0][seg_proc]
        memory_of = memory_of_all[local_rows]
        self_mask = seg_local[:, None] == seg_proc[None, :]
        cross_mask = memory_of[:, None] == memory_owner[None, :]
        queries = project(token_in, self_query).astype(jnp.bfloat16)
        key_rows = project(token_in, self_key).astype(jnp.bfloat16)
        value_rows = project(token_in, self_value).astype(jnp.bfloat16)
        key_all, value_all = (
            lax.all_gather(key_rows, "fsdp", axis=0, tiled=True),
            lax.all_gather(value_rows, "fsdp", axis=0, tiled=True),
        )
        mixed, self_total = attend_forward(queries, key_all, value_all, self_mask)
        mixed_b = mixed.astype(jnp.bfloat16)
        hidden_one, normed_one, inv_one = layer_norm(
            token_in.astype(jnp.float32) + project(mixed_b, self_out), gains[:, 0], shifts[:, 0]
        )
        hidden_one_b = hidden_one.astype(jnp.bfloat16)
        cross_queries = project(hidden_one_b, cross_query).astype(jnp.bfloat16)
        cross_keys = project(memory_in, cross_key).astype(jnp.bfloat16)
        cross_values = project(memory_in, cross_value).astype(jnp.bfloat16)
        cross_key_all, cross_value_all = (
            lax.all_gather(cross_keys, "fsdp", axis=0, tiled=True),
            lax.all_gather(cross_values, "fsdp", axis=0, tiled=True),
        )
        cross_mixed, cross_total = attend_forward(
            cross_queries, cross_key_all, cross_value_all, cross_mask
        )
        cross_mixed_b = cross_mixed.astype(jnp.bfloat16)
        hidden_two, normed_two, inv_two = layer_norm(
            hidden_one + project(cross_mixed_b, cross_out), gains[:, 1], shifts[:, 1]
        )
        hidden_two_b = hidden_two.astype(jnp.bfloat16)
        pre_act = project(hidden_two_b, first_w) + first_b.astype(jnp.float32)
        active_b = jax.nn.gelu(pre_act, approximate=True).astype(jnp.bfloat16)
        result, normed_three, inv_three = layer_norm(
            hidden_two + (project(active_b, second_w) + second_b.astype(jnp.float32)),
            gains[:, 2],
            shifts[:, 2],
        )
        result_all, cotangent_all = (
            lax.all_gather(result.astype(jnp.bfloat16), "fsdp", axis=0, tiled=True).astype(
                result.dtype
            ),
            lax.all_gather(
                cotangent[batch_index].astype(jnp.float32).astype(jnp.bfloat16),
                "fsdp",
                axis=0,
                tiled=True,
            ).astype(jnp.float32),
        )
        inverse = jnp.zeros((group_rows,), jnp.int32).at[order_rows].set(position)
        output_list.append(result_all[inverse[local_rows]])
        grad_out = cotangent_all[order_rows[local_rows]]
        weights = (
            lax.all_gather(self_attn, ("dp", "fsdp"), axis=0, tiled=True),
            lax.all_gather(cross_attn, ("dp", "fsdp"), axis=0, tiled=True),
            lax.all_gather(ffn_in, ("dp", "fsdp"), axis=0, tiled=True),
            lax.all_gather(ffn_in_bias, ("dp", "fsdp"), axis=0, tiled=True),
            lax.all_gather(ffn_out, ("dp", "fsdp"), axis=0, tiled=True),
            lax.all_gather(ffn_out_bias, ("dp", "fsdp"), axis=0, tiled=True),
            lax.all_gather(norm_gain, ("dp", "fsdp"), axis=0, tiled=True),
            lax.all_gather(norm_bias, ("dp", "fsdp"), axis=0, tiled=True),
        )
        self_w, cross_w, first_w, first_b, second_w, second_b, gains_b, shifts_b = weights
        gains = gains_b.astype(jnp.float32)
        self_query, self_key, self_value, self_out = split_four(self_w)
        cross_query, cross_key, cross_value, cross_out = split_four(cross_w)
        gain_three = jnp.sum(grad_out * normed_three, axis=0)
        shift_three = jnp.sum(grad_out, axis=0)
        grad_third = norm_back(grad_out, normed_three, inv_three, gains[:, 2])
        ffn_grad_b = grad_third.astype(jnp.bfloat16)
        second_w_grad = contract_rows(active_b, ffn_grad_b)
        second_b_grad = jnp.sum(ffn_grad_b.astype(jnp.float32), axis=0)
        act_grad = times_transposed(ffn_grad_b, second_w)
        pre_grad_b = (act_grad * gelu_slope(pre_act)).astype(jnp.bfloat16)
        first_w_grad = contract_rows(hidden_two_b, pre_grad_b)
        first_b_grad = jnp.sum(pre_grad_b.astype(jnp.float32), axis=0)
        hidden_two_grad = grad_third + times_transposed(pre_grad_b, first_w)
        gain_two = jnp.sum(hidden_two_grad * normed_two, axis=0)
        shift_two = jnp.sum(hidden_two_grad, axis=0)
        grad_second = norm_back(hidden_two_grad, normed_two, inv_two, gains[:, 1])
        cross_branch_b = grad_second.astype(jnp.bfloat16)
        cross_out_grad = contract_rows(cross_mixed_b, cross_branch_b)
        cross_mixed_grad = times_transposed(cross_branch_b, cross_out).astype(jnp.bfloat16)
        cq_grad, ck_all_grad, cv_all_grad = attend_backward(
            cross_queries, cross_key_all, cross_value_all, cross_mask, cross_total, cross_mixed_grad
        )
        ck_sum, cv_sum = (
            lax.psum_scatter(
                ck_all_grad.astype(jnp.bfloat16), "fsdp", scatter_dimension=0, tiled=True
            ).astype(jnp.float32),
            lax.psum_scatter(
                cv_all_grad.astype(jnp.bfloat16), "fsdp", scatter_dimension=0, tiled=True
            ).astype(jnp.float32),
        )
        cq_grad_b = cq_grad.astype(jnp.bfloat16)
        ck_grad_b = ck_sum.astype(jnp.bfloat16)
        cv_grad_b = cv_sum.astype(jnp.bfloat16)
        cross_grads = jnp.concatenate(
            [
                contract_rows(hidden_one_b, cq_grad_b),
                contract_rows(memory_in, ck_grad_b),
                contract_rows(memory_in, cv_grad_b),
                cross_out_grad,
            ],
            axis=0,
        )
        memory_grads.append(
            times_transposed(ck_grad_b, cross_key) + times_transposed(cv_grad_b, cross_value)
        )
        hidden_one_grad = grad_second + times_transposed(cq_grad_b, cross_query)
        gain_one = jnp.sum(hidden_one_grad * normed_one, axis=0)
        shift_one = jnp.sum(hidden_one_grad, axis=0)
        grad_first = norm_back(hidden_one_grad, normed_one, inv_one, gains[:, 0])
        self_branch_b = grad_first.astype(jnp.bfloat16)
        self_out_grad = contract_rows(mixed_b, self_branch_b)
        mixed_grad = times_transposed(self_branch_b, self_out).astype(jnp.bfloat16)
        sq_grad, sk_all_grad, sv_all_grad = attend_backward(
            queries, key_all, value_all, self_mask, self_total, mixed_grad
        )
        sk_sum, sv_sum = (
            lax.psum_scatter(
                sk_all_grad.astype(jnp.bfloat16), "fsdp", scatter_dimension=0, tiled=True
            ).astype(jnp.float32),
            lax.psum_scatter(
                sv_all_grad.astype(jnp.bfloat16), "fsdp", scatter_dimension=0, tiled=True
            ).astype(jnp.float32),
        )
        sq_grad_b = sq_grad.astype(jnp.bfloat16)
        sk_grad_b = sk_sum.astype(jnp.bfloat16)
        sv_grad_b = sv_sum.astype(jnp.bfloat16)
        self_grads = jnp.concatenate(
            [
                contract_rows(token_in, sq_grad_b),
                contract_rows(token_in, sk_grad_b),
                contract_rows(token_in, sv_grad_b),
                self_out_grad,
            ],
            axis=0,
        )
        token_grads.append(
            grad_first
            + times_transposed(sq_grad_b, self_query)
            + times_transposed(sk_grad_b, self_key)
            + times_transposed(sv_grad_b, self_value)
        )
        grad_sums = [
            grad_sums[0] + self_grads,
            grad_sums[1] + cross_grads,
            grad_sums[2] + first_w_grad,
            grad_sums[3] + first_b_grad,
            grad_sums[4] + second_w_grad,
            grad_sums[5] + second_b_grad,
            grad_sums[6] + jnp.stack([gain_one, gain_two, gain_three], axis=1),
            grad_sums[7] + jnp.stack([shift_one, shift_two, shift_three], axis=1),
        ]
    reduced = (
        lax.psum_scatter(grad_sums[0], ("dp", "fsdp"), scatter_dimension=0, tiled=True),
        lax.psum_scatter(grad_sums[1], ("dp", "fsdp"), scatter_dimension=0, tiled=True),
        lax.psum_scatter(grad_sums[2], ("dp", "fsdp"), scatter_dimension=0, tiled=True),
        lax.psum_scatter(grad_sums[3], ("dp", "fsdp"), scatter_dimension=0, tiled=True),
        lax.psum_scatter(grad_sums[4], ("dp", "fsdp"), scatter_dimension=0, tiled=True),
        lax.psum_scatter(grad_sums[5], ("dp", "fsdp"), scatter_dimension=0, tiled=True),
        lax.psum_scatter(grad_sums[6], ("dp", "fsdp"), scatter_dimension=0, tiled=True),
        lax.psum_scatter(grad_sums[7], ("dp", "fsdp"), scatter_dimension=0, tiled=True),
    )
    return (
        jnp.stack(output_list),
        jnp.stack(token_grads),
        jnp.stack(memory_grads),
        reduced[0],
        reduced[1],
        reduced[2],
        reduced[3],
        reduced[4],
        reduced[5],
        reduced[6],
        reduced[7],
    )


def solution(mesh):
    in_specs = (
        P(None, ("dp", "fsdp"), None),
        P(None, ("dp", "fsdp"), None),
        P(None, ("dp", "fsdp"), None),
        P(None, "dp", None),
        P(None, "dp", None),
        P(None, "dp", None),
        P(("dp", "fsdp"), None),
        P(("dp", "fsdp"), None),
        P(("dp", "fsdp"), None),
        P(("dp", "fsdp")),
        P(("dp", "fsdp"), None),
        P(("dp", "fsdp")),
        P(("dp", "fsdp"), None),
        P(("dp", "fsdp"), None),
    )
    out_specs = (
        P(None, ("dp", "fsdp"), None),
        P(None, ("dp", "fsdp"), None),
        P(None, ("dp", "fsdp"), None),
        P(("dp", "fsdp"), None),
        P(("dp", "fsdp"), None),
        P(("dp", "fsdp"), None),
        P(("dp", "fsdp")),
        P(("dp", "fsdp"), None),
        P(("dp", "fsdp")),
        P(("dp", "fsdp"), None),
        P(("dp", "fsdp"), None),
    )
    return jax.shard_map(local, mesh=mesh, in_specs=in_specs, out_specs=out_specs, check_vma=False)
```

profile of v0, /device:TPU:12, one launch (start us, length us, event | category | flops | bytes accessed | tf_op | source)
XLA Modules:
  0.0 2585.3 jit_solution(2145613076138458272)
XLA Ops:
  12.5 55.2 %all-gather.28.cloned.1.call-done = bf16[2048,512]{1,0:T(8,128)(2,1)} async-done(((bf16[64,512]{1,0:T(8,128)(2,1)}), bf16[2048,512]{1,0:T(8,128)(2,1)}) %all-gather.28.cloned.1.call-update) | async-done | bytes 2097168 | tf_op jit(solution)/shard_map/all_gather | solution.py:165
  72.8 53.1 %all-gather.34.cloned.1.call-done = bf16[2048,512]{1,0:T(8,128)(2,1)} async-done(((bf16[64,512]{1,0:T(8,128)(2,1)}), bf16[2048,512]{1,0:T(8,128)(2,1)}) %all-gather.34.cloned.1.call-update) | async-done | bytes 2097168 | tf_op jit(solution)/shard_map/all_gather | solution.py:166
  144.0 41.2 %all-reduce.5 = (bf16[512]{0:T(512)(128)(2,1)S(1)}, bf16[2048]{0:T(1024)(128)(2,1)S(1)}) all-reduce(bf16[512]{0:T(512)(128)(2,1)S(1)} %dynamic-update-slice.1, bf16[2048]{0:T(1024)(128)(2,1)S(1)} %dynamic-update-slice), channel_id=1, replica_groups=mesh['dp'=8,'fsdp'=4] {'dp','fsdp'}, use_global_device_ids=true, to_apply=%add.1 | all-reduce | flops 2560 | bytes 10240
  259.1 65.7 %all-gather.3 = bf16[32,16,3]{1,2,0:T(4,128)(2,1)S(1)} all-gather(bf16[1,16,3]{1,2,0:T(4,128)(2,1)S(1)} %bitcast.708), channel_id=1, replica_groups=mesh['dp'=8,'fsdp'=4] {'dp','fsdp'}, dimensions={0}, use_global_device_ids=true | all-gather | bytes 3168 | tf_op jit(solution)/shard_map/all_gather | solution.py:171
  325.0 65.3 %all-gather.4 = bf16[32,16,3]{1,2,0:T(4,128)(2,1)S(1)} all-gather(bf16[1,16,3]{1,2,0:T(4,128)(2,1)S(1)} %bitcast.709), channel_id=1, replica_groups=mesh['dp'=8,'fsdp'=4] {'dp','fsdp'}, dimensions={0}, use_global_device_ids=true | all-gather | bytes 3168 | tf_op jit(solution)/shard_map/all_gather | solution.py:172
  455.2 15.3 fusion.322
  488.1 15.4 fusion.117
  511.4 15.2 fusion.324
  544.6 15.4 fusion.116
  574.9 38.7 %all-gather.48.cloned.1.call-done = bf16[2048,512]{1,0:T(8,128)(2,1)} async-done(((bf16[512,512]{1,0:T(8,128)(2,1)}), bf16[2048,512]{1,0:T(8,128)(2,1)}) %all-gather.48.cloned.1.call-update) | async-done | bytes 2097168 | tf_op jit(solution)/shard_map/all_gather | solution.py:193
  617.6 15.5 fusion.327
  664.3 14.8 fusion.119
  680.8 25.1 all-gather.52.cloned.1.call-done
  711.0 15.2 fusion.329
  756.4 15.2 fusion.118
  778.9 19.3 all-gather.32.cloned.1.call-done
  802.1 15.5 fusion.317
  848.2 16.1 fusion.121
  866.3 24.0 all-gather.38.cloned.1.call-done
  896.2 15.2 fusion.319
  940.6 15.3 fusion.120
  993.4 15.1 fusion.89
  1010.3 15.6 fusion.83
  1029.1 15.2 fusion.95
  1044.3 22.3 multiply_reduce_fusion.1
  1066.7 28.2 %multiply_convert_fusion.1 = bf16[8,512,2048]{2,1,0:T(8,128)(2,1)} fusion(f32[8,512,2048]{2,1,0:T(8,128)} %get-tuple-element.253, f32[8,512,2048]{2,1,0:T(8,128)} %get-tuple-element.235, f32[8,512]{1,0:T(8,128)S(1)} %get-tuple-element.252, f32[8,512]{1,0:T(8,128)S(1)} %log_add_fusion.1), kind=kLoop, calls=%fused_computation.27 | loop fusion | flops 33554432 | bytes 83918848 | tf_op jit(solution)/shard_map/convert_element_type | solution.py:99
  1105.1 22.6 multiply_reduce_fusion.5
  1127.8 28.3 %multiply_convert_fusion.5 = bf16[8,512,2048]{2,1,0:T(8,128)(2,1)} fusion(f32[8,512,2048]{2,1,0:T(8,128)} %get-tuple-element.255, f32[8,512,2048]{2,1,0:T(8,128)} %get-tuple-element.225, f32[8,512]{1,0:T(8,128)S(1)} %get-tuple-element.254, f32[8,512]{1,0:T(8,128)S(1)} %log_add_fusion.5), kind=kLoop, calls=%fused_computation.39 | loop fusion | flops 33554432 | bytes 83918848 | tf_op jit(solution)/shard_map/convert_element_type | solution.py:99
  1166.5 22.2 multiply_reduce_fusion.3
  1188.8 28.7 %multiply_convert_fusion.3 = bf16[8,512,2048]{2,1,0:T(8,128)(2,1)} fusion(f32[8,512,2048]{2,1,0:T(8,128)} %get-tuple-element.257, f32[8,512,2048]{2,1,0:T(8,128)} %get-tuple-element.245, f32[8,512]{1,0:T(8,128)S(1)} %get-tuple-element.256, f32[8,512]{1,0:T(8,128)S(1)} %copy-done.120), kind=kLoop, calls=%fused_computation.33 | loop fusion | flops 33554432 | bytes 83918848 | tf_op jit(solution)/shard_map/convert_element_type | solution.py:99
  1279.0 15.3 fusion.92
  1296.1 15.2 fusion.86
  1314.2 15.2 fusion.98
  1329.4 22.2 multiply_reduce_fusion
  1351.6 28.3 %multiply_convert_fusion = bf16[8,512,2048]{2,1,0:T(8,128)(2,1)} fusion(f32[8,512,2048]{2,1,0:T(8,128)} %get-tuple-element.261, f32[8,512,2048]{2,1,0:T(8,128)} %get-tuple-element.231, f32[8,512]{1,0:T(8,128)S(1)} %get-tuple-element.260, f32[8,512]{1,0:T(8,128)S(1)} %log_add_fusion), kind=kLoop, calls=%fused_computation.24 | loop fusion | flops 33554432 | bytes 83918848 | tf_op jit(solution)/shard_map/convert_element_type | solution.py:99
  1390.2 22.3 multiply_reduce_fusion.4
  1413.0 28.2 %multiply_convert_fusion.4 = bf16[8,512,2048]{2,1,0:T(8,128)(2,1)} fusion(f32[8,512,2048]{2,1,0:T(8,128)} %get-tuple-element.265, f32[8,512,2048]{2,1,0:T(8,128)} %get-tuple-element.221, f32[8,512]{1,0:T(8,128)S(1)} %get-tuple-element.264, f32[8,512]{1,0:T(8,128)S(1)} %log_add_fusion.4), kind=kLoop, calls=%fused_computation.36 | loop fusion | flops 33554432 | bytes 83918848 | tf_op jit(solution)/shard_map/convert_element_type | solution.py:99
  1451.5 22.2 multiply_reduce_fusion.2
  1473.8 28.3 %multiply_convert_fusion.2 = bf16[8,512,2048]{2,1,0:T(8,128)(2,1)} fusion(f32[8,512,2048]{2,1,0:T(8,128)} %get-tuple-element.263, f32[8,512,2048]{2,1,0:T(8,128)} %get-tuple-element.241, f32[8,512]{1,0:T(8,128)S(1)} %get-tuple-element.262, f32[8,512]{1,0:T(8,128)S(1)} %log_add_fusion.2), kind=kLoop, calls=%fused_computation.30 | loop fusion | flops 33554432 | bytes 83918848 | tf_op jit(solution)/shard_map/convert_element_type | solution.py:99
  1679.3 43.1 %all-reduce.4 = (f32[2048]{0:T(1024)S(1)}, f32[512]{0:T(512)S(1)}) all-reduce(f32[2048]{0:T(1024)S(1)} %add_add_fusion.2, f32[512]{0:T(512)S(1)} %add_add_fusion.3), channel_id=20, replica_groups=mesh['dp'=8,'fsdp'=4] {'dp','fsdp'}, use_global_device_ids=true, to_apply=%region_84.85.clone | all-reduce | flops 2560 | bytes 20480
  1732.1 109.4 %reduce-scatter.57.cloned.1.call-done = f32[16,3]{1,0:T(8,128)} async-done(((f32[512,3]{1,0:T(8,128)}), f32[16,3]{1,0:T(8,128)}) %reduce-scatter.57.cloned.1.call-update) | async-done | bytes 208
  1842.8 45.0 %all-gather.54.cloned.1.call-done = bf16[2048,512]{0,1:T(8,128)(2,1)} async-done(((bf16[512,512]{0,1:T(8,128)(2,1)}), bf16[2048,512]{0,1:T(8,128)(2,1)}) %all-gather.54.cloned.1.call-update) | async-done | bytes 2097168 | tf_op jit(solution)/shard_map/all_gather | solution.py:225
  1896.2 37.9 %all-gather.44.cloned.1.call-done = bf16[2048,512]{0,1:T(8,128)(2,1)} async-done(((bf16[512,512]{0,1:T(8,128)(2,1)}), bf16[2048,512]{0,1:T(8,128)(2,1)}) %all-gather.44.cloned.1.call-update) | async-done | bytes 2097168 | tf_op jit(solution)/shard_map/all_gather | solution.py:225
  1943.2 37.1 %all-gather.64.cloned.1.call-done = bf16[2048,512]{0,1:T(8,128)(2,1)} async-done(((bf16[512,512]{0,1:T(8,128)(2,1)}), bf16[2048,512]{0,1:T(8,128)(2,1)}) %all-gather.64.cloned.1.call-update) | async-done | bytes 2097168 | tf_op jit(solution)/shard_map/all_gather | solution.py:225
  2006.8 122.0 %reduce-scatter.53.cloned.1.call-done = f32[64,512]{1,0:T(8,128)} async-done(((f32[2048,512]{1,0:T(8,128)}), f32[64,512]{1,0:T(8,128)}) %reduce-scatter.53.cloned.1.call-update) | async-done | bytes 131088 | tf_op jit(solution)/shard_map/reduce_scatter | solution.py:346
  2128.8 149.4 %reduce-scatter.51.cloned.1.call-done = f32[16,2048]{1,0:T(8,128)} async-done(((f32[512,2048]{1,0:T(8,128)}), f32[16,2048]{1,0:T(8,128)}) %reduce-scatter.51.cloned.1.call-update) | async-done | bytes 131088 | tf_op jit(solution)/shard_map/reduce_scatter | solution.py:344
  2278.2 150.0 %reduce-scatter.49.cloned.1.call-done = f32[64,512]{1,0:T(8,128)} async-done(((f32[2048,512]{1,0:T(8,128)}), f32[64,512]{1,0:T(8,128)}) %reduce-scatter.49.cloned.1.call-update) | async-done | bytes 131088 | tf_op jit(solution)/shard_map/reduce_scatter | solution.py:343
  2428.2 150.1 %reduce-scatter.47.cloned.1.call-done = f32[64,512]{1,0:T(8,128)} async-done(((f32[2048,512]{1,0:T(8,128)}), f32[64,512]{1,0:T(8,128)}) %reduce-scatter.47.cloned.1.call-update) | async-done | bytes 131088 | tf_op jit(solution)/shard_map/reduce_scatter | solution.py:342
  (858 shorter events, 756.4 us)
Async XLA Ops:
  7.2 60.5 %all-gather.28.cloned.1.call-start = ((), (), s32[]{:S(2)}) async-start(), calls=%async_computation.18 | async-start | bytes 2162688 | tf_op jit(solution)/shard_map/all_gather | solution.py:165
  7.9 118.0 %all-gather.34.cloned.1.call-start = ((), (), s32[]{:S(2)}) async-start(), calls=%async_computation.21 | async-start | bytes 2162688 | tf_op jit(solution)/shard_map/all_gather | solution.py:166
  8.7 401.1 %all-gather.68.cloned.1.call-start = ((), (), s32[]{:S(2)}) async-start(), calls=%async_computation.54 | async-start | bytes 2621440 | tf_op jit(solution)/shard_map/all_gather | solution.py:228
  11.3 408.5 %all-gather.70.cloned.1.call-start = ((), (), s32[]{:S(2)}) async-start(), calls=%async_computation.55 | async-start | bytes 2621440 | tf_op jit(solution)/shard_map/all_gather | solution.py:228
  11.9 419.7 %all-gather.66.cloned.1.call-start = ((), (), s32[]{:S(2)}) async-start(), calls=%async_computation.53 | async-start | bytes 2621440 | tf_op jit(solution)/shard_map/all_gather | solution.py:228
  12.4 438.5 %all-gather.58.cloned.1.call-start = ((), (), s32[]{:S(2)}) async-start(), calls=%async_computation.33 | async-start | bytes 2621440 | tf_op jit(solution)/shard_map/all_gather | solution.py:193
  70.1 414.0 %all-gather.56.cloned.1.call-start = ((), (), s32[]{:S(2)}) async-start(), calls=%async_computation.32 | async-start | bytes 2621440 | tf_op jit(solution)/shard_map/all_gather | solution.py:194
  72.8 432.7 %all-gather.62.cloned.1.call-start = ((), (), s32[]{:S(2)}) async-start(), calls=%async_computation.35 | async-start | bytes 2621440 | tf_op jit(solution)/shard_map/all_gather | solution.py:206
  128.4 412.2 %all-gather.60.cloned.1.call-start = ((), (), s32[]{:S(2)}) async-start(), calls=%async_computation.34 | async-start | bytes 2621440 | tf_op jit(solution)/shard_map/all_gather | solution.py:207
  131.0 431.5 %all-gather.40.cloned.1.call-start = ((), (), s32[]{:S(2)}) async-start(), calls=%async_computation.24 | async-start | bytes 2162688 | tf_op jit(solution)/shard_map/all_gather | solution.py:167
  131.5 436.5 %all-gather.42.cloned.1.call-start = ((), (), s32[]{:S(2)}) async-start(), calls=%async_computation.25 | async-start | bytes 2162688 | tf_op jit(solution)/shard_map/all_gather | solution.py:169
  132.3 481.3 %all-gather.48.cloned.1.call-start = ((), (), s32[]{:S(2)}) async-start(), calls=%async_computation.28 | async-start | bytes 2621440 | tf_op jit(solution)/shard_map/all_gather | solution.py:193
  134.7 525.7 %all-gather.46.cloned.1.call-start = ((), (), s32[]{:S(2)}) async-start(), calls=%async_computation.27 | async-start | bytes 2621440 | tf_op jit(solution)/shard_map/all_gather | solution.py:194
  137.1 568.9 %all-gather.52.cloned.1.call-start = ((), (), s32[]{:S(2)}) async-start(), calls=%async_computation.30 | async-start | bytes 2621440 | tf_op jit(solution)/shard_map/all_gather | solution.py:206
  139.6 612.5 %all-gather.50.cloned.1.call-start = ((), (), s32[]{:S(2)}) async-start(), calls=%async_computation.29 | async-start | bytes 2621440 | tf_op jit(solution)/shard_map/all_gather | solution.py:207
  142.1 656.1 %all-gather.32.cloned.1.call-start = ((), (), s32[]{:S(2)}) async-start(), calls=%async_computation.20 | async-start | bytes 2621440 | tf_op jit(solution)/shard_map/all_gather | solution.py:193
  203.9 640.4 %all-gather.30.cloned.1.call-start = ((), (), s32[]{:S(2)}) async-start(), calls=%async_computation.19 | async-start | bytes 2621440 | tf_op jit(solution)/shard_map/all_gather | solution.py:194
  230.7 659.7 %all-gather.38.cloned.1.call-start = ((), (), s32[]{:S(2)}) async-start(), calls=%async_computation.23 | async-start | bytes 2621440 | tf_op jit(solution)/shard_map/all_gather | solution.py:206
  246.5 78.5 %copy-start.220 = (bf16[16,3]{0,1:T(4,128)(2,1)S(1)}, bf16[16,3]{0,1:T(4,128)(2,1)}, u32[]{:S(2)}) copy-start(bf16[16,3]{0,1:T(4,128)(2,1)} %param.27) | copy-start | bytes 292
  399.0 556.9 %copy-start.171 = (f32[512,1]{0,1:T(1,128)}, f32[512,1]{0,1:T(1,128)S(1)}, u32[]{:S(2)}) copy-start(f32[512,1]{0,1:T(1,128)S(1)} %get-tuple-element.138) | copy-start | bytes 6148
  399.6 556.3 %copy-start.156 = (f32[512,1]{0,1:T(1,128)}, f32[512,1]{0,1:T(1,128)S(1)}, u32[]{:S(2)}) copy-start(f32[512,1]{0,1:T(1,128)S(1)} %get-tuple-element.135) | copy-start | bytes 6148
  405.3 531.4 %all-gather.36.cloned.1.call-start = ((), (), s32[]{:S(2)}) async-start(), calls=%async_computation.22 | async-start | bytes 2621440 | tf_op jit(solution)/shard_map/all_gather | solution.py:207
  443.8 1109.0 %reduce-scatter.41.cloned.1.call-start = ((), (), s32[]{:S(2)}) async-start(), calls=%async_computation.46 | async-start | bytes 2621440 | tf_op jit(solution)/shard_map/reduce_scatter | solution.py:276
  679.7 92.0 %copy-start.173 = (f32[512]{0:T(512)}, f32[512]{0:T(512)S(1)}, u32[]{:S(2)}) copy-start(f32[512]{0:T(512)S(1)} %broadcast_multiply_fusion.23) | copy-start | bytes 6148
  680.8 90.8 %copy-start.188 = (f32[512]{0:T(512)}, f32[512]{0:T(512)S(1)}, u32[]{:S(2)}) copy-start(f32[512]{0:T(512)S(1)} %add_rsqrt_fusion.5) | copy-start | bytes 6148
  866.1 89.8 %copy-start.34 = (f32[512,512]{0,1:T(8,128)}, f32[512,512]{0,1:T(8,128)S(1)}, u32[]{:S(2)}) copy-start(f32[512,512]{0,1:T(8,128)S(1)} %get-tuple-element.223) | copy-start | bytes 3145732
  866.2 89.8 %copy-start.176 = (f32[512]{0:T(512)}, f32[512]{0:T(512)S(1)}, u32[]{:S(2)}) copy-start(f32[512]{0:T(512)S(1)} %broadcast_multiply_fusion.26) | copy-start | bytes 6148
  1008.5 546.8 %reduce-scatter.37.cloned.1.call-start = ((), (), s32[]{:S(2)}) async-start(), calls=%async_computation.44 | async-start | bytes 2621440 | tf_op jit(solution)/shard_map/reduce_scatter | solution.py:276
  1025.9 531.9 %reduce-scatter.45.cloned.1.call-start = ((), (), s32[]{:S(2)}) async-start(), calls=%async_computation.48 | async-start | bytes 2621440 | tf_op jit(solution)/shard_map/reduce_scatter | solution.py:276
  1066.6 493.8 %reduce-scatter.43.cloned.1.call-start = ((), (), s32[]{:S(2)}) async-start(), calls=%async_computation.47 | async-start | bytes 2621440 | tf_op jit(solution)/shard_map/reduce_scatter | solution.py:273
  1127.7 435.3 %reduce-scatter.35.cloned.1.call-start = ((), (), s32[]{:S(2)}) async-start(), calls=%async_computation.43 | async-start | bytes 2621440 | tf_op jit(solution)/shard_map/reduce_scatter | solution.py:273
  1188.8 376.8 %reduce-scatter.39.cloned.1.call-start = ((), (), s32[]{:S(2)}) async-start(), calls=%async_computation.45 | async-start | bytes 2621440 | tf_op jit(solution)/shard_map/reduce_scatter | solution.py:273
  1259.3 364.7 %reduce-scatter.29.cloned.1.call-start = ((), (), s32[]{:S(2)}) async-start(), calls=%async_computation.40 | async-start | bytes 2621440 | tf_op jit(solution)/shard_map/reduce_scatter | solution.py:309
  1294.3 332.3 %reduce-scatter.25.cloned.1.call-start = ((), (), s32[]{:S(2)}) async-start(), calls=%async_computation.38 | async-start | bytes 2621440 | tf_op jit(solution)/shard_map/reduce_scatter | solution.py:309
  1311.4 317.7 %reduce-scatter.33.cloned.1.call-start = ((), (), s32[]{:S(2)}) async-start(), calls=%async_computation.42 | async-start | bytes 2621440 | tf_op jit(solution)/shard_map/reduce_scatter | solution.py:309
  1351.6 280.0 %reduce-scatter.31.cloned.1.call-start = ((), (), s32[]{:S(2)}) async-start(), calls=%async_computation.41 | async-start | bytes 2621440 | tf_op jit(solution)/shard_map/reduce_scatter | solution.py:306
  1412.5 221.5 %reduce-scatter.23.cloned.1.call-start = ((), (), s32[]{:S(2)}) async-start(), calls=%async_computation.37 | async-start | bytes 2621440 | tf_op jit(solution)/shard_map/reduce_scatter | solution.py:306
  1473.8 162.8 %reduce-scatter.27.cloned.1.call-start = ((), (), s32[]{:S(2)}) async-start(), calls=%async_computation.39 | async-start | bytes 2621440 | tf_op jit(solution)/shard_map/reduce_scatter | solution.py:306
  1512.7 218.0 %reduce-scatter.55.cloned.1.call-start = ((), (), s32[]{:S(2)}) async-start(), calls=%async_computation.56 | async-start | bytes 270336
  1514.9 326.6 %reduce-scatter.57.cloned.1.call-start = ((), (), s32[]{:S(2)}) async-start(), calls=%async_computation.57 | async-start | bytes 270336
  1515.9 372.0 %all-gather.54.cloned.1.call-start = ((), (), s32[]{:S(2)}) async-start(), calls=%async_computation.31 | async-start | bytes 2621440 | tf_op jit(solution)/shard_map/all_gather | solution.py:225
  1516.6 417.5 %all-gather.44.cloned.1.call-start = ((), (), s32[]{:S(2)}) async-start(), calls=%async_computation.26 | async-start | bytes 2621440 | tf_op jit(solution)/shard_map/all_gather | solution.py:225
  1517.4 462.9 %all-gather.64.cloned.1.call-start = ((), (), s32[]{:S(2)}) async-start(), calls=%async_computation.36 | async-start | bytes 2621440 | tf_op jit(solution)/shard_map/all_gather | solution.py:225
  1518.0 610.9 %reduce-scatter.53.cloned.1.call-start = ((), (), s32[]{:S(2)}) async-start(), calls=%async_computation.52 | async-start | bytes 4325376 | tf_op jit(solution)/shard_map/reduce_scatter | solution.py:346
  1530.2 748.1 %reduce-scatter.51.cloned.1.call-start = ((), (), s32[]{:S(2)}) async-start(), calls=%async_computation.51 | async-start | bytes 4325376 | tf_op jit(solution)/shard_map/reduce_scatter | solution.py:344
  1539.8 888.4 %reduce-scatter.49.cloned.1.call-start = ((), (), s32[]{:S(2)}) async-start(), calls=%async_computation.50 | async-start | bytes 4325376 | tf_op jit(solution)/shard_map/reduce_scatter | solution.py:343
  1573.1 1005.1 %reduce-scatter.47.cloned.1.call-start = ((), (), s32[]{:S(2)}) async-start(), calls=%async_computation.49 | async-start | bytes 4325376 | tf_op jit(solution)/shard_map/reduce_scatter | solution.py:342
  1644.9 78.7 %copy-start.6 = (bf16[2048,512]{1,0:T(8,128)(2,1)S(1)}, bf16[2048,512]{1,0:T(8,128)(2,1)}, u32[]{:S(2)}) copy-start(bf16[2048,512]{1,0:T(8,128)(2,1)} %all-gather.28.cloned.1.call-done) | copy-start | bytes 6291460
  (217 other events, 2279.7 us)
Sparse Core Ops, SparseCore 0:
  10.9 56.6 all-gather.27
  70.6 55.3 all-gather.33
  127.5 44.8 all-gather.67
  173.9 44.7 all-gather.69
  220.1 45.0 all-gather.65
  266.7 45.0 all-gather.57
  313.3 45.0 all-gather.55
  360.0 44.7 all-gather.61
  406.4 44.5 all-gather.59
  453.8 55.9 all-gather.39
  512.7 55.2 all-gather.41
  569.5 44.0 all-gather.47
  615.2 45.0 all-gather.45
  661.7 44.2 all-gather.51
  707.4 44.6 all-gather.49
  753.5 44.6 all-gather.31
  799.6 44.6 all-gather.29
  845.7 44.6 all-gather.37
  891.9 44.7 all-gather.35
  1008.6 41.9 reduce-scatter.40
  1053.0 43.1 reduce-scatter.36
  1098.5 43.1 reduce-scatter.44
  1144.1 43.1 reduce-scatter.42
  1189.5 43.1 reduce-scatter.34
  1259.4 42.0 reduce-scatter.38
  1303.7 43.0 reduce-scatter.28
  1349.1 43.1 reduce-scatter.24
  1394.6 43.1 reduce-scatter.32
  1440.9 43.1 reduce-scatter.30
  1486.2 43.1 reduce-scatter.22
  1532.4 43.1 reduce-scatter.26
  1577.9 131.2 reduce-scatter.54
  1711.3 130.1 reduce-scatter.56
  1843.1 44.7 all-gather.53
  1889.4 44.6 all-gather.43
  1935.5 44.6 all-gather.63
  1982.9 145.8 reduce-scatter.52
  2131.7 146.5 reduce-scatter.50
  2280.9 147.2 reduce-scatter.48
  2431.1 147.1 reduce-scatter.46
where the time goes:
time: 2600 us; the launch traced here: 2590 us
  waiting for transfers between devices  1070 us (41%)
  matrix products  736 us (28%)
  other arithmetic  341 us (13%)
  blocking collectives  215 us (8%)
  local copies, waits for them, and re-layouts  199 us (8%)
    convert_element_type x6, other arithmetic, attend_backward(): score_grad = (softmax_w * (soft_grad - jnp.sum(softmax_w * soft_grad, axi...  170 us
    reduce_scatter x1, waiting for transfers between devices, local(): lax.psum_scatter(grad_sums[0], ('dp', 'fsdp'), scatter_dimension=0, tiled...  150 us
    reduce_scatter x1, waiting for transfers between devices, local(): lax.psum_scatter(grad_sums[1], ('dp', 'fsdp'), scatter_dimension=0, tiled...  150 us
    reduce_scatter x1, waiting for transfers between devices, local(): lax.psum_scatter(grad_sums[2], ('dp', 'fsdp'), scatter_dimension=0, tiled...  149 us
    dot_general x6, matrix products, attend_backward(): jnp.einsum('qhd,khd->hqk', grad_heads, head_split(value_rows), preferred_...  134 us
    reduce_scatter x1, waiting for transfers between devices, local(): lax.psum_scatter(grad_sums[4], ('dp', 'fsdp'), scatter_dimension=0, tiled...  122 us
    all_gather x3, waiting for transfers between devices, local(): lax.all_gather(result.astype(jnp.bfloat16), 'fsdp', axis=0, tiled=True)  120 us
    unnamed x42, waiting for transfers between devices  116 us
  transfers between devices with their start and end apart: 40, of which 19 were waited for; matrix products, arithmetic and copies ran while one was open for 46% of the time, Pallas kernels for 0%

commit v1 on v0

v1 whole, which is shorter than its diff:
```python
import functools
import math

import jax
import jax.numpy as jnp
from jax import lax
from jax.experimental import pallas as pl
from jax.experimental.pallas import tpu as pltpu
from jax.sharding import PartitionSpec as P

D = 512
HEADS = 8
HEAD_DIM = 64
FF = 2048
MEM_LEN = 1024
SEQS = 4
NMEM = 2
GROUP = 2048
PIECE = 512
PIECES = GROUP // PIECE
QB = 256
KB = 256
NEG = -1e30
BLOCKS = 32
BROWS = D * 4 // BLOCKS
bf16 = jnp.bfloat16
f32 = jnp.float32
VMEM_LIMIT = 58 << 20


def dot(left, right, cl=1, cr=0):
    return lax.dot_general(
        left, right, (((cl,), (cr,)), ((), ())), preferred_element_type=f32
    )


def place_ends(info):
    ends, total = [], 0
    for j in range(SEQS):
        total = total + info[info[SEQS + j]]
        ends.append(total)
    return ends


def place_picks(info):
    return [info[2 * SEQS + info[SEQS + j]] for j in range(SEQS)]


def place_shifts(info, ends):
    shifts = []
    for j in range(SEQS):
        seq = info[SEQS + j]
        start = 0
        for s in range(SEQS):
            start = start + jnp.where(s < seq, info[s], 0)
        shifts.append(start - (ends[j - 1] if j else 0))
    return shifts


def by_place(rows, ends, values):
    out = jnp.full(rows.shape, values[0], jnp.int32)
    for j in range(SEQS - 1):
        out = jnp.where(rows >= ends[j], values[j + 1], out)
    return out


def piece_row(info, k):
    return pl.multiple_of(lax.rem(info[3 * SEQS] - k + PIECES, PIECES) * PIECE, PIECE)


def weight(ref, first, count, offset, rows):
    return ref[first : first + count, offset : offset + rows, :].reshape(count * rows, D)


def square(ref, index, offset=0):
    per = BLOCKS // 4
    return weight(ref, index * per, per, offset, BROWS)


def project_kernel(with_query, info, x0, x1, x2, x3, w, x_out, *outs):
    base = 0
    if with_query:
        qt_out, k_out, v_out = outs
        wq = square(w, 0, base)
    else:
        k_out, v_out = outs
    wk, wv = square(w, 1, base), square(w, 2, base)
    for k, piece in enumerate((x0, x1, x2, x3)):
        r0 = piece_row(info, k)
        rows = pl.ds(r0, PIECE)
        x = piece[...]
        x_out[rows, :] = x
        if with_query:
            q = dot(x, wq).astype(bf16) * jnp.asarray(HEAD_DIM**-0.5, bf16)
            qt_out[:, rows] = q.T
        k_out[rows, :] = dot(x, wk).astype(bf16)
        v_out[rows, :] = dot(x, wv).astype(bf16)


def key_loop(info, cross, q0, tile):
    ends = place_ends(info)
    rows = q0 + lax.broadcasted_iota(jnp.int32, (1, QB), 1)
    if cross:
        picks = place_picks(info)
        picked = by_place(rows, ends, picks)
        for mem in range(NMEM):
            need = jnp.bool_(False)
            for j in range(SEQS):
                start = ends[j - 1] if j else 0
                need = need | ((start < q0 + QB) & (ends[j] > q0) & (picks[j] == mem))
            allowed = picked == mem

            def step(j, carry, mem=mem, allowed=allowed):
                tile(pl.multiple_of(mem * MEM_LEN + j * KB, KB), None, allowed)
                return carry

            lax.fori_loop(0, jnp.where(need, MEM_LEN // KB, 0), step, 0)
    else:
        low, high = 0, GROUP
        low_row = jnp.zeros((1, QB), jnp.int32)
        high_row = jnp.full((1, QB), GROUP, jnp.int32)
        for j in range(SEQS - 1):
            low = jnp.where(q0 >= ends[j], ends[j], low)
            low_row = jnp.where(rows >= ends[j], ends[j], low_row)
        for j in reversed(range(SEQS - 1)):
            high = jnp.where(q0 + QB - 1 < ends[j], ends[j], high)
            high_row = jnp.where(rows < ends[j], ends[j], high_row)

        def step(j, carry):
            k0 = pl.multiple_of(j * KB, KB)
            keys = k0 + lax.broadcasted_iota(jnp.int32, (KB, QB), 0)
            bias = jnp.where((keys >= low_row) & (keys < high_row), 0.0, NEG)
            tile(k0, bias, None)
            return carry

        lax.fori_loop(low // KB, (high + KB - 1) // KB, step, 0)


def head_rows(h):
    return slice(h * HEAD_DIM, (h + 1) * HEAD_DIM)


def attend_kernel(cross, info, qt, k, v, ot, lse, vt, top, total, acc, bias_ref):
    i = pl.program_id(0)

    @pl.when(i == 0)
    def _():
        for c in range(GROUP // QB):
            vt[:, c * QB : (c + 1) * QB] = v[c * QB : (c + 1) * QB, :].T

    top[...] = jnp.full_like(top, NEG)
    total[...] = jnp.zeros_like(total)
    acc[...] = jnp.zeros_like(acc)

    def tile(k0, bias, allowed):
        keys = pl.ds(k0, KB)
        if bias is not None:
            bias_ref[...] = bias
        tops, totals = top[...], total[...]
        new_tops, new_totals = [], []
        group = 8
        for g in range(0, HEADS, group):
            heads = range(g, g + group)
            scores = [dot(k[keys, head_rows(h)], qt[head_rows(h), :]) for h in heads]
            parts = []
            for h, s in zip(heads, scores):
                old = tops[h : h + 1]
                if bias is not None:
                    s = s + bias_ref[...]
                    new = jnp.maximum(old, jnp.max(s, axis=0, keepdims=True))
                    base = new
                else:
                    peak = jnp.maximum(old, jnp.max(s, axis=0, keepdims=True))
                    new = jnp.where(allowed, peak, old)
                    base = jnp.where(allowed, peak, -NEG)
                decay = jnp.exp(old - new)
                p = jnp.exp(s - base)
                new_tops.append(new)
                new_totals.append(totals[h : h + 1] * decay + jnp.sum(p, axis=0, keepdims=True))
                parts.append((decay, p.astype(bf16)))
            for h, (decay, p) in zip(heads, parts):
                acc[head_rows(h), :] = acc[head_rows(h), :] * decay + dot(
                    vt[head_rows(h), keys], p
                )
        top[...] = jnp.concatenate(new_tops, axis=0)
        total[...] = jnp.concatenate(new_totals, axis=0)

    key_loop(info, cross, pl.multiple_of(i * QB, QB), tile)
    lse[...] = top[...] + jnp.log(total[...])
    inverse = 1.0 / total[...]
    for h in range(HEADS):
        ot[head_rows(h), :] = (acc[head_rows(h), :] * inverse[h : h + 1]).astype(bf16)


def attend_back_kernel(
    cross, info, qt, k, v, g, ot, lse, dqt, dk, dv, kt, dqt_acc, dk_acc, dv_acc, gt, gm, qm, bias_ref
):
    i = pl.program_id(0)

    @pl.when(i == 0)
    def _():
        dk_acc[...] = jnp.zeros_like(dk_acc)
        dv_acc[...] = jnp.zeros_like(dv_acc)
        for c in range(GROUP // QB):
            kt[:, c * QB : (c + 1) * QB] = k[c * QB : (c + 1) * QB, :].T

    gt[...] = g[...].T
    left = lax.broadcasted_iota(jnp.int32, (QB, 2 * HEAD_DIM), 1) < HEAD_DIM
    for pair in range(HEADS // 2):
        cols = slice(pair * 2 * HEAD_DIM, (pair + 1) * 2 * HEAD_DIM)
        gp = g[:, cols]
        qp = qt[cols, :].T
        zero = jnp.zeros_like(gp)
        gm[pair, :QB, :] = jnp.where(left, gp, zero)
        gm[pair, QB:, :] = jnp.where(left, zero, gp)
        qm[pair, :QB, :] = jnp.where(left, qp, zero)
        qm[pair, QB:, :] = jnp.where(left, zero, qp)
    weighted = [
        jnp.sum(
            gt[head_rows(h), :].astype(f32) * ot[head_rows(h), :].astype(f32),
            axis=0,
            keepdims=True,
        )
        for h in range(HEADS)
    ]
    dqt_acc[...] = jnp.zeros_like(dqt_acc)

    def tile(k0, bias, allowed):
        keys = pl.ds(k0, KB)
        if bias is not None:
            bias_ref[...] = bias
        lses = lse[...]
        if allowed is not None:
            lses = jnp.where(allowed, lses, -NEG)
        group = 4
        for first in range(0, HEADS, group):
            heads = range(first, first + group)
            scores = [dot(k[keys, head_rows(h)], qt[head_rows(h), :]) for h in heads]
            slopes = [dot(v[keys, head_rows(h)], gt[head_rows(h), :]) for h in heads]
            probs, grads = [], []
            for h, s, dp in zip(heads, scores, slopes):
                if bias is not None:
                    s = s + bias_ref[...]
                p = jnp.exp(s - lses[h : h + 1])
                probs.append(p.astype(bf16))
                grads.append((p * (dp - weighted[h])).astype(bf16))
            for n in range(0, group, 2):
                pair = (first + n) // 2
                cols = slice(pair * 2 * HEAD_DIM, (pair + 1) * 2 * HEAD_DIM)
                dv_acc[keys, cols] += dot(jnp.concatenate(probs[n : n + 2], axis=1), gm[pair])
                dk_acc[keys, cols] += dot(jnp.concatenate(grads[n : n + 2], axis=1), qm[pair])
            for h, ds in zip(heads, grads):
                dqt_acc[head_rows(h), :] += dot(kt[head_rows(h), keys], ds)

    key_loop(info, cross, pl.multiple_of(i * QB, QB), tile)
    dqt[...] = (dqt_acc[...] * HEAD_DIM**-0.5).astype(bf16)

    @pl.when(i == pl.num_programs(0) - 1)
    def _():
        dk[...] = dk_acc[...].astype(bf16)
        dv[...] = dv_acc[...].astype(bf16)


def norm(resid):
    center = resid - jnp.mean(resid, axis=-1, keepdims=True)
    inv = lax.rsqrt(jnp.mean(center * center, axis=-1, keepdims=True) + 1e-06)
    return center * inv, inv


def norm_back(grad, normed, inv, gain):
    scaled = grad * gain
    return inv * (
        scaled
        - jnp.mean(scaled, axis=-1, keepdims=True)
        - normed * jnp.mean(scaled * normed, axis=-1, keepdims=True)
    )


def column_sum(value):
    return jnp.sum(value, axis=0, keepdims=True)


def first_norm_kernel(ot, x, wa, wb, vecs, n1, inv1, qct):
    resid = x[...].astype(f32) + dot(ot[...], square(wa, 3), 0, 0)
    normed, inv = norm(resid)
    n1[...] = normed
    inv1[...] = inv
    hidden = (normed * vecs[0:1, :] + vecs[3:4, :]).astype(bf16)
    q = dot(hidden, square(wb, 0)).astype(bf16) * jnp.asarray(HEAD_DIM**-0.5, bf16)
    qct[...] = q.T


def ffn_kernel(
    info, oct_, n1, wb, vecs, b1, c0, c1, c2, c3,
    yg, d2, gc, g_ffn, g_co, g_b1, g_vec,
    cot, act, slope, dy, gw1, gw2, gco, yacc,
):
    i = pl.program_id(0)

    @pl.when(i == 0)
    def _():
        for k, piece in enumerate((c0, c1, c2, c3)):
            cot[pl.ds(piece_row(info, k), PIECE), :] = piece[...]
        for ref in (gw1, gw2, gco, g_b1, g_vec, yacc):
            ref[...] = jnp.zeros_like(ref)

    first_block = 2 * BROWS
    chunk = BROWS // 4

    def w1(c):
        return weight(wb, 0, BLOCKS, first_block + c * chunk, chunk)

    def w2(c):
        per = BLOCKS // 4
        return weight(wb, c * per, per, BROWS, BROWS)

    hidden_one = n1[...] * vecs[0:1, :] + vecs[3:4, :]
    n2, inv2 = norm(hidden_one + dot(oct_[...], square(wb, 3), 0, 0))
    hidden = n2 * vecs[1:2, :] + vecs[4:5, :]
    hidden_b = hidden.astype(bf16)

    factor = math.sqrt(2.0 / math.pi)
    cubic = 0.044715 * factor
    out = jnp.zeros((PIECE, D), f32)
    for c in range(4):
        cols = slice(c * D, (c + 1) * D)
        u = dot(hidden_b, w1(c)) + b1[0:1, cols]
        sq = u * u
        t = jnp.tanh(u * (factor + cubic * sq))
        half = 0.5 + 0.5 * t
        a = (u * half).astype(bf16)
        act[:, cols] = a
        slope[:, cols] = half + u * (1.0 - t * t) * (0.5 * factor + 1.5 * cubic * sq)
        out = out + dot(a, w2(c))
    n3, inv3 = norm(hidden + (out + vecs[6:7, :]))
    y = (n3 * vecs[2:3, :] + vecs[5:6, :]).astype(bf16)

    ends = place_ends(info)
    shifts = place_shifts(info, ends)
    p0 = i * PIECE
    rows = p0 + lax.broadcasted_iota(jnp.int32, (PIECE, 1), 0)
    given = rows + by_place(rows, ends, shifts)
    dy[...] = jnp.zeros_like(dy)

    def gather(c, carry):
        r0 = pl.multiple_of(c * QB, QB)
        hit = jnp.bool_(False)
        for j in range(SEQS):
            begin = jnp.maximum(ends[j - 1] if j else 0, p0)
            end = jnp.minimum(ends[j], p0 + PIECE)
            hit = hit | (
                (begin < end) & (begin + shifts[j] < r0 + QB) & (end + shifts[j] > r0)
            )

        @pl.when(hit)
        def _():
            cols = r0 + lax.broadcasted_iota(jnp.int32, (PIECE, QB), 1)
            select = jnp.where(cols == given, 1.0, 0.0).astype(bf16)
            dy[...] += dot(select, cot[pl.ds(r0, QB), :])
            yacc[pl.ds(r0, QB), :] += dot(select, y, 0, 0)

        return carry

    lax.fori_loop(0, GROUP // QB, gather, 0)

    grad = dy[...]
    g_vec[2:3, :] += column_sum(grad * n3)
    g_vec[5:6, :] += column_sum(grad)
    d3 = norm_back(grad, n3, inv3, vecs[2:3, :])
    df = d3.astype(bf16)
    g_vec[6:7, :] += column_sum(df.astype(f32))
    back = d3
    for c in range(4):
        cols = slice(c * D, (c + 1) * D)
        a = act[:, cols]
        gw2[cols, :] += dot(a, df, 0, 0)
        du = (dot(df, w2(c), 1, 1) * slope[:, cols]).astype(bf16)
        gw1[c] += dot(hidden_b, du, 0, 0)
        g_b1[0:1, cols] += column_sum(du.astype(f32))
        back = back + dot(du, w1(c), 1, 1)
    g_vec[1:2, :] += column_sum(back * n2)
    g_vec[4:5, :] += column_sum(back)
    second = norm_back(back, n2, inv2, vecs[1:2, :])
    d2[...] = second
    dco = second.astype(bf16)
    gco[...] += dot(oct_[...], dco)
    gc[...] = dot(dco, square(wb, 3), 1, 1).astype(bf16)

    @pl.when(i == pl.num_programs(0) - 1)
    def _():
        keep = info[3 * SEQS + 1] > 0
        yg[...] = yacc[...].astype(bf16)
        g_co[...] = jnp.where(keep, gco[...], 0.0).astype(bf16)
        for c in range(4):
            part = jnp.where(keep, gw1[c], 0.0).astype(bf16)
            g_ffn[:, c * chunk : (c + 1) * chunk, :] = part.reshape(BLOCKS, chunk, D)
            part = jnp.where(keep, gw2[c * D : (c + 1) * D, :], 0.0).astype(bf16)
            per = BLOCKS // 4
            g_ffn[c * per : (c + 1) * per, BROWS:, :] = part.reshape(per, BROWS, D)
        g_b1[...] = jnp.where(keep, g_b1[...], 0.0)
        g_vec[...] = jnp.where(keep, g_vec[...], 0.0)


def cross_post_kernel(
    info, dqct, dkc, dvc, mem, d2, n1, inv1, ot, wa, wb, vecs, g_co,
    dmem, d1, go, g_cross, g_wo, g_vec,
    gcq, gck, gcv, gwo,
):
    i = pl.program_id(0)

    @pl.when(i == 0)
    def _():
        for ref in (gcq, gck, gcv, gwo, g_vec):
            ref[...] = jnp.zeros_like(ref)

    m, dk, dv = mem[...], dkc[...], dvc[...]
    dmem[...] = (dot(dk, square(wb, 1), 1, 1) + dot(dv, square(wb, 2), 1, 1)).astype(bf16)
    gck[...] += dot(m, dk, 0, 0)
    gcv[...] += dot(m, dv, 0, 0)
    normed = n1[...]
    hidden = (normed * vecs[0:1, :] + vecs[3:4, :]).astype(bf16)
    dq = dqct[...].T
    gcq[...] += dot(hidden, dq, 0, 0)
    back = d2[...] + dot(dq, square(wb, 0), 1, 1)
    g_vec[0:1, :] += column_sum(back * normed)
    g_vec[3:4, :] += column_sum(back)
    first = norm_back(back, normed, inv1[...], vecs[0:1, :])
    d1[...] = first
    dao = first.astype(bf16)
    gwo[...] += dot(ot[...], dao)
    go[...] = dot(dao, square(wa, 3), 1, 1).astype(bf16)

    @pl.when(i == pl.num_programs(0) - 1)
    def _():
        keep = info[3 * SEQS + 1] > 0
        for n, ref in enumerate((gcq, gck, gcv)):
            g_cross[n * D : (n + 1) * D, :] = jnp.where(keep, ref[...], 0.0).astype(bf16)
        g_cross[3 * D :, :] = g_co[...]
        g_wo[...] = jnp.where(keep, gwo[...], 0.0).astype(bf16)
        g_vec[...] = jnp.where(keep, g_vec[...], 0.0)


def self_post_kernel(
    info, dqt, dk_ref, dv_ref, x_ref, d1, wa, g_wo, dtok, g_self, gq, gk, gv
):
    i = pl.program_id(0)

    @pl.when(i == 0)
    def _():
        for ref in (gq, gk, gv):
            ref[...] = jnp.zeros_like(ref)

    x, dk, dv = x_ref[...], dk_ref[...], dv_ref[...]
    dq = dqt[...].T
    dtok[...] = (
        d1[...]
        + dot(dq, square(wa, 0), 1, 1)
        + dot(dk, square(wa, 1), 1, 1)
        + dot(dv, square(wa, 2), 1, 1)
    ).astype(bf16)
    gq[...] += dot(x, dq, 0, 0)
    gk[...] += dot(x, dk, 0, 0)
    gv[...] += dot(x, dv, 0, 0)

    @pl.when(i == pl.num_programs(0) - 1)
    def _():
        keep = info[3 * SEQS + 1] > 0
        for n, ref in enumerate((gq, gk, gv)):
            g_self[n * D : (n + 1) * D, :] = jnp.where(keep, ref[...], 0.0).astype(bf16)
        g_self[3 * D :, :] = g_wo[...]


SMEM = pl.BlockSpec(memory_space=pltpu.SMEM)
WHOLE = pl.BlockSpec(memory_space=pltpu.VMEM)
ROWS = pl.BlockSpec((PIECE, D), lambda i: (i, 0))
COLS = pl.BlockSpec((D, PIECE), lambda i: (0, i))
ROWS_Q = pl.BlockSpec((QB, D), lambda i: (i, 0))
COLS_Q = pl.BlockSpec((D, QB), lambda i: (0, i))
HEADS_Q = pl.BlockSpec((HEADS, QB), lambda i: (0, i))
ONES = pl.BlockSpec((PIECE, 1), lambda i: (i, 0))


def fixed(*shape):
    return pl.BlockSpec(shape, lambda i: (0,) * len(shape))


def shape(dims, dtype=bf16):
    return jax.ShapeDtypeStruct(dims, dtype)


def call(kernel, name, grid, in_specs, out_specs, out_shape, scratch, flops, *args):
    return pl.pallas_call(
        kernel,
        grid=grid,
        in_specs=in_specs,
        out_specs=out_specs,
        out_shape=out_shape,
        scratch_shapes=scratch,
        name=name,
        compiler_params=pltpu.CompilerParams(vmem_limit_bytes=VMEM_LIMIT),
        cost_estimate=pl.CostEstimate(flops=flops, bytes_accessed=8 << 20, transcendentals=0),
    )(*args)


ROWMAJOR = shape((GROUP, D))
COLMAJOR = shape((D, GROUP))


def project_rows(info, pieces, w, with_query):
    outs = [ROWMAJOR] + ([COLMAJOR] if with_query else []) + [ROWMAJOR, ROWMAJOR]
    return call(
        functools.partial(project_kernel, with_query),
        "project",
        (),
        [SMEM] + [WHOLE] * 5,
        [WHOLE] * len(outs),
        outs,
        [],
        4 << 30,
        info,
        *pieces,
        w,
    )


def attend(info, qt, k, v, cross):
    return call(
        functools.partial(attend_kernel, cross),
        "attend",
        (GROUP // QB,),
        [SMEM, COLS_Q, fixed(GROUP, D), fixed(GROUP, D)],
        [COLS_Q, HEADS_Q],
        [COLMAJOR, shape((HEADS, GROUP), f32)],
        [
            pltpu.VMEM((D, GROUP), bf16),
            pltpu.VMEM((HEADS, QB), f32),
            pltpu.VMEM((HEADS, QB), f32),
            pltpu.VMEM((D, QB), f32),
            pltpu.VMEM((KB, QB), f32),
        ],
        30 << 30,
        info,
        qt,
        k,
        v,
    )


def attend_back(info, qt, k, v, g, ot, lse, cross):
    return call(
        functools.partial(attend_back_kernel, cross),
        "attend_back",
        (GROUP // QB,),
        [SMEM, COLS_Q, fixed(GROUP, D), fixed(GROUP, D), ROWS_Q, COLS_Q, HEADS_Q],
        [COLS_Q, fixed(GROUP, D), fixed(GROUP, D)],
        [COLMAJOR, ROWMAJOR, ROWMAJOR],
        [
            pltpu.VMEM((D, GROUP), bf16),
            pltpu.VMEM((D, QB), f32),
            pltpu.VMEM((GROUP, D), f32),
            pltpu.VMEM((GROUP, D), f32),
            pltpu.VMEM((D, QB), bf16),
            pltpu.VMEM((HEADS // 2, 2 * QB, 2 * HEAD_DIM), bf16),
            pltpu.VMEM((HEADS // 2, 2 * QB, 2 * HEAD_DIM), bf16),
            pltpu.VMEM((KB, QB), f32),
        ],
        60 << 30,
        info,
        qt,
        k,
        v,
        g,
        ot,
        lse,
    )


def local(
    tokens, memory, cotangent, lengths, seq_order, memory_pick,
    self_attn, cross_attn, ffn_in, ffn_in_bias, ffn_out, ffn_out_bias, norm_gain, norm_bias,
):
    axes = ("dp", "fsdp")
    n_dp, members = lax.axis_size("dp"), lax.axis_size("fsdp")
    micro = tokens.shape[0]
    owners = n_dp * members
    dp, z = lax.axis_index("dp"), lax.axis_index("fsdp")

    def offset(d):
        return d % 2 if micro < members else 0

    def unit_at(d, member):
        return member - offset(d)

    mine = unit_at(dp, z)
    valid = (mine >= 0) & (mine < micro)
    unit = jnp.clip(mine, 0, micro - 1)

    def pairs(k, into):
        out = []
        for d in range(n_dp):
            for source in range(members):
                target = (source + k) % members
                if 0 <= unit_at(d, target if into else source) < micro:
                    out.append((d * members + source, d * members + target))
        return out

    def to_unit(array):
        pieces = [lax.dynamic_index_in_dim(array, unit, 0, False)]
        for k in range(1, members):
            target = jnp.clip(unit_at(dp, lax.rem(z + k, members)), 0, micro - 1)
            part = lax.dynamic_index_in_dim(array, target, 0, False)
            pieces.append(lax.ppermute(part, axes, pairs(k, True)))
        return pieces

    def from_unit(array):
        blocks = array.reshape(members, PIECE, D)
        pieces = [lax.dynamic_index_in_dim(blocks, z, 0, False)]
        for k in range(1, members):
            part = lax.dynamic_index_in_dim(blocks, lax.rem(z + k, members), 0, False)
            pieces.append(lax.ppermute(part, axes, pairs(k, False)))
        out = []
        for b in range(micro):
            shift = lax.rem(z - offset(dp) - b + 2 * members, members)
            value = pieces[0]
            for k in range(1, members):
                value = jnp.where(shift == k, pieces[k], value)
            out.append(value.astype(f32))
        return jnp.stack(out)

    def row_of(array):
        return lax.dynamic_index_in_dim(array, unit, 0, False)[0]

    info = jnp.concatenate(
        [
            row_of(lengths),
            row_of(seq_order),
            row_of(memory_pick),
            jnp.stack([z, valid.astype(jnp.int32)]),
        ]
    ).astype(jnp.int32)

    smalls = jnp.concatenate(
        [ffn_in_bias, ffn_out_bias, norm_gain.T.reshape(-1), norm_bias.T.reshape(-1)]
    )
    rows = self_attn.shape[0]
    in_rows = ffn_in.shape[0]
    n_smalls = smalls.shape[0]
    small_row = jnp.pad(smalls, (0, 16 * D - n_smalls)).reshape(16, D)
    bundle_a = jnp.concatenate([self_attn, small_row], axis=0)
    in_blocks = ffn_in.reshape(in_rows, 4, D).transpose(1, 0, 2).reshape(4 * in_rows, D)
    bundle_b = jnp.concatenate([cross_attn, ffn_out, in_blocks], axis=0)
    all_a = lax.all_gather(bundle_a, axes, axis=0, tiled=False)
    token_pieces = to_unit(tokens)
    all_b = lax.all_gather(bundle_b, axes, axis=0, tiled=False)
    memory_pieces = to_unit(memory)
    cotangent_pieces = to_unit(cotangent)

    def blocked(array, count):
        return array.reshape(BLOCKS, count, D)

    small = all_a[:, rows, :n_smalls].astype(f32)
    wa = blocked(all_a[:, :rows], BROWS)
    if owners == BLOCKS:
        wb = all_b
    else:
        first = all_b[:, 2 * rows :].reshape(owners, 4, in_rows, D).transpose(1, 0, 2, 3)
        first = first.reshape(4, BLOCKS, BROWS // 4, D).transpose(1, 0, 2, 3)
        wb = jnp.concatenate(
            [
                blocked(all_b[:, :rows], BROWS),
                blocked(all_b[:, rows : 2 * rows], BROWS),
                blocked(first, BROWS),
            ],
            axis=1,
        )
    out_rows = D // owners
    b1 = small[:, :rows].reshape(1, FF)
    at = rows + out_rows
    vec_rows = [small[:, at + n * out_rows : at + (n + 1) * out_rows].reshape(1, D) for n in range(6)]
    vecs = jnp.concatenate(
        vec_rows + [small[:, rows:at].reshape(1, D), jnp.zeros((1, D), f32)], axis=0
    )

    x, qt, k, v = project_rows(info, token_pieces, wa, True)
    ot, lse = attend(info, qt, k, v, False)
    n1, inv1, qct = call(
        first_norm_kernel,
        "first_norm",
        (PIECES,),
        [COLS, ROWS, fixed(BLOCKS, BROWS, D), fixed(BLOCKS, 3 * BROWS, D), fixed(8, D)],
        [ROWS, ONES, COLS],
        [shape((GROUP, D), f32), shape((GROUP, 1), f32), COLMAJOR],
        [],
        2 << 30,
        ot,
        x,
        wa,
        wb,
        vecs,
    )
    mem, kc, vc = project_rows(info, memory_pieces, wb, False)
    oct_, lse_c = attend(info, qct, kc, vc, True)
    yg, d2, gc, g_ffn, g_co, g_b1, g_vec = call(
        ffn_kernel,
        "ffn",
        (PIECES,),
        [SMEM, COLS, ROWS, fixed(BLOCKS, 3 * BROWS, D), fixed(8, D), fixed(1, FF)]
        + [fixed(PIECE, D)] * 4,
        [
            fixed(GROUP, D),
            ROWS,
            ROWS,
            fixed(BLOCKS, 2 * BROWS, D),
            fixed(D, D),
            fixed(1, FF),
            fixed(8, D),
        ],
        [
            ROWMAJOR,
            shape((GROUP, D), f32),
            ROWMAJOR,
            shape((BLOCKS, 2 * BROWS, D)),
            shape((D, D)),
            shape((1, FF), f32),
            shape((8, D), f32),
        ],
        [
            pltpu.VMEM((GROUP, D), bf16),
            pltpu.VMEM((PIECE, FF), bf16),
            pltpu.VMEM((PIECE, FF), f32),
            pltpu.VMEM((PIECE, D), f32),
            pltpu.VMEM((4, D, D), f32),
            pltpu.VMEM((FF, D), f32),
            pltpu.VMEM((D, D), f32),
            pltpu.VMEM((GROUP, D), f32),
        ],
        32 << 30,
        info,
        oct_,
        n1,
        wb,
        vecs,
        b1,
        *cotangent_pieces,
    )
    layer_output = from_unit(yg)

    def owned(array, count):
        return lax.psum_scatter(array, axes, scatter_dimension=0, tiled=True).astype(f32)

    if owners == BLOCKS:
        ffn_part = owned(g_ffn, 0)[0]
    else:
        second = g_ffn[:, BROWS:].reshape(owners, rows, D)
        first = g_ffn[:, :BROWS].reshape(BLOCKS, 4, BROWS // 4, D).transpose(1, 0, 2, 3)
        first = first.reshape(4, owners, in_rows, D).transpose(1, 0, 2, 3)
        both = jnp.concatenate([first.reshape(owners, rows, D), second], axis=1)
        ffn_part = owned(both, 0)[0]
    ffn_in_grad = ffn_part[:rows].reshape(4, in_rows, D).transpose(1, 0, 2).reshape(in_rows, FF)
    ffn_out_grad = ffn_part[rows:]

    dqct, dkc, dvc = attend_back(info, qct, kc, vc, gc, oct_, lse_c, True)
    dmem, d1, go, g_cross, g_wo, g_vec_one = call(
        cross_post_kernel,
        "cross_post",
        (PIECES,),
        [SMEM, COLS, ROWS, ROWS, ROWS, ROWS, ROWS, ONES, COLS]
        + [fixed(BLOCKS, BROWS, D), fixed(BLOCKS, 3 * BROWS, D), fixed(8, D), fixed(D, D)],
        [ROWS, ROWS, ROWS, fixed(4 * D, D), fixed(D, D), fixed(8, D)],
        [
            ROWMAJOR,
            shape((GROUP, D), f32),
            ROWMAJOR,
            shape((4 * D, D)),
            shape((D, D)),
            shape((8, D), f32),
        ],
        [pltpu.VMEM((D, D), f32)] * 4,
        9 << 30,
        info,
        dqct,
        dkc,
        dvc,
        mem,
        d2,
        n1,
        inv1,
        ot,
        wa,
        wb,
        vecs,
        g_co,
    )
    memory_grad = from_unit(dmem)
    cross_attn_grad = owned(g_cross, 0)
    dqt, dk, dv = attend_back(info, qt, k, v, go, ot, lse, False)
    dtok, g_self = call(
        self_post_kernel,
        "self_post",
        (PIECES,),
        [SMEM, COLS, ROWS, ROWS, ROWS, ROWS, fixed(BLOCKS, BROWS, D), fixed(D, D)],
        [ROWS, fixed(4 * D, D)],
        [ROWMAJOR, shape((4 * D, D))],
        [pltpu.VMEM((D, D), f32)] * 3,
        7 << 30,
        info,
        dqt,
        dk,
        dv,
        x,
        d1,
        wa,
        g_wo,
    )
    input_grad = from_unit(dtok)
    g_vec = g_vec + g_vec_one
    small_grads = jnp.concatenate(
        [g_b1.reshape(owners, rows), g_vec[6].reshape(owners, out_rows)]
        + [g_vec[n].reshape(owners, out_rows) for n in range(6)],
        axis=1,
    )
    small_grads = jnp.pad(small_grads, ((0, 0), (0, 16 * D - n_smalls))).reshape(owners, 16, D)
    last = jnp.concatenate(
        [g_self.reshape(owners, rows, D), small_grads.astype(bf16)], axis=1
    )
    last = owned(last, 0)[0]
    small_out = last[rows]
    norm_part = small_out[at : at + 6 * out_rows].reshape(6, out_rows)
    return (
        layer_output,
        input_grad,
        memory_grad,
        last[:rows],
        cross_attn_grad,
        ffn_in_grad,
        small_out[:rows],
        ffn_out_grad,
        small_out[rows:at],
        norm_part[:3].T,
        norm_part[3:].T,
    )


def solution(mesh):
    rows = P(None, ("dp", "fsdp"), None)
    group = P(None, "dp", None)
    shard = P(("dp", "fsdp"), None)
    flat = P(("dp", "fsdp"))
    in_specs = (rows,) * 3 + (group,) * 3 + (shard, shard, shard, flat, shard, flat, shard, shard)
    out_specs = (rows,) * 3 + (shard, shard, shard, flat, shard, flat, shard, shard)
    return jax.shard_map(local, mesh=mesh, in_specs=in_specs, out_specs=out_specs, check_vma=False)
```

time: 2600 us -> 875 us (0.34)
  matrix products: 736 us -> 0 us
  waiting for transfers between devices: 1070 us -> 422 us
  other arithmetic: 341 us -> 21 us
  Pallas kernels: 0 us -> 302 us
  blocking collectives: 215 us -> 0 us
  local copies, waits for them, and re-layouts: 199 us -> 25.1 us
  starting transfers between devices: 2.98 us -> 81.7 us
    dot_general x126 -> x0, matrix products: 736 us -> none  [the longest x6 134 us: attend_backward(): jnp.einsum('qhd,khd->hqk', grad_heads, head_split(value_rows), preferred_...]
    reduce_scatter x16 -> x3, waiting for transfers between devices: 571 us -> 238 us  [owned(): lax.psum_scatter(array, axes, scatter_dimension=0, tiled=True).astype(f32)]
    pallas_call x0 -> x10, Pallas kernels: none -> 302 us  [call(): pl.pallas_call(kernel, grid=grid, in_specs=in_specs, out_specs=out_specs,...]
    all_gather x22 -> x2, waiting for transfers between devices: 386 us -> 90 us  [the longest x1 62.2 us: local(): all_a = lax.all_gather(bundle_a, axes, axis=0, tiled=False)]
    convert_element_type x11 -> x4, other arithmetic: 184 us -> 4.25 us  [the longest x3 3.32 us: owned(): lax.psum_scatter(array, axes, scatter_dimension=0, tiled=True).astype(f32)]
    all_gather x2 -> x0, blocking collectives: 131 us -> none  [the longest x1 65.7 us: local(): lax.all_gather(norm_gain, ('dp', 'fsdp'), axis=0, tiled=True)]
    unnamed x42 -> x5, waiting for transfers between devices: 116 us -> 0.59 us
    ppermute x0 -> x18, waiting for transfers between devices: none -> 93.6 us  [the longest x9 93.5 us: from_unit(): pieces.append(lax.ppermute(part, axes, pairs(k, False)))]
  transfers between devices with their start and end apart: 40 -> 23, of which waited for: 19 -> 10; matrix products, arithmetic and copies ran while one was open for 46% -> 4% of each run, Pallas kernels for 0% -> 19%
where the time goes in v1:
time: 875 us; the launch traced here: 867 us
  waiting for transfers between devices  422 us (48%)
  Pallas kernels  302 us (35%)
  starting transfers between devices  81.7 us (9%)
  local copies, waits for them, and re-layouts  25.1 us (3%)
  other arithmetic  21 us (2%)
  between operations  14.8 us (2%)
    pallas_call x10, Pallas kernels, call(): pl.pallas_call(kernel, grid=grid, in_specs=in_specs, out_specs=out_specs,...  302 us
    reduce_scatter x3, waiting for transfers between devices, owned(): lax.psum_scatter(array, axes, scatter_dimension=0, tiled=True).astype(f32)  238 us
    ppermute x9, waiting for transfers between devices, from_unit(): pieces.append(lax.ppermute(part, axes, pairs(k, False)))  93.5 us
    all_gather x1, waiting for transfers between devices, local(): all_a = lax.all_gather(bundle_a, axes, axis=0, tiled=False)  62.2 us
    ppermute x9, starting transfers between devices, from_unit(): pieces.append(lax.ppermute(part, axes, pairs(k, False)))  59.4 us
    all_gather x1, waiting for transfers between devices, local(): all_b = lax.all_gather(bundle_b, axes, axis=0, tiled=False)  27.9 us
    ppermute x9, starting transfers between devices, to_unit(): pieces.append(lax.ppermute(part, axes, pairs(k, True)))  22.1 us
  transfers between devices with their start and end apart: 23, of which 10 were waited for; matrix products, arithmetic and copies ran while one was open for 4% of the time, Pallas kernels for 19%

profile of v1, /device:TPU:12, one launch (start us, length us, event | category | flops | bytes accessed | tf_op | source)
XLA Modules:
  0.0 866.7 jit_solution(8285413752769033547)
XLA Ops:
  9.5 1.5 pad_maximum_fusion.2
  11.9 1.6 pad_maximum_fusion.1
  13.6 3.0 dynamic-slice_bitcast_fusion.17
  16.6 3.5 collective-permute-start
  20.1 1.3 collective-permute-start.1
  21.4 3.5 collective-permute-start.2
  26.1 3.0 collective-permute-start.3
  29.1 1.3 collective-permute-start.4
  32.9 62.2 %all-gather.5.cloned.1.call-done = bf16[2560,512]{1,0:T(8,128)(2,1)} async-done(((bf16[80,512]{1,0:T(8,128)(2,1)}), bf16[2560,512]{1,0:T(8,128)(2,1)}) %all-gather.5.cloned.1.call-update) | async-done | bytes 2621456 | tf_op jit(solution)/shard_map/all_gather | solution.py:652
  95.1 3.2 slice.137.w.wa
  98.3 2.5 collective-permute-start.5
  100.8 3.4 collective-permute-start.6
  104.2 1.3 collective-permute-start.7
  105.5 8.5 project.2
  114.0 32.4 %attend.2 = (bf16[512,2048]{1,0:T(8,128)(2,1)}, f32[8,2048]{1,0:T(8,128)}) custom-call(s32[14]{0:T(128)} %concatenate.22.info, bf16[512,2048]{1,0:T(8,128)(2,1)} %get-tuple-element.46.qt, bf16[2048,512]{1,0:T(8,128)(2,1)} %get-tuple-element.47.k, bf16[2048,512]{1,0:T(8,128)(2,1)} %get-tuple-element.48.v), custom_call_target="tpu_custom_call" | custom-call | flops 32212254720 | bytes 8388608 | tf_op jit(solution)/shard_map/attend/pallas_call | solution.py:492
  149.3 27.9 %all-gather.7.cloned.1.call-done = bf16[6144,512]{1,0:T(8,128)(2,1)} async-done(((bf16[192,512]{1,0:T(8,128)(2,1)}), bf16[6144,512]{1,0:T(8,128)(2,1)}) %all-gather.7.cloned.1.call-update) | async-done | bytes 6291472 | tf_op jit(solution)/shard_map/all_gather | solution.py:654
  177.1 9.7 %first_norm.1 = (f32[2048,512]{1,0:T(8,128)}, f32[2048,1]{1,0:T(8,128)}, bf16[512,2048]{1,0:T(8,128)(2,1)}) custom-call(bf16[512,2048]{1,0:T(8,128)(2,1)} %get-tuple-element.49.ot, bf16[2048,512]{1,0:T(8,128)(2,1)} %get-tuple-element.50.x.x_ref, bf16[32,64,512]{2,1,0:T(8,128)(2,1)} %slice.137.w.wa, bf16[32,192,512]{2,1,0:T(8,128)(2,1)} %bitcast.169, ...), custom_call_target="tpu_custom_call" | custom-call | flops 2147483648 | bytes 8388608 | tf_op jit(solution)/shard_map/first_norm/pallas_call | solution.py:492
  186.8 2.4 collective-permute-start.8
  189.3 8.0 project.3
  197.3 37.8 %attend.3 = (bf16[512,2048]{1,0:T(8,128)(2,1)}, f32[8,2048]{1,0:T(8,128)}) custom-call(s32[14]{0:T(128)} %concatenate.22.info, bf16[512,2048]{1,0:T(8,128)(2,1)} %get-tuple-element.51.qt, bf16[2048,512]{1,0:T(8,128)(2,1)} %get-tuple-element.52.k, bf16[2048,512]{1,0:T(8,128)(2,1)} %get-tuple-element.53.v), custom_call_target="tpu_custom_call" | custom-call | flops 32212254720 | bytes 8388608 | tf_op jit(solution)/shard_map/attend/pallas_call | solution.py:492
  236.2 58.6 %ffn.1 = (bf16[2048,512]{1,0:T(8,128)(2,1)}, f32[2048,512]{1,0:T(8,128)}, bf16[2048,512]{1,0:T(8,128)(2,1)}, bf16[32,128,512]{2,1,0:T(8,128)(2,1)}, bf16[512,512...) custom-call(s32[14]{0:T(128)} %concatenate.22.info, bf16[512,2048]{1,0:T(8,128)(2,1)} %get-tuple-element.54.oct_.ot, ...), custom_call_target="tpu_custom_call" | custom-call | flops 34359738368 | bytes 8388608 | tf_op jit(solution)/shard_map/ffn/pallas_call | solution.py:492
  294.8 61.0 %attend_back.2 = (bf16[512,2048]{1,0:T(8,128)(2,1)}, bf16[2048,512]{1,0:T(8,128)(2,1)}, bf16[2048,512]{1,0:T(8,128)(2,1)}) custom-call(s32[14]{0:T(128)} %concatenate.22.info, bf16[512,2048]{1,0:T(8,128)(2,1)} %get-tuple-element.51.qt, bf16[2048,512]{1,0:T(8,128)(2,1)} %get-tuple-element.52.k, bf16[2048,512]{1,0:T(8,128)(2,1)} %get-tuple-element.53.v, ...), custom_call_target="tpu_custom_call" | custom-call | flops 64424509440 | bytes 8388608 | tf_op jit(solution)/shard_map/attend_back/pallas_call | solution.py:492
  355.8 19.9 %cross_post.1 = (bf16[2048,512]{1,0:T(8,128)(2,1)}, f32[2048,512]{1,0:T(8,128)}, bf16[2048,512]{1,0:T(8,128)(2,1)}, bf16[2048,512]{1,0:T(8,128)(2,1)}, bf16[512,512]{1,0:T(8,128)(2,1)}, /*index=5*/f32[8,512]{1,0:T(8,128)}) custom-call(s32[14]{0:T(128)} %concatenate.22.info, bf16[512,2048]{1,0:T(8,128)(2,1)} %get-tuple-element.59.dqct, ...), custom_call_target="tpu_custom_call" | custom-call | flops 9663676416 | bytes 8388608 | tf_op jit(solution)/shard_map/cross_post/pallas_call | solution.py:492
  377.7 53.1 %attend_back.3 = (bf16[512,2048]{1,0:T(8,128)(2,1)}, bf16[2048,512]{1,0:T(8,128)(2,1)}, bf16[2048,512]{1,0:T(8,128)(2,1)}) custom-call(s32[14]{0:T(128)} %concatenate.22.info, bf16[512,2048]{1,0:T(8,128)(2,1)} %get-tuple-element.46.qt, bf16[2048,512]{1,0:T(8,128)(2,1)} %get-tuple-element.47.k, bf16[2048,512]{1,0:T(8,128)(2,1)} %get-tuple-element.48.v, ...), custom_call_target="tpu_custom_call" | custom-call | flops 64424509440 | bytes 8388608 | tf_op jit(solution)/shard_map/attend_back/pallas_call | solution.py:492
  430.8 12.7 %self_post.1 = (bf16[2048,512]{1,0:T(8,128)(2,1)}, bf16[2048,512]{1,0:T(8,128)(2,1)}) custom-call(s32[14]{0:T(128)} %concatenate.22.info, bf16[512,2048]{1,0:T(8,128)(2,1)} %get-tuple-element.68.dqt, bf16[2048,512]{1,0:T(8,128)(2,1)} %get-tuple-element.69.dk_ref, bf16[2048,512]{1,0:T(8,128)(2,1)} %get-tuple-element.70.dv_ref, ...), custom_call_target="tpu_custom_call" | custom-call | flops 7516192768 | bytes 8388608 | tf_op jit(solution)/shard_map/self_post/pallas_call | solution.py:492
  443.5 3.3 pad_maximum_fusion
  449.7 11.3 %collective-permute-start.15 = (bf16[512,512]{1,0:T(8,128)(2,1)}, bf16[512,512]{1,0:T(8,128)(2,1)}, u32[]{:S(2)}, u32[]{:S(2)}) collective-permute-start(bf16[512,512]{1,0:T(8,128)(2,1)} %get-tuple-element.101), channel_id=1, source_target_pairs={{0,3},{1,0},{2,1},{5,4},{6,5},{7,6},{8,11},{9,8},{10,9},{13,12},{1... | collective-permute-start | bytes 1572872 | tf_op jit(solution)/shard_map/ppermute | solution.py:620
  461.1 17.9 %collective-permute-start.16 = (bf16[512,512]{1,0:T(8,128)(2,1)}, bf16[512,512]{1,0:T(8,128)(2,1)}, u32[]{:S(2)}, u32[]{:S(2)}) collective-permute-start(bf16[512,512]{1,0:T(8,128)(2,1)} %get-tuple-element.100), channel_id=1, source_target_pairs={{0,2},{1,3},{2,0},{5,7},{6,4},{7,5},{8,10},{9,11},{10,8},{13,15},{... | collective-permute-start | bytes 1572872 | tf_op jit(solution)/shard_map/ppermute | solution.py:620
  479.0 4.6 collective-permute-start.17
  484.7 2.0 collective-permute-start.12
  486.7 1.3 collective-permute-start.13
  488.1 31.2 %collective-permute-done.15 = bf16[512,512]{1,0:T(8,128)(2,1)} collective-permute-done((bf16[512,512]{1,0:T(8,128)(2,1)}, bf16[512,512]{1,0:T(8,128)(2,1)}, u32[]{:S(2)}, u32[]{:S(2)}) %collective-permute-start.15) | collective-permute-done | bytes 524320 | tf_op jit(solution)/shard_map/ppermute | solution.py:620
  519.2 1.9 collective-permute-start.14
  521.3 5.6 collective-permute-start.10
  526.9 10.7 %collective-permute-done.17 = bf16[512,512]{1,0:T(8,128)(2,1)} collective-permute-done((bf16[512,512]{1,0:T(8,128)(2,1)}, bf16[512,512]{1,0:T(8,128)(2,1)}, u32[]{:S(2)}, u32[]{:S(2)}) %collective-permute-start.17) | collective-permute-done | bytes 524320 | tf_op jit(solution)/shard_map/ppermute | solution.py:620
  537.6 12.8 %collective-permute-start.11 = (bf16[512,512]{1,0:T(8,128)(2,1)S(1)}, bf16[512,512]{1,0:T(8,128)(2,1)S(1)}, u32[]{:S(2)}, u32[]{:S(2)}) collective-permute-start(bf16[512,512]{1,0:T(8,128)(2,1)S(1)} %get-tuple-element.105), channel_id=1, source_target_pairs={{0,1},{1,2},{2,3},{5,6},{6,7},{7,4},{8,9},{9,10},{10,11},{13,14},{... | collective-permute-start | bytes 1572872 | tf_op jit(solution)/shard_map/ppermute | solution.py:620
  550.4 1.7 fusion.2
  552.1 9.0 %collective-permute-done.12 = bf16[512,512]{1,0:T(8,128)(2,1)S(1)} collective-permute-done((bf16[512,512]{1,0:T(8,128)(2,1)}, bf16[512,512]{1,0:T(8,128)(2,1)S(1)}, u32[]{:S(2)}, u32[]{:S(2)}) %collective-permute-start.12) | collective-permute-done | bytes 524320 | tf_op jit(solution)/shard_map/ppermute | solution.py:620
  561.1 1.9 collective-permute-start.9
  563.0 1.9 maximum_convert_fusion.2
  564.9 11.1 %collective-permute-done.14 = bf16[512,512]{1,0:T(8,128)(2,1)S(1)} collective-permute-done((bf16[512,512]{1,0:T(8,128)(2,1)S(1)}, bf16[512,512]{1,0:T(8,128)(2,1)S(1)}, u32[]{:S(2)}, u32[]{:S(2)}) %collective-permute-start.14) | collective-permute-done | bytes 524320 | tf_op jit(solution)/shard_map/ppermute | solution.py:620
  577.3 1.9 maximum_convert_fusion.1
  579.2 13.1 %collective-permute-done.10 = bf16[512,512]{1,0:T(8,128)(2,1)S(1)} collective-permute-done((bf16[512,512]{1,0:T(8,128)(2,1)S(1)}, bf16[512,512]{1,0:T(8,128)(2,1)S(1)}, u32[]{:S(2)}, u32[]{:S(2)}) %collective-permute-start.10) | collective-permute-done | bytes 524320 | tf_op jit(solution)/shard_map/ppermute | solution.py:620
  592.3 18.4 %collective-permute-done.11 = bf16[512,512]{1,0:T(8,128)(2,1)S(1)} collective-permute-done((bf16[512,512]{1,0:T(8,128)(2,1)S(1)}, bf16[512,512]{1,0:T(8,128)(2,1)S(1)}, u32[]{:S(2)}, u32[]{:S(2)}) %collective-permute-start.11) | collective-permute-done | bytes 524320 | tf_op jit(solution)/shard_map/ppermute | solution.py:620
  610.9 1.9 maximum_convert_fusion
  612.8 1.5 convert_element_type.37
  614.3 94.1 %reduce-scatter.4.cloned.1.call-done = bf16[1,80,512]{2,1,0:T(8,128)(2,1)} async-done(((bf16[32,80,512]{2,1,0:T(8,128)(2,1)}), bf16[1,80,512]{2,1,0:T(8,128)(2,1)}) %reduce-scatter.4.cloned.1.call-update) | async-done | bytes 81936 | tf_op jit(solution)/shard_map/reduce_scatter | solution.py:749
  712.5 144.1 %reduce-scatter.8.cloned.1.call-done = bf16[1,128,512]{2,1,0:T(8,128)(2,1)} async-done(((bf16[32,128,512]{2,1,0:T(8,128)(2,1)}), bf16[1,128,512]{2,1,0:T(8,128)(2,1)}) %reduce-scatter.8.cloned.1.call-update) | async-done | bytes 131088 | tf_op jit(solution)/shard_map/reduce_scatter | solution.py:749
  (103 shorter events, 25.5 us)
Async XLA Ops:
  7.2 23.2 %copy-start = (s32[3,1,4]{2,1,0:T(1,128)S(1)}, s32[3,1,4]{2,1,0:T(1,128)}, u32[]{:S(2)}) copy-start(s32[3,1,4]{2,1,0:T(1,128)} %param.19) | copy-start | bytes 148
  7.2 87.9 %all-gather.5.cloned.1.call-start = ((), (), s32[]{:S(2)}) async-start(), calls=%async_computation.6 | async-start | bytes 2703360 | tf_op jit(solution)/shard_map/all_gather | solution.py:652
  11.1 166.1 %all-gather.7.cloned.1.call-start = ((), (), s32[]{:S(2)}) async-start(), calls=%async_computation.7 | async-start | bytes 6488064 | tf_op jit(solution)/shard_map/all_gather | solution.py:654
  13.5 599.3 %reduce-scatter.6.cloned.1.call-start = ((), (), s32[]{:S(2)}) async-start(), calls=%async_computation.4 | async-start | bytes 2162688 | tf_op jit(solution)/shard_map/reduce_scatter | solution.py:749
  13.6 11.3 %copy-start.2 = (bf16[3,512,512]{2,1,0:T(8,128)(2,1)S(1)}, bf16[3,512,512]{2,1,0:T(8,128)(2,1)}, u32[]{:S(2)}) copy-start(bf16[3,512,512]{2,1,0:T(8,128)(2,1)} %param.15) | copy-start | bytes 4718596
  16.6 81.7 %collective-permute-start = (bf16[512,512]{1,0:T(8,128)(2,1)}, bf16[512,512]{1,0:T(8,128)(2,1)}, u32[]{:S(2)}, u32[]{:S(2)}) collective-permute-start(bf16[512,512]{1,0:T(8,128)(2,1)} %get-tuple-element.117), channel_id=1, source_target_pairs={{0,1},{1,2},{3,0},{4,5},{5,6},{6,7},{8,9},{9,10},{11,8},{12,13},{1... | collective-permute-start | bytes 1572872 | tf_op jit(solution)/shard_map/ppermute | solution.py:612
  20.1 80.7 %collective-permute-start.1 = (bf16[512,512]{1,0:T(8,128)(2,1)}, bf16[512,512]{1,0:T(8,128)(2,1)}, u32[]{:S(2)}, u32[]{:S(2)}) collective-permute-start(bf16[512,512]{1,0:T(8,128)(2,1)} %get-tuple-element.119), channel_id=1, source_target_pairs={{0,2},{2,0},{3,1},{4,6},{5,7},{7,5},{8,10},{10,8},{11,9},{12,14},{... | collective-permute-start | bytes 1572872 | tf_op jit(solution)/shard_map/ppermute | solution.py:612
  21.4 10.3 %copy-start.3 = (bf16[3,512,512]{2,1,0:T(8,128)(2,1)S(1)}, bf16[3,512,512]{2,1,0:T(8,128)(2,1)}, u32[]{:S(2)}) copy-start(bf16[3,512,512]{2,1,0:T(8,128)(2,1)} %param.16) | copy-start | bytes 4718596
  21.4 82.8 %collective-permute-start.2 = (bf16[512,512]{1,0:T(8,128)(2,1)}, bf16[512,512]{1,0:T(8,128)(2,1)}, u32[]{:S(2)}, u32[]{:S(2)}) collective-permute-start(bf16[512,512]{1,0:T(8,128)(2,1)} %get-tuple-element.116), channel_id=1, source_target_pairs={{1,0},{2,1},{3,2},{4,7},{6,5},{7,6},{9,8},{10,9},{11,10},{12,15},{... | collective-permute-start | bytes 1572872 | tf_op jit(solution)/shard_map/ppermute | solution.py:612
  26.1 160.8 %collective-permute-start.3 = (bf16[512,512]{1,0:T(8,128)(2,1)}, bf16[512,512]{1,0:T(8,128)(2,1)}, u32[]{:S(2)}, u32[]{:S(2)}) collective-permute-start(bf16[512,512]{1,0:T(8,128)(2,1)} %get-tuple-element.113), channel_id=1, source_target_pairs={{0,1},{1,2},{3,0},{4,5},{5,6},{6,7},{8,9},{9,10},{11,8},{12,13},{1... | collective-permute-start | bytes 1572872 | tf_op jit(solution)/shard_map/ppermute | solution.py:612
  29.1 160.2 %collective-permute-start.4 = (bf16[512,512]{1,0:T(8,128)(2,1)S(1)}, bf16[512,512]{1,0:T(8,128)(2,1)}, u32[]{:S(2)}, u32[]{:S(2)}) collective-permute-start(bf16[512,512]{1,0:T(8,128)(2,1)S(1)} %get-tuple-element.115), channel_id=1, source_target_pairs={{0,2},{2,0},{3,1},{4,6},{5,7},{7,5},{8,10},{10,8},{11,9},{12,14},{... | collective-permute-start | bytes 1572872 | tf_op jit(solution)/shard_map/ppermute | solution.py:612
  95.1 5.7 copy-start.8
  95.1 9.1 %copy-start.7 = (bf16[512,512]{1,0:T(8,128)(2,1)S(1)}, bf16[512,512]{1,0:T(8,128)(2,1)}, u32[]{:S(2)}) copy-start(bf16[512,512]{1,0:T(8,128)(2,1)} %get-tuple-element.111) | copy-start | bytes 1572868
  98.3 91.0 %collective-permute-start.5 = (bf16[512,512]{1,0:T(8,128)(2,1)S(1)}, bf16[512,512]{1,0:T(8,128)(2,1)}, u32[]{:S(2)}, u32[]{:S(2)}) collective-permute-start(bf16[512,512]{1,0:T(8,128)(2,1)S(1)} %get-tuple-element.112), channel_id=1, source_target_pairs={{1,0},{2,1},{3,2},{4,7},{6,5},{7,6},{9,8},{10,9},{11,10},{12,15},{... | collective-permute-start | bytes 1572872 | tf_op jit(solution)/shard_map/ppermute | solution.py:612
  100.8 134.4 %collective-permute-start.6 = (bf16[512,512]{1,0:T(8,128)(2,1)S(1)}, bf16[512,512]{1,0:T(8,128)(2,1)S(1)}, u32[]{:S(2)}, u32[]{:S(2)}) collective-permute-start(bf16[512,512]{1,0:T(8,128)(2,1)S(1)} %copy-done.8), channel_id=1, source_target_pairs={{0,1},{1,2},{3,0},{4,5},{5,6},{6,7},{8,9},{9,10},{11,8},{12,13},{1... | collective-permute-start | bytes 1572872 | tf_op jit(solution)/shard_map/ppermute | solution.py:612
  104.2 131.0 %collective-permute-start.7 = (bf16[512,512]{1,0:T(8,128)(2,1)S(1)}, bf16[512,512]{1,0:T(8,128)(2,1)}, u32[]{:S(2)}, u32[]{:S(2)}) collective-permute-start(bf16[512,512]{1,0:T(8,128)(2,1)S(1)} %copy-done.7), channel_id=1, source_target_pairs={{0,2},{2,0},{3,1},{4,6},{5,7},{7,5},{8,10},{10,8},{11,9},{12,14},{... | collective-permute-start | bytes 1572872 | tf_op jit(solution)/shard_map/ppermute | solution.py:612
  186.8 48.3 %collective-permute-start.8 = (bf16[512,512]{1,0:T(8,128)(2,1)S(1)}, bf16[512,512]{1,0:T(8,128)(2,1)S(1)}, u32[]{:S(2)}, u32[]{:S(2)}) collective-permute-start(bf16[512,512]{1,0:T(8,128)(2,1)S(1)} %get-tuple-element.108), channel_id=1, source_target_pairs={{1,0},{2,1},{3,2},{4,7},{6,5},{7,6},{9,8},{10,9},{11,10},{12,15},{... | collective-permute-start | bytes 1572872 | tf_op jit(solution)/shard_map/ppermute | solution.py:612
  235.2 0.8 copy-start.11
  235.2 1.0 copy-start.12
  355.8 19.9 %copy-start.9 = (f32[8,512]{1,0:T(8,128)S(1)}, f32[8,512]{1,0:T(8,128)}, u32[]{:S(2)}) copy-start(f32[8,512]{1,0:T(8,128)} %get-tuple-element.77) | copy-start | bytes 49156
  355.8 21.3 %copy-start.10 = (f32[1,2048]{1,0:T(1,128)S(1)}, f32[1,2048]{1,0:T(1,128)}, u32[]{:S(2)}) copy-start(f32[1,2048]{1,0:T(1,128)} %get-tuple-element.76) | copy-start | bytes 24580
  377.6 330.9 %reduce-scatter.4.cloned.1.call-start = ((), (), s32[]{:S(2)}) async-start(), calls=%async_computation.3 | async-start | bytes 2703360 | tf_op jit(solution)/shard_map/reduce_scatter | solution.py:749
  446.8 409.8 %reduce-scatter.8.cloned.1.call-start = ((), (), s32[]{:S(2)}) async-start(), calls=%async_computation.5 | async-start | bytes 4325376 | tf_op jit(solution)/shard_map/reduce_scatter | solution.py:749
  446.9 1.6 copy-start.5
  447.5 36.2 %copy-start.6 = (bf16[2048,512]{1,0:T(8,128)(2,1)S(1)}, bf16[2048,512]{1,0:T(8,128)(2,1)}, u32[]{:S(2)}) copy-start(bf16[2048,512]{1,0:T(8,128)(2,1)} %get-tuple-element.73) | copy-start | bytes 6291460
  449.7 71.4 %copy-start.4 = (bf16[2048,512]{1,0:T(8,128)(2,1)S(1)}, bf16[2048,512]{1,0:T(8,128)(2,1)}, u32[]{:S(2)}) copy-start(bf16[2048,512]{1,0:T(8,128)(2,1)} %get-tuple-element.56) | copy-start | bytes 6291460
  449.7 69.5 %collective-permute-start.15 = (bf16[512,512]{1,0:T(8,128)(2,1)}, bf16[512,512]{1,0:T(8,128)(2,1)}, u32[]{:S(2)}, u32[]{:S(2)}) collective-permute-start(bf16[512,512]{1,0:T(8,128)(2,1)} %get-tuple-element.101), channel_id=1, source_target_pairs={{0,3},{1,0},{2,1},{5,4},{6,5},{7,6},{8,11},{9,8},{10,9},{13,12},{1... | collective-permute-start | bytes 1572872 | tf_op jit(solution)/shard_map/ppermute | solution.py:620
  461.1 60.2 %collective-permute-start.16 = (bf16[512,512]{1,0:T(8,128)(2,1)}, bf16[512,512]{1,0:T(8,128)(2,1)}, u32[]{:S(2)}, u32[]{:S(2)}) collective-permute-start(bf16[512,512]{1,0:T(8,128)(2,1)} %get-tuple-element.100), channel_id=1, source_target_pairs={{0,2},{1,3},{2,0},{5,7},{6,4},{7,5},{8,10},{9,11},{10,8},{13,15},{... | collective-permute-start | bytes 1572872 | tf_op jit(solution)/shard_map/ppermute | solution.py:620
  479.0 58.6 %collective-permute-start.17 = (bf16[512,512]{1,0:T(8,128)(2,1)}, bf16[512,512]{1,0:T(8,128)(2,1)}, u32[]{:S(2)}, u32[]{:S(2)}) collective-permute-start(bf16[512,512]{1,0:T(8,128)(2,1)} %get-tuple-element.99), channel_id=1, source_target_pairs={{0,1},{1,2},{2,3},{5,6},{6,7},{7,4},{8,9},{9,10},{10,11},{13,14},{... | collective-permute-start | bytes 1572872 | tf_op jit(solution)/shard_map/ppermute | solution.py:620
  484.7 76.3 %collective-permute-start.12 = (bf16[512,512]{1,0:T(8,128)(2,1)}, bf16[512,512]{1,0:T(8,128)(2,1)S(1)}, u32[]{:S(2)}, u32[]{:S(2)}) collective-permute-start(bf16[512,512]{1,0:T(8,128)(2,1)} %get-tuple-element.104), channel_id=1, source_target_pairs={{0,3},{1,0},{2,1},{5,4},{6,5},{7,6},{8,11},{9,8},{10,9},{13,12},{1... | collective-permute-start | bytes 1572872 | tf_op jit(solution)/shard_map/ppermute | solution.py:620
  486.7 78.2 %collective-permute-start.13 = (bf16[512,512]{1,0:T(8,128)(2,1)}, bf16[512,512]{1,0:T(8,128)(2,1)S(1)}, u32[]{:S(2)}, u32[]{:S(2)}) collective-permute-start(bf16[512,512]{1,0:T(8,128)(2,1)} %get-tuple-element.103), channel_id=1, source_target_pairs={{0,2},{1,3},{2,0},{5,7},{6,4},{7,5},{8,10},{9,11},{10,8},{13,15},{... | collective-permute-start | bytes 1572872 | tf_op jit(solution)/shard_map/ppermute | solution.py:620
  519.2 56.8 %collective-permute-start.14 = (bf16[512,512]{1,0:T(8,128)(2,1)S(1)}, bf16[512,512]{1,0:T(8,128)(2,1)S(1)}, u32[]{:S(2)}, u32[]{:S(2)}) collective-permute-start(bf16[512,512]{1,0:T(8,128)(2,1)S(1)} %get-tuple-element.102), channel_id=1, source_target_pairs={{0,1},{1,2},{2,3},{5,6},{6,7},{7,4},{8,9},{9,10},{10,11},{13,14},{... | collective-permute-start | bytes 1572872 | tf_op jit(solution)/shard_map/ppermute | solution.py:620
  521.3 71.0 %collective-permute-start.10 = (bf16[512,512]{1,0:T(8,128)(2,1)S(1)}, bf16[512,512]{1,0:T(8,128)(2,1)S(1)}, u32[]{:S(2)}, u32[]{:S(2)}) collective-permute-start(bf16[512,512]{1,0:T(8,128)(2,1)S(1)} %get-tuple-element.106), channel_id=1, source_target_pairs={{0,2},{1,3},{2,0},{5,7},{6,4},{7,5},{8,10},{9,11},{10,8},{13,15},{... | collective-permute-start | bytes 1572872 | tf_op jit(solution)/shard_map/ppermute | solution.py:620
  537.6 73.1 %collective-permute-start.11 = (bf16[512,512]{1,0:T(8,128)(2,1)S(1)}, bf16[512,512]{1,0:T(8,128)(2,1)S(1)}, u32[]{:S(2)}, u32[]{:S(2)}) collective-permute-start(bf16[512,512]{1,0:T(8,128)(2,1)S(1)} %get-tuple-element.105), channel_id=1, source_target_pairs={{0,1},{1,2},{2,3},{5,6},{6,7},{7,4},{8,9},{9,10},{10,11},{13,14},{... | collective-permute-start | bytes 1572872 | tf_op jit(solution)/shard_map/ppermute | solution.py:620
  561.1 49.6 %collective-permute-start.9 = (bf16[512,512]{1,0:T(8,128)(2,1)S(1)}, bf16[512,512]{1,0:T(8,128)(2,1)S(1)}, u32[]{:S(2)}, u32[]{:S(2)}) collective-permute-start(bf16[512,512]{1,0:T(8,128)(2,1)S(1)} %get-tuple-element.107), channel_id=1, source_target_pairs={{0,3},{1,0},{2,1},{5,4},{6,5},{7,6},{8,11},{9,8},{10,9},{13,12},{1... | collective-permute-start | bytes 1572872 | tf_op jit(solution)/shard_map/ppermute | solution.py:620
  610.9 248.9 %copy-start.1 = (s32[3,1,4]{2,1,0:T(1,128)S(1)}, s32[3,1,4]{2,1,0:T(1,128)}, u32[]{:S(2)}) copy-start(s32[3,1,4]{2,1,0:T(1,128)} %param.19) | copy-start | bytes 148
Sparse Core Ops, SparseCore 0:
  11.4 83.5 all-gather.4
  98.0 79.1 all-gather.6
  377.7 174.7 reduce-scatter.5
  554.7 153.7 reduce-scatter.3
  710.7 145.9 reduce-scatter.7

commit v2 on v1

--- a/solution.py
+++ b/solution.py
@@ -19,13 +19,18 @@
 PIECE = 512
 PIECES = GROUP // PIECE
 QB = 256
-KB = 256
+KB = 512
+FR = 512
+LANES = 128
 NEG = -1e30
 BLOCKS = 32
 BROWS = D * 4 // BLOCKS
 bf16 = jnp.bfloat16
 f32 = jnp.float32
 VMEM_LIMIT = 58 << 20
+CORE = 3 * SEQS + 2
+HALF = BLOCKS // 2
+SMALL = 16
 
 
 def dot(left, right, cl=1, cr=0):
@@ -66,6 +71,10 @@
 
 def piece_row(info, k):
     return pl.multiple_of(lax.rem(info[3 * SEQS] - k + PIECES, PIECES) * PIECE, PIECE)
+
+
+def shift_row(info, k):
+    return pl.multiple_of(lax.rem(info[3 * SEQS] + k, PIECES) * PIECE, PIECE)
 
 
 def weight(ref, first, count, offset, rows):
@@ -108,13 +117,10 @@
             for j in range(SEQS):
                 start = ends[j - 1] if j else 0
                 need = need | ((start < q0 + QB) & (ends[j] > q0) & (picks[j] == mem))
-            allowed = picked == mem
-
-            def step(j, carry, mem=mem, allowed=allowed):
-                tile(pl.multiple_of(mem * MEM_LEN + j * KB, KB), None, allowed)
-                return carry
-
-            lax.fori_loop(0, jnp.where(need, MEM_LEN // KB, 0), step, 0)
+
+            @pl.when(need)
+            def _():
+                tile(mem * MEM_LEN, MEM_LEN, None, picked == mem)
     else:
         low, high = 0, GROUP
         low_row = jnp.zeros((1, QB), jnp.int32)
@@ -125,71 +131,121 @@
         for j in reversed(range(SEQS - 1)):
             high = jnp.where(q0 + QB - 1 < ends[j], ends[j], high)
             high_row = jnp.where(rows < ends[j], ends[j], high_row)
+        low = low // LANES * LANES
+        many = (high - low) // KB
+        rest = high - low - many * KB
+        many = jnp.where(rest > KB // 2, many + 1, many)
+
+        def part(first, size):
+            k0 = pl.multiple_of(jnp.minimum(first, GROUP - size), LANES)
+            keys = k0 + lax.broadcasted_iota(jnp.int32, (size, QB), 0)
+            inside = (keys >= jnp.maximum(low_row, first)) & (keys < high_row)
+            tile(k0, size, jnp.where(inside, 0.0, NEG), None)
 
         def step(j, carry):
-            k0 = pl.multiple_of(j * KB, KB)
-            keys = k0 + lax.broadcasted_iota(jnp.int32, (KB, QB), 0)
-            bias = jnp.where((keys >= low_row) & (keys < high_row), 0.0, NEG)
-            tile(k0, bias, None)
+            part(low + j * KB, KB)
             return carry
 
-        lax.fori_loop(low // KB, (high + KB - 1) // KB, step, 0)
+        lax.fori_loop(0, many, step, 0)
+
+        @pl.when((rest > 0) & (rest <= KB // 2))
+        def _():
+            part(low + many * KB, KB // 2)
 
 
 def head_rows(h):
     return slice(h * HEAD_DIM, (h + 1) * HEAD_DIM)
 
 
+def pipelined(groups, *stages):
+    for step in range(groups + len(stages) - 1):
+        for lag, stage in enumerate(stages):
+            if 0 <= step - lag < groups:
+                stage(step - lag)
+
+
 def attend_kernel(cross, info, qt, k, v, ot, lse, vt, top, total, acc, bias_ref):
     i = pl.program_id(0)
+    q0 = pl.multiple_of(i * QB, QB)
+    group = 2
 
     @pl.when(i == 0)
     def _():
         for c in range(GROUP // QB):
             vt[:, c * QB : (c + 1) * QB] = v[c * QB : (c + 1) * QB, :].T
 
-    top[...] = jnp.full_like(top, NEG)
-    total[...] = jnp.zeros_like(total)
-    acc[...] = jnp.zeros_like(acc)
-
-    def tile(k0, bias, allowed):
-        keys = pl.ds(k0, KB)
-        if bias is not None:
-            bias_ref[...] = bias
-        tops, totals = top[...], total[...]
-        new_tops, new_totals = [], []
-        group = 8
-        for g in range(0, HEADS, group):
-            heads = range(g, g + group)
-            scores = [dot(k[keys, head_rows(h)], qt[head_rows(h), :]) for h in heads]
-            parts = []
-            for h, s in zip(heads, scores):
-                old = tops[h : h + 1]
-                if bias is not None:
-                    s = s + bias_ref[...]
-                    new = jnp.maximum(old, jnp.max(s, axis=0, keepdims=True))
-                    base = new
-                else:
-                    peak = jnp.maximum(old, jnp.max(s, axis=0, keepdims=True))
-                    new = jnp.where(allowed, peak, old)
-                    base = jnp.where(allowed, peak, -NEG)
-                decay = jnp.exp(old - new)
-                p = jnp.exp(s - base)
-                new_tops.append(new)
-                new_totals.append(totals[h : h + 1] * decay + jnp.sum(p, axis=0, keepdims=True))
-                parts.append((decay, p.astype(bf16)))
-            for h, (decay, p) in zip(heads, parts):
-                acc[head_rows(h), :] = acc[head_rows(h), :] * decay + dot(
-                    vt[head_rows(h), keys], p
-                )
-        top[...] = jnp.concatenate(new_tops, axis=0)
-        total[...] = jnp.concatenate(new_totals, axis=0)
-
-    key_loop(info, cross, pl.multiple_of(i * QB, QB), tile)
-    lse[...] = top[...] + jnp.log(total[...])
-    inverse = 1.0 / total[...]
-    for h in range(HEADS):
-        ot[head_rows(h), :] = (acc[head_rows(h), :] * inverse[h : h + 1]).astype(bf16)
+    def sweep(safe):
+        if safe:
+            top[...] = jnp.full_like(top, NEG)
+        total[...] = jnp.zeros_like(total)
+        acc[...] = jnp.zeros_like(acc)
+
+        def tile(k0, size, bias, allowed):
+            keys = pl.ds(k0, size)
+            if bias is not None:
+                bias_ref[:size, :] = bias
+            totals = total[...]
+            tops = top[...] if safe else None
+            new_tops, new_totals = [], []
+            scores, parts = {}, {}
+
+            def score(g):
+                heads = range(g * group, (g + 1) * group)
+                scores[g] = [dot(k[keys, head_rows(h)], qt[head_rows(h), :]) for h in heads]
+
+            def soften(g):
+                parts[g] = []
+                for n, s in enumerate(scores.pop(g)):
+                    h = g * group + n
+                    decay = None
+                    if bias is not None:
+                        s = s + bias_ref[:size, :]
+                    if safe:
+                        old = tops[h : h + 1]
+                        new = jnp.maximum(old, jnp.max(s, axis=0, keepdims=True))
+                        if allowed is not None:
+                            new = jnp.where(allowed, new, old)
+                        decay = jnp.exp(old - new)
+                        new_tops.append(new)
+                        s = s - new
+                    p = jnp.exp(s)
+                    if safe and allowed is not None:
+                        p = jnp.where(allowed, p, 0.0)
+                    part = jnp.sum(p, axis=0, keepdims=True)
+                    if allowed is not None:
+                        part = jnp.where(allowed, part, 0.0)
+                    before = totals[h : h + 1]
+                    new_totals.append((before * decay if safe else before) + part)
+                    parts[g].append((decay, p.astype(bf16)))
+
+            def mix(g):
+                for n, (decay, p) in enumerate(parts.pop(g)):
+                    rows = head_rows(g * group + n)
+                    part = dot(vt[rows, keys], p)
+                    if allowed is not None:
+                        part = jnp.where(allowed, part, 0.0)
+                    before = acc[rows, :]
+                    acc[rows, :] = (before * decay if safe else before) + part
+
+            pipelined(HEADS // group, score, soften, mix)
+            if safe:
+                top[...] = jnp.concatenate(new_tops, axis=0)
+            total[...] = jnp.concatenate(new_totals, axis=0)
+
+        key_loop(info, cross, q0, tile)
+        sums = total[...]
+        inverse = 1.0 / sums
+        lse[...] = jnp.log(sums) + (top[...] if safe else 0.0)
+        for h in range(HEADS):
+            ot[head_rows(h), :] = (acc[head_rows(h), :] * inverse[h : h + 1]).astype(bf16)
+
+    sweep(False)
+    sums = total[...]
+    safe_range = (jnp.min(sums) > 1e-18) & (jnp.max(sums) < 1e18)
+
+    @pl.when(jnp.logical_not(safe_range))
+    def _():
+        sweep(True)
 
 
 def attend_back_kernel(
@@ -225,32 +281,42 @@
     ]
     dqt_acc[...] = jnp.zeros_like(dqt_acc)
 
-    def tile(k0, bias, allowed):
-        keys = pl.ds(k0, KB)
+    def tile(k0, size, bias, allowed):
+        keys = pl.ds(k0, size)
         if bias is not None:
-            bias_ref[...] = bias
+            bias_ref[:size, :] = bias
         lses = lse[...]
         if allowed is not None:
             lses = jnp.where(allowed, lses, -NEG)
-        group = 4
-        for first in range(0, HEADS, group):
-            heads = range(first, first + group)
-            scores = [dot(k[keys, head_rows(h)], qt[head_rows(h), :]) for h in heads]
-            slopes = [dot(v[keys, head_rows(h)], gt[head_rows(h), :]) for h in heads]
-            probs, grads = [], []
-            for h, s, dp in zip(heads, scores, slopes):
+        group = 2
+        scores, slopes, probs, grads = {}, {}, {}, {}
+
+        def score(g):
+            heads = range(g * group, (g + 1) * group)
+            scores[g] = [dot(k[keys, head_rows(h)], qt[head_rows(h), :]) for h in heads]
+            slopes[g] = [dot(v[keys, head_rows(h)], gt[head_rows(h), :]) for h in heads]
+
+        def soften(g):
+            probs[g], grads[g] = [], []
+            for n, (s, dp) in enumerate(zip(scores.pop(g), slopes.pop(g))):
+                h = g * group + n
                 if bias is not None:
-                    s = s + bias_ref[...]
+                    s = s + bias_ref[:size, :]
                 p = jnp.exp(s - lses[h : h + 1])
-                probs.append(p.astype(bf16))
-                grads.append((p * (dp - weighted[h])).astype(bf16))
+                probs[g].append(p.astype(bf16))
+                grads[g].append((p * (dp - weighted[h])).astype(bf16))
+
+        def mix(g):
             for n in range(0, group, 2):
-                pair = (first + n) // 2
+                pair = (g * group + n) // 2
                 cols = slice(pair * 2 * HEAD_DIM, (pair + 1) * 2 * HEAD_DIM)
-                dv_acc[keys, cols] += dot(jnp.concatenate(probs[n : n + 2], axis=1), gm[pair])
-                dk_acc[keys, cols] += dot(jnp.concatenate(grads[n : n + 2], axis=1), qm[pair])
-            for h, ds in zip(heads, grads):
-                dqt_acc[head_rows(h), :] += dot(kt[head_rows(h), keys], ds)
+                dv_acc[keys, cols] += dot(jnp.concatenate(probs[g][n : n + 2], axis=1), gm[pair])
+                dk_acc[keys, cols] += dot(jnp.concatenate(grads[g][n : n + 2], axis=1), qm[pair])
+            for n, ds in enumerate(grads[g]):
+                rows = head_rows(g * group + n)
+                dqt_acc[rows, :] += dot(kt[rows, keys], ds)
+
+        pipelined(HEADS // group, score, soften, mix)
 
     key_loop(info, cross, pl.multiple_of(i * QB, QB), tile)
     dqt[...] = (dqt_acc[...] * HEAD_DIM**-0.5).astype(bf16)
@@ -292,7 +358,7 @@
 
 def ffn_kernel(
     info, oct_, n1, wb, vecs, b1, c0, c1, c2, c3,
-    yg, d2, gc, g_ffn, g_co, g_b1, g_vec,
+    y0, y1, y2, y3, d2, gc, keep_ffn, send_ffn, g_co, g_b1, g_vec,
     cot, act, slope, dy, gw1, gw2, gco, yacc,
 ):
     i = pl.program_id(0)
@@ -321,24 +387,35 @@
 
     factor = math.sqrt(2.0 / math.pi)
     cubic = 0.044715 * factor
-    out = jnp.zeros((PIECE, D), f32)
-    for c in range(4):
-        cols = slice(c * D, (c + 1) * D)
-        u = dot(hidden_b, w1(c)) + b1[0:1, cols]
+    ups, acts, outs = {}, {}, []
+
+    def cols(c):
+        return slice(c * D, (c + 1) * D)
+
+    def up(c):
+        ups[c] = dot(hidden_b, w1(c))
+
+    def bend(c):
+        u = ups.pop(c) + b1[0:1, cols(c)]
         sq = u * u
         t = jnp.tanh(u * (factor + cubic * sq))
         half = 0.5 + 0.5 * t
-        a = (u * half).astype(bf16)
-        act[:, cols] = a
-        slope[:, cols] = half + u * (1.0 - t * t) * (0.5 * factor + 1.5 * cubic * sq)
-        out = out + dot(a, w2(c))
+        acts[c] = (u * half).astype(bf16)
+        act[:, cols(c)] = acts[c]
+        slope[:, cols(c)] = half + u * (1.0 - t * t) * (0.5 * factor + 1.5 * cubic * sq)
+
+    def down(c):
+        outs.append(dot(acts.pop(c), w2(c)))
+
+    pipelined(4, up, bend, down)
+    out = (outs[0] + outs[1]) + (outs[2] + outs[3])
     n3, inv3 = norm(hidden + (out + vecs[6:7, :]))
     y = (n3 * vecs[2:3, :] + vecs[5:6, :]).astype(bf16)
 
     ends = place_ends(info)
     shifts = place_shifts(info, ends)
-    p0 = i * PIECE
-    rows = p0 + lax.broadcasted_iota(jnp.int32, (PIECE, 1), 0)
+    p0 = i * FR
+    rows = p0 + lax.broadcasted_iota(jnp.int32, (FR, 1), 0)
     given = rows + by_place(rows, ends, shifts)
     dy[...] = jnp.zeros_like(dy)
 
@@ -347,14 +424,14 @@
         hit = jnp.bool_(False)
         for j in range(SEQS):
             begin = jnp.maximum(ends[j - 1] if j else 0, p0)
-            end = jnp.minimum(ends[j], p0 + PIECE)
+            end = jnp.minimum(ends[j], p0 + FR)
             hit = hit | (
                 (begin < end) & (begin + shifts[j] < r0 + QB) & (end + shifts[j] > r0)
             )
 
         @pl.when(hit)
         def _():
-            cols = r0 + lax.broadcasted_iota(jnp.int32, (PIECE, QB), 1)
+            cols = r0 + lax.broadcasted_iota(jnp.int32, (FR, QB), 1)
             select = jnp.where(cols == given, 1.0, 0.0).astype(bf16)
             dy[...] += dot(select, cot[pl.ds(r0, QB), :])
             yacc[pl.ds(r0, QB), :] += dot(select, y, 0, 0)
@@ -369,15 +446,23 @@
     d3 = norm_back(grad, n3, inv3, vecs[2:3, :])
     df = d3.astype(bf16)
     g_vec[6:7, :] += column_sum(df.astype(f32))
-    back = d3
-    for c in range(4):
-        cols = slice(c * D, (c + 1) * D)
-        a = act[:, cols]
-        gw2[cols, :] += dot(a, df, 0, 0)
-        du = (dot(df, w2(c), 1, 1) * slope[:, cols]).astype(bf16)
+    downs, dus, backs = {}, {}, [d3]
+
+    def down_back(c):
+        downs[c] = dot(df, w2(c), 1, 1)
+        gw2[cols(c), :] += dot(act[:, cols(c)], df, 0, 0)
+
+    def bend_back(c):
+        dus[c] = (downs.pop(c) * slope[:, cols(c)]).astype(bf16)
+        g_b1[0:1, cols(c)] += column_sum(dus[c].astype(f32))
+
+    def up_back(c):
+        du = dus.pop(c)
         gw1[c] += dot(hidden_b, du, 0, 0)
-        g_b1[0:1, cols] += column_sum(du.astype(f32))
-        back = back + dot(du, w1(c), 1, 1)
+        backs.append(dot(du, w1(c), 1, 1))
+
+    pipelined(4, down_back, bend_back, up_back)
+    back = ((backs[0] + backs[1]) + (backs[2] + backs[3])) + backs[4]
     g_vec[1:2, :] += column_sum(back * n2)
     g_vec[4:5, :] += column_sum(back)
     second = norm_back(back, n2, inv2, vecs[1:2, :])
@@ -389,21 +474,35 @@
     @pl.when(i == pl.num_programs(0) - 1)
     def _():
         keep = info[3 * SEQS + 1] > 0
-        yg[...] = yacc[...].astype(bf16)
+        for k, ref in enumerate((y0, y1, y2, y3)):
+            ref[...] = yacc[pl.ds(shift_row(info, k), PIECE), :].astype(bf16)
         g_co[...] = jnp.where(keep, gco[...], 0.0).astype(bf16)
-        for c in range(4):
-            part = jnp.where(keep, gw1[c], 0.0).astype(bf16)
-            g_ffn[:, c * chunk : (c + 1) * chunk, :] = part.reshape(BLOCKS, chunk, D)
-            part = jnp.where(keep, gw2[c * D : (c + 1) * D, :], 0.0).astype(bf16)
-            per = BLOCKS // 4
-            g_ffn[c * per : (c + 1) * per, BROWS:, :] = part.reshape(per, BROWS, D)
+        for ref, core in ((keep_ffn, info[CORE]), (send_ffn, 1 - info[CORE])):
+            for n in range(4):
+                blocks = slice(4 * n, 4 * n + 4)
+                for c in range(4):
+                    r0 = pl.multiple_of((2 * n + core) * 4 * chunk, 4 * chunk)
+                    part = jnp.where(keep, gw1[c, pl.ds(r0, 4 * chunk), :], 0.0).astype(bf16)
+                    ref[blocks, c * chunk : (c + 1) * chunk, :] = part.reshape(4, chunk, D)
+                r0 = pl.multiple_of((2 * n + core) * 4 * BROWS, 4 * BROWS)
+                part = jnp.where(keep, gw2[pl.ds(r0, 4 * BROWS), :], 0.0).astype(bf16)
+                ref[blocks, BROWS:, :] = part.reshape(4, BROWS, D)
         g_b1[...] = jnp.where(keep, g_b1[...], 0.0)
         g_vec[...] = jnp.where(keep, g_vec[...], 0.0)
 
 
+def store_shifted(info, i, refs, value):
+    shift = lax.rem(i - info[3 * SEQS] + PIECES, PIECES)
+    for k, ref in enumerate(refs):
+
+        @pl.when(shift == k)
+        def _():
+            ref[...] = value
+
+
 def cross_post_kernel(
     info, dqct, dkc, dvc, mem, d2, n1, inv1, ot, wa, wb, vecs, g_co,
-    dmem, d1, go, g_cross, g_wo, g_vec,
+    m0, m1, m2, m3, d1, go, g_cross, g_wo, g_vec,
     gcq, gck, gcv, gwo,
 ):
     i = pl.program_id(0)
@@ -414,7 +513,8 @@
             ref[...] = jnp.zeros_like(ref)
 
     m, dk, dv = mem[...], dkc[...], dvc[...]
-    dmem[...] = (dot(dk, square(wb, 1), 1, 1) + dot(dv, square(wb, 2), 1, 1)).astype(bf16)
+    dmem = (dot(dk, square(wb, 1), 1, 1) + dot(dv, square(wb, 2), 1, 1)).astype(bf16)
+    store_shifted(info, i, (m0, m1, m2, m3), dmem)
     gck[...] += dot(m, dk, 0, 0)
     gcv[...] += dot(m, dv, 0, 0)
     normed = n1[...]
@@ -440,8 +540,8 @@
         g_vec[...] = jnp.where(keep, g_vec[...], 0.0)
 
 
-def self_post_kernel(
-    info, dqt, dk_ref, dv_ref, x_ref, d1, wa, g_wo, dtok, g_self, gq, gk, gv
+def self_grad_kernel(
+    info, dqt, dk_ref, dv_ref, x_ref, g_wo, g_cross, g_small, keep_out, send_out, gq, gk, gv
 ):
     i = pl.program_id(0)
 
@@ -450,24 +550,103 @@
         for ref in (gq, gk, gv):
             ref[...] = jnp.zeros_like(ref)
 
-    x, dk, dv = x_ref[...], dk_ref[...], dv_ref[...]
-    dq = dqt[...].T
-    dtok[...] = (
-        d1[...]
-        + dot(dq, square(wa, 0), 1, 1)
-        + dot(dk, square(wa, 1), 1, 1)
-        + dot(dv, square(wa, 2), 1, 1)
-    ).astype(bf16)
-    gq[...] += dot(x, dq, 0, 0)
-    gk[...] += dot(x, dk, 0, 0)
-    gv[...] += dot(x, dv, 0, 0)
+    x = x_ref[...]
+    gq[...] += dot(x, dqt[...], 0, 1)
+    gk[...] += dot(x, dk_ref[...], 0, 0)
+    gv[...] += dot(x, dv_ref[...], 0, 0)
 
     @pl.when(i == pl.num_programs(0) - 1)
     def _():
         keep = info[3 * SEQS + 1] > 0
-        for n, ref in enumerate((gq, gk, gv)):
-            g_self[n * D : (n + 1) * D, :] = jnp.where(keep, ref[...], 0.0).astype(bf16)
-        g_self[3 * D :, :] = g_wo[...]
+        rows = 4 * BROWS
+        for ref, core in ((keep_out, info[CORE]), (send_out, 1 - info[CORE])):
+            for n in range(4):
+                blocks = slice(4 * n, 4 * n + 4)
+                r0 = pl.multiple_of(core * rows, rows)
+                if n < 3:
+                    part = jnp.where(keep, (gq, gk, gv)[n][pl.ds(r0, rows), :], 0.0).astype(bf16)
+                else:
+                    part = g_wo[pl.ds(r0, rows), :]
+                ref[blocks, :BROWS, :] = part.reshape(4, BROWS, D)
+                part = g_cross[pl.ds(pl.multiple_of(r0 + n * D, rows), rows), :]
+                ref[blocks, BROWS : 2 * BROWS, :] = part.reshape(4, BROWS, D)
+                ref[blocks, 2 * BROWS :, :] = g_small[pl.ds((2 * n + core) * 4, 4), :, :]
+
+
+def self_input_kernel(info, dqt, dk, dv, d1, wa, t0, t1, t2, t3):
+    value = (
+        d1[...]
+        + dot(dqt[...], square(wa, 0), 0, 1)
+        + dot(dk[...], square(wa, 1), 1, 1)
+        + dot(dv[...], square(wa, 2), 1, 1)
+    ).astype(bf16)
+    store_shifted(info, pl.program_id(0), (t0, t1, t2, t3), value)
+
+
+def pick_kernel(count, places, *refs):
+    arrays, outs, sems = refs[:count], refs[count : 5 * count], refs[5 * count]
+    copies = []
+    for n, array in enumerate(arrays):
+        for k in range(PIECES):
+            copies.append(
+                pltpu.make_async_copy(array.at[places[k]], outs[n * PIECES + k], sems.at[n, k])
+            )
+    for copy in copies:
+        copy.start()
+    for copy in copies:
+        copy.wait()
+
+
+def place_kernel(places, near, far, out):
+    for n in range(HALF):
+        out[pl.ds(places[n], 1)] = near[n : n + 1]
+        out[pl.ds(places[HALF + n], 1)] = far[n : n + 1]
+
+
+def unpack_kernel(places, r0, r1, r2, r3, out):
+    b = pl.program_id(0)
+    for k, ref in enumerate((r0, r1, r2, r3)):
+
+        @pl.when(places[b] == k)
+        def _():
+            out[0] = ref[...].astype(f32)
+
+
+def plus(*parts):
+    total = parts[0].astype(f32)
+    for part in parts[1:]:
+        total = total + part.astype(f32)
+    return total
+
+
+def route_one_kernel(info, keep, recv, a_keep, a_send, b_keep, b_send):
+    x, y = info[CORE + 1], info[CORE + 2]
+    for n in range(2):
+        for ref, own in ((a_keep, x), (a_send, 1 - x)):
+            at = (2 * n + own) * 4
+            ref[n] = plus(keep[pl.ds(at, 2)], recv[pl.ds(at, 2)]).astype(bf16)
+        for ref, own in ((b_keep, y), (b_send, 1 - y)):
+            at = (2 * own + n) * 4 + 2
+            ref[n] = plus(keep[pl.ds(at, 2)], recv[pl.ds(at, 2)]).astype(bf16)
+
+
+def route_two_kernel(info, a, ra, b, rb, a_keep, a_send, b_keep, b_send):
+    x, y = info[CORE + 1], info[CORE + 2]
+    for ref, own in ((a_keep, y), (a_send, 1 - y)):
+        ref[...] = plus(a[own], ra[own]).astype(bf16)
+    for ref, own in ((b_keep, x), (b_send, 1 - x)):
+        ref[...] = plus(b[own], rb[own]).astype(bf16)
+
+
+def route_three_kernel(info, a, ra, b, rb, o0, o1, o2, o3, total):
+    total[0:2] = plus(a[...], ra[...]).astype(bf16)
+    total[2:4] = plus(b[...], rb[...]).astype(bf16)
+    for k, ref in enumerate((o0, o1, o2, o3)):
+        ref[...] = total[lax.rem(info[3 * SEQS] + k, PIECES)]
+
+
+def route_four_kernel(r0, r1, r2, r3, out):
+    out[...] = plus(r0[...], r1[...], r2[...], r3[...])
 
 
 SMEM = pl.BlockSpec(memory_space=pltpu.SMEM)
@@ -477,11 +656,15 @@
 ROWS_Q = pl.BlockSpec((QB, D), lambda i: (i, 0))
 COLS_Q = pl.BlockSpec((D, QB), lambda i: (0, i))
 HEADS_Q = pl.BlockSpec((HEADS, QB), lambda i: (0, i))
+ROWS_F = pl.BlockSpec((FR, D), lambda i: (i, 0))
+COLS_F = pl.BlockSpec((D, FR), lambda i: (0, i))
 ONES = pl.BlockSpec((PIECE, 1), lambda i: (i, 0))
 
 
 def fixed(*shape):
-    return pl.BlockSpec(shape, lambda i: (0,) * len(shape))
+    return pl.BlockSpec(
+        shape, lambda i: (0,) * len(shape), pipeline_mode=pl.Buffered(buffer_count=1)
+    )
 
 
 def shape(dims, dtype=bf16):
@@ -575,6 +758,110 @@
     )
 
 
+ANY = pl.BlockSpec(memory_space=pl.ANY)
+
+
+def pick_four(arrays, places):
+    n = len(arrays)
+    outs = call(
+        functools.partial(pick_kernel_args, n),
+        "pick",
+        (),
+        [SMEM] + [ANY] * n,
+        [WHOLE] * (PIECES * n),
+        [shape(a.shape[1:], a.dtype) for a in arrays for _ in range(PIECES)],
+        [pltpu.SemaphoreType.DMA((n, PIECES))],
+        1 << 20,
+        places,
+        *arrays,
+    )
+    return [list(outs[PIECES * m : PIECES * (m + 1)]) for m in range(n)]
+
+
+def pick_kernel_args(count, places, *refs):
+    pick_kernel(count, places, *refs)
+
+
+def place_blocks(places, near, far):
+    return call(
+        place_kernel,
+        "place",
+        (),
+        [SMEM, WHOLE, WHOLE],
+        WHOLE,
+        shape((BLOCKS,) + near.shape[1:]),
+        [],
+        1 << 20,
+        places,
+        near,
+        far,
+    )
+
+
+def unpack(places, pieces, micro):
+    return call(
+        unpack_kernel,
+        "unpack",
+        (micro,),
+        [SMEM] + [fixed(PIECE, D)] * PIECES,
+        pl.BlockSpec((1, PIECE, D), lambda b: (b, 0, 0)),
+        shape((micro, PIECE, D), f32),
+        [],
+        1 << 20,
+        places,
+        *pieces,
+    )
+
+
+def route_one(info, keep, recv):
+    half = shape((2, 2) + keep.shape[1:])
+    return call(
+        route_one_kernel, "route_one", (), [SMEM, WHOLE, WHOLE], [WHOLE] * 4, [half] * 4, [], 1 << 20,
+        info, keep, recv,
+    )
+
+
+def route_two(info, a, ra, b, rb):
+    half = shape(a.shape[1:])
+    return call(
+        route_two_kernel, "route_two", (), [SMEM] + [WHOLE] * 4, [WHOLE] * 4, [half] * 4, [], 1 << 20,
+        info, a, ra, b, rb,
+    )
+
+
+def route_three(info, a, ra, b, rb):
+    block = a.shape[1:]
+    return call(
+        route_three_kernel, "route_three", (), [SMEM] + [WHOLE] * 4, [WHOLE] * 4,
+        [shape(block)] * 4, [pltpu.VMEM((4,) + block, bf16)], 1 << 20,
+        info, a, ra, b, rb,
+    )
+
+
+def route_four(pieces):
+    return call(
+        route_four_kernel, "route_four", (), [WHOLE] * 4, WHOLE, shape(pieces[0].shape, f32), [], 1 << 20,
+        *pieces,
+    )
+
+
+def tie(value, *deps):
+    return lax.optimization_barrier((value, deps))[0]
+
+
+def dp_swap(array, bit):
+    n = lax.axis_size("dp")
+    return lax.ppermute(array, "dp", [(d, d ^ bit) for d in range(n)])
+
+
+def turns(arrays):
+    n = lax.axis_size("fsdp")
+    return [arrays[0]] + [
+        lax.ppermute(arrays[k], "fsdp", [(m, (m + k) % n) for m in range(n)])
+        for k in range(1, len(arrays))
+    ]
+
+
 def local(
     tokens, memory, cotangent, lengths, seq_order, memory_pick,
     self_attn, cross_attn, ffn_in, ffn_in_bias, ffn_out, ffn_out_bias, norm_gain, norm_bias,
@@ -604,38 +891,33 @@
                     out.append((d * members + source, d * members + target))
         return out
 
-    def to_unit(array):
-        pieces = [lax.dynamic_index_in_dim(array, unit, 0, False)]
-        for k in range(1, members):
-            target = jnp.clip(unit_at(dp, lax.rem(z + k, members)), 0, micro - 1)
-            part = lax.dynamic_index_in_dim(array, target, 0, False)
-            pieces.append(lax.ppermute(part, axes, pairs(k, True)))
-        return pieces
-
-    def from_unit(array):
-        blocks = array.reshape(members, PIECE, D)
-        pieces = [lax.dynamic_index_in_dim(blocks, z, 0, False)]
-        for k in range(1, members):
-            part = lax.dynamic_index_in_dim(blocks, lax.rem(z + k, members), 0, False)
-            pieces.append(lax.ppermute(part, axes, pairs(k, False)))
-        out = []
-        for b in range(micro):
-            shift = lax.rem(z - offset(dp) - b + 2 * members, members)
-            value = pieces[0]
-            for k in range(1, members):
-                value = jnp.where(shift == k, pieces[k], value)
-            out.append(value.astype(f32))
-        return jnp.stack(out)
+    boxed = n_dp == 8 and members == 4
+    shifts = jnp.arange(members, dtype=jnp.int32)
+
+    targets = jnp.clip(lax.rem(z + shifts, members) - offset(dp), 0, micro - 1)
+    sources = lax.rem(z - offset(dp) - jnp.arange(micro, dtype=jnp.int32) + 2 * members, members)
+    targets = targets.at[0].set(unit).astype(jnp.int32)
+
+    def to_unit(pieces):
+        return [pieces[0]] + [
+            lax.ppermute(pieces[k], axes, pairs(k, True)) for k in range(1, members)
+        ]
+
+    def from_unit(pieces):
+        return [pieces[0]] + [
+            lax.ppermute(pieces[k], axes, pairs(k, False)) for k in range(1, members)
+        ]
 
     def row_of(array):
         return lax.dynamic_index_in_dim(array, unit, 0, False)[0]
 
+    bits = [dp & 1, (dp >> 1) & 1, (dp >> 2) & 1] if boxed else [jnp.zeros_like(dp)] * 3
     info = jnp.concatenate(
         [
             row_of(lengths),
             row_of(seq_order),
             row_of(memory_pick),
-            jnp.stack([z, valid.astype(jnp.int32)]),
+            jnp.stack([z, valid.astype(jnp.int32), *bits]),
         ]
     ).astype(jnp.int32)
 
@@ -649,20 +931,34 @@
     bundle_a = jnp.concatenate([self_attn, small_row], axis=0)
     in_blocks = ffn_in.reshape(in_rows, 4, D).transpose(1, 0, 2).reshape(4 * in_rows, D)
     bundle_b = jnp.concatenate([cross_attn, ffn_out, in_blocks], axis=0)
-    all_a = lax.all_gather(bundle_a, axes, axis=0, tiled=False)
-    token_pieces = to_unit(tokens)
+    token_slices = pick_four([tokens], targets)[0]
+    bundle_a = tie(bundle_a, *token_slices)
+    token_pieces = to_unit(token_slices)
+    if boxed:
+        turned = turns([bundle_a] * members)
+        a0, b0 = jnp.stack(turned[:2]), jnp.stack(turned[2:])
+        a1, b1 = dp_swap(a0, 2), dp_swap(b0, 4)
+        a2 = dp_swap(jnp.stack([a0, a1]), 4)
+        b2 = dp_swap(jnp.stack([b0, b1]), 2)
+        near = jnp.concatenate([a0, a1, a2[0], a2[1], b0, b1, b2[0], b2[1]])
+        near = tie(near, *token_pieces[1:])
+        far = dp_swap(near, 1)
+        masks = jnp.array([0, 0, 2, 2, 4, 4, 6, 6, 0, 0, 4, 4, 2, 2, 6, 6], jnp.int32)
+        steps = jnp.array([0, 1] * 4 + [2, 3] * 4, jnp.int32)
+        owner = (dp ^ masks) * members + lax.rem(z - steps + members, members)
+        places = jnp.concatenate([owner, owner ^ members]).astype(jnp.int32)
+        all_a = place_blocks(places, near, far)
+    else:
+        all_a = lax.all_gather(bundle_a, axes, axis=0, tiled=False)
     all_b = lax.all_gather(bundle_b, axes, axis=0, tiled=False)
-    memory_pieces = to_unit(memory)
-    cotangent_pieces = to_unit(cotangent)
-
     def blocked(array, count):
         return array.reshape(BLOCKS, count, D)
 
     small = all_a[:, rows, :n_smalls].astype(f32)
-    wa = blocked(all_a[:, :rows], BROWS)
     if owners == BLOCKS:
-        wb = all_b
+        wa, wb = all_a, all_b
     else:
+        wa = jnp.pad(blocked(all_a[:, :rows], BROWS), ((0, 0), (0, SMALL), (0, 0)))
         first = all_b[:, 2 * rows :].reshape(owners, 4, in_rows, D).transpose(1, 0, 2, 3)
         first = first.reshape(4, BLOCKS, BROWS // 4, D).transpose(1, 0, 2, 3)
         wb = jnp.concatenate(
@@ -682,12 +978,17 @@
     )
 
     x, qt, k, v = project_rows(info, token_pieces, wa, True)
+    memory_in = tie(memory, x)
+    memory_pieces = to_unit(pick_four([memory_in], targets)[0])
     ot, lse = attend(info, qt, k, v, False)
+    ot = tie(ot, *memory_pieces[1:])
+    cotangent_in = tie(cotangent, *memory_pieces[1:])
+    cotangent_pieces = to_unit(pick_four([cotangent_in], targets)[0])
     n1, inv1, qct = call(
         first_norm_kernel,
         "first_norm",
         (PIECES,),
-        [COLS, ROWS, fixed(BLOCKS, BROWS, D), fixed(BLOCKS, 3 * BROWS, D), fixed(8, D)],
+        [COLS, ROWS, fixed(BLOCKS, BROWS + SMALL, D), fixed(BLOCKS, 3 * BROWS, D), fixed(8, D)],
         [ROWS, ONES, COLS],
         [shape((GROUP, D), f32), shape((GROUP, 1), f32), COLMAJOR],
         [],
@@ -700,35 +1001,37 @@
     )
     mem, kc, vc = project_rows(info, memory_pieces, wb, False)
     oct_, lse_c = attend(info, qct, kc, vc, True)
-    yg, d2, gc, g_ffn, g_co, g_b1, g_vec = call(
+    *y_out, d2, gc, keep_ffn, send_ffn, g_co, g_b1, g_vec = call(
         ffn_kernel,
         "ffn",
-        (PIECES,),
-        [SMEM, COLS, ROWS, fixed(BLOCKS, 3 * BROWS, D), fixed(8, D), fixed(1, FF)]
+        (GROUP // FR,),
+        [SMEM, COLS_F, ROWS_F, fixed(BLOCKS, 3 * BROWS, D), fixed(8, D), fixed(1, FF)]
         + [fixed(PIECE, D)] * 4,
         [
-            fixed(GROUP, D),
-            ROWS,
-            ROWS,
-            fixed(BLOCKS, 2 * BROWS, D),
+            *[fixed(PIECE, D)] * PIECES,
+            ROWS_F,
+            ROWS_F,
+            fixed(HALF, 2 * BROWS, D),
+            fixed(HALF, 2 * BROWS, D),
             fixed(D, D),
             fixed(1, FF),
             fixed(8, D),
         ],
         [
-            ROWMAJOR,
+            *[shape((PIECE, D))] * PIECES,
             shape((GROUP, D), f32),
             ROWMAJOR,
-            shape((BLOCKS, 2 * BROWS, D)),
+            shape((HALF, 2 * BROWS, D)),
+            shape((HALF, 2 * BROWS, D)),
             shape((D, D)),
             shape((1, FF), f32),
             shape((8, D), f32),
         ],
         [
             pltpu.VMEM((GROUP, D), bf16),
-            pltpu.VMEM((PIECE, FF), bf16),
-            pltpu.VMEM((PIECE, FF), f32),
-            pltpu.VMEM((PIECE, D), f32),
+            pltpu.VMEM((FR, FF), bf16),
+            pltpu.VMEM((FR, FF), f32),
+            pltpu.VMEM((FR, D), f32),
             pltpu.VMEM((4, D, D), f32),
             pltpu.VMEM((FF, D), f32),
             pltpu.VMEM((D, D), f32),
@@ -743,32 +1046,27 @@
         b1,
         *cotangent_pieces,
     )
-    layer_output = from_unit(yg)
-
-    def owned(array, count):
-        return lax.psum_scatter(array, axes, scatter_dimension=0, tiled=True).astype(f32)
-
-    if owners == BLOCKS:
-        ffn_part = owned(g_ffn, 0)[0]
-    else:
-        second = g_ffn[:, BROWS:].reshape(owners, rows, D)
-        first = g_ffn[:, :BROWS].reshape(BLOCKS, 4, BROWS // 4, D).transpose(1, 0, 2, 3)
-        first = first.reshape(4, owners, in_rows, D).transpose(1, 0, 2, 3)
-        both = jnp.concatenate([first.reshape(owners, rows, D), second], axis=1)
-        ffn_part = owned(both, 0)[0]
-    ffn_in_grad = ffn_part[:rows].reshape(4, in_rows, D).transpose(1, 0, 2).reshape(in_rows, FF)
-    ffn_out_grad = ffn_part[rows:]
+    y_pieces = from_unit(y_out)
+    if boxed:
+        recv_ffn = dp_swap(send_ffn, 1)
 
     dqct, dkc, dvc = attend_back(info, qct, kc, vc, gc, oct_, lse_c, True)
-    dmem, d1, go, g_cross, g_wo, g_vec_one = call(
+    if boxed:
+        recv_ffn = tie(recv_ffn, dqct)
+        ffn_a, send_a, ffn_b, send_b = route_one(info, keep_ffn, recv_ffn)
+        recv_a, recv_b = dp_swap(send_a, 2), dp_swap(send_b, 4)
+    layer_output = unpack(sources, y_pieces, micro)
+    if boxed:
+        g_co = tie(g_co, send_a, layer_output)
+    m_and_rest = call(
         cross_post_kernel,
         "cross_post",
         (PIECES,),
         [SMEM, COLS, ROWS, ROWS, ROWS, ROWS, ROWS, ONES, COLS]
-        + [fixed(BLOCKS, BROWS, D), fixed(BLOCKS, 3 * BROWS, D), fixed(8, D), fixed(D, D)],
-        [ROWS, ROWS, ROWS, fixed(4 * D, D), fixed(D, D), fixed(8, D)],
-        [
-            ROWMAJOR,
+        + [fixed(BLOCKS, BROWS + SMALL, D), fixed(BLOCKS, 3 * BROWS, D), fixed(8, D), fixed(D, D)],
+        [fixed(PIECE, D)] * PIECES + [ROWS, ROWS, fixed(4 * D, D), fixed(D, D), fixed(8, D)],
+        [shape((PIECE, D))] * PIECES
+        + [
             shape((GROUP, D), f32),
             ROWMAJOR,
             shape((4 * D, D)),
@@ -791,50 +1089,114 @@
         vecs,
         g_co,
     )
-    memory_grad = from_unit(dmem)
-    cross_attn_grad = owned(g_cross, 0)
-    dqt, dk, dv = attend_back(info, qt, k, v, go, ot, lse, False)
-    dtok, g_self = call(
-        self_post_kernel,
-        "self_post",
-        (PIECES,),
-        [SMEM, COLS, ROWS, ROWS, ROWS, ROWS, fixed(BLOCKS, BROWS, D), fixed(D, D)],
-        [ROWS, fixed(4 * D, D)],
-        [ROWMAJOR, shape((4 * D, D))],
-        [pltpu.VMEM((D, D), f32)] * 3,
-        7 << 30,
-        info,
-        dqt,
-        dk,
-        dv,
-        x,
-        d1,
-        wa,
-        g_wo,
-    )
-    input_grad = from_unit(dtok)
+    *m_out, d1, go, g_cross, g_wo, g_vec_one = m_and_rest
+    m_pieces = from_unit(m_out)
+    if boxed:
+        recv_a, recv_b, ffn_a, ffn_b = tie((recv_a, recv_b, ffn_a, ffn_b), d1)
+        ffn_a, send_a, ffn_b, send_b = route_two(info, ffn_a, recv_a, ffn_b, recv_b)
+        recv_a, recv_b = dp_swap(send_a, 4), dp_swap(send_b, 2)
+        go = tie(go, send_a)
     g_vec = g_vec + g_vec_one
     small_grads = jnp.concatenate(
         [g_b1.reshape(owners, rows), g_vec[6].reshape(owners, out_rows)]
         + [g_vec[n].reshape(owners, out_rows) for n in range(6)],
         axis=1,
     )
-    small_grads = jnp.pad(small_grads, ((0, 0), (0, 16 * D - n_smalls))).reshape(owners, 16, D)
-    last = jnp.concatenate(
-        [g_self.reshape(owners, rows, D), small_grads.astype(bf16)], axis=1
-    )
-    last = owned(last, 0)[0]
-    small_out = last[rows]
+    if boxed:
+        g_small = jnp.pad(small_grads.astype(bf16), ((0, 0), (0, SMALL * D - n_smalls)))
+        g_small = g_small.reshape(BLOCKS, SMALL, D)
+    else:
+        g_small = jnp.zeros((BLOCKS, SMALL, D), bf16)
+    dqt, dk, dv = attend_back(info, qt, k, v, go, ot, lse, False)
+    if boxed:
+        recv_a, recv_b, ffn_a, ffn_b = tie((recv_a, recv_b, ffn_a, ffn_b), dqt)
+        ffn_pieces = turns(route_three(info, ffn_a, recv_a, ffn_b, recv_b))
+    memory_grad = unpack(sources, m_pieces, micro)
+    if boxed:
+        x_late = tie(x, ffn_pieces[0], memory_grad)
+    else:
+        x_late = x
+    last_rows = 2 * BROWS + SMALL
+    keep_last, send_last = call(
+        self_grad_kernel,
+        "self_grad",
+        (PIECES,),
+        [SMEM, COLS, ROWS, ROWS, ROWS, fixed(D, D), fixed(4 * D, D), fixed(BLOCKS, SMALL, D)],
+        [fixed(HALF, last_rows, D)] * 2,
+        [shape((HALF, last_rows, D))] * 2,
+        [pltpu.VMEM((D, D), f32)] * 3,
+        4 << 30,
+        info,
+        dqt,
+        dk,
+        dv,
+        x_late,
+        g_wo,
+        g_cross,
+        g_small,
+    )
+    if boxed:
+        recv_last = dp_swap(send_last, 1)
+        ffn_part = route_four(ffn_pieces)
+        d1 = tie(d1, ffn_part)
+    d1 = tie(d1, keep_last)
+    t_out = call(
+        self_input_kernel,
+        "self_input",
+        (PIECES,),
+        [SMEM, COLS, ROWS, ROWS, ROWS, fixed(BLOCKS, BROWS + SMALL, D)],
+        [fixed(PIECE, D)] * PIECES,
+        [shape((PIECE, D))] * PIECES,
+        [],
+        4 << 30,
+        info,
+        dqt,
+        dk,
+        dv,
+        d1,
+        wa,
+    )
+    t_pieces = from_unit(t_out)
+
+    def whole_blocks(keep, send):
+        both = jnp.stack([keep, send]).reshape(2, 4, 4, -1, D)
+        return both.transpose(1, 0, 2, 3, 4).reshape(BLOCKS, -1, D)
+
+    def owned(array):
+        return lax.psum_scatter(array, axes, scatter_dimension=0, tiled=True)[0].astype(f32)
+
+    if boxed:
+        recv_last = tie(recv_last, *t_out)
+        near, send_a, far, send_b = route_one(info, keep_last, recv_last)
+        recv_a, recv_b = dp_swap(send_a, 2), dp_swap(send_b, 4)
+        near = tie(near, t_pieces[1])
+        near, send_a, far, send_b = route_two(info, near, recv_a, far, recv_b)
+        recv_a, recv_b = dp_swap(send_a, 4), dp_swap(send_b, 2)
+        near = tie(near, *t_pieces)
+        last = route_four(turns(route_three(info, near, recv_a, far, recv_b)))
+        self_attn_grad, cross_attn_grad = last[:BROWS], last[BROWS : 2 * BROWS]
+        small_out = last[2 * BROWS]
+    else:
+        ffn = whole_blocks(keep_ffn, send_ffn)
+        second = ffn[:, BROWS:].reshape(owners, rows, D)
+        first = ffn[:, :BROWS].reshape(BLOCKS, 4, BROWS // 4, D).transpose(1, 0, 2, 3)
+        first = first.reshape(4, owners, in_rows, D).transpose(1, 0, 2, 3)
+        ffn_part = owned(jnp.concatenate([first.reshape(owners, rows, D), second], axis=1))
+        rest = whole_blocks(keep_last, send_last)
+        self_attn_grad = owned(rest[:, :BROWS].reshape(owners, rows, D))
+        cross_attn_grad = owned(rest[:, BROWS : 2 * BROWS].reshape(owners, rows, D))
+        small_out = owned(small_grads)
+    ffn_in_grad = ffn_part[:rows].reshape(4, in_rows, D).transpose(1, 0, 2).reshape(in_rows, FF)
     norm_part = small_out[at : at + 6 * out_rows].reshape(6, out_rows)
     return (
         layer_output,
-        input_grad,
+        unpack(sources, t_pieces, micro),
         memory_grad,
-        last[:rows],
+        self_attn_grad,
         cross_attn_grad,
         ffn_in_grad,
         small_out[:rows],
-        ffn_out_grad,
+        ffn_part[rows:],
         small_out[rows:at],
         norm_part[:3].T,
         norm_part[3:].T,

time: 875 us -> 573 us (0.65)
  waiting for transfers between devices: 422 us -> 87.9 us
  starting transfers between devices: 81.7 us -> 107 us
  other arithmetic: 21 us -> 5.25 us
  Pallas kernels: 302 us -> 317 us
    reduce_scatter x3 -> x0, waiting for transfers between devices: 238 us -> none  [owned(): lax.psum_scatter(array, axes, scatter_dimension=0, tiled=True).astype(f32)]
    all_gather x1 -> x0, waiting for transfers between devices: 62.2 us -> none  [local(): all_a = lax.all_gather(bundle_a, axes, axis=0, tiled=False)]
    all_gather x1, waiting for transfers between devices: 27.9 us -> 0.02 us  [local(): all_b = lax.all_gather(bundle_b, axes, axis=0, tiled=False)]
    ppermute x18 -> x42, starting transfers between devices: 81.5 us -> 107 us  [the longest x15 33.5 us: dp_swap(): return lax.ppermute(array, 'dp', [(d, d ^ bit) for d in range(n)])]
    pallas_call x10 -> x26, Pallas kernels: 302 us -> 317 us  [call(): pl.pallas_call(kernel, grid=grid, in_specs=in_specs, out_specs=out_specs,...]
    unnamed x28 -> x109, local copies, waits for them, and re-layouts: 2.27 us -> 14.6 us
    another operation x8 -> x6, other arithmetic: 9.62 us -> 0.87 us  [the longest x6 8.86 us: from_unit(): return jnp.stack(out)]
    ppermute x18 -> x42, waiting for transfers between devices: 93.6 us -> 87.9 us  [the longest x9 36.5 us: to_unit(): lax.ppermute(pieces[k], axes, pairs(k, True))]
  transfers between devices with their start and end apart: 23 -> 43, of which waited for: 10 -> 14; matrix products, arithmetic and copies ran while one was open for 4% -> 2% of each run, Pallas kernels for 19% -> 42%
where the time goes in v2:
time: 573 us; the launch traced here: 562 us
  Pallas kernels  317 us (55%)
  starting transfers between devices  107 us (19%)
  waiting for transfers between devices  87.9 us (15%)
  local copies, waits for them, and re-layouts  28.8 us (5%)
  between operations  15.2 us (3%)
    pallas_call x26, Pallas kernels, call(): pl.pallas_call(kernel, grid=grid, in_specs=in_specs, out_specs=out_specs,...  317 us
    ppermute x9, waiting for transfers between devices, to_unit(): lax.ppermute(pieces[k], axes, pairs(k, True))  36.5 us
    ppermute x15, starting transfers between devices, dp_swap(): return lax.ppermute(array, 'dp', [(d, d ^ bit) for d in range(n)])  33.5 us
    ppermute x9, starting transfers between devices, from_unit(): lax.ppermute(pieces[k], axes, pairs(k, False))  29.3 us
    ppermute x9, starting transfers between devices, to_unit(): lax.ppermute(pieces[k], axes, pairs(k, True))  23.5 us
    ppermute x9, waiting for transfers between devices, from_unit(): lax.ppermute(pieces[k], axes, pairs(k, False))  21.6 us
    ppermute x9, starting transfers between devices, turns(): lax.ppermute(arrays[k], 'fsdp', [(m, (m + k) % n) for m in range(n)])  20.8 us
    ppermute x9, waiting for transfers between devices, turns(): lax.ppermute(arrays[k], 'fsdp', [(m, (m + k) % n) for m in range(n)])  17.8 us
  transfers between devices with their start and end apart: 43, of which 14 were waited for; matrix products, arithmetic and copies ran while one was open for 2% of the time, Pallas kernels for 42%

profile of v2, /device:TPU:12, one launch (start us, length us, event | category | flops | bytes accessed | tf_op | source)
XLA Modules:
  0.0 561.6 jit_solution(2574227171628695934)
XLA Ops:
  12.6 3.5 pick.3
  20.8 3.0 collective-permute-start
  26.7 3.4 collective-permute-start.2
  32.4 5.0 collective-permute-done.8
  38.0 2.9 collective-permute-done.5
  41.0 3.6 collective-permute-done.9
  44.6 16.8 %collective-permute-done.x1 = bf16[512,512]{1,0:T(8,128)(2,1)S(1)} collective-permute-done((bf16[512,512]{1,0:T(8,128)(2,1)}, bf16[512,512]{1,0:T(8,128)(2,1)S(1)}, u32[]{:S(2)}, u32[]{:S(2)}) %collective-permute-start) | collective-permute-done | bytes 524320 | tf_op jit(solution)/shard_map/ppermute | solution.py:903
  62.3 10.6 %collective-permute-done.2.x3 = bf16[512,512]{1,0:T(8,128)(2,1)} collective-permute-done((bf16[512,512]{1,0:T(8,128)(2,1)}, bf16[512,512]{1,0:T(8,128)(2,1)}, u32[]{:S(2)}, u32[]{:S(2)}) %collective-permute-start.2) | collective-permute-done | bytes 524320 | tf_op jit(solution)/shard_map/ppermute | solution.py:903
  77.0 3.6 place.1.w.wa
  80.6 8.5 %project.2 = (bf16[2048,512]{1,0:T(8,128)(2,1)}, bf16[512,2048]{1,0:T(8,128)(2,1)}, bf16[2048,512]{1,0:T(8,128)(2,1)}, bf16[2048,512]{1,0:T(8,128)(2,1)}) custom-call(s32[17]{0:T(128)} %concatenate.28.info, bf16[512,512]{1,0:T(8,128)(2,1)} %get-tuple-element.127.x0, bf16[512,512]{1,0:T(8,128)(2,1)} %copy-done.35, bf16[512,512]{1,0:T(8,128)(2,1)} %copy-done.36, ...), custom_call_target="tpu_custom_call" | custom-call | flops 4294967296 | bytes 8388608 | tf_op jit(solution)/shard_map/project/pallas_call | solution.py:675
  89.2 3.6 pick.4
  96.1 4.4 collective-permute-start.13
  100.5 22.1 %attend.2 = (bf16[512,2048]{1,0:T(8,128)(2,1)}, f32[8,2048]{1,0:T(8,128)}) custom-call(s32[17]{0:T(128)} %concatenate.28.info, bf16[512,2048]{1,0:T(8,128)(2,1)} %get-tuple-element.133.qt, bf16[2048,512]{1,0:T(8,128)(2,1)} %get-tuple-element.134.k, bf16[2048,512]{1,0:T(8,128)(2,1)} %get-tuple-element.135.v), custom_call_target="tpu_custom_call" | custom-call | flops 32212254720 | bytes 8388608 | tf_op jit(solution)/shard_map/attend/pallas_call | solution.py:675
  125.6 9.1 %collective-permute-done.13.x3 = bf16[512,512]{1,0:T(8,128)(2,1)S(1)} collective-permute-done((bf16[512,512]{1,0:T(8,128)(2,1)}, bf16[512,512]{1,0:T(8,128)(2,1)S(1)}, u32[]{:S(2)}, u32[]{:S(2)}) %collective-permute-start.13) | collective-permute-done | bytes 524320 | tf_op jit(solution)/shard_map/ppermute | solution.py:903
  134.7 3.6 pick.5
  141.5 4.8 collective-permute-start.16
  146.4 9.9 %first_norm.1 = (f32[2048,512]{1,0:T(8,128)}, f32[2048,1]{1,0:T(8,128)}, bf16[512,2048]{1,0:T(8,128)(2,1)}) custom-call(bf16[512,2048]{1,0:T(8,128)(2,1)} %get-tuple-element.142.ot, bf16[2048,512]{1,0:T(8,128)(2,1)} %get-tuple-element.203.x.x_ref, bf16[32,80,512]{2,1,0:T(8,128)(2,1)} %place.1.w.wa, bf16[32,192,512]{2,1,0:T(8,128)(2,1)} %bitcast.68, ...), custom_call_target="tpu_custom_call" | custom-call | flops 2147483648 | bytes 8388608 | tf_op jit(solution)/shard_map/first_norm/pallas_call | solution.py:675
  156.2 8.1 %project.3 = (bf16[2048,512]{1,0:T(8,128)(2,1)}, bf16[2048,512]{1,0:T(8,128)(2,1)}, bf16[2048,512]{1,0:T(8,128)(2,1)}) custom-call(s32[17]{0:T(128)} %concatenate.28.info, bf16[512,512]{1,0:T(8,128)(2,1)} %get-tuple-element.144.x0, bf16[512,512]{1,0:T(8,128)(2,1)} %copy-done.37, bf16[512,512]{1,0:T(8,128)(2,1)} %copy-done.38, bf16[512,512]{1,0:T(8,128)(2,1)} %copy-done.39, ...), custom_call_target="tpu_custom_call" | custom-call | flops 4294967296 | bytes 8388608 | tf_op jit(solution)/shard_map/project/pallas_call | solution.py:675
  164.4 21.0 %attend.3 = (bf16[512,2048]{1,0:T(8,128)(2,1)}, f32[8,2048]{1,0:T(8,128)}) custom-call(s32[17]{0:T(128)} %concatenate.28.info, bf16[512,2048]{1,0:T(8,128)(2,1)} %get-tuple-element.143.qt, bf16[2048,512]{1,0:T(8,128)(2,1)} %get-tuple-element.145.k, bf16[2048,512]{1,0:T(8,128)(2,1)} %get-tuple-element.146.v), custom_call_target="tpu_custom_call" | custom-call | flops 32212254720 | bytes 8388608 | tf_op jit(solution)/shard_map/attend/pallas_call | solution.py:675
  186.6 57.5 %ffn.1 = (bf16[512,512]{1,0:T(8,128)(2,1)}, bf16[512,512]{1,0:T(8,128)(2,1)}, bf16[512,512]{1,0:T(8,128)(2,1)}, bf16[512,512]{1,0:T(8,128)(2,1)}, f32[2048,512]{...) custom-call(s32[17]{0:T(128)} %concatenate.28.info, ...), custom_call_target="tpu_custom_call" | custom-call | flops 34359738368 | bytes 8388608 | tf_op jit(solution)/shard_map/ffn/pallas_call | solution.py:675
  246.5 2.8 collective-permute-start.18
  249.3 5.1 collective-permute-start.19
  255.4 51.3 %attend_back.2 = (bf16[512,2048]{1,0:T(8,128)(2,1)}, bf16[2048,512]{1,0:T(8,128)(2,1)}, bf16[2048,512]{1,0:T(8,128)(2,1)}) custom-call(s32[17]{0:T(128)} %concatenate.28.info, bf16[512,2048]{1,0:T(8,128)(2,1)} %get-tuple-element.143.qt, bf16[2048,512]{1,0:T(8,128)(2,1)} %get-tuple-element.145.k, bf16[2048,512]{1,0:T(8,128)(2,1)} %get-tuple-element.146.v, ...), custom_call_target="tpu_custom_call" | custom-call | flops 64424509440 | bytes 8388608 | tf_op jit(solution)/shard_map/attend_back/pallas_call | solution.py:675
  307.8 3.7 unpack.3
  312.9 3.9 route_one.2
  316.9 8.1 %collective-permute-start.21 = (bf16[2,2,128,512]{3,2,1,0:T(8,128)(2,1)}, bf16[2,2,128,512]{3,2,1,0:T(8,128)(2,1)S(1)}, u32[]{:S(2)}, u32[]{:S(2)}) collective-permute-start(bf16[2,2,128,512]{3,2,1,0:T(8,128)(2,1)} %get-tuple-element.170), channel_id=1, source_target_pairs={{0,8},{4,12},{8,0},{12,4},{16,24},{20,28},{24,16},{28,20},{1,9},{5... | collective-permute-start | bytes 1572872 | tf_op jit(solution)/shard_map/ppermute | solution.py:854
  325.0 8.6 %collective-permute-start.22 = (bf16[2,2,128,512]{3,2,1,0:T(8,128)(2,1)}, bf16[2,2,128,512]{3,2,1,0:T(8,128)(2,1)S(1)}, u32[]{:S(2)}, u32[]{:S(2)}) collective-permute-start(bf16[2,2,128,512]{3,2,1,0:T(8,128)(2,1)} %get-tuple-element.173), channel_id=1, source_target_pairs={{0,16},{4,20},{8,24},{12,28},{16,0},{20,4},{24,8},{28,12},{1,17},{... | collective-permute-start | bytes 1572872 | tf_op jit(solution)/shard_map/ppermute | solution.py:854
  333.5 21.5 %cross_post.1 = (bf16[512,512]{1,0:T(8,128)(2,1)}, bf16[512,512]{1,0:T(8,128)(2,1)}, bf16[512,512]{1,0:T(8,128)(2,1)}, bf16[512,512]{1,0:T(8,128)(2,1)}, f32[204...) custom-call(s32[17]{0:T(128)} %concatenate.28.info, ...), custom_call_target="tpu_custom_call" | custom-call | flops 9663676416 | bytes 8388608 | tf_op jit(solution)/shard_map/cross_post/pallas_call | solution.py:675
  360.9 4.5 collective-permute-start.30
  366.3 2.7 route_two.2
  370.3 50.6 %attend_back.3 = (bf16[512,2048]{1,0:T(8,128)(2,1)}, bf16[2048,512]{1,0:T(8,128)(2,1)}, bf16[2048,512]{1,0:T(8,128)(2,1)}) custom-call(s32[17]{0:T(128)} %concatenate.28.info, bf16[512,2048]{1,0:T(8,128)(2,1)} %get-tuple-element.133.qt, bf16[2048,512]{1,0:T(8,128)(2,1)} %get-tuple-element.134.k, bf16[2048,512]{1,0:T(8,128)(2,1)} %get-tuple-element.135.v, ...), custom_call_target="tpu_custom_call" | custom-call | flops 64424509440 | bytes 8388608 | tf_op jit(solution)/shard_map/attend_back/pallas_call | solution.py:675
  422.1 3.7 unpack.4
  428.8 10.3 %self_grad.1 = (bf16[16,144,512]{2,1,0:T(8,128)(2,1)}, bf16[16,144,512]{2,1,0:T(8,128)(2,1)}) custom-call(s32[17]{0:T(128)} %concatenate.28.info, bf16[512,2048]{1,0:T(8,128)(2,1)} %get-tuple-element.184.dqt, bf16[2048,512]{1,0:T(8,128)(2,1)} %get-tuple-element.185.dk_ref.dk, bf16[2048,512]{1,0:T(8,128)(2,1)} %get-tuple-element.186.dv_ref.dv, ...), custom_call_target="tpu_custom_call" | custom-call | flops 4294967296 | bytes 8388608 | tf_op jit(solution)/shard_map/self_grad/pallas_call | solution.py:675
  439.1 6.3 %collective-permute-start.34 = (bf16[16,144,512]{2,1,0:T(8,128)(2,1)}, bf16[16,144,512]{2,1,0:T(8,128)(2,1)S(1)}, u32[]{:S(2)}, u32[]{:S(2)}) collective-permute-start(bf16[16,144,512]{2,1,0:T(8,128)(2,1)} %get-tuple-element.215), channel_id=1, source_target_pairs={{0,4},{4,0},{8,12},{12,8},{16,20},{20,16},{24,28},{28,24},{1,5},{5... | collective-permute-start | bytes 7077896 | tf_op jit(solution)/shard_map/ppermute | solution.py:854
  445.3 7.5 %collective-permute-start.25 = (bf16[128,512]{1,0:T(8,128)(2,1)S(1)}, bf16[128,512]{1,0:T(8,128)(2,1)S(1)}, u32[]{:S(2)}, u32[]{:S(2)}) collective-permute-start(bf16[128,512]{1,0:T(8,128)(2,1)S(1)} %copy-done.48), channel_id=1, source_target_pairs={{0,1},{1,2},{2,3},{3,0},{4,5},{5,6},{6,7},{7,4},{8,9},{9,10},{10,1... | collective-permute-start | bytes 393224 | tf_op jit(solution)/shard_map/ppermute | solution.py:860
  452.9 6.5 %collective-permute-start.26 = (bf16[128,512]{1,0:T(8,128)(2,1)S(1)}, bf16[128,512]{1,0:T(8,128)(2,1)S(1)}, u32[]{:S(2)}, u32[]{:S(2)}) collective-permute-start(bf16[128,512]{1,0:T(8,128)(2,1)S(1)} %copy-done.47), channel_id=1, source_target_pairs={{0,2},{1,3},{2,0},{3,1},{4,6},{5,7},{6,4},{7,5},{8,10},{9,11},{10,... | collective-permute-start | bytes 393224 | tf_op jit(solution)/shard_map/ppermute | solution.py:860
  461.4 6.7 %collective-permute-done.26.r2 = bf16[128,512]{1,0:T(8,128)(2,1)S(1)} collective-permute-done((bf16[128,512]{1,0:T(8,128)(2,1)S(1)}, bf16[128,512]{1,0:T(8,128)(2,1)S(1)}, u32[]{:S(2)}, u32[]{:S(2)}) %collective-permute-start.26) | collective-permute-done | bytes 131104 | tf_op jit(solution)/shard_map/ppermute | solution.py:860
  468.1 2.8 collective-permute-done.27.r3
  473.4 9.2 %self_input.1 = (bf16[512,512]{1,0:T(8,128)(2,1)}, bf16[512,512]{1,0:T(8,128)(2,1)}, bf16[512,512]{1,0:T(8,128)(2,1)}, bf16[512,512]{1,0:T(8,128)(2,1)}) custom-call(s32[17]{0:T(128)} %concatenate.28.info, bf16[512,2048]{1,0:T(8,128)(2,1)} %get-tuple-element.184.dqt, bf16[2048,512]{1,0:T(8,128)(2,1)} %get-tuple-element.185.dk_ref.dk, ...), custom_call_target="tpu_custom_call" | custom-call | flops 4294967296 | bytes 8388608 | tf_op jit(solution)/shard_map/self_input/pallas_call | solution.py:675
  484.0 4.4 route_one.3
  491.7 4.7 collective-permute-start.32
  496.4 4.5 collective-permute-start.33
  501.0 14.3 %collective-permute-done.31.r1 = bf16[512,512]{1,0:T(8,128)(2,1)S(1)} collective-permute-done((bf16[512,512]{1,0:T(8,128)(2,1)S(1)}, bf16[512,512]{1,0:T(8,128)(2,1)S(1)}, u32[]{:S(2)}, u32[]{:S(2)}) %collective-permute-start.31) | collective-permute-done | bytes 524320 | tf_op jit(solution)/shard_map/ppermute | solution.py:908
  516.4 2.7 route_two.3
  521.7 2.7 collective-permute-done.32.r2
  524.5 4.5 collective-permute-done.33.r3
  535.5 3.7 unpack.5
  539.2 6.3 %collective-permute-done.40.r2 = bf16[144,512]{1,0:T(8,128)(2,1)S(1)} collective-permute-done((bf16[144,512]{1,0:T(8,128)(2,1)}, bf16[144,512]{1,0:T(8,128)(2,1)S(1)}, u32[]{:S(2)}, u32[]{:S(2)}) %collective-permute-start.40) | collective-permute-done | bytes 147488 | tf_op jit(solution)/shard_map/ppermute | solution.py:860
  (228 shorter events, 77.9 us)
Async XLA Ops:
  7.2 65.7 %copy-start = (s32[3,1,4]{2,1,0:T(1,128)S(1)}, s32[3,1,4]{2,1,0:T(1,128)}, u32[]{:S(2)}) copy-start(s32[3,1,4]{2,1,0:T(1,128)} %param.23) | copy-start | bytes 148
  7.2 139.1 %all-gather.3.cloned.1.call-start = ((), (), s32[]{:S(2)}) async-start(), calls=%async_computation | async-start | bytes 6488064 | tf_op jit(solution)/shard_map/all_gather | solution.py:953
  16.1 9.0 %collective-permute-start.3 = (bf16[80,512]{1,0:T(8,128)(2,1)S(1)}, bf16[80,512]{1,0:T(8,128)(2,1)S(1)}, u32[]{:S(2)}, u32[]{:S(2)}) collective-permute-start(bf16[80,512]{1,0:T(8,128)(2,1)S(1)} %pad_maximum_fusion.5), channel_id=1, source_target_pairs={{0,1},{1,2},{2,3},{3,0},{4,5},{5,6},{6,7},{7,4},{8,9},{9,10},{10,1... | collective-permute-start | bytes 245768 | tf_op jit(solution)/shard_map/ppermute | solution.py:860
  17.7 9.0 %collective-permute-start.7 = (bf16[80,512]{1,0:T(8,128)(2,1)S(1)}, bf16[80,512]{1,0:T(8,128)(2,1)S(1)}, u32[]{:S(2)}, u32[]{:S(2)}) collective-permute-start(bf16[80,512]{1,0:T(8,128)(2,1)S(1)} %pad_maximum_fusion.5), channel_id=1, source_target_pairs={{0,3},{1,0},{2,1},{3,2},{4,7},{5,4},{6,5},{7,6},{8,11},{9,8},{10,9... | collective-permute-start | bytes 245768 | tf_op jit(solution)/shard_map/ppermute | solution.py:860
  18.2 12.0 %collective-permute-start.6 = (bf16[80,512]{1,0:T(8,128)(2,1)S(1)}, bf16[80,512]{1,0:T(8,128)(2,1)S(1)}, u32[]{:S(2)}, u32[]{:S(2)}) collective-permute-start(bf16[80,512]{1,0:T(8,128)(2,1)S(1)} %pad_maximum_fusion.5), channel_id=1, source_target_pairs={{0,2},{1,3},{2,0},{3,1},{4,6},{5,7},{6,4},{7,5},{8,10},{9,11},{10,... | collective-permute-start | bytes 245768 | tf_op jit(solution)/shard_map/ppermute | solution.py:860
  20.8 40.6 %collective-permute-start = (bf16[512,512]{1,0:T(8,128)(2,1)}, bf16[512,512]{1,0:T(8,128)(2,1)S(1)}, u32[]{:S(2)}, u32[]{:S(2)}) collective-permute-start(bf16[512,512]{1,0:T(8,128)(2,1)} %get-tuple-element.128), channel_id=1, source_target_pairs={{0,1},{1,2},{3,0},{4,5},{5,6},{6,7},{8,9},{9,10},{11,8},{12,13},{1... | collective-permute-start | bytes 1572872 | tf_op jit(solution)/shard_map/ppermute | solution.py:903
  23.8 37.6 %collective-permute-start.1 = (bf16[512,512]{1,0:T(8,128)(2,1)}, bf16[512,512]{1,0:T(8,128)(2,1)S(1)}, u32[]{:S(2)}, u32[]{:S(2)}) collective-permute-start(bf16[512,512]{1,0:T(8,128)(2,1)} %get-tuple-element.129), channel_id=1, source_target_pairs={{0,2},{2,0},{3,1},{4,6},{5,7},{7,5},{8,10},{10,8},{11,9},{12,14},{... | collective-permute-start | bytes 1572872 | tf_op jit(solution)/shard_map/ppermute | solution.py:903
  25.1 5.7 %collective-permute-start.4 = (bf16[2,80,512]{2,1,0:T(8,128)(2,1)S(1)}, bf16[2,80,512]{2,1,0:T(8,128)(2,1)S(1)}, u32[]{:S(2)}, u32[]{:S(2)}) collective-permute-start(bf16[2,80,512]{2,1,0:T(8,128)(2,1)S(1)} %get-tuple-element.249), channel_id=1, source_target_pairs={{0,8},{4,12},{8,0},{12,4},{16,24},{20,28},{24,16},{28,20},{1,9},{5... | collective-permute-start | bytes 491528 | tf_op jit(solution)/shard_map/ppermute | solution.py:854
  26.7 46.2 %collective-permute-start.2 = (bf16[512,512]{1,0:T(8,128)(2,1)}, bf16[512,512]{1,0:T(8,128)(2,1)}, u32[]{:S(2)}, u32[]{:S(2)}) collective-permute-start(bf16[512,512]{1,0:T(8,128)(2,1)} %get-tuple-element.130), channel_id=1, source_target_pairs={{1,0},{2,1},{3,2},{4,7},{6,5},{7,6},{9,8},{10,9},{11,10},{12,15},{... | collective-permute-start | bytes 1572872 | tf_op jit(solution)/shard_map/ppermute | solution.py:903
  30.2 44.6 %copy-start.33 = (s32[16]{0:T(128)S(1)}, s32[16]{0:T(128)}, u32[]{:S(2)}) copy-start(s32[16]{0:T(128)} %constant.94) | copy-start | bytes 196
  30.2 44.6 %copy-start.34 = (s32[16]{0:T(128)S(1)}, s32[16]{0:T(128)}, u32[]{:S(2)}) copy-start(s32[16]{0:T(128)} %constant.81.clone) | copy-start | bytes 196
  30.2 7.2 %collective-permute-start.8 = (bf16[2,80,512]{2,1,0:T(8,128)(2,1)S(1)}, bf16[2,80,512]{2,1,0:T(8,128)(2,1)S(1)}, u32[]{:S(2)}, u32[]{:S(2)}) collective-permute-start(bf16[2,80,512]{2,1,0:T(8,128)(2,1)S(1)} %get-tuple-element.247), channel_id=1, source_target_pairs={{0,16},{4,20},{8,24},{12,28},{16,0},{20,4},{24,8},{28,12},{1,17},{... | collective-permute-start | bytes 491528 | tf_op jit(solution)/shard_map/ppermute | solution.py:854
  30.8 10.1 %collective-permute-start.5 = (bf16[2,2,80,512]{3,2,1,0:T(8,128)(2,1)S(1)}, bf16[2,2,80,512]{3,2,1,0:T(8,128)(2,1)S(1)}, u32[]{:S(2)}, u32[]{:S(2)}) collective-permute-start(bf16[2,2,80,512]{3,2,1,0:T(8,128)(2,1)S(1)} %pad_maximum_fusion), channel_id=1, source_target_pairs={{0,16},{4,20},{8,24},{12,28},{16,0},{20,4},{24,8},{28,12},{1,17},{... | collective-permute-start | bytes 983048 | tf_op jit(solution)/shard_map/ppermute | solution.py:854
  37.4 7.1 %collective-permute-start.9 = (bf16[2,2,80,512]{3,2,1,0:T(8,128)(2,1)S(1)}, bf16[2,2,80,512]{3,2,1,0:T(8,128)(2,1)S(1)}, u32[]{:S(2)}, u32[]{:S(2)}) collective-permute-start(bf16[2,2,80,512]{3,2,1,0:T(8,128)(2,1)S(1)} %pad_maximum_fusion.1), channel_id=1, source_target_pairs={{0,8},{4,12},{8,0},{12,4},{16,24},{20,28},{24,16},{28,20},{1,9},{5... | collective-permute-start | bytes 983048 | tf_op jit(solution)/shard_map/ppermute | solution.py:854
  72.9 3.0 collective-permute-start.10
  92.7 32.8 %collective-permute-start.11 = (bf16[512,512]{1,0:T(8,128)(2,1)}, bf16[512,512]{1,0:T(8,128)(2,1)S(1)}, u32[]{:S(2)}, u32[]{:S(2)}) collective-permute-start(bf16[512,512]{1,0:T(8,128)(2,1)} %get-tuple-element.139), channel_id=1, source_target_pairs={{0,1},{1,2},{3,0},{4,5},{5,6},{6,7},{8,9},{9,10},{11,8},{12,13},{1... | collective-permute-start | bytes 1572872 | tf_op jit(solution)/shard_map/ppermute | solution.py:903
  94.8 30.8 %collective-permute-start.12 = (bf16[512,512]{1,0:T(8,128)(2,1)}, bf16[512,512]{1,0:T(8,128)(2,1)S(1)}, u32[]{:S(2)}, u32[]{:S(2)}) collective-permute-start(bf16[512,512]{1,0:T(8,128)(2,1)} %get-tuple-element.140), channel_id=1, source_target_pairs={{0,2},{2,0},{3,1},{4,6},{5,7},{7,5},{8,10},{10,8},{11,9},{12,14},{... | collective-permute-start | bytes 1572872 | tf_op jit(solution)/shard_map/ppermute | solution.py:903
  96.1 38.6 %collective-permute-start.13 = (bf16[512,512]{1,0:T(8,128)(2,1)}, bf16[512,512]{1,0:T(8,128)(2,1)S(1)}, u32[]{:S(2)}, u32[]{:S(2)}) collective-permute-start(bf16[512,512]{1,0:T(8,128)(2,1)} %get-tuple-element.141), channel_id=1, source_target_pairs={{1,0},{2,1},{3,2},{4,7},{6,5},{7,6},{9,8},{10,9},{11,10},{12,15},{... | collective-permute-start | bytes 1572872 | tf_op jit(solution)/shard_map/ppermute | solution.py:903
  138.3 47.1 %collective-permute-start.14 = (bf16[512,512]{1,0:T(8,128)(2,1)}, bf16[512,512]{1,0:T(8,128)(2,1)S(1)}, u32[]{:S(2)}, u32[]{:S(2)}) collective-permute-start(bf16[512,512]{1,0:T(8,128)(2,1)} %get-tuple-element.151), channel_id=1, source_target_pairs={{0,1},{1,2},{3,0},{4,5},{5,6},{6,7},{8,9},{9,10},{11,8},{12,13},{1... | collective-permute-start | bytes 1572872 | tf_op jit(solution)/shard_map/ppermute | solution.py:903
  140.2 45.2 %collective-permute-start.15 = (bf16[512,512]{1,0:T(8,128)(2,1)}, bf16[512,512]{1,0:T(8,128)(2,1)S(1)}, u32[]{:S(2)}, u32[]{:S(2)}) collective-permute-start(bf16[512,512]{1,0:T(8,128)(2,1)} %get-tuple-element.152), channel_id=1, source_target_pairs={{0,2},{2,0},{3,1},{4,6},{5,7},{7,5},{8,10},{10,8},{11,9},{12,14},{... | collective-permute-start | bytes 1572872 | tf_op jit(solution)/shard_map/ppermute | solution.py:903
  141.5 43.9 %collective-permute-start.16 = (bf16[512,512]{1,0:T(8,128)(2,1)}, bf16[512,512]{1,0:T(8,128)(2,1)S(1)}, u32[]{:S(2)}, u32[]{:S(2)}) collective-permute-start(bf16[512,512]{1,0:T(8,128)(2,1)} %get-tuple-element.153), channel_id=1, source_target_pairs={{1,0},{2,1},{3,2},{4,7},{6,5},{7,6},{9,8},{10,9},{11,10},{12,15},{... | collective-permute-start | bytes 1572872 | tf_op jit(solution)/shard_map/ppermute | solution.py:903
  244.1 62.8 %collective-permute-start.17 = (bf16[512,512]{1,0:T(8,128)(2,1)}, bf16[512,512]{1,0:T(8,128)(2,1)S(1)}, u32[]{:S(2)}, u32[]{:S(2)}) collective-permute-start(bf16[512,512]{1,0:T(8,128)(2,1)} %get-tuple-element.155), channel_id=1, source_target_pairs={{0,1},{1,2},{2,3},{5,6},{6,7},{7,4},{8,9},{9,10},{10,11},{13,14},{... | collective-permute-start | bytes 1572872 | tf_op jit(solution)/shard_map/ppermute | solution.py:908
  246.5 60.3 %collective-permute-start.18 = (bf16[512,512]{1,0:T(8,128)(2,1)}, bf16[512,512]{1,0:T(8,128)(2,1)S(1)}, u32[]{:S(2)}, u32[]{:S(2)}) collective-permute-start(bf16[512,512]{1,0:T(8,128)(2,1)} %get-tuple-element.156), channel_id=1, source_target_pairs={{0,2},{1,3},{2,0},{5,7},{6,4},{7,5},{8,10},{9,11},{10,8},{13,15},{... | collective-permute-start | bytes 1572872 | tf_op jit(solution)/shard_map/ppermute | solution.py:908
  249.3 57.6 %collective-permute-start.19 = (bf16[512,512]{1,0:T(8,128)(2,1)}, bf16[512,512]{1,0:T(8,128)(2,1)}, u32[]{:S(2)}, u32[]{:S(2)}) collective-permute-start(bf16[512,512]{1,0:T(8,128)(2,1)} %get-tuple-element.157), channel_id=1, source_target_pairs={{0,3},{1,0},{2,1},{5,4},{6,5},{7,6},{8,11},{9,8},{10,9},{13,12},{1... | collective-permute-start | bytes 1572872 | tf_op jit(solution)/shard_map/ppermute | solution.py:908
  254.5 57.0 %collective-permute-start.20 = (bf16[16,128,512]{2,1,0:T(8,128)(2,1)}, bf16[16,128,512]{2,1,0:T(8,128)(2,1)S(1)}, u32[]{:S(2)}, u32[]{:S(2)}) collective-permute-start(bf16[16,128,512]{2,1,0:T(8,128)(2,1)} %get-tuple-element.168), channel_id=1, source_target_pairs={{0,4},{4,0},{8,12},{12,8},{16,20},{20,16},{24,28},{28,24},{1,5},{5... | collective-permute-start | bytes 6291464 | tf_op jit(solution)/shard_map/ppermute | solution.py:854
  255.4 51.3 %copy-start.31 = (f32[1,2048]{1,0:T(1,128)S(1)}, f32[1,2048]{1,0:T(1,128)}, u32[]{:S(2)}) copy-start(f32[1,2048]{1,0:T(1,128)} %get-tuple-element.206) | copy-start | bytes 24580
  316.9 48.5 %collective-permute-start.21 = (bf16[2,2,128,512]{3,2,1,0:T(8,128)(2,1)}, bf16[2,2,128,512]{3,2,1,0:T(8,128)(2,1)S(1)}, u32[]{:S(2)}, u32[]{:S(2)}) collective-permute-start(bf16[2,2,128,512]{3,2,1,0:T(8,128)(2,1)} %get-tuple-element.170), channel_id=1, source_target_pairs={{0,8},{4,12},{8,0},{12,4},{16,24},{20,28},{24,16},{28,20},{1,9},{5... | collective-permute-start | bytes 1572872 | tf_op jit(solution)/shard_map/ppermute | solution.py:854
  325.0 40.4 %collective-permute-start.22 = (bf16[2,2,128,512]{3,2,1,0:T(8,128)(2,1)}, bf16[2,2,128,512]{3,2,1,0:T(8,128)(2,1)S(1)}, u32[]{:S(2)}, u32[]{:S(2)}) collective-permute-start(bf16[2,2,128,512]{3,2,1,0:T(8,128)(2,1)} %get-tuple-element.173), channel_id=1, source_target_pairs={{0,16},{4,20},{8,24},{12,28},{16,0},{20,4},{24,8},{28,12},{1,17},{... | collective-permute-start | bytes 1572872 | tf_op jit(solution)/shard_map/ppermute | solution.py:854
  357.5 63.4 %collective-permute-start.28 = (bf16[512,512]{1,0:T(8,128)(2,1)}, bf16[512,512]{1,0:T(8,128)(2,1)S(1)}, u32[]{:S(2)}, u32[]{:S(2)}) collective-permute-start(bf16[512,512]{1,0:T(8,128)(2,1)} %get-tuple-element.200), channel_id=1, source_target_pairs={{0,1},{1,2},{2,3},{5,6},{6,7},{7,4},{8,9},{9,10},{10,11},{13,14},{... | collective-permute-start | bytes 1572872 | tf_op jit(solution)/shard_map/ppermute | solution.py:908
  359.5 61.4 %collective-permute-start.29 = (bf16[512,512]{1,0:T(8,128)(2,1)}, bf16[512,512]{1,0:T(8,128)(2,1)S(1)}, u32[]{:S(2)}, u32[]{:S(2)}) collective-permute-start(bf16[512,512]{1,0:T(8,128)(2,1)} %get-tuple-element.201), channel_id=1, source_target_pairs={{0,2},{1,3},{2,0},{5,7},{6,4},{7,5},{8,10},{9,11},{10,8},{13,15},{... | collective-permute-start | bytes 1572872 | tf_op jit(solution)/shard_map/ppermute | solution.py:908
  360.9 60.1 %collective-permute-start.30 = (bf16[512,512]{1,0:T(8,128)(2,1)}, bf16[512,512]{1,0:T(8,128)(2,1)S(1)}, u32[]{:S(2)}, u32[]{:S(2)}) collective-permute-start(bf16[512,512]{1,0:T(8,128)(2,1)} %get-tuple-element.202), channel_id=1, source_target_pairs={{0,3},{1,0},{2,1},{5,4},{6,5},{7,6},{8,11},{9,8},{10,9},{13,12},{1... | collective-permute-start | bytes 1572872 | tf_op jit(solution)/shard_map/ppermute | solution.py:908
  369.0 56.8 %collective-permute-start.23 = (bf16[2,128,512]{2,1,0:T(8,128)(2,1)}, bf16[2,128,512]{2,1,0:T(8,128)(2,1)S(1)}, u32[]{:S(2)}, u32[]{:S(2)}) collective-permute-start(bf16[2,128,512]{2,1,0:T(8,128)(2,1)} %get-tuple-element.181), channel_id=1, source_target_pairs={{0,16},{4,20},{8,24},{12,28},{16,0},{20,4},{24,8},{28,12},{1,17},{... | collective-permute-start | bytes 786440 | tf_op jit(solution)/shard_map/ppermute | solution.py:854
  370.3 55.5 %collective-permute-start.24 = (bf16[2,128,512]{2,1,0:T(8,128)(2,1)}, bf16[2,128,512]{2,1,0:T(8,128)(2,1)S(1)}, u32[]{:S(2)}, u32[]{:S(2)}) collective-permute-start(bf16[2,128,512]{2,1,0:T(8,128)(2,1)} %get-tuple-element.187), channel_id=1, source_target_pairs={{0,8},{4,12},{8,0},{12,4},{16,24},{20,28},{24,16},{28,20},{1,9},{5... | collective-permute-start | bytes 786440 | tf_op jit(solution)/shard_map/ppermute | solution.py:854
  439.1 43.5 %collective-permute-start.34 = (bf16[16,144,512]{2,1,0:T(8,128)(2,1)}, bf16[16,144,512]{2,1,0:T(8,128)(2,1)S(1)}, u32[]{:S(2)}, u32[]{:S(2)}) collective-permute-start(bf16[16,144,512]{2,1,0:T(8,128)(2,1)} %get-tuple-element.215), channel_id=1, source_target_pairs={{0,4},{4,0},{8,12},{12,8},{16,20},{20,16},{24,28},{28,24},{1,5},{5... | collective-permute-start | bytes 7077896 | tf_op jit(solution)/shard_map/ppermute | solution.py:854
  445.3 16.1 %collective-permute-start.25 = (bf16[128,512]{1,0:T(8,128)(2,1)S(1)}, bf16[128,512]{1,0:T(8,128)(2,1)S(1)}, u32[]{:S(2)}, u32[]{:S(2)}) collective-permute-start(bf16[128,512]{1,0:T(8,128)(2,1)S(1)} %copy-done.48), channel_id=1, source_target_pairs={{0,1},{1,2},{2,3},{3,0},{4,5},{5,6},{6,7},{7,4},{8,9},{9,10},{10,1... | collective-permute-start | bytes 393224 | tf_op jit(solution)/shard_map/ppermute | solution.py:860
  452.9 15.2 %collective-permute-start.26 = (bf16[128,512]{1,0:T(8,128)(2,1)S(1)}, bf16[128,512]{1,0:T(8,128)(2,1)S(1)}, u32[]{:S(2)}, u32[]{:S(2)}) collective-permute-start(bf16[128,512]{1,0:T(8,128)(2,1)S(1)} %copy-done.47), channel_id=1, source_target_pairs={{0,2},{1,3},{2,0},{3,1},{4,6},{5,7},{6,4},{7,5},{8,10},{9,11},{10,... | collective-permute-start | bytes 393224 | tf_op jit(solution)/shard_map/ppermute | solution.py:860
  459.4 11.5 %collective-permute-start.27 = (bf16[128,512]{1,0:T(8,128)(2,1)S(1)}, bf16[128,512]{1,0:T(8,128)(2,1)S(1)}, u32[]{:S(2)}, u32[]{:S(2)}) collective-permute-start(bf16[128,512]{1,0:T(8,128)(2,1)S(1)} %copy-done.46), channel_id=1, source_target_pairs={{0,3},{1,0},{2,1},{3,2},{4,7},{5,4},{6,5},{7,6},{8,11},{9,8},{10,9... | collective-permute-start | bytes 393224 | tf_op jit(solution)/shard_map/ppermute | solution.py:860
  488.4 45.8 %copy-start.6 = (f32[128,512]{1,0:T(8,128)S(1)}, f32[128,512]{1,0:T(8,128)}, u32[]{:S(2)}) copy-start(f32[128,512]{1,0:T(8,128)} %route_four.2) | copy-start | bytes 786436
  488.4 26.9 %collective-permute-start.35 = (bf16[2,2,144,512]{3,2,1,0:T(8,128)(2,1)}, bf16[2,2,144,512]{3,2,1,0:T(8,128)(2,1)S(1)}, u32[]{:S(2)}, u32[]{:S(2)}) collective-permute-start(bf16[2,2,144,512]{3,2,1,0:T(8,128)(2,1)} %get-tuple-element.219), channel_id=1, source_target_pairs={{0,8},{4,12},{8,0},{12,4},{16,24},{20,28},{24,16},{28,20},{1,9},{5... | collective-permute-start | bytes 1769480 | tf_op jit(solution)/shard_map/ppermute | solution.py:854
  488.4 26.9 %collective-permute-start.36 = (bf16[2,2,144,512]{3,2,1,0:T(8,128)(2,1)}, bf16[2,2,144,512]{3,2,1,0:T(8,128)(2,1)S(1)}, u32[]{:S(2)}, u32[]{:S(2)}) collective-permute-start(bf16[2,2,144,512]{3,2,1,0:T(8,128)(2,1)} %get-tuple-element.221), channel_id=1, source_target_pairs={{0,16},{4,20},{8,24},{12,28},{16,0},{20,4},{24,8},{28,12},{1,17},{... | collective-permute-start | bytes 1769480 | tf_op jit(solution)/shard_map/ppermute | solution.py:854
  489.8 25.5 %collective-permute-start.31 = (bf16[512,512]{1,0:T(8,128)(2,1)S(1)}, bf16[512,512]{1,0:T(8,128)(2,1)S(1)}, u32[]{:S(2)}, u32[]{:S(2)}) collective-permute-start(bf16[512,512]{1,0:T(8,128)(2,1)S(1)} %copy-done.45), channel_id=1, source_target_pairs={{0,1},{1,2},{2,3},{5,6},{6,7},{7,4},{8,9},{9,10},{10,11},{13,14},{... | collective-permute-start | bytes 1572872 | tf_op jit(solution)/shard_map/ppermute | solution.py:908
  491.7 32.7 %collective-permute-start.32 = (bf16[512,512]{1,0:T(8,128)(2,1)S(1)}, bf16[512,512]{1,0:T(8,128)(2,1)S(1)}, u32[]{:S(2)}, u32[]{:S(2)}) collective-permute-start(bf16[512,512]{1,0:T(8,128)(2,1)S(1)} %copy-done.41), channel_id=1, source_target_pairs={{0,2},{1,3},{2,0},{5,7},{6,4},{7,5},{8,10},{9,11},{10,8},{13,15},{... | collective-permute-start | bytes 1572872 | tf_op jit(solution)/shard_map/ppermute | solution.py:908
  496.4 32.6 %collective-permute-start.33 = (bf16[512,512]{1,0:T(8,128)(2,1)S(1)}, bf16[512,512]{1,0:T(8,128)(2,1)S(1)}, u32[]{:S(2)}, u32[]{:S(2)}) collective-permute-start(bf16[512,512]{1,0:T(8,128)(2,1)S(1)} %copy-done.40), channel_id=1, source_target_pairs={{0,3},{1,0},{2,1},{5,4},{6,5},{7,6},{8,11},{9,8},{10,9},{13,12},{1... | collective-permute-start | bytes 1572872 | tf_op jit(solution)/shard_map/ppermute | solution.py:908
  519.1 9.9 %collective-permute-start.37 = (bf16[2,144,512]{2,1,0:T(8,128)(2,1)}, bf16[2,144,512]{2,1,0:T(8,128)(2,1)S(1)}, u32[]{:S(2)}, u32[]{:S(2)}) collective-permute-start(bf16[2,144,512]{2,1,0:T(8,128)(2,1)} %get-tuple-element.224), channel_id=1, source_target_pairs={{0,16},{4,20},{8,24},{12,28},{16,0},{20,4},{24,8},{28,12},{1,17},{... | collective-permute-start | bytes 884744 | tf_op jit(solution)/shard_map/ppermute | solution.py:854
  519.8 9.2 %collective-permute-start.38 = (bf16[2,144,512]{2,1,0:T(8,128)(2,1)}, bf16[2,144,512]{2,1,0:T(8,128)(2,1)S(1)}, u32[]{:S(2)}, u32[]{:S(2)}) collective-permute-start(bf16[2,144,512]{2,1,0:T(8,128)(2,1)} %get-tuple-element.226), channel_id=1, source_target_pairs={{0,8},{4,12},{8,0},{12,4},{16,24},{20,28},{24,16},{28,20},{1,9},{5... | collective-permute-start | bytes 884744 | tf_op jit(solution)/shard_map/ppermute | solution.py:854
  532.2 7.1 %collective-permute-start.39 = (bf16[144,512]{1,0:T(8,128)(2,1)}, bf16[144,512]{1,0:T(8,128)(2,1)S(1)}, u32[]{:S(2)}, u32[]{:S(2)}) collective-permute-start(bf16[144,512]{1,0:T(8,128)(2,1)} %get-tuple-element.228), channel_id=1, source_target_pairs={{0,1},{1,2},{2,3},{3,0},{4,5},{5,6},{6,7},{7,4},{8,9},{9,10},{10,1... | collective-permute-start | bytes 442376 | tf_op jit(solution)/shard_map/ppermute | solution.py:860
  532.2 13.3 %collective-permute-start.40 = (bf16[144,512]{1,0:T(8,128)(2,1)}, bf16[144,512]{1,0:T(8,128)(2,1)S(1)}, u32[]{:S(2)}, u32[]{:S(2)}) collective-permute-start(bf16[144,512]{1,0:T(8,128)(2,1)} %get-tuple-element.229), channel_id=1, source_target_pairs={{0,2},{1,3},{2,0},{3,1},{4,6},{5,7},{6,4},{7,5},{8,10},{9,11},{10,... | collective-permute-start | bytes 442376 | tf_op jit(solution)/shard_map/ppermute | solution.py:860
  532.2 13.3 %collective-permute-start.41 = (bf16[144,512]{1,0:T(8,128)(2,1)}, bf16[144,512]{1,0:T(8,128)(2,1)S(1)}, u32[]{:S(2)}, u32[]{:S(2)}) collective-permute-start(bf16[144,512]{1,0:T(8,128)(2,1)} %get-tuple-element.230), channel_id=1, source_target_pairs={{0,3},{1,0},{2,1},{3,2},{4,7},{5,4},{6,5},{7,6},{8,11},{9,8},{10,9... | collective-permute-start | bytes 442376 | tf_op jit(solution)/shard_map/ppermute | solution.py:860
  (44 other events, 358.4 us)
Sparse Core Ops, SparseCore 0:
  10.9 95.8 all-gather.2

commit v3 on v2

--- a/solution.py
+++ b/solution.py
@@ -22,6 +22,7 @@
 KB = 512
 FR = 512
 LANES = 128
+KEPT = 1024
 NEG = -1e30
 BLOCKS = 32
 BROWS = D * 4 // BLOCKS
@@ -31,6 +32,8 @@
 CORE = 3 * SEQS + 2
 HALF = BLOCKS // 2
 SMALL = 16
+MICRO = 3
+SOURCES = 3 * SEQS + 5
 
 
 def dot(left, right, cl=1, cr=0):
@@ -73,10 +76,6 @@
     return pl.multiple_of(lax.rem(info[3 * SEQS] - k + PIECES, PIECES) * PIECE, PIECE)
 
 
-def shift_row(info, k):
-    return pl.multiple_of(lax.rem(info[3 * SEQS] + k, PIECES) * PIECE, PIECE)
-
-
 def weight(ref, first, count, offset, rows):
     return ref[first : first + count, offset : offset + rows, :].reshape(count * rows, D)
 
@@ -86,14 +85,20 @@
     return weight(ref, index * per, per, offset, BROWS)
 
 
-def project_kernel(with_query, info, x0, x1, x2, x3, w, x_out, *outs):
-    base = 0
+def project_kernel(kind, info, x0, x1, x2, x3, *refs):
+    with_query = kind > 0
+    if kind == 2:
+        places, near, far, x_out, qt_out, k_out, v_out, w = refs
+        for n in range(HALF):
+            w[pl.ds(places[n], 1)] = near[n : n + 1]
+            w[pl.ds(places[HALF + n], 1)] = far[n : n + 1]
+    elif kind == 1:
+        w, x_out, qt_out, k_out, v_out = refs
+    else:
+        w, x_out, k_out, v_out = refs
     if with_query:
-        qt_out, k_out, v_out = outs
-        wq = square(w, 0, base)
-    else:
-        k_out, v_out = outs
-    wk, wv = square(w, 1, base), square(w, 2, base)
+        wq = square(w, 0)
+    wk, wv = square(w, 1), square(w, 2)
     for k, piece in enumerate((x0, x1, x2, x3)):
         r0 = piece_row(info, k)
         rows = pl.ds(r0, PIECE)
@@ -106,51 +111,53 @@
         v_out[rows, :] = dot(x, wv).astype(bf16)
 
 
-def key_loop(info, cross, q0, tile):
+def memories_read(info, q0):
+    ends, picks = place_ends(info), place_picks(info)
+    rows = q0 + lax.broadcasted_iota(jnp.int32, (1, QB), 1)
+    picked = by_place(rows, ends, picks)
+    needs = []
+    for mem in range(NMEM):
+        need = jnp.bool_(False)
+        for j in range(SEQS):
+            start = ends[j - 1] if j else 0
+            need = need | ((start < q0 + QB) & (ends[j] > q0) & (picks[j] == mem))
+        needs.append(need)
+    return needs, [picked == mem for mem in range(NMEM)]
+
+
+def window(info, q0):
     ends = place_ends(info)
     rows = q0 + lax.broadcasted_iota(jnp.int32, (1, QB), 1)
-    if cross:
-        picks = place_picks(info)
-        picked = by_place(rows, ends, picks)
-        for mem in range(NMEM):
-            need = jnp.bool_(False)
-            for j in range(SEQS):
-                start = ends[j - 1] if j else 0
-                need = need | ((start < q0 + QB) & (ends[j] > q0) & (picks[j] == mem))
-
-            @pl.when(need)
-            def _():
-                tile(mem * MEM_LEN, MEM_LEN, None, picked == mem)
-    else:
-        low, high = 0, GROUP
-        low_row = jnp.zeros((1, QB), jnp.int32)
-        high_row = jnp.full((1, QB), GROUP, jnp.int32)
-        for j in range(SEQS - 1):
-            low = jnp.where(q0 >= ends[j], ends[j], low)
-            low_row = jnp.where(rows >= ends[j], ends[j], low_row)
-        for j in reversed(range(SEQS - 1)):
-            high = jnp.where(q0 + QB - 1 < ends[j], ends[j], high)
-            high_row = jnp.where(rows < ends[j], ends[j], high_row)
-        low = low // LANES * LANES
-        many = (high - low) // KB
-        rest = high - low - many * KB
-        many = jnp.where(rest > KB // 2, many + 1, many)
-
-        def part(first, size):
-            k0 = pl.multiple_of(jnp.minimum(first, GROUP - size), LANES)
-            keys = k0 + lax.broadcasted_iota(jnp.int32, (size, QB), 0)
-            inside = (keys >= jnp.maximum(low_row, first)) & (keys < high_row)
-            tile(k0, size, jnp.where(inside, 0.0, NEG), None)
-
-        def step(j, carry):
-            part(low + j * KB, KB)
-            return carry
-
-        lax.fori_loop(0, many, step, 0)
-
-        @pl.when((rest > 0) & (rest <= KB // 2))
-        def _():
-            part(low + many * KB, KB // 2)
+    low, high = 0, GROUP
+    low_row = jnp.zeros((1, QB), jnp.int32)
+    high_row = jnp.full((1, QB), GROUP, jnp.int32)
+    for j in range(SEQS - 1):
+        low = jnp.where(q0 >= ends[j], ends[j], low)
+        low_row = jnp.where(rows >= ends[j], ends[j], low_row)
+    for j in reversed(range(SEQS - 1)):
+        high = jnp.where(q0 + QB - 1 < ends[j], ends[j], high)
+        high_row = jnp.where(rows < ends[j], ends[j], high_row)
+    low = low // LANES * LANES
+    many = (high - low) // KB
+    rest = high - low - many * KB
+    many = jnp.where(rest > KB // 2, many + 1, many)
+    narrow = (rest > 0) & (rest <= KB // 2)
+
+    def place(first, size):
+        k0 = pl.multiple_of(jnp.minimum(first, GROUP - size), LANES)
+        keys = k0 + lax.broadcasted_iota(jnp.int32, (size, QB), 0)
+        inside = (keys >= jnp.maximum(low_row, first)) & (keys < high_row)
+        return k0, jnp.where(inside, 0.0, NEG)
+
+    return low, many, narrow, place
+
+
+def loop(first, last, body):
+    def step(j, carry):
+        body(j)
+        return carry
+
+    lax.fori_loop(first, last, step, 0)
 
 
 def head_rows(h):
@@ -164,7 +171,9 @@
                 stage(step - lag)
 
 
-def attend_kernel(cross, info, qt, k, v, ot, lse, vt, top, total, acc, bias_ref):
+def attend_kernel(
+    cross, info, qt, k, v, ot, lse, flags, saved, vt, top, total, peak, acc, bias_ref
+):
     i = pl.program_id(0)
     q0 = pl.multiple_of(i * QB, QB)
     group = 2
@@ -174,65 +183,103 @@
         for c in range(GROUP // QB):
             vt[:, c * QB : (c + 1) * QB] = v[c * QB : (c + 1) * QB, :].T
 
+    def tile(safe, k0, size, bias, allowed, slot):
+        keys = pl.ds(k0, size)
+        if bias is not None:
+            bias_ref[:size, :] = bias
+        totals = total[...]
+        tops = top[...] if safe else None
+        new_tops, new_totals, peaks = [], [], []
+        scores, parts = {}, {}
+
+        def score(g):
+            heads = range(g * group, (g + 1) * group)
+            scores[g] = [dot(k[keys, head_rows(h)], qt[head_rows(h), :]) for h in heads]
+
+        def soften(g):
+            parts[g] = []
+            for n, s in enumerate(scores.pop(g)):
+                h = g * group + n
+                decay = None
+                if bias is not None:
+                    s = s + bias_ref[:size, :]
+                if safe:
+                    old = tops[h : h + 1]
+                    new = jnp.maximum(old, jnp.max(s, axis=0, keepdims=True))
+                    if allowed is not None:
+                        new = jnp.where(allowed, new, old)
+                    decay = jnp.exp(old - new)
+                    new_tops.append(new)
+                    s = s - new
+                p = jnp.exp(s)
+                part = jnp.sum(p, axis=0, keepdims=True)
+                if allowed is not None:
+                    peaks.append(part)
+                    p = jnp.where(allowed, p, 0.0)
+                    part = jnp.where(allowed, part, 0.0)
+                before = totals[h : h + 1]
+                new_totals.append((before * decay if safe else before) + part)
+                low = p.astype(bf16)
+                if slot is not None:
+                    saved[0, h, pl.ds(slot, size), :] = low
+                parts[g].append((decay, low))
+
+        def mix(g):
+            for n, (decay, p) in enumerate(parts.pop(g)):
+                rows = head_rows(g * group + n)
+                before = acc[rows, :]
+                acc[rows, :] = (before * decay if safe else before) + dot(vt[rows, keys], p)
+
+        pipelined(HEADS // group, score, soften, mix)
+        if safe:
+            top[...] = jnp.concatenate(new_tops, axis=0)
+        elif peaks:
+            peak[...] = jnp.maximum(peak[...], jnp.concatenate(peaks, axis=0))
+        total[...] = jnp.concatenate(new_totals, axis=0)
+
     def sweep(safe):
         if safe:
             top[...] = jnp.full_like(top, NEG)
+        else:
+            peak[...] = jnp.zeros_like(peak)
         total[...] = jnp.zeros_like(total)
         acc[...] = jnp.zeros_like(acc)
-
-        def tile(k0, size, bias, allowed):
-            keys = pl.ds(k0, size)
-            if bias is not None:
-                bias_ref[:size, :] = bias
-            totals = total[...]
-            tops = top[...] if safe else None
-            new_tops, new_totals = [], []
-            scores, parts = {}, {}
-
-            def score(g):
-                heads = range(g * group, (g + 1) * group)
-                scores[g] = [dot(k[keys, head_rows(h)], qt[head_rows(h), :]) for h in heads]
-
-            def soften(g):
-                parts[g] = []
-                for n, s in enumerate(scores.pop(g)):
-                    h = g * group + n
-                    decay = None
-                    if bias is not None:
-                        s = s + bias_ref[:size, :]
-                    if safe:
-                        old = tops[h : h + 1]
-                        new = jnp.maximum(old, jnp.max(s, axis=0, keepdims=True))
-                        if allowed is not None:
-                            new = jnp.where(allowed, new, old)
-                        decay = jnp.exp(old - new)
-                        new_tops.append(new)
-                        s = s - new
-                    p = jnp.exp(s)
-                    if safe and allowed is not None:
-                        p = jnp.where(allowed, p, 0.0)
-                    part = jnp.sum(p, axis=0, keepdims=True)
-                    if allowed is not None:
-                        part = jnp.where(allowed, part, 0.0)
-                    before = totals[h : h + 1]
-                    new_totals.append((before * decay if safe else before) + part)
-                    parts[g].append((decay, p.astype(bf16)))
-
-            def mix(g):
-                for n, (decay, p) in enumerate(parts.pop(g)):
-                    rows = head_rows(g * group + n)
-                    part = dot(vt[rows, keys], p)
-                    if allowed is not None:
-                        part = jnp.where(allowed, part, 0.0)
-                    before = acc[rows, :]
-                    acc[rows, :] = (before * decay if safe else before) + part
-
-            pipelined(HEADS // group, score, soften, mix)
+        if cross:
+            needs, allowed = memories_read(info, q0)
+            both = needs[0] & needs[1]
             if safe:
-                top[...] = jnp.concatenate(new_tops, axis=0)
-            total[...] = jnp.concatenate(new_totals, axis=0)
-
-        key_loop(info, cross, q0, tile)
+                for mem in range(NMEM):
+
+                    @pl.when(needs[mem])
+                    def _():
+                        tile(True, mem * MEM_LEN, MEM_LEN, None, allowed[mem], None)
+            else:
+
+                @pl.when(jnp.logical_not(both))
+                def _():
+                    first = pl.multiple_of(jnp.where(needs[0], 0, MEM_LEN), MEM_LEN)
+                    tile(False, first, MEM_LEN, None, None, 0)
+
+                @pl.when(both)
+                def _():
+                    tile(False, 0, MEM_LEN, None, allowed[0], 0)
+                    tile(False, MEM_LEN, MEM_LEN, None, allowed[1], None)
+        else:
+            low, many, narrow, place = window(info, q0)
+
+            def part(j, size, slot):
+                k0, bias = place(low + j * KB, size)
+                tile(safe, k0, size, bias, None, slot)
+
+            kept = 0 if safe else jnp.minimum(many, KEPT // KB)
+            if not safe:
+                loop(0, kept, lambda j: part(j, KB, pl.multiple_of(j * KB, KB)))
+            loop(kept, many, lambda j: part(j, KB, None))
+
+            @pl.when(narrow)
+            def _():
+                part(many, KB // 2, None if safe else pl.multiple_of(kept * KB, KB))
+
         sums = total[...]
         inverse = 1.0 / sums
         lse[...] = jnp.log(sums) + (top[...] if safe else 0.0)
@@ -241,7 +288,8 @@
 
     sweep(False)
     sums = total[...]
-    safe_range = (jnp.min(sums) > 1e-18) & (jnp.max(sums) < 1e18)
+    safe_range = (jnp.min(sums) > 1e-18) & (jnp.max(sums) < 1e18) & (jnp.max(peak[...]) < 1e18)
+    flags[i] = safe_range.astype(jnp.int32)
 
     @pl.when(jnp.logical_not(safe_range))
     def _():
@@ -249,9 +297,13 @@
 
 
 def attend_back_kernel(
-    cross, info, qt, k, v, g, ot, lse, dqt, dk, dv, kt, dqt_acc, dk_acc, dv_acc, gt, gm, qm, bias_ref
+    cross, info, flags, qt, k, v, g, ot, lse, saved, dqt, dk, dv,
+    kt, dqt_acc, dk_acc, dv_acc, gt, gm, qm, bias_ref,
 ):
     i = pl.program_id(0)
+    q0 = pl.multiple_of(i * QB, QB)
+    group = 2
+    shiftless = flags[i] > 0
 
     @pl.when(i == 0)
     def _():
@@ -260,50 +312,55 @@
         for c in range(GROUP // QB):
             kt[:, c * QB : (c + 1) * QB] = k[c * QB : (c + 1) * QB, :].T
 
-    gt[...] = g[...].T
+    lses = lse[...]
+    factor = jnp.where(shiftless, jnp.exp(-lses), 1.0)
+    shifts = jnp.where(shiftless, 0.0, lses)
+    weighted = []
+    turned = g[...].T
+    for h in range(HEADS):
+        scaled = turned[head_rows(h), :].astype(f32) * factor[h : h + 1]
+        weighted.append(
+            jnp.sum(scaled * ot[head_rows(h), :].astype(f32), axis=0, keepdims=True)
+        )
+        gt[head_rows(h), :] = scaled.astype(bf16)
     left = lax.broadcasted_iota(jnp.int32, (QB, 2 * HEAD_DIM), 1) < HEAD_DIM
     for pair in range(HEADS // 2):
         cols = slice(pair * 2 * HEAD_DIM, (pair + 1) * 2 * HEAD_DIM)
-        gp = g[:, cols]
+        gp = gt[cols, :].T
         qp = qt[cols, :].T
         zero = jnp.zeros_like(gp)
         gm[pair, :QB, :] = jnp.where(left, gp, zero)
         gm[pair, QB:, :] = jnp.where(left, zero, gp)
         qm[pair, :QB, :] = jnp.where(left, qp, zero)
         qm[pair, QB:, :] = jnp.where(left, zero, qp)
-    weighted = [
-        jnp.sum(
-            gt[head_rows(h), :].astype(f32) * ot[head_rows(h), :].astype(f32),
-            axis=0,
-            keepdims=True,
-        )
-        for h in range(HEADS)
-    ]
     dqt_acc[...] = jnp.zeros_like(dqt_acc)
 
-    def tile(k0, size, bias, allowed):
+    def tile(k0, size, bias, allowed, slot):
         keys = pl.ds(k0, size)
         if bias is not None:
             bias_ref[:size, :] = bias
-        lses = lse[...]
-        if allowed is not None:
-            lses = jnp.where(allowed, lses, -NEG)
-        group = 2
+        bases = shifts if allowed is None else jnp.where(allowed, shifts, -NEG)
         scores, slopes, probs, grads = {}, {}, {}, {}
 
         def score(g):
             heads = range(g * group, (g + 1) * group)
-            scores[g] = [dot(k[keys, head_rows(h)], qt[head_rows(h), :]) for h in heads]
+            if slot is None:
+                scores[g] = [dot(k[keys, head_rows(h)], qt[head_rows(h), :]) for h in heads]
             slopes[g] = [dot(v[keys, head_rows(h)], gt[head_rows(h), :]) for h in heads]
 
         def soften(g):
             probs[g], grads[g] = [], []
-            for n, (s, dp) in enumerate(zip(scores.pop(g), slopes.pop(g))):
+            for n, dp in enumerate(slopes.pop(g)):
                 h = g * group + n
-                if bias is not None:
-                    s = s + bias_ref[:size, :]
-                p = jnp.exp(s - lses[h : h + 1])
-                probs[g].append(p.astype(bf16))
+                if slot is None:
+                    s = scores[g][n]
+                    if bias is not None:
+                        s = s + bias_ref[:size, :]
+                    p = jnp.exp(s - bases[h : h + 1])
+                    probs[g].append(p.astype(bf16))
+                else:
+                    probs[g].append(saved[0, h, pl.ds(slot, size), :])
+                    p = probs[g][n].astype(f32)
                 grads[g].append((p * (dp - weighted[h])).astype(bf16))
 
         def mix(g):
@@ -318,7 +375,39 @@
 
         pipelined(HEADS // group, score, soften, mix)
 
-    key_loop(info, cross, pl.multiple_of(i * QB, QB), tile)
+    if cross:
+        needs, allowed = memories_read(info, q0)
+
+        @pl.when(shiftless)
+        def _():
+            first = pl.multiple_of(jnp.where(needs[0], 0, MEM_LEN), MEM_LEN)
+            tile(first, MEM_LEN, None, None, 0)
+
+        for mem in range(NMEM):
+            done = shiftless & (jnp.logical_not(needs[0]) if mem else True)
+
+            @pl.when(needs[mem] & jnp.logical_not(done))
+            def _():
+                tile(mem * MEM_LEN, MEM_LEN, None, allowed[mem], None)
+    else:
+        low, many, narrow, place = window(info, q0)
+
+        def part(j, size, slot):
+            k0, bias = place(low + j * KB, size)
+            tile(k0, size, bias if slot is None else None, None, slot)
+
+        kept = jnp.where(shiftless, jnp.minimum(many, KEPT // KB), 0)
+        loop(0, kept, lambda j: part(j, KB, pl.multiple_of(j * KB, KB)))
+        loop(kept, many, lambda j: part(j, KB, None))
+
+        @pl.when(narrow & shiftless)
+        def _():
+            part(many, KB // 2, pl.multiple_of(kept * KB, KB))
+
+        @pl.when(narrow & jnp.logical_not(shiftless))
+        def _():
+            part(many, KB // 2, None)
+
     dqt[...] = (dqt_acc[...] * HEAD_DIM**-0.5).astype(bf16)
 
     @pl.when(i == pl.num_programs(0) - 1)
@@ -347,7 +436,7 @@
 
 
 def first_norm_kernel(ot, x, wa, wb, vecs, n1, inv1, qct):
-    resid = x[...].astype(f32) + dot(ot[...], square(wa, 3), 0, 0)
+    resid = x[...].astype(f32) + dot(ot[...], square(wa, 0), 0, 0)
     normed, inv = norm(resid)
     n1[...] = normed
     inv1[...] = inv
@@ -358,7 +447,7 @@
 
 def ffn_kernel(
     info, oct_, n1, wb, vecs, b1, c0, c1, c2, c3,
-    y0, y1, y2, y3, d2, gc, keep_ffn, send_ffn, g_co, g_b1, g_vec,
+    yg, d2, gc, keep_ffn, send_ffn, g_co, g_b1, g_vec,
     cot, act, slope, dy, gw1, gw2, gco, yacc,
 ):
     i = pl.program_id(0)
@@ -474,8 +563,7 @@
     @pl.when(i == pl.num_programs(0) - 1)
     def _():
         keep = info[3 * SEQS + 1] > 0
-        for k, ref in enumerate((y0, y1, y2, y3)):
-            ref[...] = yacc[pl.ds(shift_row(info, k), PIECE), :].astype(bf16)
+        yg[...] = yacc[...].astype(bf16)
         g_co[...] = jnp.where(keep, gco[...], 0.0).astype(bf16)
         for ref, core in ((keep_ffn, info[CORE]), (send_ffn, 1 - info[CORE])):
             for n in range(4):
@@ -491,21 +579,19 @@
         g_vec[...] = jnp.where(keep, g_vec[...], 0.0)
 
 
-def store_shifted(info, i, refs, value):
-    shift = lax.rem(i - info[3 * SEQS] + PIECES, PIECES)
-    for k, ref in enumerate(refs):
-
-        @pl.when(shift == k)
-        def _():
-            ref[...] = value
+def unpack_into(info, i, blocks, out):
+    @pl.when(i < MICRO)
+    def _():
+        out[0] = blocks[info[SOURCES + jnp.minimum(i, MICRO - 1)]].astype(f32)
 
 
 def cross_post_kernel(
-    info, dqct, dkc, dvc, mem, d2, n1, inv1, ot, wa, wb, vecs, g_co,
-    m0, m1, m2, m3, d1, go, g_cross, g_wo, g_vec,
+    info, blocks, dqct, dkc, dvc, mem, d2, n1, inv1, ot, wa, wb, vecs, g_co,
+    out, dmem, d1, go, g_cross, g_wo, g_vec,
     gcq, gck, gcv, gwo,
 ):
     i = pl.program_id(0)
+    unpack_into(info, i, blocks, out)
 
     @pl.when(i == 0)
     def _():
@@ -513,8 +599,7 @@
             ref[...] = jnp.zeros_like(ref)
 
     m, dk, dv = mem[...], dkc[...], dvc[...]
-    dmem = (dot(dk, square(wb, 1), 1, 1) + dot(dv, square(wb, 2), 1, 1)).astype(bf16)
-    store_shifted(info, i, (m0, m1, m2, m3), dmem)
+    dmem[...] = (dot(dk, square(wb, 1), 1, 1) + dot(dv, square(wb, 2), 1, 1)).astype(bf16)
     gck[...] += dot(m, dk, 0, 0)
     gcv[...] += dot(m, dv, 0, 0)
     normed = n1[...]
@@ -528,7 +613,7 @@
     d1[...] = first
     dao = first.astype(bf16)
     gwo[...] += dot(ot[...], dao)
-    go[...] = dot(dao, square(wa, 3), 1, 1).astype(bf16)
+    go[...] = dot(dao, square(wa, 0), 1, 1).astype(bf16)
 
     @pl.when(i == pl.num_programs(0) - 1)
     def _():
@@ -541,9 +626,12 @@
 
 
 def self_grad_kernel(
-    info, dqt, dk_ref, dv_ref, x_ref, g_wo, g_cross, g_small, keep_out, send_out, gq, gk, gv
+    info, blocks, dqt, dk_ref, dv_ref, x_ref, g_wo, g_cross, g_small,
+    out, keep_out, send_out,
+    gq, gk, gv,
 ):
     i = pl.program_id(0)
+    unpack_into(info, i, blocks, out)
 
     @pl.when(i == 0)
     def _():
@@ -570,17 +658,17 @@
                 ref[blocks, :BROWS, :] = part.reshape(4, BROWS, D)
                 part = g_cross[pl.ds(pl.multiple_of(r0 + n * D, rows), rows), :]
                 ref[blocks, BROWS : 2 * BROWS, :] = part.reshape(4, BROWS, D)
-                ref[blocks, 2 * BROWS :, :] = g_small[pl.ds((2 * n + core) * 4, 4), :, :]
-
-
-def self_input_kernel(info, dqt, dk, dv, d1, wa, t0, t1, t2, t3):
-    value = (
+                ref[blocks, 2 * BROWS :, : 2 * LANES] = g_small[pl.ds((2 * n + core) * 4, 4), :, :]
+                ref[blocks, 2 * BROWS :, 2 * LANES :] = jnp.zeros((4, SMALL, D - 2 * LANES), bf16)
+
+
+def self_input_kernel(dqt, dk, dv, d1, wa, dtok):
+    dtok[...] = (
         d1[...]
         + dot(dqt[...], square(wa, 0), 0, 1)
         + dot(dk[...], square(wa, 1), 1, 1)
         + dot(dv[...], square(wa, 2), 1, 1)
     ).astype(bf16)
-    store_shifted(info, pl.program_id(0), (t0, t1, t2, t3), value)
 
 
 def pick_kernel(count, places, *refs):
@@ -597,19 +685,8 @@
         copy.wait()
 
 
-def place_kernel(places, near, far, out):
-    for n in range(HALF):
-        out[pl.ds(places[n], 1)] = near[n : n + 1]
-        out[pl.ds(places[HALF + n], 1)] = far[n : n + 1]
-
-
-def unpack_kernel(places, r0, r1, r2, r3, out):
-    b = pl.program_id(0)
-    for k, ref in enumerate((r0, r1, r2, r3)):
-
-        @pl.when(places[b] == k)
-        def _():
-            out[0] = ref[...].astype(f32)
+def unpack_kernel(info, blocks, out):
+    unpack_into(info, pl.program_id(0), blocks, out)
 
 
 def plus(*parts):
@@ -653,9 +730,16 @@
 WHOLE = pl.BlockSpec(memory_space=pltpu.VMEM)
 ROWS = pl.BlockSpec((PIECE, D), lambda i: (i, 0))
 COLS = pl.BlockSpec((D, PIECE), lambda i: (0, i))
+BLOCKS_IN = pl.BlockSpec(
+    (PIECES, PIECE, D), lambda i: (0, 0, 0), pipeline_mode=pl.Buffered(buffer_count=1)
+)
+BATCH = pl.BlockSpec((1, PIECE, D), lambda i: (jnp.minimum(i, MICRO - 1), 0, 0))
 ROWS_Q = pl.BlockSpec((QB, D), lambda i: (i, 0))
 COLS_Q = pl.BlockSpec((D, QB), lambda i: (0, i))
 HEADS_Q = pl.BlockSpec((HEADS, QB), lambda i: (0, i))
+OUT_W = pl.BlockSpec(
+    (BLOCKS // 4, BROWS, D), lambda i: (3, 0, 0), pipeline_mode=pl.Buffered(buffer_count=1)
+)
 ROWS_F = pl.BlockSpec((FR, D), lambda i: (i, 0))
 COLS_F = pl.BlockSpec((D, FR), lambda i: (0, i))
 ONES = pl.BlockSpec((PIECE, 1), lambda i: (i, 0))
@@ -689,33 +773,50 @@
 COLMAJOR = shape((D, GROUP))
 
 
-def project_rows(info, pieces, w, with_query):
-    outs = [ROWMAJOR] + ([COLMAJOR] if with_query else []) + [ROWMAJOR, ROWMAJOR]
+def project_rows(info, pieces, weights, kind):
+    outs = [ROWMAJOR] + ([COLMAJOR] if kind else []) + [ROWMAJOR, ROWMAJOR]
+    w_specs = [WHOLE]
+    if kind == 2:
+        outs = outs + [shape((BLOCKS,) + weights[1].shape[1:])]
+        w_specs = [SMEM, WHOLE, WHOLE]
+    elif kind == 0:
+        w_specs = [fixed(BLOCKS, BROWS, D)]
     return call(
-        functools.partial(project_kernel, with_query),
+        functools.partial(project_kernel, kind),
         "project",
-        (),
-        [SMEM] + [WHOLE] * 5,
+        (1,),
+        [SMEM] + [WHOLE] * PIECES + w_specs,
         [WHOLE] * len(outs),
         outs,
         [],
         4 << 30,
         info,
         *pieces,
-        w,
-    )
+        *weights,
+    )
+
+
+def saved_rows(cross):
+    return MEM_LEN if cross else KEPT + KB // 2
 
 
 def attend(info, qt, k, v, cross):
+    keep = (HEADS, saved_rows(cross), QB)
     return call(
         functools.partial(attend_kernel, cross),
         "attend",
         (GROUP // QB,),
         [SMEM, COLS_Q, fixed(GROUP, D), fixed(GROUP, D)],
-        [COLS_Q, HEADS_Q],
-        [COLMAJOR, shape((HEADS, GROUP), f32)],
+        [COLS_Q, HEADS_Q, SMEM, pl.BlockSpec((1,) + keep, lambda i: (i, 0, 0, 0))],
+        [
+            COLMAJOR,
+            shape((HEADS, GROUP), f32),
+            shape((GROUP // QB,), jnp.int32),
+            shape((GROUP // QB,) + keep),
+        ],
         [
             pltpu.VMEM((D, GROUP), bf16),
+            pltpu.VMEM((HEADS, QB), f32),
             pltpu.VMEM((HEADS, QB), f32),
             pltpu.VMEM((HEADS, QB), f32),
             pltpu.VMEM((D, QB), f32),
@@ -729,12 +830,14 @@
     )
 
 
-def attend_back(info, qt, k, v, g, ot, lse, cross):
+def attend_back(info, qt, k, v, g, ot, lse, flags, saved, cross):
+    keep = (HEADS, saved_rows(cross), QB)
     return call(
         functools.partial(attend_back_kernel, cross),
         "attend_back",
         (GROUP // QB,),
-        [SMEM, COLS_Q, fixed(GROUP, D), fixed(GROUP, D), ROWS_Q, COLS_Q, HEADS_Q],
+        [SMEM, SMEM, COLS_Q, fixed(GROUP, D), fixed(GROUP, D), ROWS_Q, COLS_Q, HEADS_Q]
+        + [pl.BlockSpec((1,) + keep, lambda i: (i, 0, 0, 0))],
         [COLS_Q, fixed(GROUP, D), fixed(GROUP, D)],
         [COLMAJOR, ROWMAJOR, ROWMAJOR],
         [
@@ -749,12 +852,14 @@
         ],
         60 << 30,
         info,
+        flags,
         qt,
         k,
         v,
         g,
         ot,
         lse,
+        saved,
     )
 
 
@@ -782,34 +887,18 @@
     pick_kernel(count, places, *refs)
 
 
-def place_blocks(places, near, far):
-    return call(
-        place_kernel,
-        "place",
-        (),
-        [SMEM, WHOLE, WHOLE],
-        WHOLE,
-        shape((BLOCKS,) + near.shape[1:]),
-        [],
-        1 << 20,
-        places,
-        near,
-        far,
-    )
-
-
-def unpack(places, pieces, micro):
+def unpack(info, blocks, micro):
     return call(
         unpack_kernel,
         "unpack",
         (micro,),
-        [SMEM] + [fixed(PIECE, D)] * PIECES,
-        pl.BlockSpec((1, PIECE, D), lambda b: (b, 0, 0)),
+        [SMEM, BLOCKS_IN],
+        BATCH,
         shape((micro, PIECE, D), f32),
         [],
         1 << 20,
-        places,
-        *pieces,
+        info,
+        blocks,
     )
 
 
@@ -835,6 +924,29 @@
         route_three_kernel, "route_three", (), [SMEM] + [WHOLE] * 4, [WHOLE] * 4,
         [shape(block)] * 4, [pltpu.VMEM((4,) + block, bf16)], 1 << 20,
         info, a, ra, b, rb,
+    )
+
+
+def route_last_kernel(r0, r1, r2, r3, own, cross, gain, bias, out_bias, in_bias):
+    def rows(first, count):
+        part = slice(first, first + count)
+        return plus(r0[part, :], r1[part, :], r2[part, :], r3[part, :])
+
+    own[...] = rows(0, BROWS)
+    cross[...] = rows(BROWS, BROWS)
+    small = rows(2 * BROWS, SMALL)
+    turned = small[:, :LANES].T
+    gain[...] = turned[0:3]
+    bias[...] = turned[3:6]
+    out_bias[...] = turned[6:7]
+    in_bias[...] = small[0:1, LANES : LANES + BROWS]
+
+
+def route_last(pieces, rows, out_rows):
+    outs = [(rows, D), (rows, D), (3, out_rows), (3, out_rows), (1, out_rows), (1, rows)]
+    return call(
+        route_last_kernel, "route_last", (), [WHOLE] * 4, [WHOLE] * 6, [shape(o, f32) for o in outs], [],
+        1 << 20, *pieces,
     )
 
 
@@ -882,34 +994,33 @@
     valid = (mine >= 0) & (mine < micro)
     unit = jnp.clip(mine, 0, micro - 1)
 
-    def pairs(k, into):
+    def pairs(k):
         out = []
         for d in range(n_dp):
             for source in range(members):
                 target = (source + k) % members
-                if 0 <= unit_at(d, target if into else source) < micro:
+                if 0 <= unit_at(d, target) < micro:
                     out.append((d * members + source, d * members + target))
         return out
 
+    def to_unit(pieces):
+        return [pieces[0]] + [
+            lax.ppermute(pieces[k], axes, pairs(k)) for k in range(1, members)
+        ]
+
+    def from_unit(rows_of_unit):
+        blocks = rows_of_unit.reshape(members, PIECE, D)
+        return lax.all_to_all(blocks, "fsdp", split_axis=0, concat_axis=0)
+
+    def row_of(array):
+        return lax.dynamic_index_in_dim(array, unit, 0, False)[0]
+
     boxed = n_dp == 8 and members == 4
     shifts = jnp.arange(members, dtype=jnp.int32)
 
     targets = jnp.clip(lax.rem(z + shifts, members) - offset(dp), 0, micro - 1)
-    sources = lax.rem(z - offset(dp) - jnp.arange(micro, dtype=jnp.int32) + 2 * members, members)
+    sources = jnp.arange(micro, dtype=jnp.int32) + offset(dp)
     targets = targets.at[0].set(unit).astype(jnp.int32)
-
-    def to_unit(pieces):
-        return [pieces[0]] + [
-            lax.ppermute(pieces[k], axes, pairs(k, True)) for k in range(1, members)
-        ]
-
-    def from_unit(pieces):
-        return [pieces[0]] + [
-            lax.ppermute(pieces[k], axes, pairs(k, False)) for k in range(1, members)
-        ]
-
-    def row_of(array):
-        return lax.dynamic_index_in_dim(array, unit, 0, False)[0]
 
     bits = [dp & 1, (dp >> 1) & 1, (dp >> 2) & 1] if boxed else [jnp.zeros_like(dp)] * 3
     info = jnp.concatenate(
@@ -918,6 +1029,7 @@
             row_of(seq_order),
             row_of(memory_pick),
             jnp.stack([z, valid.astype(jnp.int32), *bits]),
+            sources,
         ]
     ).astype(jnp.int32)
 
@@ -927,38 +1039,39 @@
     rows = self_attn.shape[0]
     in_rows = ffn_in.shape[0]
     n_smalls = smalls.shape[0]
+    token_slices = pick_four([tokens], targets)[0]
+    smalls = tie(smalls, token_slices)
     small_row = jnp.pad(smalls, (0, 16 * D - n_smalls)).reshape(16, D)
     bundle_a = jnp.concatenate([self_attn, small_row], axis=0)
     in_blocks = ffn_in.reshape(in_rows, 4, D).transpose(1, 0, 2).reshape(4 * in_rows, D)
     bundle_b = jnp.concatenate([cross_attn, ffn_out, in_blocks], axis=0)
-    token_slices = pick_four([tokens], targets)[0]
-    bundle_a = tie(bundle_a, *token_slices)
-    token_pieces = to_unit(token_slices)
     if boxed:
         turned = turns([bundle_a] * members)
+    token_pieces = to_unit(token_slices)
+    late = tie([memory, cotangent], token_slices)
+    memory_slices, cotangent_slices = pick_four(late, targets)
+    if boxed:
         a0, b0 = jnp.stack(turned[:2]), jnp.stack(turned[2:])
         a1, b1 = dp_swap(a0, 2), dp_swap(b0, 4)
         a2 = dp_swap(jnp.stack([a0, a1]), 4)
         b2 = dp_swap(jnp.stack([b0, b1]), 2)
         near = jnp.concatenate([a0, a1, a2[0], a2[1], b0, b1, b2[0], b2[1]])
-        near = tie(near, *token_pieces[1:])
-        far = dp_swap(near, 1)
         masks = jnp.array([0, 0, 2, 2, 4, 4, 6, 6, 0, 0, 4, 4, 2, 2, 6, 6], jnp.int32)
         steps = jnp.array([0, 1] * 4 + [2, 3] * 4, jnp.int32)
         owner = (dp ^ masks) * members + lax.rem(z - steps + members, members)
         places = jnp.concatenate([owner, owner ^ members]).astype(jnp.int32)
-        all_a = place_blocks(places, near, far)
+        near = tie(near, token_pieces[1:], memory_slices, cotangent_slices, info, places)
+        far = dp_swap(near, 1)
     else:
         all_a = lax.all_gather(bundle_a, axes, axis=0, tiled=False)
-    all_b = lax.all_gather(bundle_b, axes, axis=0, tiled=False)
+        wa = jnp.pad(all_a[:, :rows].reshape(BLOCKS, BROWS, D), ((0, 0), (0, SMALL), (0, 0)))
+    all_b = lax.all_gather(tie(bundle_b, token_slices), axes, axis=0, tiled=False)
     def blocked(array, count):
         return array.reshape(BLOCKS, count, D)
 
-    small = all_a[:, rows, :n_smalls].astype(f32)
     if owners == BLOCKS:
-        wa, wb = all_a, all_b
+        wb = all_b
     else:
-        wa = jnp.pad(blocked(all_a[:, :rows], BROWS), ((0, 0), (0, SMALL), (0, 0)))
         first = all_b[:, 2 * rows :].reshape(owners, 4, in_rows, D).transpose(1, 0, 2, 3)
         first = first.reshape(4, BLOCKS, BROWS // 4, D).transpose(1, 0, 2, 3)
         wb = jnp.concatenate(
@@ -969,6 +1082,12 @@
             ],
             axis=1,
         )
+    if boxed:
+        x, qt, k, v, wa = project_rows(info, token_pieces, (places, near, far), 2)
+        all_a = wa
+    else:
+        x, qt, k, v = project_rows(info, token_pieces, (wa,), 1)
+    small = all_a[:, rows, :n_smalls].astype(f32)
     out_rows = D // owners
     b1 = small[:, :rows].reshape(1, FF)
     at = rows + out_rows
@@ -977,18 +1096,15 @@
         vec_rows + [small[:, rows:at].reshape(1, D), jnp.zeros((1, D), f32)], axis=0
     )
 
-    x, qt, k, v = project_rows(info, token_pieces, wa, True)
-    memory_in = tie(memory, x)
-    memory_pieces = to_unit(pick_four([memory_in], targets)[0])
-    ot, lse = attend(info, qt, k, v, False)
+    memory_pieces = to_unit(tie(memory_slices, x))
+    ot, *self_saved = attend(info, qt, k, v, False)
     ot = tie(ot, *memory_pieces[1:])
-    cotangent_in = tie(cotangent, *memory_pieces[1:])
-    cotangent_pieces = to_unit(pick_four([cotangent_in], targets)[0])
+    cotangent_pieces = to_unit(tie(cotangent_slices, memory_pieces[1:], ot))
     n1, inv1, qct = call(
         first_norm_kernel,
         "first_norm",
         (PIECES,),
-        [COLS, ROWS, fixed(BLOCKS, BROWS + SMALL, D), fixed(BLOCKS, 3 * BROWS, D), fixed(8, D)],
+        [COLS, ROWS, OUT_W, fixed(BLOCKS, BROWS, D), fixed(8, D)],
         [ROWS, ONES, COLS],
         [shape((GROUP, D), f32), shape((GROUP, 1), f32), COLMAJOR],
         [],
@@ -999,16 +1115,16 @@
         wb,
         vecs,
     )
-    mem, kc, vc = project_rows(info, memory_pieces, wb, False)
-    oct_, lse_c = attend(info, qct, kc, vc, True)
-    *y_out, d2, gc, keep_ffn, send_ffn, g_co, g_b1, g_vec = call(
+    mem, kc, vc = project_rows(info, memory_pieces, (wb,), 0)
+    oct_, *cross_saved = attend(info, qct, kc, vc, True)
+    y_out, d2, gc, keep_ffn, send_ffn, g_co, g_b1, g_vec = call(
         ffn_kernel,
         "ffn",
         (GROUP // FR,),
         [SMEM, COLS_F, ROWS_F, fixed(BLOCKS, 3 * BROWS, D), fixed(8, D), fixed(1, FF)]
         + [fixed(PIECE, D)] * 4,
         [
-            *[fixed(PIECE, D)] * PIECES,
+            fixed(GROUP, D),
             ROWS_F,
             ROWS_F,
             fixed(HALF, 2 * BROWS, D),
@@ -1018,7 +1134,7 @@
             fixed(8, D),
         ],
         [
-            *[shape((PIECE, D))] * PIECES,
+            ROWMAJOR,
             shape((GROUP, D), f32),
             ROWMAJOR,
             shape((HALF, 2 * BROWS, D)),
@@ -1048,25 +1164,26 @@
     )
     y_pieces = from_unit(y_out)
     if boxed:
-        recv_ffn = dp_swap(send_ffn, 1)
-
-    dqct, dkc, dvc = attend_back(info, qct, kc, vc, gc, oct_, lse_c, True)
+        ffn_a, send_a, ffn_b, send_b = route_one(info, keep_ffn, dp_swap(send_ffn, 1))
+        recv_a, recv_b = dp_swap(send_a, 2), dp_swap(send_b, 4)
+        gc = tie(gc, send_a)
+
+    dqct, dkc, dvc = attend_back(info, qct, kc, vc, gc, oct_, *cross_saved, True)
     if boxed:
-        recv_ffn = tie(recv_ffn, dqct)
-        ffn_a, send_a, ffn_b, send_b = route_one(info, keep_ffn, recv_ffn)
-        recv_a, recv_b = dp_swap(send_a, 2), dp_swap(send_b, 4)
-    layer_output = unpack(sources, y_pieces, micro)
-    if boxed:
-        g_co = tie(g_co, send_a, layer_output)
-    m_and_rest = call(
+        recv_a, recv_b, ffn_a, ffn_b = tie((recv_a, recv_b, ffn_a, ffn_b), dqct)
+        ffn_a, send_a, ffn_b, send_b = route_two(info, ffn_a, recv_a, ffn_b, recv_b)
+        recv_a, recv_b = dp_swap(send_a, 4), dp_swap(send_b, 2)
+        g_co = tie(g_co, send_a)
+    layer_output, *m_and_rest = call(
         cross_post_kernel,
         "cross_post",
         (PIECES,),
-        [SMEM, COLS, ROWS, ROWS, ROWS, ROWS, ROWS, ONES, COLS]
-        + [fixed(BLOCKS, BROWS + SMALL, D), fixed(BLOCKS, 3 * BROWS, D), fixed(8, D), fixed(D, D)],
-        [fixed(PIECE, D)] * PIECES + [ROWS, ROWS, fixed(4 * D, D), fixed(D, D), fixed(8, D)],
-        [shape((PIECE, D))] * PIECES
-        + [
+        [SMEM, BLOCKS_IN, COLS, ROWS, ROWS, ROWS, ROWS, ROWS, ONES, COLS]
+        + [OUT_W, fixed(BLOCKS, BROWS, D), fixed(8, D), fixed(D, D)],
+        [BATCH, ROWS, ROWS, ROWS, fixed(4 * D, D), fixed(D, D), fixed(8, D)],
+        [
+            shape((micro, PIECE, D), f32),
+            ROWMAJOR,
             shape((GROUP, D), f32),
             ROWMAJOR,
             shape((4 * D, D)),
@@ -1076,6 +1193,7 @@
         [pltpu.VMEM((D, D), f32)] * 4,
         9 << 30,
         info,
+        y_pieces,
         dqct,
         dkc,
         dvc,
@@ -1089,44 +1207,59 @@
         vecs,
         g_co,
     )
-    *m_out, d1, go, g_cross, g_wo, g_vec_one = m_and_rest
+    m_out, d1, go, g_cross, g_wo, g_vec_one = m_and_rest
     m_pieces = from_unit(m_out)
     if boxed:
         recv_a, recv_b, ffn_a, ffn_b = tie((recv_a, recv_b, ffn_a, ffn_b), d1)
-        ffn_a, send_a, ffn_b, send_b = route_two(info, ffn_a, recv_a, ffn_b, recv_b)
-        recv_a, recv_b = dp_swap(send_a, 4), dp_swap(send_b, 2)
-        go = tie(go, send_a)
+        ffn_pieces = turns(route_three(info, ffn_a, recv_a, ffn_b, recv_b))
+        go = tie(go, ffn_pieces[0])
     g_vec = g_vec + g_vec_one
-    small_grads = jnp.concatenate(
-        [g_b1.reshape(owners, rows), g_vec[6].reshape(owners, out_rows)]
-        + [g_vec[n].reshape(owners, out_rows) for n in range(6)],
-        axis=1,
-    )
     if boxed:
-        g_small = jnp.pad(small_grads.astype(bf16), ((0, 0), (0, SMALL * D - n_smalls)))
-        g_small = g_small.reshape(BLOCKS, SMALL, D)
+        columns = g_vec.reshape(8, BLOCKS, SMALL).transpose(1, 2, 0)
+        columns = jnp.pad(columns, ((0, 0), (0, 0), (0, LANES - 8)))
+        first = jnp.pad(g_b1.reshape(BLOCKS, 1, rows), ((0, 0), (0, SMALL - 1), (0, LANES - rows)))
+        g_small = jnp.concatenate([columns, first], axis=2).astype(bf16)
     else:
-        g_small = jnp.zeros((BLOCKS, SMALL, D), bf16)
-    dqt, dk, dv = attend_back(info, qt, k, v, go, ot, lse, False)
+        g_small = jnp.zeros((BLOCKS, SMALL, 2 * LANES), bf16)
+        small_grads = jnp.concatenate(
+            [g_b1.reshape(owners, rows), g_vec[6].reshape(owners, out_rows)]
+            + [g_vec[n].reshape(owners, out_rows) for n in range(6)],
+            axis=1,
+        )
+    dqt, dk, dv = attend_back(info, qt, k, v, go, ot, *self_saved, False)
+    x_late = x
     if boxed:
-        recv_a, recv_b, ffn_a, ffn_b = tie((recv_a, recv_b, ffn_a, ffn_b), dqt)
-        ffn_pieces = turns(route_three(info, ffn_a, recv_a, ffn_b, recv_b))
-    memory_grad = unpack(sources, m_pieces, micro)
-    if boxed:
-        x_late = tie(x, ffn_pieces[0], memory_grad)
-    else:
-        x_late = x
+        ffn_part = route_four(tie(ffn_pieces, dqt))
+        d1 = tie(d1, ffn_part)
     last_rows = 2 * BROWS + SMALL
-    keep_last, send_last = call(
+    t_out = call(
+        self_input_kernel,
+        "self_input",
+        (PIECES,),
+        [COLS, ROWS, ROWS, ROWS, fixed(3 * BLOCKS // 4, BROWS, D)],
+        ROWS,
+        ROWMAJOR,
+        [],
+        4 << 30,
+        dqt,
+        dk,
+        dv,
+        d1,
+        wa,
+    )
+    t_pieces = from_unit(t_out)
+    x_late = tie(x_late, t_out)
+    memory_grad, keep_last, send_last = call(
         self_grad_kernel,
         "self_grad",
         (PIECES,),
-        [SMEM, COLS, ROWS, ROWS, ROWS, fixed(D, D), fixed(4 * D, D), fixed(BLOCKS, SMALL, D)],
-        [fixed(HALF, last_rows, D)] * 2,
-        [shape((HALF, last_rows, D))] * 2,
+        [SMEM, BLOCKS_IN, COLS, ROWS, ROWS, ROWS, fixed(D, D), fixed(4 * D, D), fixed(BLOCKS, SMALL, 2 * LANES)],
+        [BATCH] + [fixed(HALF, last_rows, D)] * 2,
+        [shape((micro, PIECE, D), f32)] + [shape((HALF, last_rows, D))] * 2,
         [pltpu.VMEM((D, D), f32)] * 3,
         4 << 30,
         info,
+        m_pieces,
         dqt,
         dk,
         dv,
@@ -1137,26 +1270,8 @@
     )
     if boxed:
         recv_last = dp_swap(send_last, 1)
-        ffn_part = route_four(ffn_pieces)
-        d1 = tie(d1, ffn_part)
-    d1 = tie(d1, keep_last)
-    t_out = call(
-        self_input_kernel,
-        "self_input",
-        (PIECES,),
-        [SMEM, COLS, ROWS, ROWS, ROWS, fixed(BLOCKS, BROWS + SMALL, D)],
-        [fixed(PIECE, D)] * PIECES,
-        [shape((PIECE, D))] * PIECES,
-        [],
-        4 << 30,
-        info,
-        dqt,
-        dk,
-        dv,
-        d1,
-        wa,
-    )
-    t_pieces = from_unit(t_out)
+        near, send_a, far, send_b = route_one(info, keep_last, recv_last)
+        recv_a, recv_b = dp_swap(send_a, 2), dp_swap(send_b, 4)
 
     def whole_blocks(keep, send):
         both = jnp.stack([keep, send]).reshape(2, 4, 4, -1, D)
@@ -1166,17 +1281,16 @@
         return lax.psum_scatter(array, axes, scatter_dimension=0, tiled=True)[0].astype(f32)
 
     if boxed:
-        recv_last = tie(recv_last, *t_out)
-        near, send_a, far, send_b = route_one(info, keep_last, recv_last)
-        recv_a, recv_b = dp_swap(send_a, 2), dp_swap(send_b, 4)
-        near = tie(near, t_pieces[1])
+        recv_a = tie(recv_a, t_pieces)
         near, send_a, far, send_b = route_two(info, near, recv_a, far, recv_b)
         recv_a, recv_b = dp_swap(send_a, 4), dp_swap(send_b, 2)
-        near = tie(near, *t_pieces)
-        last = route_four(turns(route_three(info, near, recv_a, far, recv_b)))
-        self_attn_grad, cross_attn_grad = last[:BROWS], last[BROWS : 2 * BROWS]
-        small_out = last[2 * BROWS]
+        input_grad = unpack(info, t_pieces, micro)
+        last_pieces = turns(route_three(info, near, recv_a, far, recv_b))
+        self_attn_grad, cross_attn_grad, gain_grad, bias_grad, out_bias, in_bias = route_last(
+            last_pieces, rows, out_rows
+        )
     else:
+        input_grad = unpack(info, t_pieces, micro)
         ffn = whole_blocks(keep_ffn, send_ffn)
         second = ffn[:, BROWS:].reshape(owners, rows, D)
         first = ffn[:, :BROWS].reshape(BLOCKS, 4, BROWS // 4, D).transpose(1, 0, 2, 3)
@@ -1186,20 +1300,23 @@
         self_attn_grad = owned(rest[:, :BROWS].reshape(owners, rows, D))
         cross_attn_grad = owned(rest[:, BROWS : 2 * BROWS].reshape(owners, rows, D))
         small_out = owned(small_grads)
+        at = rows + out_rows
+        norm_part = small_out[at : at + 6 * out_rows].reshape(6, out_rows)
+        gain_grad, bias_grad = norm_part[:3], norm_part[3:]
+        in_bias, out_bias = small_out[:rows], small_out[rows:at]
     ffn_in_grad = ffn_part[:rows].reshape(4, in_rows, D).transpose(1, 0, 2).reshape(in_rows, FF)
-    norm_part = small_out[at : at + 6 * out_rows].reshape(6, out_rows)
     return (
         layer_output,
-        unpack(sources, t_pieces, micro),
+        input_grad,
         memory_grad,
         self_attn_grad,
         cross_attn_grad,
         ffn_in_grad,
-        small_out[:rows],
+        in_bias.reshape(rows),
         ffn_part[rows:],
-        small_out[rows:at],
-        norm_part[:3].T,
-        norm_part[3:].T,
+        out_bias.reshape(out_rows),
+        gain_grad.T,
+        bias_grad.T,
     )
 
 

time: 573 us -> 517 us (0.902)
  starting transfers between devices: 107 us -> 85.5 us
  Pallas kernels: 317 us -> 305 us
  local copies, waits for them, and re-layouts: 28.8 us -> 17.6 us
  waiting for transfers between devices: 87.9 us -> 80.7 us
    ppermute x18 -> x9, starting transfers between devices: 52.8 us -> 22.5 us  [to_unit(): lax.ppermute(pieces[k], axes, pairs(k))]
    ppermute x18 -> x9, waiting for transfers between devices: 58.1 us -> 32.9 us  [to_unit(): lax.ppermute(pieces[k], axes, pairs(k))]
    ppermute x15, waiting for transfers between devices: 12 us -> 31.6 us  [dp_swap(): return lax.ppermute(array, 'dp', [(d, d ^ bit) for d in range(n)])]
    all_to_all x0 -> x3, starting transfers between devices: none -> 17.3 us  [from_unit(): return lax.all_to_all(blocks, 'fsdp', split_axis=0, concat_axis=0)]
    pallas_call x26 -> x22, Pallas kernels: 317 us -> 305 us  [call(): pl.pallas_call(kernel, grid=grid, in_specs=in_specs, out_specs=out_specs,...]
    ppermute x9, waiting for transfers between devices: 17.8 us -> 6.46 us  [turns(): lax.ppermute(arrays[k], 'fsdp', [(m, (m + k) % n) for m in range(n)])]
    all_to_all x0 -> x3, waiting for transfers between devices: none -> 9.71 us  [from_unit(): return lax.all_to_all(blocks, 'fsdp', split_axis=0, concat_axis=0)]
    slice x7 -> x0, local copies, waits for them, and re-layouts: 6.29 us -> none  [the longest x1 1.68 us: local(): self_attn_grad, cross_attn_grad = (last[:BROWS], last[BROWS:2 * BROWS])]
  transfers between devices with their start and end apart: 43 -> 37, of which waited for: 14 -> 17; matrix products, arithmetic and copies ran while one was open for 2% -> 2% of each run, Pallas kernels for 42% -> 45%
where the time goes in v3:
time: 517 us; the launch traced here: 508 us
  Pallas kernels  305 us (59%)
  starting transfers between devices  85.5 us (17%)
  waiting for transfers between devices  80.7 us (16%)
  local copies, waits for them, and re-layouts  17.6 us (3%)
  between operations  15 us (3%)
    pallas_call x22, Pallas kernels, call(): pl.pallas_call(kernel, grid=grid, in_specs=in_specs, out_specs=out_specs,...  305 us
    ppermute x9, waiting for transfers between devices, to_unit(): lax.ppermute(pieces[k], axes, pairs(k))  32.9 us
    ppermute x15, waiting for transfers between devices, dp_swap(): return lax.ppermute(array, 'dp', [(d, d ^ bit) for d in range(n)])  31.6 us
    ppermute x15, starting transfers between devices, dp_swap(): return lax.ppermute(array, 'dp', [(d, d ^ bit) for d in range(n)])  30.6 us
    ppermute x9, starting transfers between devices, to_unit(): lax.ppermute(pieces[k], axes, pairs(k))  22.5 us
    all_to_all x3, starting transfers between devices, from_unit(): return lax.all_to_all(blocks, 'fsdp', split_axis=0, concat_axis=0)  17.3 us
    ppermute x9, starting transfers between devices, turns(): lax.ppermute(arrays[k], 'fsdp', [(m, (m + k) % n) for m in range(n)])  15 us
    unnamed x103, local copies, waits for them, and re-layouts  11.6 us
  transfers between devices with their start and end apart: 37, of which 17 were waited for; matrix products, arithmetic and copies ran while one was open for 2% of the time, Pallas kernels for 45%

profile of v3, /device:TPU:12, one launch (start us, length us, event | category | flops | bytes accessed | tf_op | source)
XLA Modules:
  0.0 508.3 jit_solution(15497513834643294671)
XLA Ops:
  8.7 3.5 pick.2
  14.2 2.7 collective-permute-start.6
  26.7 4.9 pick.3
  31.7 3.5 collective-permute-start.2
  37.5 4.8 collective-permute-done.8
  42.9 2.9 collective-permute-done.5
  45.8 3.6 collective-permute-done.9
  49.5 9.2 %collective-permute-done.x1 = bf16[512,512]{1,0:T(8,128)(2,1)S(1)} collective-permute-done((bf16[512,512]{1,0:T(8,128)(2,1)}, bf16[512,512]{1,0:T(8,128)(2,1)S(1)}, u32[]{:S(2)}, u32[]{:S(2)}) %collective-permute-start) | collective-permute-done | bytes 524320 | tf_op jit(solution)/shard_map/ppermute | solution.py:1008
  58.7 13.0 %collective-permute-done.2.x3 = bf16[512,512]{1,0:T(8,128)(2,1)S(1)} collective-permute-done((bf16[512,512]{1,0:T(8,128)(2,1)S(1)}, bf16[512,512]{1,0:T(8,128)(2,1)S(1)}, u32[]{:S(2)}, u32[]{:S(2)}) %collective-permute-start.2) | collective-permute-done | bytes 524320 | tf_op jit(solution)/shard_map/ppermute | solution.py:1008
  71.8 3.0 collective-permute-done.10.refs_2_
  75.9 9.4 %project.2 = (bf16[2048,512]{1,0:T(8,128)(2,1)}, bf16[512,2048]{1,0:T(8,128)(2,1)}, bf16[2048,512]{1,0:T(8,128)(2,1)}, bf16[2048,512]{1,0:T(8,128)(2,1)}, bf16[32,80,512]{2,1,0:T(8,128)(2,1)}) custom-call(s32[20]{0:T(128)} %concatenate.28.info, bf16[512,512]{1,0:T(8,128)(2,1)} %get-tuple-element.140.x0, bf16[512,512]{1,0:T(8,128)(2,1)} %copy-done.39, ...), custom_call_target="tpu_custom_call" | custom-call | flops 4294967296 | bytes 8388608 | tf_op jit(solution)/shard_map/project/pallas_call | solution.py:759
  85.3 1.9 collective-permute-start.11
  88.5 4.6 collective-permute-start.13
  93.1 24.6 %attend.2 = (bf16[512,2048]{1,0:T(8,128)(2,1)}, f32[8,2048]{1,0:T(8,128)}, s32[8]{0:T(128)}, bf16[8,8,1280,256]{3,2,1,0:T(8,128)(2,1)}) custom-call(s32[20]{0:T(128)} %concatenate.28.info, bf16[512,2048]{1,0:T(8,128)(2,1)} %get-tuple-element.156.qt, bf16[2048,512]{1,0:T(8,128)(2,1)} %get-tuple-element.157.k, bf16[2048,512]{1,0:T(8,128)(2,1)} %get-tuple-element.158.v), custom_call_target="tpu_custom_call" | custom-call | flops 32212254720 | bytes 8388608 | tf_op jit(solution)/shard_map/attend/pallas_call | solution.py:759
  120.7 10.7 %collective-permute-done.13.x3 = bf16[512,512]{1,0:T(8,128)(2,1)} collective-permute-done((bf16[512,512]{1,0:T(8,128)(2,1)S(1)}, bf16[512,512]{1,0:T(8,128)(2,1)}, u32[]{:S(2)}, u32[]{:S(2)}) %collective-permute-start.13) | collective-permute-done | bytes 524320 | tf_op jit(solution)/shard_map/ppermute | solution.py:1008
  134.6 4.8 collective-permute-start.16
  139.5 8.1 %first_norm.1 = (f32[2048,512]{1,0:T(8,128)}, f32[2048,1]{1,0:T(8,128)}, bf16[512,2048]{1,0:T(8,128)(2,1)}) custom-call(bf16[512,2048]{1,0:T(8,128)(2,1)} %get-tuple-element.164.ot, bf16[2048,512]{1,0:T(8,128)(2,1)} %get-tuple-element.229.x.x_ref, bf16[32,80,512]{2,1,0:T(8,128)(2,1)} %get-tuple-element.165.wa, bf16[32,192,512]{2,1,0:T(8,128)(2,1)} %bitcast.70, ...), custom_call_target="tpu_custom_call" | custom-call | flops 2147483648 | bytes 8388608 | tf_op jit(solution)/shard_map/first_norm/pallas_call | solution.py:759
  147.6 6.7 %project.3 = (bf16[2048,512]{1,0:T(8,128)(2,1)}, bf16[2048,512]{1,0:T(8,128)(2,1)}, bf16[2048,512]{1,0:T(8,128)(2,1)}) custom-call(s32[20]{0:T(128)} %concatenate.28.info, bf16[512,512]{1,0:T(8,128)(2,1)} %get-tuple-element.168.x0, bf16[512,512]{1,0:T(8,128)(2,1)} %collective-permute-done.11.x1, bf16[512,512]{1,0:T(8,128)(2,1)} %collective-permute-done.12.x2, ...), custom_call_target="tpu_custom_call" | custom-call | flops 4294967296 | bytes 8388608 | tf_op jit(solution)/shard_map/project/pallas_call | solution.py:759
  154.3 25.6 %attend.3 = (bf16[512,2048]{1,0:T(8,128)(2,1)}, f32[8,2048]{1,0:T(8,128)}, s32[8]{0:T(128)}, bf16[8,8,1024,256]{3,2,1,0:T(8,128)(2,1)}) custom-call(s32[20]{0:T(128)} %concatenate.28.info, bf16[512,2048]{1,0:T(8,128)(2,1)} %get-tuple-element.167.qt, bf16[2048,512]{1,0:T(8,128)(2,1)} %get-tuple-element.169.k, bf16[2048,512]{1,0:T(8,128)(2,1)} %get-tuple-element.170.v), custom_call_target="tpu_custom_call" | custom-call | flops 32212254720 | bytes 8388608 | tf_op jit(solution)/shard_map/attend/pallas_call | solution.py:759
  181.1 65.2 %ffn.1 = (bf16[2048,512]{1,0:T(8,128)(2,1)}, f32[2048,512]{1,0:T(8,128)}, bf16[2048,512]{1,0:T(8,128)(2,1)}, bf16[16,128,512]{2,1,0:T(8,128)(2,1)}, bf16[16,128,...) custom-call(s32[20]{0:T(128)} %concatenate.28.info, ...), custom_call_target="tpu_custom_call" | custom-call | flops 34359738368 | bytes 8388608 | tf_op jit(solution)/shard_map/ffn/pallas_call | solution.py:759
  246.5 6.1 %all-to-all-start = ((bf16[4,512,512]{2,1,0:T(8,128)(2,1)}), bf16[4,512,512]{2,1,0:T(8,128)(2,1)S(1)}, u32[]{:S(2)}, u32[]{:S(2)}) async-start(bf16[4,512,512]{2,1,0:T(8,128)(2,1)} %bitcast.75), calls=%async_computation | async-start | bytes 4194304 | tf_op jit(solution)/shard_map/all_to_all | solution.py:1013
  252.8 4.0 route_one.2
  256.8 2.3 collective-permute-start.18
  259.1 50.7 %attend_back.2 = (bf16[512,2048]{1,0:T(8,128)(2,1)}, bf16[2048,512]{1,0:T(8,128)(2,1)}, bf16[2048,512]{1,0:T(8,128)(2,1)}) custom-call(s32[20]{0:T(128)} %concatenate.28.info, s32[8]{0:T(128)} %get-tuple-element.178.flags, bf16[512,2048]{1,0:T(8,128)(2,1)} %get-tuple-element.167.qt, bf16[2048,512]{1,0:T(8,128)(2,1)} %get-tuple-element.169.k, ...), custom_call_target="tpu_custom_call" | custom-call | flops 64424509440 | bytes 8388608 | tf_op jit(solution)/shard_map/attend_back/pallas_call | solution.py:759
  310.7 2.7 route_two.2
  313.4 7.2 %collective-permute-start.20 = (bf16[2,128,512]{2,1,0:T(8,128)(2,1)}, bf16[2,128,512]{2,1,0:T(8,128)(2,1)S(1)}, u32[]{:S(2)}, u32[]{:S(2)}) collective-permute-start(bf16[2,128,512]{2,1,0:T(8,128)(2,1)} %get-tuple-element.200), channel_id=1, source_target_pairs={{0,16},{4,20},{8,24},{12,28},{16,0},{20,4},{24,8},{28,12},{1,17},{... | collective-permute-start | bytes 786440 | tf_op jit(solution)/shard_map/ppermute | solution.py:966
  321.9 19.2 %cross_post.1 = (f32[3,512,512]{2,1,0:T(8,128)}, bf16[2048,512]{1,0:T(8,128)(2,1)}, f32[2048,512]{1,0:T(8,128)}, bf16[2048,512]{1,0:T(8,128)(2,1)}, bf16[2048,51...) custom-call(s32[20]{0:T(128)} %concatenate.28.info, bf16[4,512,512]{2,1,0:T(8,128)(2,1)} %copy-done.4, ...), custom_call_target="tpu_custom_call" | custom-call | flops 9663676416 | bytes 8388608 | tf_op jit(solution)/shard_map/cross_post/pallas_call | solution.py:759
  342.0 2.2 route_three.2
  346.4 2.0 collective-permute-start.24
  348.4 5.0 all-to-all-start.2
  353.4 41.7 %attend_back.3 = (bf16[512,2048]{1,0:T(8,128)(2,1)}, bf16[2048,512]{1,0:T(8,128)(2,1)}, bf16[2048,512]{1,0:T(8,128)(2,1)}) custom-call(s32[20]{0:T(128)} %concatenate.28.info, s32[8]{0:T(128)} %get-tuple-element.203.flags, bf16[512,2048]{1,0:T(8,128)(2,1)} %get-tuple-element.156.qt, bf16[2048,512]{1,0:T(8,128)(2,1)} %get-tuple-element.157.k, ...), custom_call_target="tpu_custom_call" | custom-call | flops 64424509440 | bytes 8388608 | tf_op jit(solution)/shard_map/attend_back/pallas_call | solution.py:759
  398.6 8.3 %self_input.1 = bf16[2048,512]{1,0:T(8,128)(2,1)} custom-call(bf16[512,2048]{1,0:T(8,128)(2,1)} %get-tuple-element.217.dqt, bf16[2048,512]{1,0:T(8,128)(2,1)} %get-tuple-element.218.dk.dk_ref, bf16[2048,512]{1,0:T(8,128)(2,1)} %get-tuple-element.219.dv.dv_ref, f32[2048,512]{1,0:T(8,128)} %get-tuple-element.227.d1, bf16[32,80,512]{2,1,0:T(8,128)(2,1)} %get-tuple-element.165.wa), custom_call_target="tpu_custom_call" | custom-call | flops 4294967296 | bytes 8388608 | tf_op jit(solution)/shard_map/self_input/pallas_call | solution.py:759
  408.2 6.2 %all-to-all-start.1 = ((bf16[4,512,512]{2,1,0:T(8,128)(2,1)}), bf16[4,512,512]{2,1,0:T(8,128)(2,1)S(1)}, u32[]{:S(2)}, u32[]{:S(2)}) async-start(bf16[4,512,512]{2,1,0:T(8,128)(2,1)} %bitcast.76), calls=%async_computation.1 | async-start | bytes 4194304 | tf_op jit(solution)/shard_map/all_to_all | solution.py:1013
  414.4 11.8 %self_grad.1 = (f32[3,512,512]{2,1,0:T(8,128)}, bf16[16,144,512]{2,1,0:T(8,128)(2,1)}, bf16[16,144,512]{2,1,0:T(8,128)(2,1)}) custom-call(s32[20]{0:T(128)} %concatenate.28.info, bf16[4,512,512]{2,1,0:T(8,128)(2,1)} %copy-done.5, bf16[512,2048]{1,0:T(8,128)(2,1)} %get-tuple-element.217.dqt, bf16[2048,512]{1,0:T(8,128)(2,1)} %get-tuple-element.218.dk.dk_ref, ...), custom_call_target="tpu_custom_call" | custom-call | flops 4294967296 | bytes 8388608 | tf_op jit(solution)/shard_map/self_grad/pallas_call | solution.py:759
  426.2 5.5 %collective-permute-start.25 = (bf16[16,144,512]{2,1,0:T(8,128)(2,1)}, bf16[16,144,512]{2,1,0:T(8,128)(2,1)S(1)}, u32[]{:S(2)}, u32[]{:S(2)}) collective-permute-start(bf16[16,144,512]{2,1,0:T(8,128)(2,1)} %get-tuple-element.237), channel_id=1, source_target_pairs={{0,4},{4,0},{8,12},{12,8},{16,20},{20,16},{24,28},{28,24},{1,5},{5... | collective-permute-start | bytes 7077896 | tf_op jit(solution)/shard_map/ppermute | solution.py:966
  431.7 4.4 collective-permute-done.25.recv
  437.4 4.2 route_one.3
  441.7 4.4 collective-permute-start.26
  446.1 9.7 %all-to-all-done.1.blocks = bf16[4,512,512]{2,1,0:T(8,128)(2,1)S(1)} async-done(((bf16[4,512,512]{2,1,0:T(8,128)(2,1)}), bf16[4,512,512]{2,1,0:T(8,128)(2,1)S(1)}, u32[]{:S(2)}, u32[]{:S(2)}) %all-to-all-start.1) | async-done | bytes 2097184 | tf_op jit(solution)/shard_map/all_to_all | solution.py:1013
  455.8 4.1 collective-permute-done.26.ra
  462.3 2.8 route_two.3
  465.0 6.5 %collective-permute-start.28 = (bf16[2,144,512]{2,1,0:T(8,128)(2,1)}, bf16[2,144,512]{2,1,0:T(8,128)(2,1)S(1)}, u32[]{:S(2)}, u32[]{:S(2)}) collective-permute-start(bf16[2,144,512]{2,1,0:T(8,128)(2,1)} %get-tuple-element.244), channel_id=1, source_target_pairs={{0,16},{4,20},{8,24},{12,28},{16,0},{20,4},{24,8},{28,12},{1,17},{... | collective-permute-start | bytes 884744 | tf_op jit(solution)/shard_map/ppermute | solution.py:966
  471.5 5.9 %collective-permute-done.28.ra = bf16[2,144,512]{2,1,0:T(8,128)(2,1)S(1)} collective-permute-done((bf16[2,144,512]{2,1,0:T(8,128)(2,1)}, bf16[2,144,512]{2,1,0:T(8,128)(2,1)S(1)}, u32[]{:S(2)}, u32[]{:S(2)}) %collective-permute-start.28) | collective-permute-done | bytes 294944 | tf_op jit(solution)/shard_map/ppermute | solution.py:966
  479.6 2.3 route_three.3
  482.0 2.0 collective-permute-start.30
  484.0 4.2 collective-permute-start.31
  489.5 3.7 unpack.1
  496.4 2.2 collective-permute-done.32.r3
  (193 shorter events, 49.2 us)
Async XLA Ops:
  7.2 15.7 %copy-start = (s32[3,1,4]{2,1,0:T(1,128)S(1)}, s32[3,1,4]{2,1,0:T(1,128)}, u32[]{:S(2)}) copy-start(s32[3,1,4]{2,1,0:T(1,128)} %param.23) | copy-start | bytes 148
  7.3 132.2 %all-gather.3.cloned.1.call-start = ((), (), s32[]{:S(2)}) async-start(), calls=%async_computation.3 | async-start | bytes 6488064 | tf_op jit(solution)/shard_map/all_gather | solution.py:1068
  13.8 17.8 %copy-start.35 = (bf16[512,512]{1,0:T(8,128)(2,1)S(1)}, bf16[512,512]{1,0:T(8,128)(2,1)}, u32[]{:S(2)}) copy-start(bf16[512,512]{1,0:T(8,128)(2,1)} %get-tuple-element.143) | copy-start | bytes 1572868
  14.2 17.5 %collective-permute-start.6 = (bf16[80,512]{1,0:T(8,128)(2,1)S(1)}, bf16[80,512]{1,0:T(8,128)(2,1)S(1)}, u32[]{:S(2)}, u32[]{:S(2)}) collective-permute-start(bf16[80,512]{1,0:T(8,128)(2,1)S(1)} %constant_dynamic-update-slice_fusion), channel_id=1, source_target_pairs={{0,2},{1,3},{2,0},{3,1},{4,6},{5,7},{6,4},{7,5},{8,10},{9,11},{10,... | collective-permute-start | bytes 245768 | tf_op jit(solution)/shard_map/ppermute | solution.py:972
  16.9 18.3 %collective-permute-start.7 = (bf16[80,512]{1,0:T(8,128)(2,1)S(1)}, bf16[80,512]{1,0:T(8,128)(2,1)S(1)}, u32[]{:S(2)}, u32[]{:S(2)}) collective-permute-start(bf16[80,512]{1,0:T(8,128)(2,1)S(1)} %constant_dynamic-update-slice_fusion), channel_id=1, source_target_pairs={{0,3},{1,0},{2,1},{3,2},{4,7},{5,4},{6,5},{7,6},{8,11},{9,8},{10,9... | collective-permute-start | bytes 245768 | tf_op jit(solution)/shard_map/ppermute | solution.py:972
  17.3 6.6 %collective-permute-start.3 = (bf16[80,512]{1,0:T(8,128)(2,1)S(1)}, bf16[80,512]{1,0:T(8,128)(2,1)S(1)}, u32[]{:S(2)}, u32[]{:S(2)}) collective-permute-start(bf16[80,512]{1,0:T(8,128)(2,1)S(1)} %constant_dynamic-update-slice_fusion), channel_id=1, source_target_pairs={{0,1},{1,2},{2,3},{3,0},{4,5},{5,6},{6,7},{7,4},{8,9},{9,10},{10,1... | collective-permute-start | bytes 245768 | tf_op jit(solution)/shard_map/ppermute | solution.py:972
  18.9 39.8 %collective-permute-start = (bf16[512,512]{1,0:T(8,128)(2,1)}, bf16[512,512]{1,0:T(8,128)(2,1)S(1)}, u32[]{:S(2)}, u32[]{:S(2)}) collective-permute-start(bf16[512,512]{1,0:T(8,128)(2,1)} %get-tuple-element.141), channel_id=1, source_target_pairs={{0,1},{1,2},{3,0},{4,5},{5,6},{6,7},{8,9},{9,10},{11,8},{12,13},{1... | collective-permute-start | bytes 1572872 | tf_op jit(solution)/shard_map/ppermute | solution.py:1008
  20.8 37.9 %collective-permute-start.1 = (bf16[512,512]{1,0:T(8,128)(2,1)}, bf16[512,512]{1,0:T(8,128)(2,1)}, u32[]{:S(2)}, u32[]{:S(2)}) collective-permute-start(bf16[512,512]{1,0:T(8,128)(2,1)} %get-tuple-element.142), channel_id=1, source_target_pairs={{0,2},{2,0},{3,1},{4,6},{5,7},{7,5},{8,10},{10,8},{11,9},{12,14},{... | collective-permute-start | bytes 1572872 | tf_op jit(solution)/shard_map/ppermute | solution.py:1008
  23.9 11.9 %collective-permute-start.4 = (bf16[2,80,512]{2,1,0:T(8,128)(2,1)S(1)}, bf16[2,80,512]{2,1,0:T(8,128)(2,1)S(1)}, u32[]{:S(2)}, u32[]{:S(2)}) collective-permute-start(bf16[2,80,512]{2,1,0:T(8,128)(2,1)S(1)} %get-tuple-element.264), channel_id=1, source_target_pairs={{0,8},{4,12},{8,0},{12,4},{16,24},{20,28},{24,16},{28,20},{1,9},{5... | collective-permute-start | bytes 491528 | tf_op jit(solution)/shard_map/ppermute | solution.py:966
  31.7 40.0 %collective-permute-start.2 = (bf16[512,512]{1,0:T(8,128)(2,1)S(1)}, bf16[512,512]{1,0:T(8,128)(2,1)S(1)}, u32[]{:S(2)}, u32[]{:S(2)}) collective-permute-start(bf16[512,512]{1,0:T(8,128)(2,1)S(1)} %copy-done.35), channel_id=1, source_target_pairs={{1,0},{2,1},{3,2},{4,7},{6,5},{7,6},{9,8},{10,9},{11,10},{12,15},{... | collective-permute-start | bytes 1572872 | tf_op jit(solution)/shard_map/ppermute | solution.py:1008
  35.2 7.0 %collective-permute-start.8 = (bf16[2,80,512]{2,1,0:T(8,128)(2,1)S(1)}, bf16[2,80,512]{2,1,0:T(8,128)(2,1)S(1)}, u32[]{:S(2)}, u32[]{:S(2)}) collective-permute-start(bf16[2,80,512]{2,1,0:T(8,128)(2,1)S(1)} %get-tuple-element.262), channel_id=1, source_target_pairs={{0,16},{4,20},{8,24},{12,28},{16,0},{20,4},{24,8},{28,12},{1,17},{... | collective-permute-start | bytes 491528 | tf_op jit(solution)/shard_map/ppermute | solution.py:966
  35.9 9.9 %collective-permute-start.5 = (bf16[2,2,80,512]{3,2,1,0:T(8,128)(2,1)S(1)}, bf16[2,2,80,512]{3,2,1,0:T(8,128)(2,1)S(1)}, u32[]{:S(2)}, u32[]{:S(2)}) collective-permute-start(bf16[2,2,80,512]{3,2,1,0:T(8,128)(2,1)S(1)} %pad_maximum_fusion), channel_id=1, source_target_pairs={{0,16},{4,20},{8,24},{12,28},{16,0},{20,4},{24,8},{28,12},{1,17},{... | collective-permute-start | bytes 983048 | tf_op jit(solution)/shard_map/ppermute | solution.py:966
  42.3 7.1 %collective-permute-start.9 = (bf16[2,2,80,512]{3,2,1,0:T(8,128)(2,1)S(1)}, bf16[2,2,80,512]{3,2,1,0:T(8,128)(2,1)S(1)}, u32[]{:S(2)}, u32[]{:S(2)}) collective-permute-start(bf16[2,2,80,512]{3,2,1,0:T(8,128)(2,1)S(1)} %pad_maximum_fusion.1), channel_id=1, source_target_pairs={{0,8},{4,12},{8,0},{12,4},{16,24},{20,28},{24,16},{28,20},{1,9},{5... | collective-permute-start | bytes 983048 | tf_op jit(solution)/shard_map/ppermute | solution.py:966
  49.4 25.4 %copy-start.25 = (bf16[16,80,512]{2,1,0:T(8,128)(2,1)}, bf16[16,80,512]{2,1,0:T(8,128)(2,1)S(1)}, u32[]{:S(2)}) copy-start(bf16[16,80,512]{2,1,0:T(8,128)(2,1)S(1)} %fusion.3.refs_1_) | copy-start | bytes 3932164
  71.7 16.8 %copy-start.36 = (bf16[512,512]{1,0:T(8,128)(2,1)S(1)}, bf16[512,512]{1,0:T(8,128)(2,1)}, u32[]{:S(2)}) copy-start(bf16[512,512]{1,0:T(8,128)(2,1)} %get-tuple-element.163) | copy-start | bytes 1572868
  71.7 3.1 collective-permute-start.10
  85.3 35.4 %collective-permute-start.11 = (bf16[512,512]{1,0:T(8,128)(2,1)S(1)}, bf16[512,512]{1,0:T(8,128)(2,1)}, u32[]{:S(2)}, u32[]{:S(2)}) collective-permute-start(bf16[512,512]{1,0:T(8,128)(2,1)S(1)} %copy-done.38), channel_id=1, source_target_pairs={{0,1},{1,2},{3,0},{4,5},{5,6},{6,7},{8,9},{9,10},{11,8},{12,13},{1... | collective-permute-start | bytes 1572872 | tf_op jit(solution)/shard_map/ppermute | solution.py:1008
  87.2 33.5 %collective-permute-start.12 = (bf16[512,512]{1,0:T(8,128)(2,1)S(1)}, bf16[512,512]{1,0:T(8,128)(2,1)}, u32[]{:S(2)}, u32[]{:S(2)}) collective-permute-start(bf16[512,512]{1,0:T(8,128)(2,1)S(1)} %copy-done.37), channel_id=1, source_target_pairs={{0,2},{2,0},{3,1},{4,6},{5,7},{7,5},{8,10},{10,8},{11,9},{12,14},{... | collective-permute-start | bytes 1572872 | tf_op jit(solution)/shard_map/ppermute | solution.py:1008
  88.5 42.9 %collective-permute-start.13 = (bf16[512,512]{1,0:T(8,128)(2,1)S(1)}, bf16[512,512]{1,0:T(8,128)(2,1)}, u32[]{:S(2)}, u32[]{:S(2)}) collective-permute-start(bf16[512,512]{1,0:T(8,128)(2,1)S(1)} %copy-done.36), channel_id=1, source_target_pairs={{1,0},{2,1},{3,2},{4,7},{6,5},{7,6},{9,8},{10,9},{11,10},{12,15},{... | collective-permute-start | bytes 1572872 | tf_op jit(solution)/shard_map/ppermute | solution.py:1008
  93.1 38.3 %copy-start.34 = (bf16[512,512]{1,0:T(8,128)(2,1)S(1)}, bf16[512,512]{1,0:T(8,128)(2,1)}, u32[]{:S(2)}) copy-start(bf16[512,512]{1,0:T(8,128)(2,1)} %get-tuple-element.174) | copy-start | bytes 1572868
  93.1 40.2 %copy-start.33 = (bf16[512,512]{1,0:T(8,128)(2,1)S(1)}, bf16[512,512]{1,0:T(8,128)(2,1)}, u32[]{:S(2)}) copy-start(bf16[512,512]{1,0:T(8,128)(2,1)} %get-tuple-element.175) | copy-start | bytes 1572868
  93.1 41.5 %copy-start.32 = (bf16[512,512]{1,0:T(8,128)(2,1)S(1)}, bf16[512,512]{1,0:T(8,128)(2,1)}, u32[]{:S(2)}) copy-start(bf16[512,512]{1,0:T(8,128)(2,1)} %get-tuple-element.176) | copy-start | bytes 1572868
  131.4 48.5 %collective-permute-start.14 = (bf16[512,512]{1,0:T(8,128)(2,1)S(1)}, bf16[512,512]{1,0:T(8,128)(2,1)S(1)}, u32[]{:S(2)}, u32[]{:S(2)}) collective-permute-start(bf16[512,512]{1,0:T(8,128)(2,1)S(1)} %copy-done.34), channel_id=1, source_target_pairs={{0,1},{1,2},{3,0},{4,5},{5,6},{6,7},{8,9},{9,10},{11,8},{12,13},{1... | collective-permute-start | bytes 1572872 | tf_op jit(solution)/shard_map/ppermute | solution.py:1008
  133.3 46.6 %collective-permute-start.15 = (bf16[512,512]{1,0:T(8,128)(2,1)S(1)}, bf16[512,512]{1,0:T(8,128)(2,1)S(1)}, u32[]{:S(2)}, u32[]{:S(2)}) collective-permute-start(bf16[512,512]{1,0:T(8,128)(2,1)S(1)} %copy-done.33), channel_id=1, source_target_pairs={{0,2},{2,0},{3,1},{4,6},{5,7},{7,5},{8,10},{10,8},{11,9},{12,14},{... | collective-permute-start | bytes 1572872 | tf_op jit(solution)/shard_map/ppermute | solution.py:1008
  134.6 45.3 %collective-permute-start.16 = (bf16[512,512]{1,0:T(8,128)(2,1)S(1)}, bf16[512,512]{1,0:T(8,128)(2,1)S(1)}, u32[]{:S(2)}, u32[]{:S(2)}) collective-permute-start(bf16[512,512]{1,0:T(8,128)(2,1)S(1)} %copy-done.32), channel_id=1, source_target_pairs={{1,0},{2,1},{3,2},{4,7},{6,5},{7,6},{9,8},{10,9},{11,10},{12,15},{... | collective-permute-start | bytes 1572872 | tf_op jit(solution)/shard_map/ppermute | solution.py:1008
  246.3 6.5 %collective-permute-start.17 = (bf16[16,128,512]{2,1,0:T(8,128)(2,1)}, bf16[16,128,512]{2,1,0:T(8,128)(2,1)}, u32[]{:S(2)}, u32[]{:S(2)}) collective-permute-start(bf16[16,128,512]{2,1,0:T(8,128)(2,1)} %get-tuple-element.181), channel_id=1, source_target_pairs={{0,4},{4,0},{8,12},{12,8},{16,20},{20,16},{24,28},{28,24},{1,5},{5... | collective-permute-start | bytes 6291464 | tf_op jit(solution)/shard_map/ppermute | solution.py:966
  246.5 74.1 %all-to-all-start = ((bf16[4,512,512]{2,1,0:T(8,128)(2,1)}), bf16[4,512,512]{2,1,0:T(8,128)(2,1)S(1)}, u32[]{:S(2)}, u32[]{:S(2)}) async-start(bf16[4,512,512]{2,1,0:T(8,128)(2,1)} %bitcast.75), calls=%async_computation | async-start | bytes 4194304 | tf_op jit(solution)/shard_map/all_to_all | solution.py:1013
  256.8 53.0 %collective-permute-start.18 = (bf16[2,2,128,512]{3,2,1,0:T(8,128)(2,1)}, bf16[2,2,128,512]{3,2,1,0:T(8,128)(2,1)S(1)}, u32[]{:S(2)}, u32[]{:S(2)}) collective-permute-start(bf16[2,2,128,512]{3,2,1,0:T(8,128)(2,1)} %get-tuple-element.182), channel_id=1, source_target_pairs={{0,8},{4,12},{8,0},{12,4},{16,24},{20,28},{24,16},{28,20},{1,9},{5... | collective-permute-start | bytes 1572872 | tf_op jit(solution)/shard_map/ppermute | solution.py:966
  259.1 50.7 %collective-permute-start.19 = (bf16[2,2,128,512]{3,2,1,0:T(8,128)(2,1)}, bf16[2,2,128,512]{3,2,1,0:T(8,128)(2,1)S(1)}, u32[]{:S(2)}, u32[]{:S(2)}) collective-permute-start(bf16[2,2,128,512]{3,2,1,0:T(8,128)(2,1)} %get-tuple-element.193), channel_id=1, source_target_pairs={{0,16},{4,20},{8,24},{12,28},{16,0},{20,4},{24,8},{28,12},{1,17},{... | collective-permute-start | bytes 1572872 | tf_op jit(solution)/shard_map/ppermute | solution.py:966
  313.4 27.8 %collective-permute-start.20 = (bf16[2,128,512]{2,1,0:T(8,128)(2,1)}, bf16[2,128,512]{2,1,0:T(8,128)(2,1)S(1)}, u32[]{:S(2)}, u32[]{:S(2)}) collective-permute-start(bf16[2,128,512]{2,1,0:T(8,128)(2,1)} %get-tuple-element.200), channel_id=1, source_target_pairs={{0,16},{4,20},{8,24},{12,28},{16,0},{20,4},{24,8},{28,12},{1,17},{... | collective-permute-start | bytes 786440 | tf_op jit(solution)/shard_map/ppermute | solution.py:966
  320.7 20.6 %collective-permute-start.21 = (bf16[2,128,512]{2,1,0:T(8,128)(2,1)}, bf16[2,128,512]{2,1,0:T(8,128)(2,1)S(1)}, u32[]{:S(2)}, u32[]{:S(2)}) collective-permute-start(bf16[2,128,512]{2,1,0:T(8,128)(2,1)} %get-tuple-element.205), channel_id=1, source_target_pairs={{0,8},{4,12},{8,0},{12,4},{16,24},{20,28},{24,16},{28,20},{1,9},{5... | collective-permute-start | bytes 786440 | tf_op jit(solution)/shard_map/ppermute | solution.py:966
  344.3 51.8 %collective-permute-start.22 = (bf16[128,512]{1,0:T(8,128)(2,1)}, bf16[128,512]{1,0:T(8,128)(2,1)S(1)}, u32[]{:S(2)}, u32[]{:S(2)}) collective-permute-start(bf16[128,512]{1,0:T(8,128)(2,1)} %get-tuple-element.220), channel_id=1, source_target_pairs={{0,1},{1,2},{2,3},{3,0},{4,5},{5,6},{6,7},{7,4},{8,9},{9,10},{10,1... | collective-permute-start | bytes 393224 | tf_op jit(solution)/shard_map/ppermute | solution.py:972
  345.4 50.6 %collective-permute-start.23 = (bf16[128,512]{1,0:T(8,128)(2,1)}, bf16[128,512]{1,0:T(8,128)(2,1)S(1)}, u32[]{:S(2)}, u32[]{:S(2)}) collective-permute-start(bf16[128,512]{1,0:T(8,128)(2,1)} %get-tuple-element.221), channel_id=1, source_target_pairs={{0,2},{1,3},{2,0},{3,1},{4,6},{5,7},{6,4},{7,5},{8,10},{9,11},{10,... | collective-permute-start | bytes 393224 | tf_op jit(solution)/shard_map/ppermute | solution.py:972
  346.4 49.7 %collective-permute-start.24 = (bf16[128,512]{1,0:T(8,128)(2,1)}, bf16[128,512]{1,0:T(8,128)(2,1)S(1)}, u32[]{:S(2)}, u32[]{:S(2)}) collective-permute-start(bf16[128,512]{1,0:T(8,128)(2,1)} %get-tuple-element.222), channel_id=1, source_target_pairs={{0,3},{1,0},{2,1},{3,2},{4,7},{5,4},{6,5},{7,6},{8,11},{9,8},{10,9... | collective-permute-start | bytes 393224 | tf_op jit(solution)/shard_map/ppermute | solution.py:972
  348.4 58.5 %all-to-all-start.2 = ((bf16[4,512,512]{2,1,0:T(8,128)(2,1)}), bf16[4,512,512]{2,1,0:T(8,128)(2,1)S(1)}, u32[]{:S(2)}, u32[]{:S(2)}) async-start(bf16[4,512,512]{2,1,0:T(8,128)(2,1)} %bitcast.74), calls=%async_computation.2 | async-start | bytes 4194304 | tf_op jit(solution)/shard_map/all_to_all | solution.py:1013
  353.4 41.7 %copy-start.22 = (f32[8,512]{1,0:T(8,128)S(1)}, f32[8,512]{1,0:T(8,128)}, u32[]{:S(2)}) copy-start(f32[8,512]{1,0:T(8,128)} %get-tuple-element.232) | copy-start | bytes 49156
  353.4 41.7 %copy-start.23 = (f32[8,512]{1,0:T(8,128)S(1)}, f32[8,512]{1,0:T(8,128)}, u32[]{:S(2)}) copy-start(f32[8,512]{1,0:T(8,128)} %get-tuple-element.233) | copy-start | bytes 49156
  408.2 47.6 %all-to-all-start.1 = ((bf16[4,512,512]{2,1,0:T(8,128)(2,1)}), bf16[4,512,512]{2,1,0:T(8,128)(2,1)S(1)}, u32[]{:S(2)}, u32[]{:S(2)}) async-start(bf16[4,512,512]{2,1,0:T(8,128)(2,1)} %bitcast.76), calls=%async_computation.1 | async-start | bytes 4194304 | tf_op jit(solution)/shard_map/all_to_all | solution.py:1013
  426.2 9.9 %collective-permute-start.25 = (bf16[16,144,512]{2,1,0:T(8,128)(2,1)}, bf16[16,144,512]{2,1,0:T(8,128)(2,1)S(1)}, u32[]{:S(2)}, u32[]{:S(2)}) collective-permute-start(bf16[16,144,512]{2,1,0:T(8,128)(2,1)} %get-tuple-element.237), channel_id=1, source_target_pairs={{0,4},{4,0},{8,12},{12,8},{16,20},{20,16},{24,28},{28,24},{1,5},{5... | collective-permute-start | bytes 7077896 | tf_op jit(solution)/shard_map/ppermute | solution.py:966
  441.7 46.5 %copy-start.6 = (f32[128,512]{1,0:T(8,128)S(1)}, f32[128,512]{1,0:T(8,128)}, u32[]{:S(2)}) copy-start(f32[128,512]{1,0:T(8,128)} %route_four.1) | copy-start | bytes 786436
  441.7 18.3 %collective-permute-start.26 = (bf16[2,2,144,512]{3,2,1,0:T(8,128)(2,1)}, bf16[2,2,144,512]{3,2,1,0:T(8,128)(2,1)S(1)}, u32[]{:S(2)}, u32[]{:S(2)}) collective-permute-start(bf16[2,2,144,512]{3,2,1,0:T(8,128)(2,1)} %get-tuple-element.239), channel_id=1, source_target_pairs={{0,8},{4,12},{8,0},{12,4},{16,24},{20,28},{24,16},{28,20},{1,9},{5... | collective-permute-start | bytes 1769480 | tf_op jit(solution)/shard_map/ppermute | solution.py:966
  446.1 15.3 %collective-permute-start.27 = (bf16[2,2,144,512]{3,2,1,0:T(8,128)(2,1)}, bf16[2,2,144,512]{3,2,1,0:T(8,128)(2,1)S(1)}, u32[]{:S(2)}, u32[]{:S(2)}) collective-permute-start(bf16[2,2,144,512]{3,2,1,0:T(8,128)(2,1)} %get-tuple-element.242), channel_id=1, source_target_pairs={{0,16},{4,20},{8,24},{12,28},{16,0},{20,4},{24,8},{28,12},{1,17},{... | collective-permute-start | bytes 1769480 | tf_op jit(solution)/shard_map/ppermute | solution.py:966
  455.8 33.7 %copy-start.2 = (bf16[4,512,512]{2,1,0:T(8,128)(2,1)}, bf16[4,512,512]{2,1,0:T(8,128)(2,1)S(1)}, u32[]{:S(2)}) copy-start(bf16[4,512,512]{2,1,0:T(8,128)(2,1)S(1)} %all-to-all-done.1.blocks) | copy-start | bytes 6291460
  465.0 12.4 %collective-permute-start.28 = (bf16[2,144,512]{2,1,0:T(8,128)(2,1)}, bf16[2,144,512]{2,1,0:T(8,128)(2,1)S(1)}, u32[]{:S(2)}, u32[]{:S(2)}) collective-permute-start(bf16[2,144,512]{2,1,0:T(8,128)(2,1)} %get-tuple-element.244), channel_id=1, source_target_pairs={{0,16},{4,20},{8,24},{12,28},{16,0},{20,4},{24,8},{28,12},{1,17},{... | collective-permute-start | bytes 884744 | tf_op jit(solution)/shard_map/ppermute | solution.py:966
  471.5 7.4 %collective-permute-start.29 = (bf16[2,144,512]{2,1,0:T(8,128)(2,1)}, bf16[2,144,512]{2,1,0:T(8,128)(2,1)S(1)}, u32[]{:S(2)}, u32[]{:S(2)}) collective-permute-start(bf16[2,144,512]{2,1,0:T(8,128)(2,1)} %get-tuple-element.246), channel_id=1, source_target_pairs={{0,8},{4,12},{8,0},{12,4},{16,24},{20,28},{24,16},{28,20},{1,9},{5... | collective-permute-start | bytes 884744 | tf_op jit(solution)/shard_map/ppermute | solution.py:966
  482.0 12.8 %collective-permute-start.30 = (bf16[144,512]{1,0:T(8,128)(2,1)}, bf16[144,512]{1,0:T(8,128)(2,1)S(1)}, u32[]{:S(2)}, u32[]{:S(2)}) collective-permute-start(bf16[144,512]{1,0:T(8,128)(2,1)} %get-tuple-element.248), channel_id=1, source_target_pairs={{0,1},{1,2},{2,3},{3,0},{4,5},{5,6},{6,7},{7,4},{8,9},{9,10},{10,1... | collective-permute-start | bytes 442376 | tf_op jit(solution)/shard_map/ppermute | solution.py:972
  484.0 12.5 %collective-permute-start.31 = (bf16[144,512]{1,0:T(8,128)(2,1)}, bf16[144,512]{1,0:T(8,128)(2,1)S(1)}, u32[]{:S(2)}, u32[]{:S(2)}) collective-permute-start(bf16[144,512]{1,0:T(8,128)(2,1)} %get-tuple-element.249), channel_id=1, source_target_pairs={{0,2},{1,3},{2,0},{3,1},{4,6},{5,7},{6,4},{7,5},{8,10},{9,11},{10,... | collective-permute-start | bytes 442376 | tf_op jit(solution)/shard_map/ppermute | solution.py:972
  488.2 10.5 %collective-permute-start.32 = (bf16[144,512]{1,0:T(8,128)(2,1)}, bf16[144,512]{1,0:T(8,128)(2,1)S(1)}, u32[]{:S(2)}, u32[]{:S(2)}) collective-permute-start(bf16[144,512]{1,0:T(8,128)(2,1)} %get-tuple-element.250), channel_id=1, source_target_pairs={{0,3},{1,0},{2,1},{3,2},{4,7},{5,4},{6,5},{7,6},{8,11},{9,8},{10,9... | collective-permute-start | bytes 442376 | tf_op jit(solution)/shard_map/ppermute | solution.py:972
  (35 other events, 153.9 us)
Sparse Core Ops, SparseCore 0:
  14.0 93.1 all-gather.2

commit v4 on v3

--- a/solution.py
+++ b/solution.py
@@ -446,31 +446,29 @@
 
 
 def ffn_kernel(
-    info, oct_, n1, wb, vecs, b1, c0, c1, c2, c3,
+    info, oct_, n1, wo, wf, vecs, b1, c0, c1, c2, c3,
     yg, d2, gc, keep_ffn, send_ffn, g_co, g_b1, g_vec,
-    cot, act, slope, dy, gw1, gw2, gco, yacc,
+    act, pre, hid, third, slope, dy, gw, gco,
 ):
     i = pl.program_id(0)
 
     @pl.when(i == 0)
     def _():
-        for k, piece in enumerate((c0, c1, c2, c3)):
-            cot[pl.ds(piece_row(info, k), PIECE), :] = piece[...]
-        for ref in (gw1, gw2, gco, g_b1, g_vec, yacc):
+        for ref in (gco, g_b1, g_vec, yg):
             ref[...] = jnp.zeros_like(ref)
 
-    first_block = 2 * BROWS
+    rows_here = pl.ds(pl.multiple_of(i * FR, FR), FR)
     chunk = BROWS // 4
 
     def w1(c):
-        return weight(wb, 0, BLOCKS, first_block + c * chunk, chunk)
+        return weight(wf, 0, BLOCKS, BROWS + c * chunk, chunk)
 
     def w2(c):
         per = BLOCKS // 4
-        return weight(wb, c * per, per, BROWS, BROWS)
+        return weight(wf, c * per, per, 0, BROWS)
 
     hidden_one = n1[...] * vecs[0:1, :] + vecs[3:4, :]
-    n2, inv2 = norm(hidden_one + dot(oct_[...], square(wb, 3), 0, 0))
+    n2, inv2 = norm(hidden_one + dot(oct_[...], square(wo, 0), 0, 0))
     hidden = n2 * vecs[1:2, :] + vecs[4:5, :]
     hidden_b = hidden.astype(bf16)
 
@@ -490,7 +488,7 @@
         t = jnp.tanh(u * (factor + cubic * sq))
         half = 0.5 + 0.5 * t
         acts[c] = (u * half).astype(bf16)
-        act[:, cols(c)] = acts[c]
+        act[rows_here, cols(c)] = acts[c]
         slope[:, cols(c)] = half + u * (1.0 - t * t) * (0.5 * factor + 1.5 * cubic * sq)
 
     def down(c):
@@ -508,38 +506,35 @@
     given = rows + by_place(rows, ends, shifts)
     dy[...] = jnp.zeros_like(dy)
 
-    def gather(c, carry):
-        r0 = pl.multiple_of(c * QB, QB)
+    for k, piece in enumerate((c0, c1, c2, c3)):
+        r0 = piece_row(info, k)
         hit = jnp.bool_(False)
         for j in range(SEQS):
             begin = jnp.maximum(ends[j - 1] if j else 0, p0)
             end = jnp.minimum(ends[j], p0 + FR)
             hit = hit | (
-                (begin < end) & (begin + shifts[j] < r0 + QB) & (end + shifts[j] > r0)
+                (begin < end) & (begin + shifts[j] < r0 + PIECE) & (end + shifts[j] > r0)
             )
 
         @pl.when(hit)
         def _():
-            cols = r0 + lax.broadcasted_iota(jnp.int32, (FR, QB), 1)
-            select = jnp.where(cols == given, 1.0, 0.0).astype(bf16)
-            dy[...] += dot(select, cot[pl.ds(r0, QB), :])
-            yacc[pl.ds(r0, QB), :] += dot(select, y, 0, 0)
-
-        return carry
-
-    lax.fori_loop(0, GROUP // QB, gather, 0)
+            columns = r0 + lax.broadcasted_iota(jnp.int32, (FR, PIECE), 1)
+            select = jnp.where(columns == given, 1.0, 0.0).astype(bf16)
+            dy[...] += dot(select, piece[...])
+            yg[pl.ds(r0, PIECE), :] += dot(select, y, 0, 0).astype(bf16)
 
     grad = dy[...]
     g_vec[2:3, :] += column_sum(grad * n3)
     g_vec[5:6, :] += column_sum(grad)
     d3 = norm_back(grad, n3, inv3, vecs[2:3, :])
     df = d3.astype(bf16)
+    hid[rows_here, :] = hidden_b
+    third[rows_here, :] = df
     g_vec[6:7, :] += column_sum(df.astype(f32))
     downs, dus, backs = {}, {}, [d3]
 
     def down_back(c):
         downs[c] = dot(df, w2(c), 1, 1)
-        gw2[cols(c), :] += dot(act[:, cols(c)], df, 0, 0)
 
     def bend_back(c):
         dus[c] = (downs.pop(c) * slope[:, cols(c)]).astype(bf16)
@@ -547,7 +542,7 @@
 
     def up_back(c):
         du = dus.pop(c)
-        gw1[c] += dot(hidden_b, du, 0, 0)
+        pre[rows_here, cols(c)] = du
         backs.append(dot(du, w1(c), 1, 1))
 
     pipelined(4, down_back, bend_back, up_back)
@@ -558,23 +553,26 @@
     d2[...] = second
     dco = second.astype(bf16)
     gco[...] += dot(oct_[...], dco)
-    gc[...] = dot(dco, square(wb, 3), 1, 1).astype(bf16)
+    gc[...] = dot(dco, square(wo, 0), 1, 1).astype(bf16)
 
     @pl.when(i == pl.num_programs(0) - 1)
     def _():
         keep = info[3 * SEQS + 1] > 0
-        yg[...] = yacc[...].astype(bf16)
         g_co[...] = jnp.where(keep, gco[...], 0.0).astype(bf16)
-        for ref, core in ((keep_ffn, info[CORE]), (send_ffn, 1 - info[CORE])):
-            for n in range(4):
-                blocks = slice(4 * n, 4 * n + 4)
-                for c in range(4):
+        targets = ((keep_ffn, info[CORE]), (send_ffn, 1 - info[CORE]))
+        for c in range(4):
+            gw[...] = jnp.where(keep, dot(hid[...], pre[:, cols(c)], 0, 0), 0.0)
+            for ref, core in targets:
+                for n in range(4):
                     r0 = pl.multiple_of((2 * n + core) * 4 * chunk, 4 * chunk)
-                    part = jnp.where(keep, gw1[c, pl.ds(r0, 4 * chunk), :], 0.0).astype(bf16)
-                    ref[blocks, c * chunk : (c + 1) * chunk, :] = part.reshape(4, chunk, D)
-                r0 = pl.multiple_of((2 * n + core) * 4 * BROWS, 4 * BROWS)
-                part = jnp.where(keep, gw2[pl.ds(r0, 4 * BROWS), :], 0.0).astype(bf16)
-                ref[blocks, BROWS:, :] = part.reshape(4, BROWS, D)
+                    part = gw[pl.ds(r0, 4 * chunk), :].astype(bf16).reshape(4, chunk, D)
+                    ref[4 * n : 4 * n + 4, c * chunk : (c + 1) * chunk, :] = part
+        for c in range(4):
+            gw[...] = jnp.where(keep, dot(act[:, cols(c)], third[...], 0, 0), 0.0)
+            for ref, core in targets:
+                r0 = pl.multiple_of(core * 4 * BROWS, 4 * BROWS)
+                part = gw[pl.ds(r0, 4 * BROWS), :].astype(bf16).reshape(4, BROWS, D)
+                ref[4 * c : 4 * c + 4, BROWS:, :] = part
         g_b1[...] = jnp.where(keep, g_b1[...], 0.0)
         g_vec[...] = jnp.where(keep, g_vec[...], 0.0)
 
@@ -626,12 +624,11 @@
 
 
 def self_grad_kernel(
-    info, blocks, dqt, dk_ref, dv_ref, x_ref, g_wo, g_cross, g_small,
-    out, keep_out, send_out,
+    info, dqt, dk_ref, dv_ref, x_ref, g_wo, g_cross, g_small,
+    keep_out, send_out,
     gq, gk, gv,
 ):
     i = pl.program_id(0)
-    unpack_into(info, i, blocks, out)
 
     @pl.when(i == 0)
     def _():
@@ -1044,7 +1041,7 @@
     small_row = jnp.pad(smalls, (0, 16 * D - n_smalls)).reshape(16, D)
     bundle_a = jnp.concatenate([self_attn, small_row], axis=0)
     in_blocks = ffn_in.reshape(in_rows, 4, D).transpose(1, 0, 2).reshape(4 * in_rows, D)
-    bundle_b = jnp.concatenate([cross_attn, ffn_out, in_blocks], axis=0)
+    bundle_f = jnp.concatenate([ffn_out, in_blocks], axis=0)
     if boxed:
         turned = turns([bundle_a] * members)
     token_pieces = to_unit(token_slices)
@@ -1065,23 +1062,18 @@
     else:
         all_a = lax.all_gather(bundle_a, axes, axis=0, tiled=False)
         wa = jnp.pad(all_a[:, :rows].reshape(BLOCKS, BROWS, D), ((0, 0), (0, SMALL), (0, 0)))
-    all_b = lax.all_gather(tie(bundle_b, token_slices), axes, axis=0, tiled=False)
+    all_b = lax.all_gather(tie(cross_attn, token_slices), axes, axis=0, tiled=False)
+    all_f = lax.all_gather(tie(bundle_f, token_slices), axes, axis=0, tiled=False)
     def blocked(array, count):
         return array.reshape(BLOCKS, count, D)
 
     if owners == BLOCKS:
-        wb = all_b
+        wb, wf = all_b, all_f
     else:
-        first = all_b[:, 2 * rows :].reshape(owners, 4, in_rows, D).transpose(1, 0, 2, 3)
+        first = all_f[:, rows:].reshape(owners, 4, in_rows, D).transpose(1, 0, 2, 3)
         first = first.reshape(4, BLOCKS, BROWS // 4, D).transpose(1, 0, 2, 3)
-        wb = jnp.concatenate(
-            [
-                blocked(all_b[:, :rows], BROWS),
-                blocked(all_b[:, rows : 2 * rows], BROWS),
-                blocked(first, BROWS),
-            ],
-            axis=1,
-        )
+        wb = blocked(all_b, BROWS)
+        wf = jnp.concatenate([blocked(all_f[:, :rows], BROWS), blocked(first, BROWS)], axis=1)
     if boxed:
         x, qt, k, v, wa = project_rows(info, token_pieces, (places, near, far), 2)
         all_a = wa
@@ -1121,7 +1113,7 @@
         ffn_kernel,
         "ffn",
         (GROUP // FR,),
-        [SMEM, COLS_F, ROWS_F, fixed(BLOCKS, 3 * BROWS, D), fixed(8, D), fixed(1, FF)]
+        [SMEM, COLS_F, ROWS_F, OUT_W, fixed(BLOCKS, 2 * BROWS, D), fixed(8, D), fixed(1, FF)]
         + [fixed(PIECE, D)] * 4,
         [
             fixed(GROUP, D),
@@ -1144,20 +1136,21 @@
             shape((8, D), f32),
         ],
         [
+            pltpu.VMEM((GROUP, FF), bf16),
+            pltpu.VMEM((GROUP, FF), bf16),
             pltpu.VMEM((GROUP, D), bf16),
-            pltpu.VMEM((FR, FF), bf16),
+            pltpu.VMEM((GROUP, D), bf16),
             pltpu.VMEM((FR, FF), f32),
             pltpu.VMEM((FR, D), f32),
-            pltpu.VMEM((4, D, D), f32),
-            pltpu.VMEM((FF, D), f32),
             pltpu.VMEM((D, D), f32),
-            pltpu.VMEM((GROUP, D), f32),
+            pltpu.VMEM((D, D), f32),
         ],
         32 << 30,
         info,
         oct_,
         n1,
         wb,
+        wf,
         vecs,
         b1,
         *cotangent_pieces,
@@ -1229,8 +1222,7 @@
     dqt, dk, dv = attend_back(info, qt, k, v, go, ot, *self_saved, False)
     x_late = x
     if boxed:
-        ffn_part = route_four(tie(ffn_pieces, dqt))
-        d1 = tie(d1, ffn_part)
+        d1 = tie(d1, ffn_pieces, m_pieces)
     last_rows = 2 * BROWS + SMALL
     t_out = call(
         self_input_kernel,
@@ -1249,17 +1241,16 @@
     )
     t_pieces = from_unit(t_out)
     x_late = tie(x_late, t_out)
-    memory_grad, keep_last, send_last = call(
+    keep_last, send_last = call(
         self_grad_kernel,
         "self_grad",
         (PIECES,),
-        [SMEM, BLOCKS_IN, COLS, ROWS, ROWS, ROWS, fixed(D, D), fixed(4 * D, D), fixed(BLOCKS, SMALL, 2 * LANES)],
-        [BATCH] + [fixed(HALF, last_rows, D)] * 2,
-        [shape((micro, PIECE, D), f32)] + [shape((HALF, last_rows, D))] * 2,
+        [SMEM, COLS, ROWS, ROWS, ROWS, fixed(D, D), fixed(4 * D, D), fixed(BLOCKS, SMALL, 2 * LANES)],
+        [fixed(HALF, last_rows, D)] * 2,
+        [shape((HALF, last_rows, D))] * 2,
         [pltpu.VMEM((D, D), f32)] * 3,
         4 << 30,
         info,
-        m_pieces,
         dqt,
         dk,
         dv,
@@ -1282,14 +1273,19 @@
 
     if boxed:
         recv_a = tie(recv_a, t_pieces)
+        ffn_part = route_four(tie(ffn_pieces, send_a))
+        memory_grad = unpack(info, tie(m_pieces, send_a), micro)
+        near = tie(near, ffn_part, memory_grad)
         near, send_a, far, send_b = route_two(info, near, recv_a, far, recv_b)
         recv_a, recv_b = dp_swap(send_a, 4), dp_swap(send_b, 2)
-        input_grad = unpack(info, t_pieces, micro)
+        input_grad = unpack(info, tie(t_pieces, send_a), micro)
+        near = tie(near, input_grad)
         last_pieces = turns(route_three(info, near, recv_a, far, recv_b))
         self_attn_grad, cross_attn_grad, gain_grad, bias_grad, out_bias, in_bias = route_last(
             last_pieces, rows, out_rows
         )
     else:
+        memory_grad = unpack(info, m_pieces, micro)
         input_grad = unpack(info, t_pieces, micro)
         ffn = whole_blocks(keep_ffn, send_ffn)
         second = ffn[:, BROWS:].reshape(owners, rows, D)

time: 517 us -> 506 us (0.979)
  waiting for transfers between devices: 80.7 us -> 73.1 us
    ppermute x9, waiting for transfers between devices: 6.46 us -> 18.1 us  [turns(): lax.ppermute(arrays[k], 'fsdp', [(m, (m + k) % n) for m in range(n)])]
    ppermute x9, waiting for transfers between devices: 32.9 us -> 26.1 us  [to_unit(): lax.ppermute(pieces[k], axes, pairs(k))]
    ppermute x15, waiting for transfers between devices: 31.6 us -> 24.8 us  [dp_swap(): return lax.ppermute(array, 'dp', [(d, d ^ bit) for d in range(n)])]
    ppermute x15, starting transfers between devices: 30.6 us -> 24.4 us  [dp_swap(): return lax.ppermute(array, 'dp', [(d, d ^ bit) for d in range(n)])]
    all_to_all x3, waiting for transfers between devices: 9.71 us -> 4.1 us  [from_unit(): return lax.all_to_all(blocks, 'fsdp', split_axis=0, concat_axis=0)]
    pallas_call x22 -> x23, Pallas kernels: 305 us -> 308 us  [call(): pl.pallas_call(kernel, grid=grid, in_specs=in_specs, out_specs=out_specs,...]
    unnamed x103 -> x89, local copies, waits for them, and re-layouts: 11.6 us -> 10 us
  transfers between devices with their start and end apart: 37 -> 38, of which waited for: 17 -> 22; matrix products, arithmetic and copies ran while one was open for 2% -> 2% of each run, Pallas kernels for 45% -> 44%
where the time goes in v4:
time: 506 us; the launch traced here: 502 us
  Pallas kernels  308 us (61%)
  starting transfers between devices  84.6 us (17%)
  waiting for transfers between devices  73.1 us (14%)
  local copies, waits for them, and re-layouts  16.5 us (3%)
  between operations  14.9 us (3%)
    pallas_call x23, Pallas kernels, call(): pl.pallas_call(kernel, grid=grid, in_specs=in_specs, out_specs=out_specs,...  308 us
    ppermute x9, waiting for transfers between devices, to_unit(): lax.ppermute(pieces[k], axes, pairs(k))  26.1 us
    ppermute x15, waiting for transfers between devices, dp_swap(): return lax.ppermute(array, 'dp', [(d, d ^ bit) for d in range(n)])  24.8 us
    ppermute x15, starting transfers between devices, dp_swap(): return lax.ppermute(array, 'dp', [(d, d ^ bit) for d in range(n)])  24.4 us
    ppermute x9, starting transfers between devices, to_unit(): lax.ppermute(pieces[k], axes, pairs(k))  22.5 us
    all_to_all x3, starting transfers between devices, from_unit(): return lax.all_to_all(blocks, 'fsdp', split_axis=0, concat_axis=0)  21.1 us
    ppermute x9, waiting for transfers between devices, turns(): lax.ppermute(arrays[k], 'fsdp', [(m, (m + k) % n) for m in range(n)])  18.1 us
    ppermute x9, starting transfers between devices, turns(): lax.ppermute(arrays[k], 'fsdp', [(m, (m + k) % n) for m in range(n)])  16.6 us
  transfers between devices with their start and end apart: 38, of which 22 were waited for; matrix products, arithmetic and copies ran while one was open for 2% of the time, Pallas kernels for 44%

profile of v4, /device:TPU:12, one launch (start us, length us, event | category | flops | bytes accessed | tf_op | source)
XLA Modules:
  0.0 502.1 jit_solution(14943657443589169959)
XLA Ops:
  7.8 3.5 pick.2
  15.1 2.6 collective-permute-start.6
  17.7 2.5 collective-permute-start.3
  28.6 4.8 pick.3
  33.5 3.5 collective-permute-start.2
  39.3 3.9 collective-permute-done.8
  43.8 3.8 collective-permute-done.5
  47.7 3.9 collective-permute-done.9
  51.7 5.9 %collective-permute-done.x1 = bf16[512,512]{1,0:T(8,128)(2,1)S(1)} collective-permute-done((bf16[512,512]{1,0:T(8,128)(2,1)}, bf16[512,512]{1,0:T(8,128)(2,1)S(1)}, u32[]{:S(2)}, u32[]{:S(2)}) %collective-permute-start) | collective-permute-done | bytes 524320 | tf_op jit(solution)/shard_map/ppermute | solution.py:1005
  57.6 5.6 %collective-permute-done.2.x3 = bf16[512,512]{1,0:T(8,128)(2,1)S(1)} collective-permute-done((bf16[512,512]{1,0:T(8,128)(2,1)S(1)}, bf16[512,512]{1,0:T(8,128)(2,1)S(1)}, u32[]{:S(2)}, u32[]{:S(2)}) %collective-permute-start.2) | collective-permute-done | bytes 524320 | tf_op jit(solution)/shard_map/ppermute | solution.py:1005
  67.3 9.4 %project.2 = (bf16[2048,512]{1,0:T(8,128)(2,1)}, bf16[512,2048]{1,0:T(8,128)(2,1)}, bf16[2048,512]{1,0:T(8,128)(2,1)}, bf16[2048,512]{1,0:T(8,128)(2,1)}, bf16[32,80,512]{2,1,0:T(8,128)(2,1)}) custom-call(s32[20]{0:T(128)} %concatenate.28.info, bf16[512,512]{1,0:T(8,128)(2,1)} %get-tuple-element.144.x0, bf16[512,512]{1,0:T(8,128)(2,1)} %copy-done.34, ...), custom_call_target="tpu_custom_call" | custom-call | flops 4294967296 | bytes 8388608 | tf_op jit(solution)/shard_map/project/pallas_call | solution.py:756
  79.9 4.6 collective-permute-start.13
  84.5 24.1 %attend.2 = (bf16[512,2048]{1,0:T(8,128)(2,1)}, f32[8,2048]{1,0:T(8,128)}, s32[8]{0:T(128)}, bf16[8,8,1280,256]{3,2,1,0:T(8,128)(2,1)}) custom-call(s32[20]{0:T(128)} %concatenate.28.info, bf16[512,2048]{1,0:T(8,128)(2,1)} %get-tuple-element.160.qt, bf16[2048,512]{1,0:T(8,128)(2,1)} %get-tuple-element.161.k, bf16[2048,512]{1,0:T(8,128)(2,1)} %get-tuple-element.162.v), custom_call_target="tpu_custom_call" | custom-call | flops 32212254720 | bytes 8388608 | tf_op jit(solution)/shard_map/attend/pallas_call | solution.py:756
  111.6 6.7 %collective-permute-done.13.x3 = bf16[512,512]{1,0:T(8,128)(2,1)} collective-permute-done((bf16[512,512]{1,0:T(8,128)(2,1)S(1)}, bf16[512,512]{1,0:T(8,128)(2,1)}, u32[]{:S(2)}, u32[]{:S(2)}) %collective-permute-start.13) | collective-permute-done | bytes 524320 | tf_op jit(solution)/shard_map/ppermute | solution.py:1005
  118.4 3.0 collective-permute-start.14
  122.7 3.7 collective-permute-start.16
  126.4 8.1 %first_norm.1 = (f32[2048,512]{1,0:T(8,128)}, f32[2048,1]{1,0:T(8,128)}, bf16[512,2048]{1,0:T(8,128)(2,1)}) custom-call(bf16[512,2048]{1,0:T(8,128)(2,1)} %get-tuple-element.168.ot, bf16[2048,512]{1,0:T(8,128)(2,1)} %get-tuple-element.230.x.x_ref, bf16[32,80,512]{2,1,0:T(8,128)(2,1)} %get-tuple-element.169.wa, bf16[32,64,512]{2,1,0:T(8,128)(2,1)} %bitcast.71, ...), custom_call_target="tpu_custom_call" | custom-call | flops 2147483648 | bytes 8388608 | tf_op jit(solution)/shard_map/first_norm/pallas_call | solution.py:756
  134.6 6.8 %project.3 = (bf16[2048,512]{1,0:T(8,128)(2,1)}, bf16[2048,512]{1,0:T(8,128)(2,1)}, bf16[2048,512]{1,0:T(8,128)(2,1)}) custom-call(s32[20]{0:T(128)} %concatenate.28.info, bf16[512,512]{1,0:T(8,128)(2,1)} %get-tuple-element.172.x0, bf16[512,512]{1,0:T(8,128)(2,1)} %copy-done.36, bf16[512,512]{1,0:T(8,128)(2,1)} %copy-done.37, ...), custom_call_target="tpu_custom_call" | custom-call | flops 4294967296 | bytes 8388608 | tf_op jit(solution)/shard_map/project/pallas_call | solution.py:756
  141.3 25.6 %attend.3 = (bf16[512,2048]{1,0:T(8,128)(2,1)}, f32[8,2048]{1,0:T(8,128)}, s32[8]{0:T(128)}, bf16[8,8,1024,256]{3,2,1,0:T(8,128)(2,1)}) custom-call(s32[20]{0:T(128)} %concatenate.28.info, bf16[512,2048]{1,0:T(8,128)(2,1)} %get-tuple-element.171.qt, bf16[2048,512]{1,0:T(8,128)(2,1)} %get-tuple-element.173.k, bf16[2048,512]{1,0:T(8,128)(2,1)} %get-tuple-element.174.v), custom_call_target="tpu_custom_call" | custom-call | flops 32212254720 | bytes 8388608 | tf_op jit(solution)/shard_map/attend/pallas_call | solution.py:756
  167.0 7.8 %collective-permute-done.16.c3 = bf16[512,512]{1,0:T(8,128)(2,1)} collective-permute-done((bf16[512,512]{1,0:T(8,128)(2,1)S(1)}, bf16[512,512]{1,0:T(8,128)(2,1)}, u32[]{:S(2)}, u32[]{:S(2)}) %collective-permute-start.16) | collective-permute-done | bytes 524320 | tf_op jit(solution)/shard_map/ppermute | solution.py:1005
  174.8 68.5 %ffn.1 = (bf16[2048,512]{1,0:T(8,128)(2,1)}, f32[2048,512]{1,0:T(8,128)}, bf16[2048,512]{1,0:T(8,128)(2,1)}, bf16[16,128,512]{2,1,0:T(8,128)(2,1)}, bf16[16,128,...) custom-call(s32[20]{0:T(128)} %concatenate.28.info, ...), custom_call_target="tpu_custom_call" | custom-call | flops 34359738368 | bytes 8388608 | tf_op jit(solution)/shard_map/ffn/pallas_call | solution.py:756
  243.4 4.2 all-to-all-start
  247.8 3.9 route_one.2
  254.1 50.3 %attend_back.2 = (bf16[512,2048]{1,0:T(8,128)(2,1)}, bf16[2048,512]{1,0:T(8,128)(2,1)}, bf16[2048,512]{1,0:T(8,128)(2,1)}) custom-call(s32[20]{0:T(128)} %concatenate.28.info, s32[8]{0:T(128)} %get-tuple-element.183.flags, bf16[512,2048]{1,0:T(8,128)(2,1)} %get-tuple-element.171.qt, bf16[2048,512]{1,0:T(8,128)(2,1)} %get-tuple-element.173.k, ...), custom_call_target="tpu_custom_call" | custom-call | flops 64424509440 | bytes 8388608 | tf_op jit(solution)/shard_map/attend_back/pallas_call | solution.py:756
  305.3 2.7 route_two.2
  308.3 6.7 %collective-permute-start.21 = (bf16[2,128,512]{2,1,0:T(8,128)(2,1)}, bf16[2,128,512]{2,1,0:T(8,128)(2,1)S(1)}, u32[]{:S(2)}, u32[]{:S(2)}) collective-permute-start(bf16[2,128,512]{2,1,0:T(8,128)(2,1)} %get-tuple-element.210), channel_id=1, source_target_pairs={{0,8},{4,12},{8,0},{12,4},{16,24},{20,28},{24,16},{28,20},{1,9},{5... | collective-permute-start | bytes 786440 | tf_op jit(solution)/shard_map/ppermute | solution.py:963
  316.3 19.3 %cross_post.1 = (f32[3,512,512]{2,1,0:T(8,128)}, bf16[2048,512]{1,0:T(8,128)(2,1)}, f32[2048,512]{1,0:T(8,128)}, bf16[2048,512]{1,0:T(8,128)(2,1)}, bf16[2048,51...) custom-call(s32[20]{0:T(128)} %concatenate.28.info, bf16[4,512,512]{2,1,0:T(8,128)(2,1)} %copy-done.5, ...), custom_call_target="tpu_custom_call" | custom-call | flops 9663676416 | bytes 8388608 | tf_op jit(solution)/shard_map/cross_post/pallas_call | solution.py:756
  335.6 8.6 %all-to-all-start.1 = ((bf16[4,512,512]{2,1,0:T(8,128)(2,1)}), bf16[4,512,512]{2,1,0:T(8,128)(2,1)S(1)}, u32[]{:S(2)}, u32[]{:S(2)}) async-start(bf16[4,512,512]{2,1,0:T(8,128)(2,1)} %bitcast.75), calls=%async_computation.1 | async-start | bytes 4194304 | tf_op jit(solution)/shard_map/all_to_all | solution.py:1010
  345.0 2.2 route_three.2
  351.6 39.7 %attend_back.3 = (bf16[512,2048]{1,0:T(8,128)(2,1)}, bf16[2048,512]{1,0:T(8,128)(2,1)}, bf16[2048,512]{1,0:T(8,128)(2,1)}) custom-call(s32[20]{0:T(128)} %concatenate.28.info, s32[8]{0:T(128)} %get-tuple-element.208.flags, bf16[512,2048]{1,0:T(8,128)(2,1)} %get-tuple-element.160.qt, bf16[2048,512]{1,0:T(8,128)(2,1)} %get-tuple-element.161.k, ...), custom_call_target="tpu_custom_call" | custom-call | flops 64424509440 | bytes 8388608 | tf_op jit(solution)/shard_map/attend_back/pallas_call | solution.py:756
  392.2 4.8 collective-permute-done.22.r1
  400.2 9.0 %self_input.1 = bf16[2048,512]{1,0:T(8,128)(2,1)} custom-call(bf16[512,2048]{1,0:T(8,128)(2,1)} %get-tuple-element.222.dqt, bf16[2048,512]{1,0:T(8,128)(2,1)} %get-tuple-element.223.dk.dk_ref, bf16[2048,512]{1,0:T(8,128)(2,1)} %get-tuple-element.224.dv.dv_ref, f32[2048,512]{1,0:T(8,128)} %get-tuple-element.229.d1, bf16[32,80,512]{2,1,0:T(8,128)(2,1)} %get-tuple-element.169.wa), custom_call_target="tpu_custom_call" | custom-call | flops 4294967296 | bytes 8388608 | tf_op jit(solution)/shard_map/self_input/pallas_call | solution.py:756
  409.3 8.3 %all-to-all-start.2 = ((bf16[4,512,512]{2,1,0:T(8,128)(2,1)}), bf16[4,512,512]{2,1,0:T(8,128)(2,1)S(1)}, u32[]{:S(2)}, u32[]{:S(2)}) async-start(bf16[4,512,512]{2,1,0:T(8,128)(2,1)} %bitcast.77), calls=%async_computation.2 | async-start | bytes 4194304 | tf_op jit(solution)/shard_map/all_to_all | solution.py:1010
  417.6 10.1 %self_grad.1 = (bf16[16,144,512]{2,1,0:T(8,128)(2,1)}, bf16[16,144,512]{2,1,0:T(8,128)(2,1)}) custom-call(s32[20]{0:T(128)} %concatenate.28.info, bf16[512,2048]{1,0:T(8,128)(2,1)} %get-tuple-element.222.dqt, bf16[2048,512]{1,0:T(8,128)(2,1)} %get-tuple-element.223.dk.dk_ref, bf16[2048,512]{1,0:T(8,128)(2,1)} %get-tuple-element.224.dv.dv_ref, ...), custom_call_target="tpu_custom_call" | custom-call | flops 4294967296 | bytes 8388608 | tf_op jit(solution)/shard_map/self_grad/pallas_call | solution.py:756
  427.8 4.7 collective-permute-done.25.recv
  433.9 4.2 route_one.3
  439.6 6.1 %collective-permute-start.27 = (bf16[2,2,144,512]{3,2,1,0:T(8,128)(2,1)}, bf16[2,2,144,512]{3,2,1,0:T(8,128)(2,1)S(1)}, u32[]{:S(2)}, u32[]{:S(2)}) collective-permute-start(bf16[2,2,144,512]{3,2,1,0:T(8,128)(2,1)} %get-tuple-element.248), channel_id=1, source_target_pairs={{0,16},{4,20},{8,24},{12,28},{16,0},{20,4},{24,8},{28,12},{1,17},{... | collective-permute-start | bytes 1769480 | tf_op jit(solution)/shard_map/ppermute | solution.py:963
  445.8 3.7 unpack.2
  451.3 2.4 collective-permute-done.26.ra
  453.7 4.1 all-to-all-done.2.blocks
  460.1 2.7 route_two.3
  462.8 2.6 collective-permute-start.29
  465.9 3.7 unpack.3
  473.1 2.3 route_three.3
  475.4 2.4 collective-permute-start.30
  477.9 4.2 collective-permute-start.31
  483.4 5.3 %collective-permute-done.30.r1 = bf16[144,512]{1,0:T(8,128)(2,1)S(1)} collective-permute-done((bf16[144,512]{1,0:T(8,128)(2,1)}, bf16[144,512]{1,0:T(8,128)(2,1)S(1)}, u32[]{:S(2)}, u32[]{:S(2)}) %collective-permute-start.30) | collective-permute-done | bytes 147488 | tf_op jit(solution)/shard_map/ppermute | solution.py:969
  490.3 2.1 collective-permute-done.32.r3
  (183 shorter events, 58.4 us)
Async XLA Ops:
  7.2 119.2 %all-gather.5.cloned.1.call-start = ((), (), s32[]{:S(2)}) async-start(), calls=%async_computation.3 | async-start | bytes 2162688 | tf_op jit(solution)/shard_map/all_gather | solution.py:1065
  11.4 163.4 %all-gather.7.cloned.1.call-start = ((), (), s32[]{:S(2)}) async-start(), calls=%async_computation.4 | async-start | bytes 4325376 | tf_op jit(solution)/shard_map/all_gather | solution.py:1066
  14.6 18.8 %collective-permute-start.7 = (bf16[80,512]{1,0:T(8,128)(2,1)S(1)}, bf16[80,512]{1,0:T(8,128)(2,1)S(1)}, u32[]{:S(2)}, u32[]{:S(2)}) collective-permute-start(bf16[80,512]{1,0:T(8,128)(2,1)S(1)} %constant_dynamic-update-slice_fusion), channel_id=1, source_target_pairs={{0,3},{1,0},{2,1},{3,2},{4,7},{5,4},{6,5},{7,6},{8,11},{9,8},{10,9... | collective-permute-start | bytes 245768 | tf_op jit(solution)/shard_map/ppermute | solution.py:969
  15.1 21.9 %collective-permute-start.6 = (bf16[80,512]{1,0:T(8,128)(2,1)S(1)}, bf16[80,512]{1,0:T(8,128)(2,1)S(1)}, u32[]{:S(2)}, u32[]{:S(2)}) collective-permute-start(bf16[80,512]{1,0:T(8,128)(2,1)S(1)} %constant_dynamic-update-slice_fusion), channel_id=1, source_target_pairs={{0,2},{1,3},{2,0},{3,1},{4,6},{5,7},{6,4},{7,5},{8,10},{9,11},{10,... | collective-permute-start | bytes 245768 | tf_op jit(solution)/shard_map/ppermute | solution.py:969
  17.7 8.1 %collective-permute-start.3 = (bf16[80,512]{1,0:T(8,128)(2,1)S(1)}, bf16[80,512]{1,0:T(8,128)(2,1)S(1)}, u32[]{:S(2)}, u32[]{:S(2)}) collective-permute-start(bf16[80,512]{1,0:T(8,128)(2,1)S(1)} %constant_dynamic-update-slice_fusion), channel_id=1, source_target_pairs={{0,1},{1,2},{2,3},{3,0},{4,5},{5,6},{6,7},{7,4},{8,9},{9,10},{10,1... | collective-permute-start | bytes 245768 | tf_op jit(solution)/shard_map/ppermute | solution.py:969
  20.2 37.4 %collective-permute-start = (bf16[512,512]{1,0:T(8,128)(2,1)}, bf16[512,512]{1,0:T(8,128)(2,1)S(1)}, u32[]{:S(2)}, u32[]{:S(2)}) collective-permute-start(bf16[512,512]{1,0:T(8,128)(2,1)} %get-tuple-element.145), channel_id=1, source_target_pairs={{0,1},{1,2},{3,0},{4,5},{5,6},{6,7},{8,9},{9,10},{11,8},{12,13},{1... | collective-permute-start | bytes 1572872 | tf_op jit(solution)/shard_map/ppermute | solution.py:1005
  22.1 35.5 %collective-permute-start.1 = (bf16[512,512]{1,0:T(8,128)(2,1)}, bf16[512,512]{1,0:T(8,128)(2,1)}, u32[]{:S(2)}, u32[]{:S(2)}) collective-permute-start(bf16[512,512]{1,0:T(8,128)(2,1)} %get-tuple-element.146), channel_id=1, source_target_pairs={{0,2},{2,0},{3,1},{4,6},{5,7},{7,5},{8,10},{10,8},{11,9},{12,14},{... | collective-permute-start | bytes 1572872 | tf_op jit(solution)/shard_map/ppermute | solution.py:1005
  25.9 11.8 %collective-permute-start.4 = (bf16[2,80,512]{2,1,0:T(8,128)(2,1)S(1)}, bf16[2,80,512]{2,1,0:T(8,128)(2,1)S(1)}, u32[]{:S(2)}, u32[]{:S(2)}) collective-permute-start(bf16[2,80,512]{2,1,0:T(8,128)(2,1)S(1)} %get-tuple-element.272), channel_id=1, source_target_pairs={{0,8},{4,12},{8,0},{12,4},{16,24},{20,28},{24,16},{28,20},{1,9},{5... | collective-permute-start | bytes 491528 | tf_op jit(solution)/shard_map/ppermute | solution.py:963
  33.5 29.7 %collective-permute-start.2 = (bf16[512,512]{1,0:T(8,128)(2,1)S(1)}, bf16[512,512]{1,0:T(8,128)(2,1)S(1)}, u32[]{:S(2)}, u32[]{:S(2)}) collective-permute-start(bf16[512,512]{1,0:T(8,128)(2,1)S(1)} %copy-done.32), channel_id=1, source_target_pairs={{1,0},{2,1},{3,2},{4,7},{6,5},{7,6},{9,8},{10,9},{11,10},{12,15},{... | collective-permute-start | bytes 1572872 | tf_op jit(solution)/shard_map/ppermute | solution.py:1005
  37.0 26.2 %copy-start.21 = (bf16[16,2048]{1,0:T(8,128)(2,1)S(1)}, bf16[16,2048]{1,0:T(8,128)(2,1)}, u32[]{:S(2)}) copy-start(bf16[16,2048]{1,0:T(8,128)(2,1)} %param.26) | copy-start | bytes 196612
  37.0 27.0 %copy-start.22 = (bf16[64,512]{1,0:T(8,128)(2,1)S(1)}, bf16[64,512]{1,0:T(8,128)(2,1)}, u32[]{:S(2)}) copy-start(bf16[64,512]{1,0:T(8,128)(2,1)} %param.28) | copy-start | bytes 196612
  37.1 6.1 %collective-permute-start.8 = (bf16[2,80,512]{2,1,0:T(8,128)(2,1)S(1)}, bf16[2,80,512]{2,1,0:T(8,128)(2,1)S(1)}, u32[]{:S(2)}, u32[]{:S(2)}) collective-permute-start(bf16[2,80,512]{2,1,0:T(8,128)(2,1)S(1)} %get-tuple-element.270), channel_id=1, source_target_pairs={{0,16},{4,20},{8,24},{12,28},{16,0},{20,4},{24,8},{28,12},{1,17},{... | collective-permute-start | bytes 491528 | tf_op jit(solution)/shard_map/ppermute | solution.py:963
  37.7 10.0 %collective-permute-start.5 = (bf16[2,2,80,512]{3,2,1,0:T(8,128)(2,1)S(1)}, bf16[2,2,80,512]{3,2,1,0:T(8,128)(2,1)S(1)}, u32[]{:S(2)}, u32[]{:S(2)}) collective-permute-start(bf16[2,2,80,512]{3,2,1,0:T(8,128)(2,1)S(1)} %pad_maximum_fusion), channel_id=1, source_target_pairs={{0,16},{4,20},{8,24},{12,28},{16,0},{20,4},{24,8},{28,12},{1,17},{... | collective-permute-start | bytes 983048 | tf_op jit(solution)/shard_map/ppermute | solution.py:963
  43.2 8.5 %collective-permute-start.9 = (bf16[2,2,80,512]{3,2,1,0:T(8,128)(2,1)S(1)}, bf16[2,2,80,512]{3,2,1,0:T(8,128)(2,1)S(1)}, u32[]{:S(2)}, u32[]{:S(2)}) collective-permute-start(bf16[2,2,80,512]{3,2,1,0:T(8,128)(2,1)S(1)} %pad_maximum_fusion.1), channel_id=1, source_target_pairs={{0,8},{4,12},{8,0},{12,4},{16,24},{20,28},{24,16},{28,20},{1,9},{5... | collective-permute-start | bytes 983048 | tf_op jit(solution)/shard_map/ppermute | solution.py:963
  63.2 3.0 collective-permute-start.10
  76.7 34.9 %collective-permute-start.11 = (bf16[512,512]{1,0:T(8,128)(2,1)}, bf16[512,512]{1,0:T(8,128)(2,1)S(1)}, u32[]{:S(2)}, u32[]{:S(2)}) collective-permute-start(bf16[512,512]{1,0:T(8,128)(2,1)} %get-tuple-element.165), channel_id=1, source_target_pairs={{0,1},{1,2},{3,0},{4,5},{5,6},{6,7},{8,9},{9,10},{11,8},{12,13},{1... | collective-permute-start | bytes 1572872 | tf_op jit(solution)/shard_map/ppermute | solution.py:1005
  78.6 33.0 %collective-permute-start.12 = (bf16[512,512]{1,0:T(8,128)(2,1)}, bf16[512,512]{1,0:T(8,128)(2,1)S(1)}, u32[]{:S(2)}, u32[]{:S(2)}) collective-permute-start(bf16[512,512]{1,0:T(8,128)(2,1)} %get-tuple-element.166), channel_id=1, source_target_pairs={{0,2},{2,0},{3,1},{4,6},{5,7},{7,5},{8,10},{10,8},{11,9},{12,14},{... | collective-permute-start | bytes 1572872 | tf_op jit(solution)/shard_map/ppermute | solution.py:1005
  79.9 38.4 %collective-permute-start.13 = (bf16[512,512]{1,0:T(8,128)(2,1)S(1)}, bf16[512,512]{1,0:T(8,128)(2,1)}, u32[]{:S(2)}, u32[]{:S(2)}) collective-permute-start(bf16[512,512]{1,0:T(8,128)(2,1)S(1)} %copy-done.33), channel_id=1, source_target_pairs={{1,0},{2,1},{3,2},{4,7},{6,5},{7,6},{9,8},{10,9},{11,10},{12,15},{... | collective-permute-start | bytes 1572872 | tf_op jit(solution)/shard_map/ppermute | solution.py:1005
  84.5 33.9 %copy-start.31 = (bf16[512,512]{1,0:T(8,128)(2,1)S(1)}, bf16[512,512]{1,0:T(8,128)(2,1)}, u32[]{:S(2)}) copy-start(bf16[512,512]{1,0:T(8,128)(2,1)} %get-tuple-element.179) | copy-start | bytes 1572868
  84.5 36.8 %copy-start.30 = (bf16[512,512]{1,0:T(8,128)(2,1)S(1)}, bf16[512,512]{1,0:T(8,128)(2,1)}, u32[]{:S(2)}) copy-start(bf16[512,512]{1,0:T(8,128)(2,1)} %get-tuple-element.180) | copy-start | bytes 1572868
  84.5 38.1 %copy-start.29 = (bf16[512,512]{1,0:T(8,128)(2,1)S(1)}, bf16[512,512]{1,0:T(8,128)(2,1)}, u32[]{:S(2)}) copy-start(bf16[512,512]{1,0:T(8,128)(2,1)} %get-tuple-element.181) | copy-start | bytes 1572868
  111.6 22.9 %copy-start.36 = (bf16[512,512]{1,0:T(8,128)(2,1)}, bf16[512,512]{1,0:T(8,128)(2,1)S(1)}, u32[]{:S(2)}) copy-start(bf16[512,512]{1,0:T(8,128)(2,1)S(1)} %collective-permute-done.11.x1) | copy-start | bytes 1572868
  111.6 22.9 %copy-start.37 = (bf16[512,512]{1,0:T(8,128)(2,1)}, bf16[512,512]{1,0:T(8,128)(2,1)S(1)}, u32[]{:S(2)}) copy-start(bf16[512,512]{1,0:T(8,128)(2,1)S(1)} %collective-permute-done.12.x2) | copy-start | bytes 1572868
  118.4 48.6 %collective-permute-start.14 = (bf16[512,512]{1,0:T(8,128)(2,1)S(1)}, bf16[512,512]{1,0:T(8,128)(2,1)S(1)}, u32[]{:S(2)}, u32[]{:S(2)}) collective-permute-start(bf16[512,512]{1,0:T(8,128)(2,1)S(1)} %copy-done.31), channel_id=1, source_target_pairs={{0,1},{1,2},{3,0},{4,5},{5,6},{6,7},{8,9},{9,10},{11,8},{12,13},{1... | collective-permute-start | bytes 1572872 | tf_op jit(solution)/shard_map/ppermute | solution.py:1005
  121.4 45.6 %collective-permute-start.15 = (bf16[512,512]{1,0:T(8,128)(2,1)S(1)}, bf16[512,512]{1,0:T(8,128)(2,1)}, u32[]{:S(2)}, u32[]{:S(2)}) collective-permute-start(bf16[512,512]{1,0:T(8,128)(2,1)S(1)} %copy-done.30), channel_id=1, source_target_pairs={{0,2},{2,0},{3,1},{4,6},{5,7},{7,5},{8,10},{10,8},{11,9},{12,14},{... | collective-permute-start | bytes 1572872 | tf_op jit(solution)/shard_map/ppermute | solution.py:1005
  122.7 52.1 %collective-permute-start.16 = (bf16[512,512]{1,0:T(8,128)(2,1)S(1)}, bf16[512,512]{1,0:T(8,128)(2,1)}, u32[]{:S(2)}, u32[]{:S(2)}) collective-permute-start(bf16[512,512]{1,0:T(8,128)(2,1)S(1)} %copy-done.29), channel_id=1, source_target_pairs={{1,0},{2,1},{3,2},{4,7},{6,5},{7,6},{9,8},{10,9},{11,10},{12,15},{... | collective-permute-start | bytes 1572872 | tf_op jit(solution)/shard_map/ppermute | solution.py:1005
  243.3 4.6 collective-permute-start.17
  243.4 71.6 %all-to-all-start = ((bf16[4,512,512]{2,1,0:T(8,128)(2,1)}), bf16[4,512,512]{2,1,0:T(8,128)(2,1)S(1)}, u32[]{:S(2)}, u32[]{:S(2)}) async-start(bf16[4,512,512]{2,1,0:T(8,128)(2,1)} %bitcast.76), calls=%async_computation | async-start | bytes 4194304 | tf_op jit(solution)/shard_map/all_to_all | solution.py:1010
  251.8 52.6 %collective-permute-start.18 = (bf16[2,2,128,512]{3,2,1,0:T(8,128)(2,1)}, bf16[2,2,128,512]{3,2,1,0:T(8,128)(2,1)S(1)}, u32[]{:S(2)}, u32[]{:S(2)}) collective-permute-start(bf16[2,2,128,512]{3,2,1,0:T(8,128)(2,1)} %get-tuple-element.187), channel_id=1, source_target_pairs={{0,8},{4,12},{8,0},{12,4},{16,24},{20,28},{24,16},{28,20},{1,9},{5... | collective-permute-start | bytes 1572872 | tf_op jit(solution)/shard_map/ppermute | solution.py:963
  252.4 52.0 %collective-permute-start.19 = (bf16[2,2,128,512]{3,2,1,0:T(8,128)(2,1)}, bf16[2,2,128,512]{3,2,1,0:T(8,128)(2,1)S(1)}, u32[]{:S(2)}, u32[]{:S(2)}) collective-permute-start(bf16[2,2,128,512]{3,2,1,0:T(8,128)(2,1)} %get-tuple-element.198), channel_id=1, source_target_pairs={{0,16},{4,20},{8,24},{12,28},{16,0},{20,4},{24,8},{28,12},{1,17},{... | collective-permute-start | bytes 1572872 | tf_op jit(solution)/shard_map/ppermute | solution.py:963
  308.0 36.2 %collective-permute-start.20 = (bf16[2,128,512]{2,1,0:T(8,128)(2,1)}, bf16[2,128,512]{2,1,0:T(8,128)(2,1)S(1)}, u32[]{:S(2)}, u32[]{:S(2)}) collective-permute-start(bf16[2,128,512]{2,1,0:T(8,128)(2,1)} %get-tuple-element.205), channel_id=1, source_target_pairs={{0,16},{4,20},{8,24},{12,28},{16,0},{20,4},{24,8},{28,12},{1,17},{... | collective-permute-start | bytes 786440 | tf_op jit(solution)/shard_map/ppermute | solution.py:963
  308.3 35.9 %collective-permute-start.21 = (bf16[2,128,512]{2,1,0:T(8,128)(2,1)}, bf16[2,128,512]{2,1,0:T(8,128)(2,1)S(1)}, u32[]{:S(2)}, u32[]{:S(2)}) collective-permute-start(bf16[2,128,512]{2,1,0:T(8,128)(2,1)} %get-tuple-element.210), channel_id=1, source_target_pairs={{0,8},{4,12},{8,0},{12,4},{16,24},{20,28},{24,16},{28,20},{1,9},{5... | collective-permute-start | bytes 786440 | tf_op jit(solution)/shard_map/ppermute | solution.py:963
  335.6 64.6 %all-to-all-start.1 = ((bf16[4,512,512]{2,1,0:T(8,128)(2,1)}), bf16[4,512,512]{2,1,0:T(8,128)(2,1)S(1)}, u32[]{:S(2)}, u32[]{:S(2)}) async-start(bf16[4,512,512]{2,1,0:T(8,128)(2,1)} %bitcast.75), calls=%async_computation.1 | async-start | bytes 4194304 | tf_op jit(solution)/shard_map/all_to_all | solution.py:1010
  347.2 49.8 %collective-permute-start.22 = (bf16[128,512]{1,0:T(8,128)(2,1)}, bf16[128,512]{1,0:T(8,128)(2,1)S(1)}, u32[]{:S(2)}, u32[]{:S(2)}) collective-permute-start(bf16[128,512]{1,0:T(8,128)(2,1)} %get-tuple-element.225), channel_id=1, source_target_pairs={{0,1},{1,2},{2,3},{3,0},{4,5},{5,6},{6,7},{7,4},{8,9},{9,10},{10,1... | collective-permute-start | bytes 393224 | tf_op jit(solution)/shard_map/ppermute | solution.py:969
  348.7 49.7 %collective-permute-start.23 = (bf16[128,512]{1,0:T(8,128)(2,1)}, bf16[128,512]{1,0:T(8,128)(2,1)S(1)}, u32[]{:S(2)}, u32[]{:S(2)}) collective-permute-start(bf16[128,512]{1,0:T(8,128)(2,1)} %get-tuple-element.226), channel_id=1, source_target_pairs={{0,2},{1,3},{2,0},{3,1},{4,6},{5,7},{6,4},{7,5},{8,10},{9,11},{10,... | collective-permute-start | bytes 393224 | tf_op jit(solution)/shard_map/ppermute | solution.py:969
  349.6 50.6 %collective-permute-start.24 = (bf16[128,512]{1,0:T(8,128)(2,1)}, bf16[128,512]{1,0:T(8,128)(2,1)S(1)}, u32[]{:S(2)}, u32[]{:S(2)}) collective-permute-start(bf16[128,512]{1,0:T(8,128)(2,1)} %get-tuple-element.227), channel_id=1, source_target_pairs={{0,3},{1,0},{2,1},{3,2},{4,7},{5,4},{6,5},{7,6},{8,11},{9,8},{10,9... | collective-permute-start | bytes 393224 | tf_op jit(solution)/shard_map/ppermute | solution.py:969
  351.6 39.7 %copy-start.23 = (f32[8,512]{1,0:T(8,128)S(1)}, f32[8,512]{1,0:T(8,128)}, u32[]{:S(2)}) copy-start(f32[8,512]{1,0:T(8,128)} %get-tuple-element.233) | copy-start | bytes 49156
  351.6 39.7 %copy-start.24 = (f32[8,512]{1,0:T(8,128)S(1)}, f32[8,512]{1,0:T(8,128)}, u32[]{:S(2)}) copy-start(f32[8,512]{1,0:T(8,128)} %get-tuple-element.234) | copy-start | bytes 49156
  409.3 48.5 %all-to-all-start.2 = ((bf16[4,512,512]{2,1,0:T(8,128)(2,1)}), bf16[4,512,512]{2,1,0:T(8,128)(2,1)S(1)}, u32[]{:S(2)}, u32[]{:S(2)}) async-start(bf16[4,512,512]{2,1,0:T(8,128)(2,1)} %bitcast.77), calls=%async_computation.2 | async-start | bytes 4194304 | tf_op jit(solution)/shard_map/all_to_all | solution.py:1010
  427.7 4.7 collective-permute-start.25
  438.1 15.6 %collective-permute-start.26 = (bf16[2,2,144,512]{3,2,1,0:T(8,128)(2,1)}, bf16[2,2,144,512]{3,2,1,0:T(8,128)(2,1)S(1)}, u32[]{:S(2)}, u32[]{:S(2)}) collective-permute-start(bf16[2,2,144,512]{3,2,1,0:T(8,128)(2,1)} %get-tuple-element.239), channel_id=1, source_target_pairs={{0,8},{4,12},{8,0},{12,4},{16,24},{20,28},{24,16},{28,20},{1,9},{5... | collective-permute-start | bytes 1769480 | tf_op jit(solution)/shard_map/ppermute | solution.py:963
  439.6 19.7 %collective-permute-start.27 = (bf16[2,2,144,512]{3,2,1,0:T(8,128)(2,1)}, bf16[2,2,144,512]{3,2,1,0:T(8,128)(2,1)S(1)}, u32[]{:S(2)}, u32[]{:S(2)}) collective-permute-start(bf16[2,2,144,512]{3,2,1,0:T(8,128)(2,1)} %get-tuple-element.248), channel_id=1, source_target_pairs={{0,16},{4,20},{8,24},{12,28},{16,0},{20,4},{24,8},{28,12},{1,17},{... | collective-permute-start | bytes 1769480 | tf_op jit(solution)/shard_map/ppermute | solution.py:963
  462.8 8.4 %collective-permute-start.29 = (bf16[2,144,512]{2,1,0:T(8,128)(2,1)}, bf16[2,144,512]{2,1,0:T(8,128)(2,1)S(1)}, u32[]{:S(2)}, u32[]{:S(2)}) collective-permute-start(bf16[2,144,512]{2,1,0:T(8,128)(2,1)} %get-tuple-element.254), channel_id=1, source_target_pairs={{0,8},{4,12},{8,0},{12,4},{16,24},{20,28},{24,16},{28,20},{1,9},{5... | collective-permute-start | bytes 884744 | tf_op jit(solution)/shard_map/ppermute | solution.py:963
  465.4 6.9 %collective-permute-start.28 = (bf16[2,144,512]{2,1,0:T(8,128)(2,1)}, bf16[2,144,512]{2,1,0:T(8,128)(2,1)S(1)}, u32[]{:S(2)}, u32[]{:S(2)}) collective-permute-start(bf16[2,144,512]{2,1,0:T(8,128)(2,1)} %get-tuple-element.249), channel_id=1, source_target_pairs={{0,16},{4,20},{8,24},{12,28},{16,0},{20,4},{24,8},{28,12},{1,17},{... | collective-permute-start | bytes 884744 | tf_op jit(solution)/shard_map/ppermute | solution.py:963
  465.9 29.1 %copy-start.1 = (s32[3,1,4]{2,1,0:T(1,128)S(1)}, s32[3,1,4]{2,1,0:T(1,128)}, u32[]{:S(2)}) copy-start(s32[3,1,4]{2,1,0:T(1,128)} %param.23) | copy-start | bytes 148
  475.4 13.2 %collective-permute-start.30 = (bf16[144,512]{1,0:T(8,128)(2,1)}, bf16[144,512]{1,0:T(8,128)(2,1)S(1)}, u32[]{:S(2)}, u32[]{:S(2)}) collective-permute-start(bf16[144,512]{1,0:T(8,128)(2,1)} %get-tuple-element.256), channel_id=1, source_target_pairs={{0,1},{1,2},{2,3},{3,0},{4,5},{5,6},{6,7},{7,4},{8,9},{9,10},{10,1... | collective-permute-start | bytes 442376 | tf_op jit(solution)/shard_map/ppermute | solution.py:969
  477.9 12.5 %collective-permute-start.31 = (bf16[144,512]{1,0:T(8,128)(2,1)}, bf16[144,512]{1,0:T(8,128)(2,1)S(1)}, u32[]{:S(2)}, u32[]{:S(2)}) collective-permute-start(bf16[144,512]{1,0:T(8,128)(2,1)} %get-tuple-element.257), channel_id=1, source_target_pairs={{0,2},{1,3},{2,0},{3,1},{4,6},{5,7},{6,4},{7,5},{8,10},{9,11},{10,... | collective-permute-start | bytes 442376 | tf_op jit(solution)/shard_map/ppermute | solution.py:969
  482.1 10.4 %collective-permute-start.32 = (bf16[144,512]{1,0:T(8,128)(2,1)}, bf16[144,512]{1,0:T(8,128)(2,1)S(1)}, u32[]{:S(2)}, u32[]{:S(2)}) collective-permute-start(bf16[144,512]{1,0:T(8,128)(2,1)} %get-tuple-element.258), channel_id=1, source_target_pairs={{0,3},{1,0},{2,1},{3,2},{4,7},{5,4},{6,5},{7,6},{8,11},{9,8},{10,9... | collective-permute-start | bytes 442376 | tf_op jit(solution)/shard_map/ppermute | solution.py:969
  (29 other events, 176.4 us)
Sparse Core Ops, SparseCore 0:
  11.5 69.2 all-gather.4
  84.4 89.2 all-gather.6

commit v5 on v4

--- a/solution.py
+++ b/solution.py
@@ -623,9 +623,9 @@
         g_vec[...] = jnp.where(keep, g_vec[...], 0.0)
 
 
-def self_grad_kernel(
-    info, dqt, dk_ref, dv_ref, x_ref, g_wo, g_cross, g_small,
-    keep_out, send_out,
+def self_post_kernel(
+    info, dqt, dk_ref, dv_ref, x_ref, d1, wa, g_wo, g_cross, g_small,
+    dtok, keep_out, send_out,
     gq, gk, gv,
 ):
     i = pl.program_id(0)
@@ -635,10 +635,16 @@
         for ref in (gq, gk, gv):
             ref[...] = jnp.zeros_like(ref)
 
-    x = x_ref[...]
-    gq[...] += dot(x, dqt[...], 0, 1)
-    gk[...] += dot(x, dk_ref[...], 0, 0)
-    gv[...] += dot(x, dv_ref[...], 0, 0)
+    x, dk, dv, dq = x_ref[...], dk_ref[...], dv_ref[...], dqt[...].T
+    dtok[...] = (
+        d1[...]
+        + dot(dq, square(wa, 0), 1, 1)
+        + dot(dk, square(wa, 1), 1, 1)
+        + dot(dv, square(wa, 2), 1, 1)
+    ).astype(bf16)
+    gq[...] += dot(x, dq, 0, 0)
+    gk[...] += dot(x, dk, 0, 0)
+    gv[...] += dot(x, dv, 0, 0)
 
     @pl.when(i == pl.num_programs(0) - 1)
     def _():
@@ -657,15 +663,6 @@
                 ref[blocks, BROWS : 2 * BROWS, :] = part.reshape(4, BROWS, D)
                 ref[blocks, 2 * BROWS :, : 2 * LANES] = g_small[pl.ds((2 * n + core) * 4, 4), :, :]
                 ref[blocks, 2 * BROWS :, 2 * LANES :] = jnp.zeros((4, SMALL, D - 2 * LANES), bf16)
-
-
-def self_input_kernel(dqt, dk, dv, d1, wa, dtok):
-    dtok[...] = (
-        d1[...]
-        + dot(dqt[...], square(wa, 0), 0, 1)
-        + dot(dk[...], square(wa, 1), 1, 1)
-        + dot(dv[...], square(wa, 2), 1, 1)
-    ).astype(bf16)
 
 
 def pick_kernel(count, places, *refs):
@@ -1220,45 +1217,30 @@
             axis=1,
         )
     dqt, dk, dv = attend_back(info, qt, k, v, go, ot, *self_saved, False)
-    x_late = x
     if boxed:
         d1 = tie(d1, ffn_pieces, m_pieces)
     last_rows = 2 * BROWS + SMALL
-    t_out = call(
-        self_input_kernel,
-        "self_input",
+    t_out, keep_last, send_last = call(
+        self_post_kernel,
+        "self_post",
         (PIECES,),
-        [COLS, ROWS, ROWS, ROWS, fixed(3 * BLOCKS // 4, BROWS, D)],
-        ROWS,
-        ROWMAJOR,
-        [],
-        4 << 30,
-        dqt,
-        dk,
-        dv,
-        d1,
-        wa,
-    )
-    t_pieces = from_unit(t_out)
-    x_late = tie(x_late, t_out)
-    keep_last, send_last = call(
-        self_grad_kernel,
-        "self_grad",
-        (PIECES,),
-        [SMEM, COLS, ROWS, ROWS, ROWS, fixed(D, D), fixed(4 * D, D), fixed(BLOCKS, SMALL, 2 * LANES)],
-        [fixed(HALF, last_rows, D)] * 2,
-        [shape((HALF, last_rows, D))] * 2,
+        [SMEM, COLS, ROWS, ROWS, ROWS, ROWS, fixed(3 * BLOCKS // 4, BROWS, D), fixed(D, D), fixed(4 * D, D), fixed(BLOCKS, SMALL, 2 * LANES)],
+        [ROWS] + [fixed(HALF, last_rows, D)] * 2,
+        [ROWMAJOR] + [shape((HALF, last_rows, D))] * 2,
         [pltpu.VMEM((D, D), f32)] * 3,
         4 << 30,
         info,
         dqt,
         dk,
         dv,
-        x_late,
+        x,
+        d1,
+        wa,
         g_wo,
         g_cross,
         g_small,
     )
+    t_pieces = from_unit(t_out)
     if boxed:
         recv_last = dp_swap(send_last, 1)
         near, send_a, far, send_b = route_one(info, keep_last, recv_last)
@@ -1272,7 +1254,6 @@
         return lax.psum_scatter(array, axes, scatter_dimension=0, tiled=True)[0].astype(f32)
 
     if boxed:
-        recv_a = tie(recv_a, t_pieces)
         ffn_part = route_four(tie(ffn_pieces, send_a))
         memory_grad = unpack(info, tie(m_pieces, send_a), micro)
         near = tie(near, ffn_part, memory_grad)

time: 506 us -> 511 us (level)
  waiting for transfers between devices: 73.1 us -> 81.1 us
  Pallas kernels: 308 us -> 301 us
    all_to_all x3, waiting for transfers between devices: 4.1 us -> 18.3 us  [from_unit(): return lax.all_to_all(blocks, 'fsdp', split_axis=0, concat_axis=0)]
    pallas_call x23 -> x22, Pallas kernels: 308 us -> 301 us  [call(): pl.pallas_call(kernel, grid=grid, in_specs=in_specs, out_specs=out_specs,...]
  transfers between devices with their start and end apart: 38 -> 38, of which waited for: 22 -> 18; matrix products, arithmetic and copies ran while one was open for 2% -> 2% of each run, Pallas kernels for 44% -> 42%
where the time goes in v5:
time: 511 us; the launch traced here: 505 us
  Pallas kernels  301 us (59%)
  starting transfers between devices  86.4 us (17%)
  waiting for transfers between devices  81.1 us (16%)
  local copies, waits for them, and re-layouts  16.5 us (3%)
  between operations  14.9 us (3%)
    pallas_call x22, Pallas kernels, call(): pl.pallas_call(kernel, grid=grid, in_specs=in_specs, out_specs=out_specs,...  301 us
    ppermute x15, starting transfers between devices, dp_swap(): return lax.ppermute(array, 'dp', [(d, d ^ bit) for d in range(n)])  27.1 us
    ppermute x9, waiting for transfers between devices, to_unit(): lax.ppermute(pieces[k], axes, pairs(k))  25.1 us
    ppermute x9, starting transfers between devices, to_unit(): lax.ppermute(pieces[k], axes, pairs(k))  22.5 us
    ppermute x15, waiting for transfers between devices, dp_swap(): return lax.ppermute(array, 'dp', [(d, d ^ bit) for d in range(n)])  21.4 us
    all_to_all x3, starting transfers between devices, from_unit(): return lax.all_to_all(blocks, 'fsdp', split_axis=0, concat_axis=0)  21.1 us
    all_to_all x3, waiting for transfers between devices, from_unit(): return lax.all_to_all(blocks, 'fsdp', split_axis=0, concat_axis=0)  18.3 us
    ppermute x9, waiting for transfers between devices, turns(): lax.ppermute(arrays[k], 'fsdp', [(m, (m + k) % n) for m in range(n)])  16.2 us
  transfers between devices with their start and end apart: 38, of which 18 were waited for; matrix products, arithmetic and copies ran while one was open for 2% of the time, Pallas kernels for 42%

profile of v5, /device:TPU:12, one launch (start us, length us, event | category | flops | bytes accessed | tf_op | source)
XLA Modules:
  0.0 504.8 jit_solution(13793562870034435264)
XLA Ops:
  7.8 3.5 pick.2
  15.1 2.6 collective-permute-start.6
  17.7 2.5 collective-permute-start.3
  20.2 1.9 collective-permute-start
  28.7 4.9 pick.3
  33.6 3.5 collective-permute-start.2
  39.4 3.9 collective-permute-done.8
  43.9 3.8 collective-permute-done.5
  47.8 3.8 collective-permute-done.9
  51.7 5.9 %collective-permute-done.x1 = bf16[512,512]{1,0:T(8,128)(2,1)S(1)} collective-permute-done((bf16[512,512]{1,0:T(8,128)(2,1)}, bf16[512,512]{1,0:T(8,128)(2,1)S(1)}, u32[]{:S(2)}, u32[]{:S(2)}) %collective-permute-start) | collective-permute-done | bytes 524320 | tf_op jit(solution)/shard_map/ppermute | solution.py:1002
  57.6 5.6 %collective-permute-done.2.x3 = bf16[512,512]{1,0:T(8,128)(2,1)S(1)} collective-permute-done((bf16[512,512]{1,0:T(8,128)(2,1)S(1)}, bf16[512,512]{1,0:T(8,128)(2,1)S(1)}, u32[]{:S(2)}, u32[]{:S(2)}) %collective-permute-start.2) | collective-permute-done | bytes 524320 | tf_op jit(solution)/shard_map/ppermute | solution.py:1002
  67.3 9.4 %project.2 = (bf16[2048,512]{1,0:T(8,128)(2,1)}, bf16[512,2048]{1,0:T(8,128)(2,1)}, bf16[2048,512]{1,0:T(8,128)(2,1)}, bf16[2048,512]{1,0:T(8,128)(2,1)}, bf16[32,80,512]{2,1,0:T(8,128)(2,1)}) custom-call(s32[20]{0:T(128)} %concatenate.28.info, bf16[512,512]{1,0:T(8,128)(2,1)} %get-tuple-element.143.x0, bf16[512,512]{1,0:T(8,128)(2,1)} %copy-done.32, ...), custom_call_target="tpu_custom_call" | custom-call | flops 4294967296 | bytes 8388608 | tf_op jit(solution)/shard_map/project/pallas_call | solution.py:753
  76.7 1.9 collective-permute-start.11
  79.9 4.5 collective-permute-start.13
  84.5 26.2 %attend.2 = (bf16[512,2048]{1,0:T(8,128)(2,1)}, f32[8,2048]{1,0:T(8,128)}, s32[8]{0:T(128)}, bf16[8,8,1280,256]{3,2,1,0:T(8,128)(2,1)}) custom-call(s32[20]{0:T(128)} %concatenate.28.info, bf16[512,2048]{1,0:T(8,128)(2,1)} %get-tuple-element.159.qt, bf16[2048,512]{1,0:T(8,128)(2,1)} %get-tuple-element.160.k, bf16[2048,512]{1,0:T(8,128)(2,1)} %get-tuple-element.161.v), custom_call_target="tpu_custom_call" | custom-call | flops 32212254720 | bytes 8388608 | tf_op jit(solution)/shard_map/attend/pallas_call | solution.py:753
  113.7 4.6 collective-permute-done.13.x3
  118.3 1.9 collective-permute-start.14
  121.5 4.8 collective-permute-start.16
  126.4 8.1 %first_norm.1 = (f32[2048,512]{1,0:T(8,128)}, f32[2048,1]{1,0:T(8,128)}, bf16[512,2048]{1,0:T(8,128)(2,1)}) custom-call(bf16[512,2048]{1,0:T(8,128)(2,1)} %get-tuple-element.167.ot, bf16[2048,512]{1,0:T(8,128)(2,1)} %get-tuple-element.163.x.x_ref, bf16[32,80,512]{2,1,0:T(8,128)(2,1)} %get-tuple-element.168.wa, bf16[32,64,512]{2,1,0:T(8,128)(2,1)} %bitcast.71, ...), custom_call_target="tpu_custom_call" | custom-call | flops 2147483648 | bytes 8388608 | tf_op jit(solution)/shard_map/first_norm/pallas_call | solution.py:753
  134.5 6.7 %project.3 = (bf16[2048,512]{1,0:T(8,128)(2,1)}, bf16[2048,512]{1,0:T(8,128)(2,1)}, bf16[2048,512]{1,0:T(8,128)(2,1)}) custom-call(s32[20]{0:T(128)} %concatenate.28.info, bf16[512,512]{1,0:T(8,128)(2,1)} %get-tuple-element.171.x0, bf16[512,512]{1,0:T(8,128)(2,1)} %copy-done.34, bf16[512,512]{1,0:T(8,128)(2,1)} %copy-done.35, bf16[512,512]{1,0:T(8,128)(2,1)} %copy-done.36, ...), custom_call_target="tpu_custom_call" | custom-call | flops 4294967296 | bytes 8388608 | tf_op jit(solution)/shard_map/project/pallas_call | solution.py:753
  141.2 23.6 %attend.3 = (bf16[512,2048]{1,0:T(8,128)(2,1)}, f32[8,2048]{1,0:T(8,128)}, s32[8]{0:T(128)}, bf16[8,8,1024,256]{3,2,1,0:T(8,128)(2,1)}) custom-call(s32[20]{0:T(128)} %concatenate.28.info, bf16[512,2048]{1,0:T(8,128)(2,1)} %get-tuple-element.170.qt, bf16[2048,512]{1,0:T(8,128)(2,1)} %get-tuple-element.172.k, bf16[2048,512]{1,0:T(8,128)(2,1)} %get-tuple-element.173.v), custom_call_target="tpu_custom_call" | custom-call | flops 32212254720 | bytes 8388608 | tf_op jit(solution)/shard_map/attend/pallas_call | solution.py:753
  164.8 9.0 %collective-permute-done.16.c3 = bf16[512,512]{1,0:T(8,128)(2,1)} collective-permute-done((bf16[512,512]{1,0:T(8,128)(2,1)S(1)}, bf16[512,512]{1,0:T(8,128)(2,1)}, u32[]{:S(2)}, u32[]{:S(2)}) %collective-permute-start.16) | collective-permute-done | bytes 524320 | tf_op jit(solution)/shard_map/ppermute | solution.py:1002
  173.8 64.9 %ffn.1 = (bf16[2048,512]{1,0:T(8,128)(2,1)}, f32[2048,512]{1,0:T(8,128)}, bf16[2048,512]{1,0:T(8,128)(2,1)}, bf16[16,128,512]{2,1,0:T(8,128)(2,1)}, bf16[16,128,...) custom-call(s32[20]{0:T(128)} %concatenate.28.info, ...), custom_call_target="tpu_custom_call" | custom-call | flops 34359738368 | bytes 8388608 | tf_op jit(solution)/shard_map/ffn/pallas_call | solution.py:753
  238.7 2.4 collective-permute-start.17
  241.1 6.7 %all-to-all-start = ((bf16[4,512,512]{2,1,0:T(8,128)(2,1)}), bf16[4,512,512]{2,1,0:T(8,128)(2,1)S(1)}, u32[]{:S(2)}, u32[]{:S(2)}) async-start(bf16[4,512,512]{2,1,0:T(8,128)(2,1)} %bitcast.76), calls=%async_computation | async-start | bytes 4194304 | tf_op jit(solution)/shard_map/all_to_all | solution.py:1007
  247.9 4.0 route_one.2
  252.5 45.0 %attend_back.2 = (bf16[512,2048]{1,0:T(8,128)(2,1)}, bf16[2048,512]{1,0:T(8,128)(2,1)}, bf16[2048,512]{1,0:T(8,128)(2,1)}) custom-call(s32[20]{0:T(128)} %concatenate.28.info, s32[8]{0:T(128)} %get-tuple-element.182.flags, bf16[512,2048]{1,0:T(8,128)(2,1)} %get-tuple-element.170.qt, bf16[2048,512]{1,0:T(8,128)(2,1)} %get-tuple-element.172.k, ...), custom_call_target="tpu_custom_call" | custom-call | flops 64424509440 | bytes 8388608 | tf_op jit(solution)/shard_map/attend_back/pallas_call | solution.py:753
  298.5 2.7 route_two.2
  301.2 6.6 %collective-permute-start.20 = (bf16[2,128,512]{2,1,0:T(8,128)(2,1)}, bf16[2,128,512]{2,1,0:T(8,128)(2,1)S(1)}, u32[]{:S(2)}, u32[]{:S(2)}) collective-permute-start(bf16[2,128,512]{2,1,0:T(8,128)(2,1)} %get-tuple-element.204), channel_id=1, source_target_pairs={{0,16},{4,20},{8,24},{12,28},{16,0},{20,4},{24,8},{28,12},{1,17},{... | collective-permute-start | bytes 786440 | tf_op jit(solution)/shard_map/ppermute | solution.py:960
  307.8 7.3 %collective-permute-start.21 = (bf16[2,128,512]{2,1,0:T(8,128)(2,1)}, bf16[2,128,512]{2,1,0:T(8,128)(2,1)S(1)}, u32[]{:S(2)}, u32[]{:S(2)}) collective-permute-start(bf16[2,128,512]{2,1,0:T(8,128)(2,1)} %get-tuple-element.209), channel_id=1, source_target_pairs={{0,8},{4,12},{8,0},{12,4},{16,24},{20,28},{24,16},{28,20},{1,9},{5... | collective-permute-start | bytes 786440 | tf_op jit(solution)/shard_map/ppermute | solution.py:960
  316.4 19.3 %cross_post.1 = (f32[3,512,512]{2,1,0:T(8,128)}, bf16[2048,512]{1,0:T(8,128)(2,1)}, f32[2048,512]{1,0:T(8,128)}, bf16[2048,512]{1,0:T(8,128)(2,1)}, bf16[2048,51...) custom-call(s32[20]{0:T(128)} %concatenate.28.info, bf16[4,512,512]{2,1,0:T(8,128)(2,1)} %copy-done.4, ...), custom_call_target="tpu_custom_call" | custom-call | flops 9663676416 | bytes 8388608 | tf_op jit(solution)/shard_map/cross_post/pallas_call | solution.py:753
  335.7 6.8 %all-to-all-start.1 = ((bf16[4,512,512]{2,1,0:T(8,128)(2,1)}), bf16[4,512,512]{2,1,0:T(8,128)(2,1)S(1)}, u32[]{:S(2)}, u32[]{:S(2)}) async-start(bf16[4,512,512]{2,1,0:T(8,128)(2,1)} %bitcast.75), calls=%async_computation.1 | async-start | bytes 4194304 | tf_op jit(solution)/shard_map/all_to_all | solution.py:1007
  343.3 2.2 route_three.2
  347.9 2.0 collective-permute-start.24
  349.9 45.8 %attend_back.3 = (bf16[512,2048]{1,0:T(8,128)(2,1)}, bf16[2048,512]{1,0:T(8,128)(2,1)}, bf16[2048,512]{1,0:T(8,128)(2,1)}) custom-call(s32[20]{0:T(128)} %concatenate.28.info, s32[8]{0:T(128)} %get-tuple-element.207.flags, bf16[512,2048]{1,0:T(8,128)(2,1)} %get-tuple-element.159.qt, bf16[2048,512]{1,0:T(8,128)(2,1)} %get-tuple-element.160.k, ...), custom_call_target="tpu_custom_call" | custom-call | flops 64424509440 | bytes 8388608 | tf_op jit(solution)/shard_map/attend_back/pallas_call | solution.py:753
  400.9 14.6 %self_post.1 = (bf16[2048,512]{1,0:T(8,128)(2,1)}, bf16[16,144,512]{2,1,0:T(8,128)(2,1)}, bf16[16,144,512]{2,1,0:T(8,128)(2,1)}) custom-call(s32[20]{0:T(128)} %concatenate.28.info, bf16[512,2048]{1,0:T(8,128)(2,1)} %get-tuple-element.221.dqt, bf16[2048,512]{1,0:T(8,128)(2,1)} %get-tuple-element.222.dk_ref, bf16[2048,512]{1,0:T(8,128)(2,1)} %get-tuple-element.223.dv_ref, ...), custom_call_target="tpu_custom_call" | custom-call | flops 4294967296 | bytes 8388608 | tf_op jit(solution)/shard_map/self_post/pallas_call | solution.py:753
  415.7 7.5 %all-to-all-start.2 = ((bf16[4,512,512]{2,1,0:T(8,128)(2,1)}), bf16[4,512,512]{2,1,0:T(8,128)(2,1)S(1)}, u32[]{:S(2)}, u32[]{:S(2)}) async-start(bf16[4,512,512]{2,1,0:T(8,128)(2,1)} %bitcast.77), calls=%async_computation.2 | async-start | bytes 4194304 | tf_op jit(solution)/shard_map/all_to_all | solution.py:1007
  423.2 4.3 route_one.3
  427.5 3.1 collective-permute-start.27
  431.6 3.7 unpack.2
  437.2 6.8 %collective-permute-done.27.rb = bf16[2,2,144,512]{3,2,1,0:T(8,128)(2,1)S(1)} collective-permute-done((bf16[2,2,144,512]{3,2,1,0:T(8,128)(2,1)}, bf16[2,2,144,512]{3,2,1,0:T(8,128)(2,1)S(1)}, u32[]{:S(2)}, u32[]{:S(2)}) %collective-permute-start.27) | collective-permute-done | bytes 589856 | tf_op jit(solution)/shard_map/ppermute | solution.py:960
  446.3 2.7 route_two.3
  450.7 18.3 %all-to-all-done.2.blocks = bf16[4,512,512]{2,1,0:T(8,128)(2,1)S(1)} async-done(((bf16[4,512,512]{2,1,0:T(8,128)(2,1)}), bf16[4,512,512]{2,1,0:T(8,128)(2,1)S(1)}, u32[]{:S(2)}, u32[]{:S(2)}) %all-to-all-start.2) | async-done | bytes 2097184 | tf_op jit(solution)/shard_map/all_to_all | solution.py:1007
  470.4 3.7 unpack.3
  474.9 2.3 route_three.3
  478.7 4.2 collective-permute-start.31
  485.5 6.7 %collective-permute-done.31.r2 = bf16[144,512]{1,0:T(8,128)(2,1)S(1)} collective-permute-done((bf16[144,512]{1,0:T(8,128)(2,1)}, bf16[144,512]{1,0:T(8,128)(2,1)S(1)}, u32[]{:S(2)}, u32[]{:S(2)}) %collective-permute-start.31) | collective-permute-done | bytes 147488 | tf_op jit(solution)/shard_map/ppermute | solution.py:966
  492.2 3.0 collective-permute-done.32.r3
  (178 shorter events, 50.4 us)
Async XLA Ops:
  7.2 119.2 %all-gather.5.cloned.1.call-start = ((), (), s32[]{:S(2)}) async-start(), calls=%async_computation.3 | async-start | bytes 2162688 | tf_op jit(solution)/shard_map/all_gather | solution.py:1062
  11.3 22.2 %copy-start.31 = (bf16[512,512]{1,0:T(8,128)(2,1)S(1)}, bf16[512,512]{1,0:T(8,128)(2,1)}, u32[]{:S(2)}) copy-start(bf16[512,512]{1,0:T(8,128)(2,1)} %get-tuple-element.146) | copy-start | bytes 1572868
  11.4 162.4 %all-gather.7.cloned.1.call-start = ((), (), s32[]{:S(2)}) async-start(), calls=%async_computation.4 | async-start | bytes 4325376 | tf_op jit(solution)/shard_map/all_gather | solution.py:1063
  14.6 18.9 %collective-permute-start.7 = (bf16[80,512]{1,0:T(8,128)(2,1)S(1)}, bf16[80,512]{1,0:T(8,128)(2,1)S(1)}, u32[]{:S(2)}, u32[]{:S(2)}) collective-permute-start(bf16[80,512]{1,0:T(8,128)(2,1)S(1)} %constant_dynamic-update-slice_fusion), channel_id=1, source_target_pairs={{0,3},{1,0},{2,1},{3,2},{4,7},{5,4},{6,5},{7,6},{8,11},{9,8},{10,9... | collective-permute-start | bytes 245768 | tf_op jit(solution)/shard_map/ppermute | solution.py:966
  15.1 22.0 %collective-permute-start.6 = (bf16[80,512]{1,0:T(8,128)(2,1)S(1)}, bf16[80,512]{1,0:T(8,128)(2,1)S(1)}, u32[]{:S(2)}, u32[]{:S(2)}) collective-permute-start(bf16[80,512]{1,0:T(8,128)(2,1)S(1)} %constant_dynamic-update-slice_fusion), channel_id=1, source_target_pairs={{0,2},{1,3},{2,0},{3,1},{4,6},{5,7},{6,4},{7,5},{8,10},{9,11},{10,... | collective-permute-start | bytes 245768 | tf_op jit(solution)/shard_map/ppermute | solution.py:966
  17.7 8.1 %collective-permute-start.3 = (bf16[80,512]{1,0:T(8,128)(2,1)S(1)}, bf16[80,512]{1,0:T(8,128)(2,1)S(1)}, u32[]{:S(2)}, u32[]{:S(2)}) collective-permute-start(bf16[80,512]{1,0:T(8,128)(2,1)S(1)} %constant_dynamic-update-slice_fusion), channel_id=1, source_target_pairs={{0,1},{1,2},{2,3},{3,0},{4,5},{5,6},{6,7},{7,4},{8,9},{9,10},{10,1... | collective-permute-start | bytes 245768 | tf_op jit(solution)/shard_map/ppermute | solution.py:966
  20.2 37.4 %collective-permute-start = (bf16[512,512]{1,0:T(8,128)(2,1)}, bf16[512,512]{1,0:T(8,128)(2,1)S(1)}, u32[]{:S(2)}, u32[]{:S(2)}) collective-permute-start(bf16[512,512]{1,0:T(8,128)(2,1)} %get-tuple-element.144), channel_id=1, source_target_pairs={{0,1},{1,2},{3,0},{4,5},{5,6},{6,7},{8,9},{9,10},{11,8},{12,13},{1... | collective-permute-start | bytes 1572872 | tf_op jit(solution)/shard_map/ppermute | solution.py:1002
  22.1 35.5 %collective-permute-start.1 = (bf16[512,512]{1,0:T(8,128)(2,1)}, bf16[512,512]{1,0:T(8,128)(2,1)}, u32[]{:S(2)}, u32[]{:S(2)}) collective-permute-start(bf16[512,512]{1,0:T(8,128)(2,1)} %get-tuple-element.145), channel_id=1, source_target_pairs={{0,2},{2,0},{3,1},{4,6},{5,7},{7,5},{8,10},{10,8},{11,9},{12,14},{... | collective-permute-start | bytes 1572872 | tf_op jit(solution)/shard_map/ppermute | solution.py:1002
  25.9 11.9 %collective-permute-start.4 = (bf16[2,80,512]{2,1,0:T(8,128)(2,1)S(1)}, bf16[2,80,512]{2,1,0:T(8,128)(2,1)S(1)}, u32[]{:S(2)}, u32[]{:S(2)}) collective-permute-start(bf16[2,80,512]{2,1,0:T(8,128)(2,1)S(1)} %get-tuple-element.270), channel_id=1, source_target_pairs={{0,8},{4,12},{8,0},{12,4},{16,24},{20,28},{24,16},{28,20},{1,9},{5... | collective-permute-start | bytes 491528 | tf_op jit(solution)/shard_map/ppermute | solution.py:960
  33.6 29.6 %collective-permute-start.2 = (bf16[512,512]{1,0:T(8,128)(2,1)S(1)}, bf16[512,512]{1,0:T(8,128)(2,1)S(1)}, u32[]{:S(2)}, u32[]{:S(2)}) collective-permute-start(bf16[512,512]{1,0:T(8,128)(2,1)S(1)} %copy-done.31), channel_id=1, source_target_pairs={{1,0},{2,1},{3,2},{4,7},{6,5},{7,6},{9,8},{10,9},{11,10},{12,15},{... | collective-permute-start | bytes 1572872 | tf_op jit(solution)/shard_map/ppermute | solution.py:1002
  37.1 26.1 %copy-start.20 = (bf16[16,2048]{1,0:T(8,128)(2,1)S(1)}, bf16[16,2048]{1,0:T(8,128)(2,1)}, u32[]{:S(2)}) copy-start(bf16[16,2048]{1,0:T(8,128)(2,1)} %param.26) | copy-start | bytes 196612
  37.1 26.9 %copy-start.21 = (bf16[64,512]{1,0:T(8,128)(2,1)S(1)}, bf16[64,512]{1,0:T(8,128)(2,1)}, u32[]{:S(2)}) copy-start(bf16[64,512]{1,0:T(8,128)(2,1)} %param.28) | copy-start | bytes 196612
  37.2 6.1 %collective-permute-start.8 = (bf16[2,80,512]{2,1,0:T(8,128)(2,1)S(1)}, bf16[2,80,512]{2,1,0:T(8,128)(2,1)S(1)}, u32[]{:S(2)}, u32[]{:S(2)}) collective-permute-start(bf16[2,80,512]{2,1,0:T(8,128)(2,1)S(1)} %get-tuple-element.268), channel_id=1, source_target_pairs={{0,16},{4,20},{8,24},{12,28},{16,0},{20,4},{24,8},{28,12},{1,17},{... | collective-permute-start | bytes 491528 | tf_op jit(solution)/shard_map/ppermute | solution.py:960
  37.8 10.0 %collective-permute-start.5 = (bf16[2,2,80,512]{3,2,1,0:T(8,128)(2,1)S(1)}, bf16[2,2,80,512]{3,2,1,0:T(8,128)(2,1)S(1)}, u32[]{:S(2)}, u32[]{:S(2)}) collective-permute-start(bf16[2,2,80,512]{3,2,1,0:T(8,128)(2,1)S(1)} %pad_maximum_fusion), channel_id=1, source_target_pairs={{0,16},{4,20},{8,24},{12,28},{16,0},{20,4},{24,8},{28,12},{1,17},{... | collective-permute-start | bytes 983048 | tf_op jit(solution)/shard_map/ppermute | solution.py:960
  43.3 8.4 %collective-permute-start.9 = (bf16[2,2,80,512]{3,2,1,0:T(8,128)(2,1)S(1)}, bf16[2,2,80,512]{3,2,1,0:T(8,128)(2,1)S(1)}, u32[]{:S(2)}, u32[]{:S(2)}) collective-permute-start(bf16[2,2,80,512]{3,2,1,0:T(8,128)(2,1)S(1)} %pad_maximum_fusion.1), channel_id=1, source_target_pairs={{0,8},{4,12},{8,0},{12,4},{16,24},{20,28},{24,16},{28,20},{1,9},{5... | collective-permute-start | bytes 983048 | tf_op jit(solution)/shard_map/ppermute | solution.py:960
  63.2 3.0 collective-permute-start.10
  76.7 36.9 %collective-permute-start.11 = (bf16[512,512]{1,0:T(8,128)(2,1)}, bf16[512,512]{1,0:T(8,128)(2,1)S(1)}, u32[]{:S(2)}, u32[]{:S(2)}) collective-permute-start(bf16[512,512]{1,0:T(8,128)(2,1)} %get-tuple-element.164), channel_id=1, source_target_pairs={{0,1},{1,2},{3,0},{4,5},{5,6},{6,7},{8,9},{9,10},{11,8},{12,13},{1... | collective-permute-start | bytes 1572872 | tf_op jit(solution)/shard_map/ppermute | solution.py:1002
  78.6 35.0 %collective-permute-start.12 = (bf16[512,512]{1,0:T(8,128)(2,1)}, bf16[512,512]{1,0:T(8,128)(2,1)S(1)}, u32[]{:S(2)}, u32[]{:S(2)}) collective-permute-start(bf16[512,512]{1,0:T(8,128)(2,1)} %get-tuple-element.165), channel_id=1, source_target_pairs={{0,2},{2,0},{3,1},{4,6},{5,7},{7,5},{8,10},{10,8},{11,9},{12,14},{... | collective-permute-start | bytes 1572872 | tf_op jit(solution)/shard_map/ppermute | solution.py:1002
  79.9 38.3 %collective-permute-start.13 = (bf16[512,512]{1,0:T(8,128)(2,1)}, bf16[512,512]{1,0:T(8,128)(2,1)S(1)}, u32[]{:S(2)}, u32[]{:S(2)}) collective-permute-start(bf16[512,512]{1,0:T(8,128)(2,1)} %get-tuple-element.166), channel_id=1, source_target_pairs={{1,0},{2,1},{3,2},{4,7},{6,5},{7,6},{9,8},{10,9},{11,10},{12,15},{... | collective-permute-start | bytes 1572872 | tf_op jit(solution)/shard_map/ppermute | solution.py:1002
  84.5 33.8 %copy-start.30 = (bf16[512,512]{1,0:T(8,128)(2,1)S(1)}, bf16[512,512]{1,0:T(8,128)(2,1)}, u32[]{:S(2)}) copy-start(bf16[512,512]{1,0:T(8,128)(2,1)} %get-tuple-element.178) | copy-start | bytes 1572868
  84.5 35.7 %copy-start.29 = (bf16[512,512]{1,0:T(8,128)(2,1)S(1)}, bf16[512,512]{1,0:T(8,128)(2,1)}, u32[]{:S(2)}) copy-start(bf16[512,512]{1,0:T(8,128)(2,1)} %get-tuple-element.179) | copy-start | bytes 1572868
  84.5 37.0 %copy-start.28 = (bf16[512,512]{1,0:T(8,128)(2,1)S(1)}, bf16[512,512]{1,0:T(8,128)(2,1)}, u32[]{:S(2)}) copy-start(bf16[512,512]{1,0:T(8,128)(2,1)} %get-tuple-element.180) | copy-start | bytes 1572868
  118.3 46.6 %collective-permute-start.14 = (bf16[512,512]{1,0:T(8,128)(2,1)S(1)}, bf16[512,512]{1,0:T(8,128)(2,1)}, u32[]{:S(2)}, u32[]{:S(2)}) collective-permute-start(bf16[512,512]{1,0:T(8,128)(2,1)S(1)} %copy-done.30), channel_id=1, source_target_pairs={{0,1},{1,2},{3,0},{4,5},{5,6},{6,7},{8,9},{9,10},{11,8},{12,13},{1... | collective-permute-start | bytes 1572872 | tf_op jit(solution)/shard_map/ppermute | solution.py:1002
  120.2 44.6 %collective-permute-start.15 = (bf16[512,512]{1,0:T(8,128)(2,1)S(1)}, bf16[512,512]{1,0:T(8,128)(2,1)}, u32[]{:S(2)}, u32[]{:S(2)}) collective-permute-start(bf16[512,512]{1,0:T(8,128)(2,1)S(1)} %copy-done.29), channel_id=1, source_target_pairs={{0,2},{2,0},{3,1},{4,6},{5,7},{7,5},{8,10},{10,8},{11,9},{12,14},{... | collective-permute-start | bytes 1572872 | tf_op jit(solution)/shard_map/ppermute | solution.py:1002
  121.5 52.3 %collective-permute-start.16 = (bf16[512,512]{1,0:T(8,128)(2,1)S(1)}, bf16[512,512]{1,0:T(8,128)(2,1)}, u32[]{:S(2)}, u32[]{:S(2)}) collective-permute-start(bf16[512,512]{1,0:T(8,128)(2,1)S(1)} %copy-done.28), channel_id=1, source_target_pairs={{1,0},{2,1},{3,2},{4,7},{6,5},{7,6},{9,8},{10,9},{11,10},{12,15},{... | collective-permute-start | bytes 1572872 | tf_op jit(solution)/shard_map/ppermute | solution.py:1002
  238.7 9.2 %collective-permute-start.17 = (bf16[16,128,512]{2,1,0:T(8,128)(2,1)}, bf16[16,128,512]{2,1,0:T(8,128)(2,1)}, u32[]{:S(2)}, u32[]{:S(2)}) collective-permute-start(bf16[16,128,512]{2,1,0:T(8,128)(2,1)} %get-tuple-element.185), channel_id=1, source_target_pairs={{0,4},{4,0},{8,12},{12,8},{16,20},{20,16},{24,28},{28,24},{1,5},{5... | collective-permute-start | bytes 6291464 | tf_op jit(solution)/shard_map/ppermute | solution.py:960
  241.1 74.0 %all-to-all-start = ((bf16[4,512,512]{2,1,0:T(8,128)(2,1)}), bf16[4,512,512]{2,1,0:T(8,128)(2,1)S(1)}, u32[]{:S(2)}, u32[]{:S(2)}) async-start(bf16[4,512,512]{2,1,0:T(8,128)(2,1)} %bitcast.76), calls=%async_computation | async-start | bytes 4194304 | tf_op jit(solution)/shard_map/all_to_all | solution.py:1007
  251.9 45.7 %collective-permute-start.18 = (bf16[2,2,128,512]{3,2,1,0:T(8,128)(2,1)}, bf16[2,2,128,512]{3,2,1,0:T(8,128)(2,1)S(1)}, u32[]{:S(2)}, u32[]{:S(2)}) collective-permute-start(bf16[2,2,128,512]{3,2,1,0:T(8,128)(2,1)} %get-tuple-element.186), channel_id=1, source_target_pairs={{0,8},{4,12},{8,0},{12,4},{16,24},{20,28},{24,16},{28,20},{1,9},{5... | collective-permute-start | bytes 1572872 | tf_op jit(solution)/shard_map/ppermute | solution.py:960
  251.9 45.7 %collective-permute-start.19 = (bf16[2,2,128,512]{3,2,1,0:T(8,128)(2,1)}, bf16[2,2,128,512]{3,2,1,0:T(8,128)(2,1)S(1)}, u32[]{:S(2)}, u32[]{:S(2)}) collective-permute-start(bf16[2,2,128,512]{3,2,1,0:T(8,128)(2,1)} %get-tuple-element.197), channel_id=1, source_target_pairs={{0,16},{4,20},{8,24},{12,28},{16,0},{20,4},{24,8},{28,12},{1,17},{... | collective-permute-start | bytes 1572872 | tf_op jit(solution)/shard_map/ppermute | solution.py:960
  301.2 41.3 %collective-permute-start.20 = (bf16[2,128,512]{2,1,0:T(8,128)(2,1)}, bf16[2,128,512]{2,1,0:T(8,128)(2,1)S(1)}, u32[]{:S(2)}, u32[]{:S(2)}) collective-permute-start(bf16[2,128,512]{2,1,0:T(8,128)(2,1)} %get-tuple-element.204), channel_id=1, source_target_pairs={{0,16},{4,20},{8,24},{12,28},{16,0},{20,4},{24,8},{28,12},{1,17},{... | collective-permute-start | bytes 786440 | tf_op jit(solution)/shard_map/ppermute | solution.py:960
  307.8 34.6 %collective-permute-start.21 = (bf16[2,128,512]{2,1,0:T(8,128)(2,1)}, bf16[2,128,512]{2,1,0:T(8,128)(2,1)S(1)}, u32[]{:S(2)}, u32[]{:S(2)}) collective-permute-start(bf16[2,128,512]{2,1,0:T(8,128)(2,1)} %get-tuple-element.209), channel_id=1, source_target_pairs={{0,8},{4,12},{8,0},{12,4},{16,24},{20,28},{24,16},{28,20},{1,9},{5... | collective-permute-start | bytes 786440 | tf_op jit(solution)/shard_map/ppermute | solution.py:960
  335.7 65.2 %all-to-all-start.1 = ((bf16[4,512,512]{2,1,0:T(8,128)(2,1)}), bf16[4,512,512]{2,1,0:T(8,128)(2,1)S(1)}, u32[]{:S(2)}, u32[]{:S(2)}) async-start(bf16[4,512,512]{2,1,0:T(8,128)(2,1)} %bitcast.75), calls=%async_computation.1 | async-start | bytes 4194304 | tf_op jit(solution)/shard_map/all_to_all | solution.py:1007
  345.5 51.7 %collective-permute-start.22 = (bf16[128,512]{1,0:T(8,128)(2,1)}, bf16[128,512]{1,0:T(8,128)(2,1)S(1)}, u32[]{:S(2)}, u32[]{:S(2)}) collective-permute-start(bf16[128,512]{1,0:T(8,128)(2,1)} %get-tuple-element.224), channel_id=1, source_target_pairs={{0,1},{1,2},{2,3},{3,0},{4,5},{5,6},{6,7},{7,4},{8,9},{9,10},{10,1... | collective-permute-start | bytes 393224 | tf_op jit(solution)/shard_map/ppermute | solution.py:966
  347.0 52.1 %collective-permute-start.23 = (bf16[128,512]{1,0:T(8,128)(2,1)}, bf16[128,512]{1,0:T(8,128)(2,1)S(1)}, u32[]{:S(2)}, u32[]{:S(2)}) collective-permute-start(bf16[128,512]{1,0:T(8,128)(2,1)} %get-tuple-element.225), channel_id=1, source_target_pairs={{0,2},{1,3},{2,0},{3,1},{4,6},{5,7},{6,4},{7,5},{8,10},{9,11},{10,... | collective-permute-start | bytes 393224 | tf_op jit(solution)/shard_map/ppermute | solution.py:966
  347.9 53.0 %collective-permute-start.24 = (bf16[128,512]{1,0:T(8,128)(2,1)}, bf16[128,512]{1,0:T(8,128)(2,1)S(1)}, u32[]{:S(2)}, u32[]{:S(2)}) collective-permute-start(bf16[128,512]{1,0:T(8,128)(2,1)} %get-tuple-element.226), channel_id=1, source_target_pairs={{0,3},{1,0},{2,1},{3,2},{4,7},{5,4},{6,5},{7,6},{8,11},{9,8},{10,9... | collective-permute-start | bytes 393224 | tf_op jit(solution)/shard_map/ppermute | solution.py:966
  349.9 45.8 %copy-start.22 = (f32[8,512]{1,0:T(8,128)S(1)}, f32[8,512]{1,0:T(8,128)}, u32[]{:S(2)}) copy-start(f32[8,512]{1,0:T(8,128)} %get-tuple-element.231) | copy-start | bytes 49156
  349.9 45.9 %copy-start.23 = (f32[8,512]{1,0:T(8,128)S(1)}, f32[8,512]{1,0:T(8,128)}, u32[]{:S(2)}) copy-start(f32[8,512]{1,0:T(8,128)} %get-tuple-element.232) | copy-start | bytes 49156
  415.6 7.7 %collective-permute-start.25 = (bf16[16,144,512]{2,1,0:T(8,128)(2,1)}, bf16[16,144,512]{2,1,0:T(8,128)(2,1)}, u32[]{:S(2)}, u32[]{:S(2)}) collective-permute-start(bf16[16,144,512]{2,1,0:T(8,128)(2,1)} %get-tuple-element.236), channel_id=1, source_target_pairs={{0,4},{4,0},{8,12},{12,8},{16,20},{20,16},{24,28},{28,24},{1,5},{5... | collective-permute-start | bytes 7077896 | tf_op jit(solution)/shard_map/ppermute | solution.py:960
  415.7 53.4 %all-to-all-start.2 = ((bf16[4,512,512]{2,1,0:T(8,128)(2,1)}), bf16[4,512,512]{2,1,0:T(8,128)(2,1)S(1)}, u32[]{:S(2)}, u32[]{:S(2)}) async-start(bf16[4,512,512]{2,1,0:T(8,128)(2,1)} %bitcast.77), calls=%async_computation.2 | async-start | bytes 4194304 | tf_op jit(solution)/shard_map/all_to_all | solution.py:1007
  427.5 16.6 %collective-permute-start.27 = (bf16[2,2,144,512]{3,2,1,0:T(8,128)(2,1)}, bf16[2,2,144,512]{3,2,1,0:T(8,128)(2,1)S(1)}, u32[]{:S(2)}, u32[]{:S(2)}) collective-permute-start(bf16[2,2,144,512]{3,2,1,0:T(8,128)(2,1)} %get-tuple-element.246), channel_id=1, source_target_pairs={{0,16},{4,20},{8,24},{12,28},{16,0},{20,4},{24,8},{28,12},{1,17},{... | collective-permute-start | bytes 1769480 | tf_op jit(solution)/shard_map/ppermute | solution.py:960
  430.6 14.9 %collective-permute-start.26 = (bf16[2,2,144,512]{3,2,1,0:T(8,128)(2,1)}, bf16[2,2,144,512]{3,2,1,0:T(8,128)(2,1)S(1)}, u32[]{:S(2)}, u32[]{:S(2)}) collective-permute-start(bf16[2,2,144,512]{3,2,1,0:T(8,128)(2,1)} %get-tuple-element.238), channel_id=1, source_target_pairs={{0,8},{4,12},{8,0},{12,4},{16,24},{20,28},{24,16},{28,20},{1,9},{5... | collective-permute-start | bytes 1769480 | tf_op jit(solution)/shard_map/ppermute | solution.py:960
  449.1 25.0 %collective-permute-start.29 = (bf16[2,144,512]{2,1,0:T(8,128)(2,1)}, bf16[2,144,512]{2,1,0:T(8,128)(2,1)S(1)}, u32[]{:S(2)}, u32[]{:S(2)}) collective-permute-start(bf16[2,144,512]{2,1,0:T(8,128)(2,1)} %get-tuple-element.252), channel_id=1, source_target_pairs={{0,8},{4,12},{8,0},{12,4},{16,24},{20,28},{24,16},{28,20},{1,9},{5... | collective-permute-start | bytes 884744 | tf_op jit(solution)/shard_map/ppermute | solution.py:960
  450.3 32.7 %copy-start.5 = (f32[128,512]{1,0:T(8,128)S(1)}, f32[128,512]{1,0:T(8,128)}, u32[]{:S(2)}) copy-start(f32[128,512]{1,0:T(8,128)} %route_four.1) | copy-start | bytes 786436
  450.3 23.8 %collective-permute-start.28 = (bf16[2,144,512]{2,1,0:T(8,128)(2,1)}, bf16[2,144,512]{2,1,0:T(8,128)(2,1)S(1)}, u32[]{:S(2)}, u32[]{:S(2)}) collective-permute-start(bf16[2,144,512]{2,1,0:T(8,128)(2,1)} %get-tuple-element.247), channel_id=1, source_target_pairs={{0,16},{4,20},{8,24},{12,28},{16,0},{20,4},{24,8},{28,12},{1,17},{... | collective-permute-start | bytes 884744 | tf_op jit(solution)/shard_map/ppermute | solution.py:960
  470.4 27.3 %copy-start.1 = (s32[3,1,4]{2,1,0:T(1,128)S(1)}, s32[3,1,4]{2,1,0:T(1,128)}, u32[]{:S(2)}) copy-start(s32[3,1,4]{2,1,0:T(1,128)} %param.23) | copy-start | bytes 148
  477.3 8.2 %collective-permute-start.30 = (bf16[144,512]{1,0:T(8,128)(2,1)}, bf16[144,512]{1,0:T(8,128)(2,1)S(1)}, u32[]{:S(2)}, u32[]{:S(2)}) collective-permute-start(bf16[144,512]{1,0:T(8,128)(2,1)} %get-tuple-element.254), channel_id=1, source_target_pairs={{0,1},{1,2},{2,3},{3,0},{4,5},{5,6},{6,7},{7,4},{8,9},{9,10},{10,1... | collective-permute-start | bytes 442376 | tf_op jit(solution)/shard_map/ppermute | solution.py:966
  478.7 13.4 %collective-permute-start.31 = (bf16[144,512]{1,0:T(8,128)(2,1)}, bf16[144,512]{1,0:T(8,128)(2,1)S(1)}, u32[]{:S(2)}, u32[]{:S(2)}) collective-permute-start(bf16[144,512]{1,0:T(8,128)(2,1)} %get-tuple-element.255), channel_id=1, source_target_pairs={{0,2},{1,3},{2,0},{3,1},{4,6},{5,7},{6,4},{7,5},{8,10},{9,11},{10,... | collective-permute-start | bytes 442376 | tf_op jit(solution)/shard_map/ppermute | solution.py:966
  482.9 12.3 %collective-permute-start.32 = (bf16[144,512]{1,0:T(8,128)(2,1)}, bf16[144,512]{1,0:T(8,128)(2,1)S(1)}, u32[]{:S(2)}, u32[]{:S(2)}) collective-permute-start(bf16[144,512]{1,0:T(8,128)(2,1)} %get-tuple-element.256), channel_id=1, source_target_pairs={{0,3},{1,0},{2,1},{3,2},{4,7},{5,4},{6,5},{7,6},{8,11},{9,8},{10,9... | collective-permute-start | bytes 442376 | tf_op jit(solution)/shard_map/ppermute | solution.py:966
  (27 other events, 191.9 us)
Sparse Core Ops, SparseCore 0:
  11.5 69.2 all-gather.4
  84.4 87.8 all-gather.6
